TPU v7x, 32 devices: a whole 2x2x4 slice. The times are simulated.
32 devices in a mesh: dp: 4 (over y, x), expert: 8 (over z, core).
Axes of the slice: x: 2, y: 2, z: 4, core: 2. Of those that a mesh axis runs over, the one named last changes fastest.
Arguments:
- tokens: bfloat16 [64, 128, 1536], P('dp', 'expert'), may hold values from -6 to 6
- cotangent: bfloat16 [64, 128, 1536], P('dp', 'expert'), may hold values from -6 to 6
- lengths: int32 [64, 4], P('dp'), may hold values from 0 to 128, as said below
- placement: int32 [64], P('dp'), may hold values from 0 to 15, as said below
- routes: int32 [8192, 4], P(('dp', 'expert')), may hold values from 0 to 15, all different within a row
- priority: int32 [8192, 4], P(('dp', 'expert')), may hold values from 0 to 1023, as said below
- g_attn: bfloat16 [1536], P(('dp', 'expert')), may hold values from 0.099609375 to 1.8984375
- w_query: bfloat16 [1536, 1536], P(('dp', 'expert')), may hold values from -0.15625 to 0.15625
- key_projection: bfloat16 [1536, 256], P(('dp', 'expert')), may hold values from -0.15625 to 0.15625
- value_projection: bfloat16 [1536, 256], P(('dp', 'expert')), may hold values from -0.15625 to 0.15625
- w_out: bfloat16 [1536, 1536], P(('dp', 'expert')), may hold values from -1.25 to 1.25
- g_moe: bfloat16 [1536], P(('dp', 'expert')), may hold values from 0.099609375 to 1.8984375
- w_router: bfloat16 [1536, 16], P(('dp', 'expert')), may hold values from -0.078125 to 0.078125
- w_gate: bfloat16 [16, 1536, 768], P('expert', 'dp'), may hold values from -0.15625 to 0.15625
- w_up: bfloat16 [16, 1536, 768], P('expert', 'dp'), may hold values from -0.15625 to 0.15625
- w_down: bfloat16 [16, 768, 1536], P('expert', None, 'dp'), may hold values from -0.625 to 0.625
Outputs:
- output: bfloat16 [64, 128, 1536], P('dp', 'expert')
- input_grad: bfloat16 [64, 128, 1536], P('dp', 'expert')
- grad_g_attn: float32 [1536], P(('dp', 'expert'))
- grad_query: float32 [1536, 1536], P(('dp', 'expert'))
- grad_key: float32 [1536, 256], P(('dp', 'expert'))
- value_weight_gradient: float32 [1536, 256], P(('dp', 'expert'))
- grad_out: float32 [1536, 1536], P(('dp', 'expert'))
- grad_g_moe: float32 [1536], P(('dp', 'expert'))
- grad_router: float32 [1536, 16], P(('dp', 'expert'))
- grad_gate: float32 [16, 1536, 768], P('expert', 'dp')
- grad_up: float32 [16, 1536, 768], P('expert', 'dp')
- grad_down: float32 [16, 768, 1536], P('expert', None, 'dp')
Inputs may be any that keep to these rules, and one draw needn't show every extreme that they name: `lengths`: each row sums to 128; zeros are empty documents. In every group of 16 sequences of one index of dp, some sequence is one document of 128. `placement`: each aligned group of 16 entries (the sequences of one index of dp) is a permutation of 0 to 15. `routes`: each row names 4 different experts. `priority`: the entries of each aligned block of 256 rows (one device) are a permutation of 0 to 1023.
All inputs are finite; a program needn't handle non-finite values.
Results may differ from a plain program's by a relative error of at most 0.015.
The roundings to bfloat16 on the way count: a program that leaves them out, or rounds other values in their place, can miss the bound.
Values may be sent and summed in bfloat16 or wider, within the bound.
No kernel may reach another device: no remote copies, remote signals or barrier semaphores. Data moves between devices by JAX's collectives and lax.ppermute only.
A program may use at most 192 MiB of HBM per device.

v0:
```python
import math

import jax
import jax.numpy as jnp
from jax import lax
from jax.sharding import PartitionSpec as P

QUERY_HEADS = 12
KEY_VALUE_HEADS = 2
HEAD_SIZE = 128
TOPK = 4
SEQ_DEV = 2


EPSILON = 1e-06
ROPE_BASE = 1000000.0
NEG_FILL = -1e30


def contract(left, right, left_dims, right_dims):
    return lax.dot_general(
        left, right, ((left_dims, right_dims), ((), ())), preferred_element_type=jnp.float32
    )


def sequence_layout(doc_lens, seq_len):
    token_steps = jnp.arange(seq_len, dtype=jnp.int32)
    doc_ends = jnp.cumsum(doc_lens)
    doc_index = jnp.sum((token_steps[:, None] >= doc_ends[None, :-1]).astype(jnp.int32), axis=1)
    doc_starts = doc_ends - doc_lens
    doc_slots = jnp.arange(doc_lens.shape[0], dtype=jnp.int32)
    start_of = jnp.sum(
        jnp.where(doc_slots[None, :] == doc_index[:, None], doc_starts[None, :], 0), axis=1
    )
    return ((token_steps - start_of).astype(jnp.float32), doc_index)


def device_layout(dev_lens, seq_len):
    positions, doc_index = jax.vmap(lambda single: sequence_layout(single, seq_len))(dev_lens)
    doc_count = dev_lens.shape[1]
    labels = doc_index + doc_count * jnp.arange(dev_lens.shape[0], dtype=jnp.int32)[:, None]
    return (positions.reshape(-1), labels.reshape(-1))


def rope_tables(positions, head_dim):
    freq_index = jnp.arange(head_dim // 2, dtype=jnp.float32)
    frequency = jnp.exp(freq_index * (-2.0 / head_dim) * math.log(ROPE_BASE))
    angle_table = positions[:, None] * frequency[None, :]
    return (jnp.cos(angle_table), jnp.sin(angle_table))


def apply_rotation(values, cosine_table, sine_values):
    half_size = values.shape[-1] // 2
    first_half = values[..., :half_size]
    second_half = values[..., half_size:]
    cos_wide = cosine_table[:, None, :]
    sin_wide = sine_values[:, None, :]
    return jnp.concatenate(
        [
            first_half * cos_wide - second_half * sin_wide,
            second_half * cos_wide + first_half * sin_wide,
        ],
        axis=-1,
    )


def rotate_back(values, cosine_table, sine_values):
    half_size = values.shape[-1] // 2
    first_half = values[..., :half_size]
    second_half = values[..., half_size:]
    cos_wide = cosine_table[:, None, :]
    sin_wide = sine_values[:, None, :]
    return jnp.concatenate(
        [
            first_half * cos_wide + second_half * sin_wide,
            second_half * cos_wide - first_half * sin_wide,
        ],
        axis=-1,
    )


def slot_ranks(route_flat, prio_flat, expert_count):
    pair_count = route_flat.shape[0]
    by_priority = (
        jnp.zeros((pair_count,), jnp.int32)
        .at[prio_flat]
        .set(jnp.arange(pair_count, dtype=jnp.int32))
    )
    sorted_experts = route_flat[by_priority]
    one_hot = (
        sorted_experts[:, None] == jnp.arange(expert_count, dtype=jnp.int32)[None, :]
    ).astype(jnp.int32)
    running = jnp.cumsum(one_hot, axis=0)
    sorted_rank = jnp.sum(running * one_hot, axis=1) - 1
    return sorted_rank[prio_flat]


def norm_back(inputs, inverse, gain, grad_normed):
    scaled = grad_normed * gain
    grad_gain = jnp.sum(grad_normed * inputs * inverse, axis=0)
    grad_inputs = inverse * scaled - inputs * inverse**3 * jnp.mean(
        scaled * inputs, axis=-1, keepdims=True
    )
    return (grad_gain, grad_inputs)


def body(
    tokens,
    cotangent,
    lengths,
    placement,
    routes,
    priority,
    g_attn,
    w_query,
    key_projection,
    value_projection,
    w_out,
    g_moe,
    w_router,
    w_gate,
    w_up,
    w_down,
):
    row_seqs, piece_len, width = tokens.shape
    expert_devices = lax.axis_size("expert")
    my_index = lax.axis_index("expert")
    seq_len = piece_len * expert_devices
    token_count = SEQ_DEV * seq_len
    query_group_width = QUERY_HEADS // KEY_VALUE_HEADS
    score_scale = HEAD_SIZE ** (-0.5)
    code_list = jnp.arange(row_seqs, dtype=jnp.int32)
    source = jnp.sum(
        jnp.where(placement[:, None] == code_list[None, :], code_list[:, None], 0), axis=0
    )
    send_tokens = tokens[source].reshape(expert_devices, SEQ_DEV, piece_len, width)
    send_grads = cotangent[source].reshape(expert_devices, SEQ_DEV, piece_len, width)
    got_tokens, got_grads = (
        lax.all_to_all(send_tokens, "expert", split_axis=0, concat_axis=2, tiled=True),
        lax.all_to_all(send_grads, "expert", split_axis=0, concat_axis=2, tiled=True),
    )
    x_local = got_tokens.reshape(token_count, width).astype(jnp.float32)
    dy_local = got_grads.reshape(token_count, width).astype(jnp.float32)
    own_seqs = lax.dynamic_slice_in_dim(source, my_index * SEQ_DEV, SEQ_DEV)
    positions, labels = device_layout(lengths[own_seqs], seq_len)
    cosine_table, sine_values = rope_tables(positions, HEAD_SIZE)
    token_steps = jnp.arange(token_count, dtype=jnp.int32)
    allowed = jnp.logical_and(
        labels[:, None] == labels[None, :], token_steps[:, None] >= token_steps[None, :]
    )
    attn_weights = (
        lax.all_gather(g_attn, ("dp", "expert"), axis=0, tiled=True),
        lax.all_gather(w_query, ("dp", "expert"), axis=0, tiled=True),
        lax.all_gather(key_projection, ("dp", "expert"), axis=0, tiled=True),
        lax.all_gather(value_projection, ("dp", "expert"), axis=0, tiled=True),
        lax.all_gather(w_out, ("dp", "expert"), axis=0, tiled=True),
        lax.all_gather(g_moe, ("dp", "expert"), axis=0, tiled=True),
        lax.all_gather(w_router, ("dp", "expert"), axis=0, tiled=True),
    )
    expert_weights = (
        lax.all_gather(w_gate, "dp", axis=1, tiled=True),
        lax.all_gather(w_up, "dp", axis=1, tiled=True),
        lax.all_gather(w_down, "dp", axis=2, tiled=True),
    )
    gain_attn, query_full, key_full, value_full, out_full, gain_moe, router_full = attn_weights
    gate_full, up_full, down_full = expert_weights
    gain_attn = gain_attn.astype(jnp.float32)
    gain_moe = gain_moe.astype(jnp.float32)
    inv_attn = lax.rsqrt(jnp.mean(x_local * x_local, axis=-1, keepdims=True) + EPSILON)
    normed_attn = (x_local * inv_attn * gain_attn).astype(jnp.bfloat16)
    query_raw = jnp.dot(normed_attn, query_full, preferred_element_type=jnp.float32)
    key_unrotated = jnp.dot(normed_attn, key_full, preferred_element_type=jnp.float32)
    value_low = (
        jnp.dot(normed_attn, value_full, preferred_element_type=jnp.float32)
        .astype(jnp.bfloat16)
        .reshape(token_count, KEY_VALUE_HEADS, HEAD_SIZE)
    )
    query_rotated = (
        apply_rotation(
            query_raw.reshape(token_count, QUERY_HEADS, HEAD_SIZE), cosine_table, sine_values
        )
        .astype(jnp.bfloat16)
        .reshape(token_count, KEY_VALUE_HEADS, query_group_width, HEAD_SIZE)
    )
    key_rotated = apply_rotation(
        key_unrotated.reshape(token_count, KEY_VALUE_HEADS, HEAD_SIZE), cosine_table, sine_values
    ).astype(jnp.bfloat16)

    def masked_scores():
        raw_scores = (
            jnp.einsum(
                "qhgd,khd->hgqk", query_rotated, key_rotated, preferred_element_type=jnp.float32
            )
            * score_scale
        )
        return jnp.where(allowed, raw_scores, NEG_FILL)

    scores = masked_scores()
    score_top = jnp.max(scores, axis=-1, keepdims=True)
    exp_scores = jnp.exp(scores - score_top)
    totals = jnp.sum(exp_scores, axis=-1, keepdims=True)
    attn_probs = exp_scores / totals
    log_totals = score_top + jnp.log(totals)
    mixed_heads = jnp.einsum(
        "hgqk,khd->qhgd",
        attn_probs.astype(jnp.bfloat16),
        value_low,
        preferred_element_type=jnp.float32,
    )
    mixed_low = mixed_heads.reshape(token_count, QUERY_HEADS * HEAD_SIZE).astype(jnp.bfloat16)
    residual = x_local + jnp.dot(mixed_low, out_full, preferred_element_type=jnp.float32)
    inv_moe = lax.rsqrt(jnp.mean(residual * residual, axis=-1, keepdims=True) + EPSILON)
    normed_moe = (residual * inv_moe * gain_moe).astype(jnp.bfloat16)
    expert_count = router_full.shape[1]
    per_device = expert_count // expert_devices
    logits = jnp.dot(normed_moe, router_full, preferred_element_type=jnp.float32)
    selector = (
        routes[:, :, None] == jnp.arange(expert_count, dtype=jnp.int32)[None, None, :]
    ).astype(jnp.float32)
    chosen = jnp.sum(selector * logits[:, None, :], axis=-1)
    gates = jax.nn.softmax(chosen, axis=-1)
    capacity = (9 * token_count * TOPK + 64 * expert_count - 1) // (64 * expert_count) * 8
    route_flat = routes.reshape(-1)
    ranks = slot_ranks(route_flat, priority.reshape(-1), expert_count)
    dummy_row = expert_count * capacity
    slot_rows = jnp.where(ranks < capacity, route_flat * capacity + ranks, dummy_row)
    pair_token = jnp.arange(token_count * TOPK, dtype=jnp.int32) // TOPK
    outbound = (
        jnp.zeros((dummy_row + 1, width), jnp.bfloat16).at[slot_rows].set(normed_moe[pair_token])
    )
    outbound = outbound[:dummy_row].reshape(expert_devices, per_device, capacity, width)
    inbound = lax.all_to_all(outbound, "expert", split_axis=0, concat_axis=0, tiled=True)
    pre_gate = jnp.einsum("slcd,ldf->slcf", inbound, gate_full, preferred_element_type=jnp.float32)
    pre_up = jnp.einsum("slcd,ldf->slcf", inbound, up_full, preferred_element_type=jnp.float32)
    activated, gelu_pull = jax.vjp(jax.nn.gelu, pre_gate)
    hidden = (activated * pre_up).astype(jnp.bfloat16)
    expert_out = jnp.einsum(
        "slcf,lfd->slcd", hidden, down_full, preferred_element_type=jnp.float32
    ).astype(jnp.bfloat16)
    returned = lax.all_to_all(expert_out, "expert", split_axis=0, concat_axis=0, tiled=True)
    out_table = jnp.concatenate(
        [returned.reshape(dummy_row, width), jnp.zeros((1, width), jnp.bfloat16)], axis=0
    )
    pair_out = out_table[slot_rows].reshape(token_count, TOPK, width)
    final = residual
    for choice_index in range(TOPK):
        final = final + gates[:, choice_index : choice_index + 1] * pair_out[
            :, choice_index
        ].astype(jnp.float32)
    out_low = final.astype(jnp.bfloat16)
    back_attn = (
        lax.all_gather(g_attn, ("dp", "expert"), axis=0, tiled=True),
        lax.all_gather(w_query, ("dp", "expert"), axis=0, tiled=True),
        lax.all_gather(key_projection, ("dp", "expert"), axis=0, tiled=True),
        lax.all_gather(value_projection, ("dp", "expert"), axis=0, tiled=True),
        lax.all_gather(w_out, ("dp", "expert"), axis=0, tiled=True),
        lax.all_gather(g_moe, ("dp", "expert"), axis=0, tiled=True),
        lax.all_gather(w_router, ("dp", "expert"), axis=0, tiled=True),
    )
    back_expert = (
        lax.all_gather(w_gate, "dp", axis=1, tiled=True),
        lax.all_gather(w_up, "dp", axis=1, tiled=True),
        lax.all_gather(w_down, "dp", axis=2, tiled=True),
    )
    query_back, key_back, value_back, out_back, router_back = (
        back_attn[1],
        back_attn[2],
        back_attn[3],
        back_attn[4],
        back_attn[6],
    )
    gate_back, up_back, down_back = back_expert
    grad_pair = jnp.sum(dy_local[:, None, :] * pair_out.astype(jnp.float32), axis=-1)
    grad_chosen = gates * (grad_pair - jnp.sum(gates * grad_pair, axis=-1, keepdims=True))
    grad_logits = jnp.sum(selector * grad_chosen[:, :, None], axis=1).astype(jnp.bfloat16)
    grad_router = contract(normed_moe, grad_logits, (0,), (0,))
    grad_normed_moe = contract(grad_logits, router_back, (1,), (1,))
    pair_grad = (
        (gates[:, :, None] * dy_local[:, None, :])
        .astype(jnp.bfloat16)
        .reshape(token_count * TOPK, width)
    )
    grad_table = jnp.zeros((dummy_row + 1, width), jnp.bfloat16).at[slot_rows].set(pair_grad)
    grad_table = grad_table[:dummy_row].reshape(expert_devices, per_device, capacity, width)
    grad_inbound = lax.all_to_all(grad_table, "expert", split_axis=0, concat_axis=0, tiled=True)
    grad_down = jnp.einsum(
        "slcf,slcd->lfd", hidden, grad_inbound, preferred_element_type=jnp.float32
    )
    grad_hidden = jnp.einsum(
        "slcd,lfd->slcf", grad_inbound, down_back, preferred_element_type=jnp.float32
    )
    grad_pre_gate = gelu_pull(grad_hidden * pre_up)[0].astype(jnp.bfloat16)
    grad_pre_up = (grad_hidden * activated).astype(jnp.bfloat16)
    grad_gate = jnp.einsum(
        "slcd,slcf->ldf", inbound, grad_pre_gate, preferred_element_type=jnp.float32
    )
    grad_up = jnp.einsum("slcd,slcf->ldf", inbound, grad_pre_up, preferred_element_type=jnp.float32)
    grad_inputs = jnp.einsum(
        "slcf,ldf->slcd", grad_pre_gate, gate_back, preferred_element_type=jnp.float32
    )
    grad_inputs = (
        grad_inputs
        + jnp.einsum("slcf,ldf->slcd", grad_pre_up, up_back, preferred_element_type=jnp.float32)
    ).astype(jnp.bfloat16)
    grad_back = lax.all_to_all(grad_inputs, "expert", split_axis=0, concat_axis=0, tiled=True)
    grad_rows_table = jnp.concatenate(
        [grad_back.reshape(dummy_row, width), jnp.zeros((1, width), jnp.bfloat16)], axis=0
    )
    grad_rows = grad_rows_table[slot_rows].reshape(token_count, TOPK, width)
    for choice_index in range(TOPK):
        grad_normed_moe = grad_normed_moe + grad_rows[:, choice_index].astype(jnp.float32)
    grad_gain_moe, grad_through = norm_back(residual, inv_moe, gain_moe, grad_normed_moe)
    grad_residual = dy_local + grad_through
    grad_attn = grad_residual.astype(jnp.bfloat16)
    grad_out = contract(mixed_low, grad_attn, (0,), (0,))
    grad_mixed = (
        contract(grad_attn, out_back, (1,), (1,))
        .astype(jnp.bfloat16)
        .reshape(token_count, KEY_VALUE_HEADS, query_group_width, HEAD_SIZE)
    )
    probs_again = jnp.exp(masked_scores() - log_totals)
    grad_probs = jnp.einsum(
        "qhgd,khd->hgqk", grad_mixed, value_low, preferred_element_type=jnp.float32
    )
    value_weight_gradient = jnp.einsum(
        "hgqk,qhgd->khd",
        probs_again.astype(jnp.bfloat16),
        grad_mixed,
        preferred_element_type=jnp.float32,
    )
    inner_sum = jnp.sum(probs_again * grad_probs, axis=-1, keepdims=True)
    grad_scores = (probs_again * (grad_probs - inner_sum)).astype(jnp.bfloat16)
    grad_query_rot = (
        jnp.einsum("hgqk,khd->qhgd", grad_scores, key_rotated, preferred_element_type=jnp.float32)
        * score_scale
    )
    grad_key_rot = (
        jnp.einsum("hgqk,qhgd->khd", grad_scores, query_rotated, preferred_element_type=jnp.float32)
        * score_scale
    )
    grad_query_low = (
        rotate_back(
            grad_query_rot.reshape(token_count, QUERY_HEADS, HEAD_SIZE), cosine_table, sine_values
        )
        .reshape(token_count, QUERY_HEADS * HEAD_SIZE)
        .astype(jnp.bfloat16)
    )
    grad_key_low = (
        rotate_back(grad_key_rot, cosine_table, sine_values)
        .reshape(token_count, KEY_VALUE_HEADS * HEAD_SIZE)
        .astype(jnp.bfloat16)
    )
    value_gradient_narrow = value_weight_gradient.reshape(
        token_count, KEY_VALUE_HEADS * HEAD_SIZE
    ).astype(jnp.bfloat16)
    grad_query = contract(normed_attn, grad_query_low, (0,), (0,))
    grad_key = contract(normed_attn, grad_key_low, (0,), (0,))
    grad_value_w = contract(normed_attn, value_gradient_narrow, (0,), (0,))
    grad_normed_attn = contract(grad_query_low, query_back, (1,), (1,))
    grad_normed_attn = grad_normed_attn + contract(grad_key_low, key_back, (1,), (1,))
    grad_normed_attn = grad_normed_attn + contract(value_gradient_narrow, value_back, (1,), (1,))
    grad_gain_attn, grad_through_attn = norm_back(x_local, inv_attn, gain_attn, grad_normed_attn)
    grad_x = (grad_residual + grad_through_attn).astype(jnp.bfloat16)
    owned_grads = (
        lax.psum_scatter(grad_gain_attn, ("dp", "expert"), scatter_dimension=0, tiled=True),
        lax.psum_scatter(grad_query, ("dp", "expert"), scatter_dimension=0, tiled=True),
        lax.psum_scatter(grad_key, ("dp", "expert"), scatter_dimension=0, tiled=True),
        lax.psum_scatter(grad_value_w, ("dp", "expert"), scatter_dimension=0, tiled=True),
        lax.psum_scatter(grad_out, ("dp", "expert"), scatter_dimension=0, tiled=True),
        lax.psum_scatter(grad_gain_moe, ("dp", "expert"), scatter_dimension=0, tiled=True),
        lax.psum_scatter(grad_router, ("dp", "expert"), scatter_dimension=0, tiled=True),
    )
    owned_expert = (
        lax.psum_scatter(
            grad_gate.astype(jnp.bfloat16), "dp", scatter_dimension=1, tiled=True
        ).astype(jnp.float32),
        lax.psum_scatter(
            grad_up.astype(jnp.bfloat16), "dp", scatter_dimension=1, tiled=True
        ).astype(jnp.float32),
        lax.psum_scatter(
            grad_down.astype(jnp.bfloat16), "dp", scatter_dimension=2, tiled=True
        ).astype(jnp.float32),
    )
    back_out, back_grad = (
        lax.all_to_all(
            out_low.reshape(1, SEQ_DEV, seq_len, width),
            "expert",
            split_axis=2,
            concat_axis=0,
            tiled=True,
        ),
        lax.all_to_all(
            grad_x.reshape(1, SEQ_DEV, seq_len, width),
            "expert",
            split_axis=2,
            concat_axis=0,
            tiled=True,
        ),
    )
    output = back_out.reshape(row_seqs, piece_len, width)[placement]
    input_grad = back_grad.reshape(row_seqs, piece_len, width)[placement]
    return (
        output,
        input_grad,
        owned_grads[0],
        owned_grads[1],
        owned_grads[2],
        owned_grads[3],
        owned_grads[4],
        owned_grads[5],
        owned_grads[6],
        owned_expert[0],
        owned_expert[1],
        owned_expert[2],
    )


def solution(mesh):
    return jax.shard_map(
        body,
        mesh=mesh,
        in_specs=(
            P("dp", "expert", None),
            P("dp", "expert", None),
            P("dp", None),
            P("dp"),
            P(("dp", "expert"), None),
            P(("dp", "expert"), None),
            P(("dp", "expert")),
            P(("dp", "expert"), None),
            P(("dp", "expert"), None),
            P(("dp", "expert"), None),
            P(("dp", "expert"), None),
            P(("dp", "expert")),
            P(("dp", "expert"), None),
            P("expert", "dp", None),
            P("expert", "dp", None),
            P("expert", None, "dp"),
        ),
        out_specs=(
            P("dp", "expert", None),
            P("dp", "expert", None),
            P(("dp", "expert")),
            P(("dp", "expert"), None),
            P(("dp", "expert"), None),
            P(("dp", "expert"), None),
            P(("dp", "expert"), None),
            P(("dp", "expert")),
            P(("dp", "expert"), None),
            P("expert", "dp", None),
            P("expert", "dp", None),
            P("expert", None, "dp"),
        ),
        check_vma=False,
    )
```

profile of v0, /device:TPU:0, one launch (start us, length us, event | category | flops | bytes accessed | tf_op | source)
XLA Modules:
  0.0 1287.6 jit_solution(1909468668480972249)
XLA Ops:
  11.7 6.3 all-to-all-start
  19.4 43.5 %all-reduce.7 = (bf16[1536]{0:T(1024)(128)(2,1)S(1)}, bf16[1536]{0:T(1024)(128)(2,1)S(1)}) all-reduce(bf16[1536]{0:T(1024)(128)(2,1)S(1)} %dynamic-update-slice, bf16[1536]{0:T(1024)(128)(2,1)S(1)} %dynamic-update-slice.1), channel_id=1, replica_groups=mesh['dp'=4,'expert'=8] {'dp','expert'}, use_global_device_ids=true, to_apply=%add.2 | all-reduce | flops 3072 | bytes 12288
  64.1 45.4 %all_gather.40 = bf16[1536,256]{1,0:T(8,128)(2,1)S(1)} all-gather(bf16[48,256]{1,0:T(8,128)(2,1)S(1)} %copy-done.43), channel_id=1, replica_groups=mesh['dp'=4,'expert'=8] {'dp','expert'}, dimensions={0}, use_global_device_ids=true | all-gather | bytes 811008 | tf_op jit(solution)/shard_map/all_gather | solution.py:154
  110.5 4.3 scatter_custom_fusion
  114.8 4.5 gather_fusion.2
  119.4 4.5 reduce-window.6
  124.7 4.5 gather_fusion.3
  130.9 43.3 %all_gather.39 = bf16[1536,256]{1,0:T(8,128)(2,1)S(1)} all-gather(bf16[48,256]{1,0:T(8,128)(2,1)S(1)} %copy-done.44), channel_id=1, replica_groups=mesh['dp'=4,'expert'=8] {'dp','expert'}, dimensions={0}, use_global_device_ids=true | all-gather | bytes 811008 | tf_op jit(solution)/shard_map/all_gather | solution.py:155
  176.2 6.7 copy.264
  182.9 4.0 fusion.112
  194.4 4.1 multiply_reduce_fusion.3
  199.8 18.6 %scatter_custom_fusion.1 = bf16[1153,1536]{1,0:T(8,128)(2,1)} fusion(s32[1024]{0:T(1024)S(1)} %bitcast.371, bf16[256,1536]{1,0:T(8,128)(2,1)S(1)} %multiply_convert_fusion.2, s32[1024]{0:T(1024)} %broadcast_clamp_fusion.1, bf16[]{:T(256)} %constant.26.clone.1), kind=kCustom, calls=%fused_computation.59 | custom fusion | bytes 3542528 | tf_op jit(solution)/shard_map/scatter | solution.py:229
  218.4 4.5 slice.127
  222.9 4.6 all-to-all-start.1
  229.7 77.8 %all-to-all-done.1 = bf16[8,2,72,1536]{3,2,1,0:T(8,128)(2,1)} async-done(((bf16[8,2,72,1536]{3,2,1,0:T(8,128)(2,1)}), bf16[8,2,72,1536]{3,2,1,0:T(8,128)(2,1)}, u32[]{:S(2)}, u32[]{:S(2)}) %all-to-all-start.1) | async-done | bytes 3538976 | tf_op jit(solution)/shard_map/all_to_all | solution.py:232
  307.5 4.0 all-to-all-start.4
  311.5 8.1 fusion.6
  319.5 10.2 fusion.25
  329.7 5.8 fusion.28
  337.6 5.2 all-to-all-start.2
  342.8 109.7 %all-gather = bf16[32,48,16]{1,2,0:T(8,128)(2,1)S(1)} all-gather(bf16[1,48,16]{1,2,0:T(8,128)(2,1)S(1)} %bitcast.383), channel_id=1, replica_groups=mesh['dp'=4,'expert'=8] {'dp','expert'}, dimensions={0}, use_global_device_ids=true | all-gather | bytes 50688 | tf_op jit(solution)/shard_map/all_gather | solution.py:158
  453.1 3.7 mul.533
  456.8 7.9 mul.540
  465.1 4.0 concatenate.29
  469.1 9.8 gather_fusion.4
  478.9 6.1 reshape.605
  485.0 3.6 multiply_reduce_fusion
  489.0 9.2 scatter_custom_fusion.2
  498.2 4.0 slice.135
  502.1 4.5 all-to-all-start.5
  508.6 80.5 %all-to-all-done.5 = bf16[8,2,72,1536]{3,2,1,0:T(8,128)(2,1)} async-done(((bf16[8,2,72,1536]{3,2,1,0:T(8,128)(2,1)}), bf16[8,2,72,1536]{3,2,1,0:T(8,128)(2,1)}, u32[]{:S(2)}, u32[]{:S(2)}) %all-to-all-start.5) | async-done | bytes 3538976 | tf_op jit(solution)/shard_map/all_to_all | solution.py:285
  589.1 8.7 bitcast_convert_fusion
  597.8 12.5 copy.330
  610.3 5.5 copy.341
  615.8 11.7 fusion.23
  628.8 8.6 bitcast_convert_fusion.2
  637.4 5.7 fusion
  643.2 5.8 fusion.31
  649.0 2.2 copy.290
  651.1 4.5 all-to-all-start.6
  655.9 8.8 bitcast_convert_fusion.1
  664.7 11.9 fusion.108
  676.6 59.0 %all-to-all-done.6 = bf16[8,2,72,1536]{3,2,1,0:T(8,128)(2,1)} async-done(((bf16[8,2,72,1536]{3,2,1,0:T(8,128)(2,1)}), bf16[8,2,72,1536]{3,2,1,0:T(8,128)(2,1)}, u32[]{:S(2)}, u32[]{:S(2)}) %all-to-all-start.6) | async-done | bytes 3538976 | tf_op jit(solution)/shard_map/all_to_all | solution.py:305
  735.6 4.0 concatenate.30
  739.6 9.7 gather_fusion.7
  749.4 6.2 reshape.611
  755.6 10.5 fusion.107
  769.0 2.2 subtract_add_fusion
  774.1 2.9 fusion.35
  782.0 2.7 fusion.83
  787.9 5.1 fusion.115
  794.6 5.0 fusion.86
  802.5 4.5 all-to-all-start.3
  806.9 3.9 fusion.114
  815.3 12.6 all-to-all-done.3
  827.9 3.5 all-to-all-start.7
  832.9 41.2 %all-reduce.6 = (f32[1536]{0:T(1024)S(1)}, f32[1536]{0:T(1024)S(1)}) all-reduce(f32[1536]{0:T(1024)S(1)} %get-tuple-element.14, f32[1536]{0:T(1024)S(1)} %copy-done.45), channel_id=2, replica_groups=mesh['dp'=4,'expert'=8] {'dp','expert'}, use_global_device_ids=true, to_apply=%region_24.25.clone | all-reduce | flops 3072 | bytes 24576
  879.7 2.9 reshape.759
  886.1 2.8 convert_element_type.316
  889.0 2.9 convert_element_type.318
  891.8 3.9 reduce-scatter.15.cloned.1.call-done
  895.7 101.9 %reduce-scatter.17.cloned.1.call-done = f32[48,256]{1,0:T(8,128)} async-done(((f32[1536,256]{1,0:T(8,128)}), f32[48,256]{1,0:T(8,128)}) %reduce-scatter.17.cloned.1.call-update) | async-done | bytes 49168 | tf_op jit(solution)/shard_map/reduce_scatter | solution.py:368
  997.7 140.9 %reduce-scatter.13.cloned.1.call-done = f32[48,1536]{1,0:T(8,128)} async-done(((f32[1536,1536]{1,0:T(8,128)}), f32[48,1536]{1,0:T(8,128)}) %reduce-scatter.13.cloned.1.call-update) | async-done | bytes 294928 | tf_op jit(solution)/shard_map/reduce_scatter | solution.py:366
  1138.6 142.2 %reduce-scatter.19.cloned.1.call-done = f32[48,1536]{1,0:T(8,128)} async-done(((f32[1536,1536]{1,0:T(8,128)}), f32[48,1536]{1,0:T(8,128)}) %reduce-scatter.19.cloned.1.call-update) | async-done | bytes 294928 | tf_op jit(solution)/shard_map/reduce_scatter | solution.py:369
  (272 shorter events, 63.0 us)
Async XLA Ops:
  7.2 3.1 copy-start
  7.2 11.5 copy-start.40
  7.2 11.7 copy-start.50
  7.2 11.9 copy-start.51
  7.2 55.7 %copy-start.49 = (s32[16,4]{0,1:T(4,128)S(1)}, s32[16,4]{0,1:T(4,128)}, u32[]{:S(2)}) copy-start(s32[16,4]{0,1:T(4,128)} %param.18) | copy-start | bytes 772
  7.2 56.8 %copy-start.43 = (bf16[48,256]{1,0:T(8,128)(2,1)S(1)}, bf16[48,256]{1,0:T(8,128)(2,1)}, u32[]{:S(2)}) copy-start(bf16[48,256]{1,0:T(8,128)(2,1)} %param.24) | copy-start | bytes 73732
  7.2 169.0 %all-gather.7.cloned.1.call-start = ((), (), s32[]{:S(2)}) async-start(), calls=%async_computation.16 | async-start | bytes 4866048 | tf_op jit(solution)/shard_map/all_gather | solution.py:153
  8.0 186.4 %all-gather.9.cloned.1.call-start = ((), (), s32[]{:S(2)}) async-start(), calls=%async_computation.17 | async-start | bytes 4866048 | tf_op jit(solution)/shard_map/all_gather | solution.py:156
  8.7 302.7 %all-gather.11.cloned.1.call-start = ((), (), s32[]{:S(2)}) async-start(), calls=%async_computation.18 | async-start | bytes 5898240 | tf_op jit(solution)/shard_map/all_gather | solution.py:161
  10.2 8.6 copy-start.46
  10.3 99.6 %copy-start.47 = (s32[256,4]{0,1:T(4,128)S(1)}, s32[256,4]{0,1:T(4,128)}, u32[]{:S(2)}) copy-start(s32[256,4]{0,1:T(4,128)} %param.21) | copy-start | bytes 12292
  11.7 162.5 %all-to-all-start = ((bf16[8,2,16,1536]{3,2,1,0:T(8,128)(2,1)}), bf16[8,2,16,1536]{3,2,1,0:T(8,128)(2,1)S(1)}, u32[]{:S(2)}, u32[]{:S(2)}) async-start(bf16[8,2,16,1536]{3,2,1,0:T(8,128)(2,1)} %bitcast.2), calls=%async_computation | async-start | bytes 1572864 | tf_op jit(solution)/shard_map/all_to_all | solution.py:139
  18.1 301.5 %all-gather.13.cloned.1.call-start = ((), (), s32[]{:S(2)}) async-start(), calls=%async_computation.19 | async-start | bytes 5898240 | tf_op jit(solution)/shard_map/all_gather | solution.py:162
  62.9 112.4 %copy-start.36 = (f32[1536]{0:T(1024)}, f32[1536]{0:T(1024)S(1)}, u32[]{:S(2)}) copy-start(f32[1536]{0:T(1024)S(1)} %convert_element_type.257) | copy-start | bytes 18436
  109.8 88.7 %copy-start.38 = (f32[1536]{0:T(1024)}, f32[1536]{0:T(1024)S(1)}, u32[]{:S(2)}) copy-start(f32[1536]{0:T(1024)S(1)} %convert_element_type.269) | copy-start | bytes 18436
  119.4 11.5 copy-start.44
  130.9 56.0 %copy-start.25 = (f32[256,64]{0,1:T(8,128)}, f32[256,64]{0,1:T(8,128)S(1)}, u32[]{:S(2)}) copy-start(f32[256,64]{0,1:T(8,128)S(1)} %get-tuple-element.46) | copy-start | bytes 196612
  130.9 56.0 %copy-start.27 = (f32[256,64]{0,1:T(8,128)}, f32[256,64]{0,1:T(8,128)S(1)}, u32[]{:S(2)}) copy-start(f32[256,64]{0,1:T(8,128)S(1)} %get-tuple-element.47) | copy-start | bytes 196612
  174.2 1.8 copy-start.4
  174.8 8.1 copy-start.6
  175.3 14.7 %copy-start.32 = (bf16[256,2,64]{0,2,1:T(8,128)(2,1)}, bf16[256,2,64]{0,2,1:T(8,128)(2,1)S(1)}, u32[]{:S(2)}) copy-start(bf16[256,2,64]{0,2,1:T(8,128)(2,1)S(1)} %get-tuple-element.40) | copy-start | bytes 196612
  175.3 14.7 %copy-start.33 = (bf16[256,2,64]{0,2,1:T(8,128)(2,1)}, bf16[256,2,64]{0,2,1:T(8,128)(2,1)S(1)}, u32[]{:S(2)}) copy-start(bf16[256,2,64]{0,2,1:T(8,128)(2,1)S(1)} %get-tuple-element.41) | copy-start | bytes 196612
  176.0 16.4 %copy-start.34 = (bf16[256,256]{0,1:T(8,128)(2,1)}, bf16[256,256]{0,1:T(8,128)(2,1)S(1)}, u32[]{:S(2)}) copy-start(bf16[256,256]{0,1:T(8,128)(2,1)S(1)} %convolution_convert_fusion.1) | copy-start | bytes 393220
  188.3 4.1 copy-start.12
  190.0 2.4 copy-start.14
  191.9 1.7 copy-start.2
  194.4 4.1 copy-start.29
  222.9 5.2 copy-start.31
  222.9 84.6 %all-to-all-start.1 = ((bf16[8,2,72,1536]{3,2,1,0:T(8,128)(2,1)}), bf16[8,2,72,1536]{3,2,1,0:T(8,128)(2,1)}, u32[]{:S(2)}, u32[]{:S(2)}) async-start(bf16[8,2,72,1536]{3,2,1,0:T(8,128)(2,1)} %bitcast.340), calls=%async_computation.1 | async-start | bytes 7077888 | tf_op jit(solution)/shard_map/all_to_all | solution.py:232
  227.5 102.2 %all-gather.15.cloned.1.call-start = ((), (), s32[]{:S(2)}) async-start(), calls=%async_computation.20 | async-start | bytes 5898240 | tf_op jit(solution)/shard_map/all_gather | solution.py:163
  307.5 30.1 %all-to-all-start.4 = ((bf16[8,2,16,1536]{3,2,1,0:T(8,128)(2,1)}), bf16[8,2,16,1536]{3,2,1,0:T(8,128)(2,1)S(1)}, u32[]{:S(2)}, u32[]{:S(2)}) async-start(bf16[8,2,16,1536]{3,2,1,0:T(8,128)(2,1)} %bitcast.57), calls=%async_computation.4 | async-start | bytes 1572864 | tf_op jit(solution)/shard_map/all_to_all | solution.py:140
  337.6 5.2 copy-start.48
  337.6 127.5 %all-to-all-start.2 = ((bf16[8,2,72,1536]{3,2,1,0:T(8,128)(2,1)}), bf16[8,2,72,1536]{3,2,1,0:T(8,128)(2,1)}, u32[]{:S(2)}, u32[]{:S(2)}) async-start(bf16[8,2,72,1536]{3,2,1,0:T(8,128)(2,1)} %copy.277), calls=%async_computation.2 | async-start | bytes 7077888 | tf_op jit(solution)/shard_map/all_to_all | solution.py:240
  502.1 87.0 %all-to-all-start.5 = ((bf16[8,2,72,1536]{3,2,1,0:T(8,128)(2,1)}), bf16[8,2,72,1536]{3,2,1,0:T(8,128)(2,1)}, u32[]{:S(2)}, u32[]{:S(2)}) async-start(bf16[8,2,72,1536]{3,2,1,0:T(8,128)(2,1)} %bitcast.339), calls=%async_computation.5 | async-start | bytes 7077888 | tf_op jit(solution)/shard_map/all_to_all | solution.py:285
  506.6 324.9 %reduce-scatter.25.cloned.1.call-start = ((), (), s32[]{:S(2)}) async-start(), calls=%async_computation.27 | async-start | bytes 811008
  508.1 371.5 %reduce-scatter.27.cloned.1.call-start = ((), (), s32[]{:S(2)}) async-start(), calls=%async_computation.28 | async-start | bytes 5898240
  615.8 270.3 %reduce-scatter.21.cloned.1.call-start = ((), (), s32[]{:S(2)}) async-start(), calls=%async_computation.25 | async-start | bytes 5898240 | tf_op jit(solution)/shard_map/reduce_scatter | solution.py:374
  637.4 5.8 copy-start.54
  651.1 84.5 %all-to-all-start.6 = ((bf16[8,2,72,1536]{3,2,1,0:T(8,128)(2,1)}), bf16[8,2,72,1536]{3,2,1,0:T(8,128)(2,1)}, u32[]{:S(2)}, u32[]{:S(2)}) async-start(bf16[8,2,72,1536]{3,2,1,0:T(8,128)(2,1)} %copy.290), calls=%async_computation.6 | async-start | bytes 7077888 | tf_op jit(solution)/shard_map/all_to_all | solution.py:305
  655.6 233.3 %reduce-scatter.23.cloned.1.call-start = ((), (), s32[]{:S(2)}) async-start(), calls=%async_computation.26 | async-start | bytes 5898240 | tf_op jit(solution)/shard_map/reduce_scatter | solution.py:377
  664.7 231.1 %reduce-scatter.15.cloned.1.call-start = ((), (), s32[]{:S(2)}) async-start(), calls=%async_computation.22 | async-start | bytes 1622016 | tf_op jit(solution)/shard_map/reduce_scatter | solution.py:367
  755.6 10.5 copy-start.23
  755.6 10.5 copy-start.39
  766.1 1.5 copy-start.18
  766.1 1.9 copy-start.19
  766.1 2.4 copy-start.20
  766.1 2.9 copy-start.21
  766.1 6.3 slice-start
  769.0 3.4 slice-start.1
  772.4 1.7 copy-start.35
  774.1 3.6 copy-start.3
  782.0 215.7 %reduce-scatter.17.cloned.1.call-start = ((), (), s32[]{:S(2)}) async-start(), calls=%async_computation.23 | async-start | bytes 1622016 | tf_op jit(solution)/shard_map/reduce_scatter | solution.py:368
  786.3 352.3 %reduce-scatter.13.cloned.1.call-start = ((), (), s32[]{:S(2)}) async-start(), calls=%async_computation.21 | async-start | bytes 9732096 | tf_op jit(solution)/shard_map/reduce_scatter | solution.py:366
  793.0 1.4 copy-start.9
  793.0 1.6 copy-start.30
  793.1 487.7 %reduce-scatter.19.cloned.1.call-start = ((), (), s32[]{:S(2)}) async-start(), calls=%async_computation.24 | async-start | bytes 9732096 | tf_op jit(solution)/shard_map/reduce_scatter | solution.py:369
  802.5 25.4 %all-to-all-start.3 = ((bf16[1,2,128,1536]{3,1,0,2:T(2,128)(2,1)}), bf16[1,2,128,1536]{3,1,0,2:T(2,128)(2,1)}, u32[]{:S(2)}, u32[]{:S(2)}) async-start(bf16[1,2,128,1536]{3,1,0,2:T(2,128)(2,1)} %copy.282), calls=%async_computation.3 | async-start | bytes 1572864 | tf_op jit(solution)/shard_map/all_to_all | solution.py:385
  806.9 3.9 copy-start.11
  810.9 1.4 copy-start.17
  810.9 1.4 copy-start.37
  813.1 18.4 %copy-start.52 = (s32[16]{0:T(128)S(1)}, s32[16]{0:T(128)}, u32[]{:S(2)}) copy-start(s32[16]{0:T(128)} %param.19) | copy-start | bytes 196
  813.1 19.9 %copy-start.45 = (f32[1536]{0:T(1024)S(1)}, f32[1536]{0:T(1024)}, u32[]{:S(2)}) copy-start(f32[1536]{0:T(1024)} %get-tuple-element.12) | copy-start | bytes 18436
  827.9 48.6 %all-to-all-start.7 = ((bf16[1,2,128,1536]{3,1,0,2:T(2,128)(2,1)}), bf16[1,2,128,1536]{3,1,0,2:T(2,128)(2,1)S(1)}, u32[]{:S(2)}, u32[]{:S(2)}) async-start(bf16[1,2,128,1536]{3,1,0,2:T(2,128)(2,1)} %copy.302), calls=%async_computation.7 | async-start | bytes 1572864 | tf_op jit(solution)/shard_map/all_to_all | solution.py:392
  884.6 396.2 %copy-start.1 = (bf16[16,16,1536]{2,1,0:T(8,128)(2,1)S(1)}, bf16[16,16,1536]{2,1,0:T(8,128)(2,1)}, u32[]{:S(2)}) copy-start(bf16[16,16,1536]{2,1,0:T(8,128)(2,1)} %param.16) | copy-start | bytes 2359300
  (14 other events, 15.2 us)
Sparse Core Ops, SparseCore 0:
  11.1 72.4 all-gather.6
  86.6 64.7 all-gather.8
  153.2 56.8 all-gather.10
  211.9 57.0 all-gather.12
  270.6 56.9 all-gather.14
  512.3 100.7 reduce-scatter.24
  616.1 56.1 reduce-scatter.26
  675.2 57.0 reduce-scatter.20
  735.3 57.0 reduce-scatter.22
  798.0 97.6 reduce-scatter.14
  901.6 96.0 reduce-scatter.16
  1004.0 134.5 reduce-scatter.12
  1146.1 134.6 reduce-scatter.18
where the time goes:
time: 1290 us
  waiting for transfers between devices  622 us (48%)
  blocking collectives  283 us (22%)
  local copies, waits for them, and re-layouts  179 us (14%)
  matrix products  116 us (9%)
  starting transfers between devices  38.2 us (3%)
  other arithmetic  34.4 us (3%)
  between operations  15.4 us (1%)
    reduce_scatter x1, waiting for transfers between devices, body(): lax.psum_scatter(grad_out, ('dp', 'expert'), scatter_dimension=0, tiled=T...  142 us
    reduce_scatter x1, waiting for transfers between devices, body(): lax.psum_scatter(grad_query, ('dp', 'expert'), scatter_dimension=0, tiled...  141 us
    all_gather x1, blocking collectives, body(): lax.all_gather(w_router, ('dp', 'expert'), axis=0, tiled=True)  110 us
    reduce_scatter x1, waiting for transfers between devices, body(): lax.psum_scatter(grad_value_w, ('dp', 'expert'), scatter_dimension=0, til...  102 us
    unnamed x2, blocking collectives  84.6 us
    all_to_all x1, waiting for transfers between devices, body(): lax.all_to_all(grad_table, 'expert', split_axis=0, concat_axis=0, tiled=T...  80.5 us
    all_to_all x1, waiting for transfers between devices, body(): lax.all_to_all(outbound, 'expert', split_axis=0, concat_axis=0, tiled=True)  77.8 us
    all_to_all x1, waiting for transfers between devices, body(): lax.all_to_all(grad_inputs, 'expert', split_axis=0, concat_axis=0, tiled=...  59 us
  transfers between devices with their start and end apart: 21, of which 8 were waited for; matrix products, arithmetic and copies ran while one was open for 22% of the time, Pallas kernels for 0%

commit v1 on v0

v1 whole, which is shorter than its diff:
```python
import math

import jax
import jax.numpy as jnp
from jax import lax
from jax.experimental import pallas as pl
from jax.experimental.pallas import tpu as pltpu
from jax.sharding import PartitionSpec as P

QUERY_HEADS = 12
KEY_VALUE_HEADS = 2
HEAD_SIZE = 128
TOPK = 4
SEQ_DEV = 2


EPSILON = 1e-06
ROPE_BASE = 1000000.0
NEG_FILL = -1e30


def contract(left, right, left_dims, right_dims):
    return lax.dot_general(
        left, right, ((left_dims, right_dims), ((), ())), preferred_element_type=jnp.float32
    )


def sequence_layout(doc_lens, seq_len):
    token_steps = jnp.arange(seq_len, dtype=jnp.int32)
    doc_ends = jnp.cumsum(doc_lens)
    doc_index = jnp.sum((token_steps[:, None] >= doc_ends[None, :-1]).astype(jnp.int32), axis=1)
    doc_starts = doc_ends - doc_lens
    doc_slots = jnp.arange(doc_lens.shape[0], dtype=jnp.int32)
    start_of = jnp.sum(
        jnp.where(doc_slots[None, :] == doc_index[:, None], doc_starts[None, :], 0), axis=1
    )
    return ((token_steps - start_of).astype(jnp.float32), doc_index)


def device_layout(dev_lens, seq_len):
    positions, doc_index = jax.vmap(lambda single: sequence_layout(single, seq_len))(dev_lens)
    doc_count = dev_lens.shape[1]
    labels = doc_index + doc_count * jnp.arange(dev_lens.shape[0], dtype=jnp.int32)[:, None]
    return (positions.reshape(-1), labels.reshape(-1))


def rope_tables(positions, head_dim):
    freq_index = jnp.arange(head_dim // 2, dtype=jnp.float32)
    frequency = jnp.exp(freq_index * (-2.0 / head_dim) * math.log(ROPE_BASE))
    angle_table = positions[:, None] * frequency[None, :]
    return (jnp.cos(angle_table), jnp.sin(angle_table))


def apply_rotation(values, cosine_table, sine_values):
    half_size = values.shape[-1] // 2
    first_half = values[..., :half_size]
    second_half = values[..., half_size:]
    cos_wide = cosine_table[:, None, :]
    sin_wide = sine_values[:, None, :]
    return jnp.concatenate(
        [
            first_half * cos_wide - second_half * sin_wide,
            second_half * cos_wide + first_half * sin_wide,
        ],
        axis=-1,
    )


def rotate_back(values, cosine_table, sine_values):
    half_size = values.shape[-1] // 2
    first_half = values[..., :half_size]
    second_half = values[..., half_size:]
    cos_wide = cosine_table[:, None, :]
    sin_wide = sine_values[:, None, :]
    return jnp.concatenate(
        [
            first_half * cos_wide + second_half * sin_wide,
            second_half * cos_wide - first_half * sin_wide,
        ],
        axis=-1,
    )


def slot_ranks(route_flat, prio_flat):
    same = route_flat[:, None] == route_flat[None, :]
    ahead = prio_flat[None, :] < prio_flat[:, None]
    return jnp.sum(jnp.logical_and(same, ahead).astype(jnp.int32), axis=1)


def norm_back(inputs, inverse, gain, grad_normed):
    scaled = grad_normed * gain
    grad_gain = jnp.sum(grad_normed * inputs * inverse, axis=0)
    grad_inputs = inverse * scaled - inputs * inverse**3 * jnp.mean(
        scaled * inputs, axis=-1, keepdims=True
    )
    return (grad_gain, grad_inputs)


def swap_x(value):
    return lax.ppermute(value, "dp", [(i, i ^ 1) for i in range(4)])


def swap_y(value):
    return lax.ppermute(value, "dp", [(i, i ^ 2) for i in range(4)])


def swap_core(value):
    return lax.ppermute(value, "expert", [(i, i ^ 1) for i in range(8)])


def shift_up(value):
    return lax.ppermute(value, "expert", [(i, (i + 2) % 8) for i in range(8)])


def shift_down(value):
    return lax.ppermute(value, "expert", [(i, (i + 6) % 8) for i in range(8)])


def halves(value, axis):
    size = value.shape[axis]
    step = {1: 128, 2: 16}.get(value.ndim - axis, 1)
    cut = size // 2 // step * step
    return (
        lax.slice_in_dim(value, 0, cut, axis=axis),
        lax.slice_in_dim(value, cut, size, axis=axis),
    )


def gather_z(value, axis):
    below = shift_up(value)
    above = shift_down(value)
    far = jnp.concatenate(
        [shift_up(halves(below, axis)[0]), shift_down(halves(above, axis)[1])], axis=axis
    )
    return [value, below, above, far]


def gather_plane(value, axis):
    from_x = swap_x(value)
    from_y = swap_y(value)
    far = jnp.concatenate(
        [swap_x(halves(from_y, axis)[0]), swap_y(halves(from_x, axis)[1])], axis=axis
    )
    return [value, from_x, from_y, far]


def add_low(left, right):
    return (left.astype(jnp.float32) + right.astype(jnp.float32)).astype(jnp.bfloat16)


def scatter_z(blocks, axis):
    own, to_below, to_above, far = blocks
    far_a, far_b = halves(far, axis)
    up_a, up_b = halves(to_above, axis)
    down_a, down_b = halves(to_below, axis)
    got_a = shift_up(far_a)
    got_b = shift_down(far_b)
    up_b = shift_up(up_b)
    down_a = shift_down(down_a)
    up_a = shift_up(add_low(up_a, got_a))
    down_b = shift_down(add_low(down_b, got_b))
    first = jnp.concatenate([up_a, up_b], axis=axis).astype(jnp.float32)
    second = jnp.concatenate([down_a, down_b], axis=axis).astype(jnp.float32)
    return own.astype(jnp.float32) + first + second


def scatter_plane(blocks, axis):
    own, to_x, to_y, far = blocks
    far_a, far_b = halves(far, axis)
    x_a, x_b = halves(to_x, axis)
    y_a, y_b = halves(to_y, axis)
    got_a = swap_x(far_a)
    got_b = swap_y(far_b)
    x_a = swap_x(x_a)
    y_b = swap_y(y_b)
    x_b = swap_x(add_low(x_b, got_b))
    y_a = swap_y(add_low(y_a, got_a))
    first = jnp.concatenate([x_a, x_b], axis=axis).astype(jnp.float32)
    second = jnp.concatenate([y_a, y_b], axis=axis).astype(jnp.float32)
    return own.astype(jnp.float32) + first + second


def any_spec():
    return pl.BlockSpec(memory_space=pl.ANY)


def smem_spec():
    return pl.BlockSpec(memory_space=pltpu.SMEM)


def staged(out_ref, hold, sems):
    pltpu.make_async_copy(hold, hold, sems.at[0]).wait()
    copy = pltpu.make_async_copy(hold, out_ref, sems.at[1])
    copy.start()
    copy.wait()


def place_kernel(index_ref, src_ref, out_ref, hold, sems):
    for j in range(src_ref.shape[0]):
        pltpu.make_async_copy(src_ref.at[j], hold.at[index_ref[j]], sems.at[0]).start()
    staged(out_ref, hold, sems)


def take_kernel(index_ref, src_ref, out_ref, hold, sems):
    for j in range(src_ref.shape[0]):
        pltpu.make_async_copy(src_ref.at[index_ref[j]], hold.at[j], sems.at[0]).start()
    staged(out_ref, hold, sems)


def deal_kernel(seq_ref, rel_ref, src_ref, out_ref, hold, sems):
    devices = out_ref.shape[0]
    piece = out_ref.shape[1] // SEQ_DEV // devices
    for b in range(devices):
        for k in range(SEQ_DEV):
            row = pl.multiple_of(seq_ref[b * SEQ_DEV + k] * piece, piece)
            for j in range(devices):
                pltpu.make_async_copy(
                    src_ref.at[rel_ref[j], pl.ds(row, piece), :],
                    hold.at[b, pl.ds((k * devices + j) * piece, piece), :],
                    sems.at[0],
                ).start()
    staged(out_ref, hold, sems)


def move_blocks(kernel, shape, scalars, arrays):
    dtype = arrays[0].dtype
    return pl.pallas_call(
        kernel,
        out_shape=jax.ShapeDtypeStruct(shape, dtype),
        in_specs=[smem_spec()] * len(scalars) + [any_spec()] * len(arrays),
        out_specs=any_spec(),
        scratch_shapes=[pltpu.VMEM(shape, dtype), pltpu.SemaphoreType.DMA((2,))],
        compiler_params=pltpu.CompilerParams(vmem_limit_bytes=40 * 1024 * 1024),
    )(*scalars, *arrays)


def join_kernel(axis, index_ref, own_ref, x_ref, y_ref, a_ref, b_ref, out_ref, hold, sems):
    me = index_ref[0]
    step = own_ref.shape[axis]

    def window(e, owner):
        start = pl.multiple_of(owner * step, step)
        if axis == 1:
            return hold.at[e, pl.ds(start, step), :]
        return hold.at[e, :, pl.ds(start, step)]

    for e in range(2):
        pltpu.make_async_copy(own_ref.at[e], window(e, me), sems.at[0]).start()
        pltpu.make_async_copy(x_ref.at[e], window(e, me ^ 1), sems.at[0]).start()
        pltpu.make_async_copy(y_ref.at[e], window(e, me ^ 2), sems.at[0]).start()
    pltpu.make_async_copy(a_ref.at[0], window(0, me ^ 3), sems.at[0]).start()
    pltpu.make_async_copy(b_ref.at[0], window(1, me ^ 3), sems.at[0]).start()
    staged(out_ref, hold, sems)


def gather_experts(value, axis, tuned):
    if not tuned:
        return lax.all_gather(value, "dp", axis=axis, tiled=True)
    from_x = swap_x(value)
    from_y = swap_y(value)
    far_a = swap_x(from_y[:1])
    far_b = swap_y(from_x[1:])
    shape = list(value.shape)
    shape[axis] *= 4
    index = lax.axis_index("dp").reshape(1)
    return move_blocks(
        lambda *refs: join_kernel(axis, *refs),
        tuple(shape),
        [index],
        [value, from_x, from_y, far_a, far_b],
    )


def scatter_experts(value, axis, tuned):
    if not tuned:
        return lax.psum_scatter(value, "dp", scatter_dimension=axis, tiled=True).astype(jnp.float32)
    me = lax.axis_index("dp")
    step = value.shape[axis] // 4
    blocks = [
        lax.dynamic_slice_in_dim(value, (me ^ k) * step, step, axis=axis) for k in range(4)
    ]
    own, to_x, to_y, far = blocks
    got_a = swap_x(far[:1])
    got_b = swap_y(far[1:])
    x_a = swap_x(to_x[:1])
    y_b = swap_y(to_y[1:])
    x_b = swap_x(add_low(to_x[1:], got_b))
    y_a = swap_y(add_low(to_y[:1], got_a))
    first = jnp.concatenate([x_a, x_b], axis=0).astype(jnp.float32)
    second = jnp.concatenate([y_a, y_b], axis=0).astype(jnp.float32)
    return own.astype(jnp.float32) + first + second


def expert_order(tuned, count):
    if not tuned:
        return jnp.arange(count, dtype=jnp.int32)
    me = lax.axis_index("expert")
    level, core = me // 2, me % 2
    order = [
        ((level + off) % 4) * 2 + (core + flip) % 2 for flip in range(2) for off in (0, 3, 1, 2)
    ]
    return jnp.stack(order).astype(jnp.int32)


def gather_expert_axis(value, tuned):
    if not tuned:
        return lax.all_gather(value, "expert", axis=0, tiled=False)
    parts = jnp.stack(gather_z(value, 0))
    return jnp.concatenate([parts, swap_core(parts)], axis=0)


def scatter_expert_axis(blocks, tuned):
    if not tuned:
        return lax.psum_scatter(blocks, "expert", scatter_dimension=0, tiled=False).astype(
            jnp.float32
        )
    mine = add_low(blocks[:4], swap_core(blocks[4:]))
    return scatter_z([mine[0], mine[1], mine[2], mine[3]], 0)


def all_order():
    me = lax.axis_index("expert")
    plane = lax.axis_index("dp")
    level, core = me // 2, me % 2
    order = [
        ((plane ^ k) * 4 + (level + off) % 4) * 2 + (core + flip) % 2
        for flip in range(2)
        for k in range(4)
        for off in (0, 3, 1, 2)
    ]
    return jnp.stack(order).astype(jnp.int32)


def gather_all(value, tuned):
    if not tuned:
        return lax.all_gather(value, ("dp", "expert"), axis=0, tiled=True)
    level = jnp.stack(gather_z(value, 1))
    parts = jnp.stack(gather_plane(level, 0))
    parts = jnp.stack([parts, swap_core(parts)])
    parts = parts.reshape((32,) + value.shape)
    placed = move_blocks(place_kernel, parts.shape, [all_order()], [parts])
    return placed.reshape(32 * value.shape[0], value.shape[1])


def scatter_all(value, tuned):
    if not tuned:
        return lax.psum_scatter(value, ("dp", "expert"), scatter_dimension=0, tiled=True).astype(
            jnp.float32
        )
    rows = value.shape[0] // 32
    parts = value.reshape(32, rows, value.shape[1])
    parts = move_blocks(take_kernel, parts.shape, [all_order()], [parts])
    parts = parts.reshape(2, 4, 4, rows, value.shape[1])
    mine = add_low(parts[0], swap_core(parts[1]))
    level = scatter_plane([mine[0], mine[1], mine[2], mine[3]], 0).astype(jnp.bfloat16)
    return scatter_z([level[0], level[1], level[2], level[3]], 1)


def pad_columns(value, width):
    return jnp.pad(value, ((0, 0), (0, width - value.shape[1])))


def body(
    tokens,
    cotangent,
    lengths,
    placement,
    routes,
    priority,
    g_attn,
    w_query,
    key_projection,
    value_projection,
    w_out,
    g_moe,
    w_router,
    w_gate,
    w_up,
    w_down,
):
    row_seqs, piece_len, width = tokens.shape
    expert_devices = lax.axis_size("expert")
    tuned = expert_devices == 8 and lax.axis_size("dp") == 4
    my_index = lax.axis_index("expert")
    seq_len = piece_len * expert_devices
    token_count = SEQ_DEV * seq_len
    query_group_width = QUERY_HEADS // KEY_VALUE_HEADS
    query_width = w_query.shape[1]
    kv_width = key_projection.shape[1]
    expert_count = w_router.shape[1]
    per_device = expert_count // expert_devices
    capacity = (9 * token_count * TOPK + 64 * expert_count - 1) // (64 * expert_count) * 8
    score_scale = HEAD_SIZE ** (-0.5)
    code_list = jnp.arange(row_seqs, dtype=jnp.int32)
    source = jnp.sum(
        jnp.where(placement[:, None] == code_list[None, :], code_list[:, None], 0), axis=0
    )
    send_tokens = tokens[source].reshape(expert_devices, SEQ_DEV, piece_len, width)
    got_tokens = lax.all_to_all(send_tokens, "expert", split_axis=0, concat_axis=2, tiled=True)
    x_local = got_tokens.reshape(token_count, width).astype(jnp.float32)
    pack_in = jnp.concatenate(
        [w_query, key_projection, value_projection, pad_columns(g_attn[:, None], 128)], axis=1
    )
    pack_out = jnp.concatenate(
        [w_out, pad_columns(jnp.concatenate([w_router, g_moe[:, None]], axis=1), 128)], axis=1
    )
    full_in = gather_all(pack_in, tuned)
    full_out = gather_all(pack_out, tuned)
    query_full = full_in[:, :query_width]
    key_full = full_in[:, query_width : query_width + kv_width]
    value_full = full_in[:, query_width + kv_width : query_width + 2 * kv_width]
    gain_attn = full_in[:, query_width + 2 * kv_width].astype(jnp.float32)
    out_full = full_out[:, :width]
    router_full = full_out[:, width : width + expert_count]
    gain_moe = full_out[:, width + expert_count].astype(jnp.float32)
    ranks = slot_ranks(routes.reshape(-1), priority.reshape(-1)).reshape(token_count, TOPK)
    codes = jnp.minimum(ranks, capacity) + 1
    expert_list = jnp.arange(expert_count, dtype=jnp.int32)
    picks = routes[None, :, :] == expert_list[:, None, None]
    code_table = jnp.sum(jnp.where(picks, codes[None], 0), axis=2)
    table_rows = -(-expert_count // 16) * 16
    table = jnp.zeros((table_rows, width), jnp.bfloat16)
    table = table.at[:expert_count, :token_count].set(code_table.astype(jnp.bfloat16))
    early = jnp.concatenate([cotangent.reshape(token_count, width), table], axis=0)
    early_all = gather_expert_axis(early, tuned)
    order = expert_order(tuned, expert_devices)
    rel_of = jnp.zeros((expert_devices,), jnp.int32)
    for b in range(expert_devices):
        rel_of = jnp.where(jnp.arange(expert_devices) == order[b], b, rel_of)
    seqs = source.reshape(expert_devices, SEQ_DEV)[order].reshape(-1)
    if piece_len % 16 == 0:
        shape = (expert_devices, token_count, width)
        grads_all = move_blocks(deal_kernel, shape, [seqs, rel_of], [early_all])
    else:
        pieces = early_all[:, :token_count].reshape(expert_devices, row_seqs, piece_len, width)
        pieces = pieces[rel_of][:, seqs].reshape(
            expert_devices, expert_devices, SEQ_DEV, piece_len, width
        )
        grads_all = pieces.transpose(1, 2, 0, 3, 4).reshape(expert_devices, token_count, width)
    codes_all = early_all[:, token_count : token_count + expert_count, :token_count].astype(
        jnp.int32
    )
    own_codes = lax.dynamic_slice_in_dim(codes_all, my_index * per_device, per_device, axis=1)
    dy_local = grads_all[rel_of[my_index]].astype(jnp.float32)
    gate_full = gather_experts(w_gate, 1, tuned)
    up_full = gather_experts(w_up, 1, tuned)
    down_full = gather_experts(w_down, 2, tuned)

    own_seqs = lax.dynamic_slice_in_dim(source, my_index * SEQ_DEV, SEQ_DEV)
    positions, labels = device_layout(lengths[own_seqs], seq_len)
    cosine_table, sine_values = rope_tables(positions, HEAD_SIZE)
    token_steps = jnp.arange(token_count, dtype=jnp.int32)
    allowed = jnp.logical_and(
        labels[:, None] == labels[None, :], token_steps[:, None] >= token_steps[None, :]
    )
    inv_attn = lax.rsqrt(jnp.mean(x_local * x_local, axis=-1, keepdims=True) + EPSILON)
    normed_attn = (x_local * inv_attn * gain_attn).astype(jnp.bfloat16)
    query_raw = jnp.dot(normed_attn, query_full, preferred_element_type=jnp.float32)
    key_unrotated = jnp.dot(normed_attn, key_full, preferred_element_type=jnp.float32)
    value_low = (
        jnp.dot(normed_attn, value_full, preferred_element_type=jnp.float32)
        .astype(jnp.bfloat16)
        .reshape(token_count, KEY_VALUE_HEADS, HEAD_SIZE)
    )
    query_rotated = (
        apply_rotation(
            query_raw.reshape(token_count, QUERY_HEADS, HEAD_SIZE), cosine_table, sine_values
        )
        .astype(jnp.bfloat16)
        .reshape(token_count, KEY_VALUE_HEADS, query_group_width, HEAD_SIZE)
    )
    key_rotated = apply_rotation(
        key_unrotated.reshape(token_count, KEY_VALUE_HEADS, HEAD_SIZE), cosine_table, sine_values
    ).astype(jnp.bfloat16)

    def masked_scores():
        raw_scores = (
            jnp.einsum(
                "qhgd,khd->hgqk", query_rotated, key_rotated, preferred_element_type=jnp.float32
            )
            * score_scale
        )
        return jnp.where(allowed, raw_scores, NEG_FILL)

    scores = masked_scores()
    score_top = jnp.max(scores, axis=-1, keepdims=True)
    exp_scores = jnp.exp(scores - score_top)
    totals = jnp.sum(exp_scores, axis=-1, keepdims=True)
    attn_probs = exp_scores / totals
    log_totals = score_top + jnp.log(totals)
    mixed_heads = jnp.einsum(
        "hgqk,khd->qhgd",
        attn_probs.astype(jnp.bfloat16),
        value_low,
        preferred_element_type=jnp.float32,
    )
    mixed_low = mixed_heads.reshape(token_count, QUERY_HEADS * HEAD_SIZE).astype(jnp.bfloat16)
    residual = x_local + jnp.dot(mixed_low, out_full, preferred_element_type=jnp.float32)
    inv_moe = lax.rsqrt(jnp.mean(residual * residual, axis=-1, keepdims=True) + EPSILON)
    normed_moe = (residual * inv_moe * gain_moe).astype(jnp.bfloat16)
    normed_all = gather_expert_axis(normed_moe, tuned)
    logits_all = jnp.einsum(
        "btd,de->bet", normed_all, router_full, preferred_element_type=jnp.float32
    )
    chosen_all = codes_all > 0
    top_all = jnp.max(jnp.where(chosen_all, logits_all, NEG_FILL), axis=1, keepdims=True)
    exp_all = jnp.where(chosen_all, jnp.exp(logits_all - top_all), 0.0)
    gates_all = exp_all / jnp.sum(exp_all, axis=1, keepdims=True)
    own_gates = lax.dynamic_slice_in_dim(gates_all, my_index * per_device, per_device, axis=1)
    my_block = rel_of[my_index]
    gates = gates_all[my_block]
    chosen = chosen_all[my_block]
    slot_list = jnp.arange(capacity, dtype=jnp.int32) + 1
    slot_hit = own_codes[:, :, None, :] == slot_list[None, None, :, None]
    slot_gate = jnp.sum(jnp.where(slot_hit, own_gates[:, :, None, :], 0.0), axis=-1)
    slot_one = slot_hit.astype(jnp.bfloat16)
    inbound = jnp.einsum(
        "blrt,btd->lbrd", slot_one, normed_all, preferred_element_type=jnp.float32
    ).astype(jnp.bfloat16)
    grad_slots = jnp.einsum(
        "blrt,btd->lbrd", slot_one, grads_all, preferred_element_type=jnp.float32
    )
    slot_gate = jnp.swapaxes(slot_gate, 0, 1)[..., None]
    pre_gate = jnp.einsum("lbrd,ldf->lbrf", inbound, gate_full, preferred_element_type=jnp.float32)
    pre_up = jnp.einsum("lbrd,ldf->lbrf", inbound, up_full, preferred_element_type=jnp.float32)
    activated, gelu_pull = jax.vjp(jax.nn.gelu, pre_gate)
    hidden = (activated * pre_up).astype(jnp.bfloat16)
    expert_out = (
        jnp.einsum("lbrf,lfd->lbrd", hidden, down_full, preferred_element_type=jnp.float32)
        .astype(jnp.bfloat16)
        .astype(jnp.float32)
    )
    grad_gate_slot = jnp.sum(grad_slots * expert_out, axis=-1)
    weighted = (slot_gate * expert_out).astype(jnp.bfloat16)
    back_out = jnp.einsum(
        "blrt,lbrd->btd", slot_one, weighted, preferred_element_type=jnp.float32
    ).astype(jnp.bfloat16)
    gate_grads = jnp.einsum(
        "blrt,lbr->blt",
        slot_hit.astype(jnp.float32),
        grad_gate_slot,
        precision=lax.Precision.HIGHEST,
        preferred_element_type=jnp.float32,
    )
    high = gate_grads.astype(jnp.bfloat16)
    low = (gate_grads - high.astype(jnp.float32)).astype(jnp.bfloat16)
    both = jnp.concatenate([high, low], axis=2)
    grad_table = jnp.zeros((expert_devices, table_rows, width), jnp.bfloat16)
    grad_table = lax.dynamic_update_slice(
        grad_table, both, (0, my_index * per_device, 0)
    )
    summed = scatter_expert_axis(jnp.concatenate([back_out, grad_table], axis=1), tuned)
    out_low = (residual + summed[:token_count]).astype(jnp.bfloat16)
    grad_pair = (
        summed[token_count : token_count + expert_count, :token_count]
        + summed[token_count : token_count + expert_count, token_count : 2 * token_count]
    )
    grad_inbound = (slot_gate * grad_slots).astype(jnp.bfloat16)
    grad_down = jnp.einsum(
        "lbrf,lbrd->lfd", hidden, grad_inbound, preferred_element_type=jnp.float32
    ).astype(jnp.bfloat16)
    grad_hidden = jnp.einsum(
        "lbrd,lfd->lbrf", grad_inbound, down_full, preferred_element_type=jnp.float32
    )
    grad_pre_gate = gelu_pull(grad_hidden * pre_up)[0].astype(jnp.bfloat16)
    grad_pre_up = (grad_hidden * activated).astype(jnp.bfloat16)
    grad_inputs = jnp.einsum(
        "lbrf,ldf->lbrd", grad_pre_gate, gate_full, preferred_element_type=jnp.float32
    )
    grad_inputs = (
        grad_inputs
        + jnp.einsum("lbrf,ldf->lbrd", grad_pre_up, up_full, preferred_element_type=jnp.float32)
    ).astype(jnp.bfloat16)
    back_grad = jnp.einsum(
        "blrt,lbrd->btd", slot_one, grad_inputs, preferred_element_type=jnp.float32
    ).astype(jnp.bfloat16)
    grad_moe = scatter_expert_axis(back_grad, tuned)
    grad_gate = jnp.einsum(
        "lbrd,lbrf->ldf", inbound, grad_pre_gate, preferred_element_type=jnp.float32
    ).astype(jnp.bfloat16)
    grad_up = jnp.einsum(
        "lbrd,lbrf->ldf", inbound, grad_pre_up, preferred_element_type=jnp.float32
    ).astype(jnp.bfloat16)
    owned_down = scatter_experts(grad_down, 2, tuned)
    owned_gate = scatter_experts(grad_gate, 1, tuned)
    owned_up = scatter_experts(grad_up, 1, tuned)
    grad_chosen = gates * (grad_pair - jnp.sum(gates * grad_pair, axis=0, keepdims=True))
    grad_logits = jnp.where(chosen, grad_chosen, 0.0).T.astype(jnp.bfloat16)
    grad_router = contract(normed_moe, grad_logits, (0,), (0,))
    grad_normed_moe = contract(grad_logits, router_full, (1,), (1,)) + grad_moe
    grad_gain_moe, grad_through = norm_back(residual, inv_moe, gain_moe, grad_normed_moe)
    grad_residual = dy_local + grad_through
    grad_attn = grad_residual.astype(jnp.bfloat16)
    grad_out = contract(mixed_low, grad_attn, (0,), (0,))
    side_out = jnp.concatenate([grad_router, grad_gain_moe[:, None]], axis=1)
    owned_out = scatter_all(
        jnp.concatenate([grad_out, pad_columns(side_out, 128)], axis=1).astype(jnp.bfloat16), tuned
    )
    grad_mixed = (
        contract(grad_attn, out_full, (1,), (1,))
        .astype(jnp.bfloat16)
        .reshape(token_count, KEY_VALUE_HEADS, query_group_width, HEAD_SIZE)
    )
    probs_again = jnp.exp(masked_scores() - log_totals)
    grad_probs = jnp.einsum(
        "qhgd,khd->hgqk", grad_mixed, value_low, preferred_element_type=jnp.float32
    )
    value_weight_gradient = jnp.einsum(
        "hgqk,qhgd->khd",
        probs_again.astype(jnp.bfloat16),
        grad_mixed,
        preferred_element_type=jnp.float32,
    )
    inner_sum = jnp.sum(probs_again * grad_probs, axis=-1, keepdims=True)
    grad_scores = (probs_again * (grad_probs - inner_sum)).astype(jnp.bfloat16)
    grad_query_rot = (
        jnp.einsum("hgqk,khd->qhgd", grad_scores, key_rotated, preferred_element_type=jnp.float32)
        * score_scale
    )
    grad_key_rot = (
        jnp.einsum("hgqk,qhgd->khd", grad_scores, query_rotated, preferred_element_type=jnp.float32)
        * score_scale
    )
    grad_query_low = (
        rotate_back(
            grad_query_rot.reshape(token_count, QUERY_HEADS, HEAD_SIZE), cosine_table, sine_values
        )
        .reshape(token_count, QUERY_HEADS * HEAD_SIZE)
        .astype(jnp.bfloat16)
    )
    grad_key_low = (
        rotate_back(grad_key_rot, cosine_table, sine_values)
        .reshape(token_count, KEY_VALUE_HEADS * HEAD_SIZE)
        .astype(jnp.bfloat16)
    )
    value_gradient_narrow = value_weight_gradient.reshape(
        token_count, KEY_VALUE_HEADS * HEAD_SIZE
    ).astype(jnp.bfloat16)
    grad_query = contract(normed_attn, grad_query_low, (0,), (0,))
    grad_key = contract(normed_attn, grad_key_low, (0,), (0,))
    grad_value_w = contract(normed_attn, value_gradient_narrow, (0,), (0,))
    grad_normed_attn = contract(grad_query_low, query_full, (1,), (1,))
    grad_normed_attn = grad_normed_attn + contract(grad_key_low, key_full, (1,), (1,))
    grad_normed_attn = grad_normed_attn + contract(value_gradient_narrow, value_full, (1,), (1,))
    grad_gain_attn, grad_through_attn = norm_back(x_local, inv_attn, gain_attn, grad_normed_attn)
    grad_x = (grad_residual + grad_through_attn).astype(jnp.bfloat16)
    owned_in = scatter_all(
        jnp.concatenate(
            [grad_query, grad_key, grad_value_w, pad_columns(grad_gain_attn[:, None], 128)], axis=1
        ).astype(jnp.bfloat16),
        tuned,
    )
    deal_out, deal_grad = (
        lax.all_to_all(
            out_low.reshape(1, SEQ_DEV, seq_len, width),
            "expert",
            split_axis=2,
            concat_axis=0,
            tiled=True,
        ),
        lax.all_to_all(
            grad_x.reshape(1, SEQ_DEV, seq_len, width),
            "expert",
            split_axis=2,
            concat_axis=0,
            tiled=True,
        ),
    )
    output = deal_out.reshape(row_seqs, piece_len, width)[placement]
    input_grad = deal_grad.reshape(row_seqs, piece_len, width)[placement]
    return (
        output,
        input_grad,
        owned_in[:, query_width + 2 * kv_width],
        owned_in[:, :query_width],
        owned_in[:, query_width : query_width + kv_width],
        owned_in[:, query_width + kv_width : query_width + 2 * kv_width],
        owned_out[:, :width],
        owned_out[:, width + expert_count],
        owned_out[:, width : width + expert_count],
        owned_gate,
        owned_up,
        owned_down,
    )


def solution(mesh):
    return jax.shard_map(
        body,
        mesh=mesh,
        in_specs=(
            P("dp", "expert", None),
            P("dp", "expert", None),
            P("dp", None),
            P("dp"),
            P(("dp", "expert"), None),
            P(("dp", "expert"), None),
            P(("dp", "expert")),
            P(("dp", "expert"), None),
            P(("dp", "expert"), None),
            P(("dp", "expert"), None),
            P(("dp", "expert"), None),
            P(("dp", "expert")),
            P(("dp", "expert"), None),
            P("expert", "dp", None),
            P("expert", "dp", None),
            P("expert", None, "dp"),
        ),
        out_specs=(
            P("dp", "expert", None),
            P("dp", "expert", None),
            P(("dp", "expert")),
            P(("dp", "expert"), None),
            P(("dp", "expert"), None),
            P(("dp", "expert"), None),
            P(("dp", "expert"), None),
            P(("dp", "expert")),
            P(("dp", "expert"), None),
            P("expert", "dp", None),
            P("expert", "dp", None),
            P("expert", None, "dp"),
        ),
        check_vma=False,
    )
```

time: 1290 us -> 768 us (0.60)
  waiting for transfers between devices: 622 us -> 243 us
  blocking collectives: 283 us -> 0 us
  starting transfers between devices: 38.2 us -> 156 us
  local copies, waits for them, and re-layouts: 179 us -> 93.9 us
  other arithmetic: 34.4 us -> 87.7 us
  Pallas kernels: 0 us -> 51.4 us
    reduce_scatter x6 -> x0, waiting for transfers between devices: 389 us -> none  [the longest x1 142 us: body(): lax.psum_scatter(grad_out, ('dp', 'expert'), scatter_dimension=0, tiled=T...]
    ppermute x0 -> x98, waiting for transfers between devices: none -> 243 us  [the longest x20 110 us: shift_down(): return lax.ppermute(value, 'expert', [(i, (i + 6) % 8) for i in range(8)])]
    all_to_all x5 -> x0, waiting for transfers between devices: 217 us -> none  [the longest x1 80.5 us: body(): lax.all_to_all(grad_table, 'expert', split_axis=0, concat_axis=0, tiled=T...]
    all_gather x3 -> x0, blocking collectives: 198 us -> none  [the longest x1 110 us: body(): lax.all_gather(w_router, ('dp', 'expert'), axis=0, tiled=True)]
    ppermute x0 -> x98, starting transfers between devices: none -> 141 us  [the longest x20 54.2 us: shift_down(): return lax.ppermute(value, 'expert', [(i, (i + 6) % 8) for i in range(8)])]
    unnamed x2 -> x0, blocking collectives: 84.6 us -> none
    pallas_call x0 -> x8, Pallas kernels: none -> 51.4 us  [move_blocks(): pl.pallas_call(kernel, out_shape=jax.ShapeDtypeStruct(shape, dtype), in_s...]
    gather x7 -> x3, local copies, waits for them, and re-layouts: 33.1 us -> 5.01 us  [the longest x1 2.73 us: body(): output = deal_out.reshape(row_seqs, piece_len, width)[placement]]
  transfers between devices with their start and end apart: 21 -> 101, of which waited for: 8 -> 41; matrix products, arithmetic and copies ran while one was open for 22% -> 29% of each run, Pallas kernels for 0% -> 7%
where the time goes in v1:
time: 768 us; the launch traced here: 761 us
  waiting for transfers between devices  243 us (32%)
  starting transfers between devices  156 us (20%)
  matrix products  124 us (16%)
  local copies, waits for them, and re-layouts  93.9 us (12%)
  other arithmetic  87.7 us (11%)
  Pallas kernels  51.4 us (7%)
    ppermute x20, waiting for transfers between devices, shift_down(): return lax.ppermute(value, 'expert', [(i, (i + 6) % 8) for i in range(8)])  110 us
    ppermute x25, waiting for transfers between devices, swap_x(): return lax.ppermute(value, 'dp', [(i, i ^ 1) for i in range(4)])  64.4 us
    ppermute x20, waiting for transfers between devices, shift_up(): return lax.ppermute(value, 'expert', [(i, (i + 2) % 8) for i in range(8)])  54.8 us
    ppermute x20, starting transfers between devices, shift_down(): return lax.ppermute(value, 'expert', [(i, (i + 6) % 8) for i in range(8)])  54.2 us
    pallas_call x8, Pallas kernels, move_blocks(): pl.pallas_call(kernel, out_shape=jax.ShapeDtypeStruct(shape, dtype), in_s...  51.4 us
    ppermute x25, starting transfers between devices, swap_x(): return lax.ppermute(value, 'dp', [(i, i ^ 1) for i in range(4)])  35.9 us
    ppermute x25, starting transfers between devices, swap_y(): return lax.ppermute(value, 'dp', [(i, i ^ 2) for i in range(4)])  30.3 us
    dot_general x10, matrix products, contract(): lax.dot_general(left, right, ((left_dims, right_dims), ((), ())), preferr...  24 us
  transfers between devices with their start and end apart: 101, of which 41 were waited for; matrix products, arithmetic and copies ran while one was open for 29% of the time, Pallas kernels for 7%

profile of v1, /device:TPU:0, one launch (start us, length us, event | category | flops | bytes accessed | tf_op | source)
XLA Modules:
  0.0 761.4 jit_solution(13034992393851164141)
XLA Ops:
  2.5 5.1 collective-permute-start.1
  10.0 3.8 collective-permute-start.10
  16.1 5.1 all-to-all-start
  26.2 3.9 collective-permute-start.12
  30.2 3.8 collective-permute-start.3
  34.2 8.7 %collective-permute-done.11 = bf16[48,768]{1,0:T(8,128)(2,1)S(1)} collective-permute-done((bf16[48,768]{1,0:T(8,128)(2,1)S(1)}, bf16[48,768]{1,0:T(8,128)(2,1)S(1)}, u32[]{:S(2)}, u32[]{:S(2)}) %collective-permute-start.11) | collective-permute-done | bytes 73760 | tf_op jit(solution)/shard_map/ppermute | solution.py:112
  56.5 7.4 collective-permute-done.13
  68.1 13.6 %collective-permute-done.4 = bf16[4,48,2176]{2,1,0:T(8,128)(2,1)S(1)} collective-permute-done((bf16[4,48,2176]{2,1,0:T(8,128)(2,1)}, bf16[4,48,2176]{2,1,0:T(8,128)(2,1)S(1)}, u32[]{:S(2)}, u32[]{:S(2)}) %collective-permute-start.4) | collective-permute-done | bytes 835616 | tf_op jit(solution)/shard_map/ppermute | solution.py:100
  88.9 6.3 collective-permute-start.18
  98.5 4.2 fusion.168
  102.7 3.5 fusion.167
  106.2 22.0 %collective-permute-done.19 = bf16[272,1536]{1,0:T(8,128)(2,1)S(1)} collective-permute-done((bf16[272,1536]{1,0:T(8,128)(2,1)S(1)}, bf16[272,1536]{1,0:T(8,128)(2,1)S(1)}, u32[]{:S(2)}, u32[]{:S(2)}) %collective-permute-start.19) | collective-permute-done | bytes 835616 | tf_op jit(solution)/shard_map/ppermute | solution.py:116
  137.5 14.5 %collective-permute-done.20 = bf16[128,1536]{1,0:T(8,128)(2,1)S(1)} collective-permute-done((bf16[128,1536]{1,0:T(8,128)(2,1)}, bf16[128,1536]{1,0:T(8,128)(2,1)S(1)}, u32[]{:S(2)}, u32[]{:S(2)}) %collective-permute-start.20) | collective-permute-done | bytes 393248 | tf_op jit(solution)/shard_map/ppermute | solution.py:112
  164.5 7.8 %shard_map.248 = bf16[32,48,1664]{2,1,0:T(8,128)(2,1)S(1)} custom-call(s32[32]{0:T(128)S(1)} %stack.365.index_ref, bf16[32,48,1664]{2,1,0:T(8,128)(2,1)S(1)} %bitcast.506), custom_call_target="tpu_custom_call" | custom-call | tf_op jit(solution)/shard_map/pallas_call | solution.py:227
  175.0 3.6 pad_maximum_fusion
  178.7 9.9 %shard_map.247 = bf16[32,48,2176]{2,1,0:T(8,128)(2,1)S(1)} custom-call(s32[32]{0:T(128)S(1)} %stack.365.index_ref, bf16[32,48,2176]{2,1,0:T(8,128)(2,1)S(1)} %bitcast.505), custom_call_target="tpu_custom_call" | custom-call | tf_op jit(solution)/shard_map/pallas_call | solution.py:227
  197.7 6.6 copy.284
  205.8 4.1 fusion.177
  246.7 4.9 collective-permute-done.23
  253.0 14.2 %collective-permute-done.24 = bf16[256,1536]{1,0:T(8,128)(2,1)} collective-permute-done((bf16[256,1536]{1,0:T(8,128)(2,1)}, bf16[256,1536]{1,0:T(8,128)(2,1)}, u32[]{:S(2)}, u32[]{:S(2)}) %collective-permute-start.24) | collective-permute-done | bytes 786464 | tf_op jit(solution)/shard_map/ppermute | solution.py:116
  284.4 5.5 collective-permute-done.26
  290.0 3.2 pad_maximum_fusion.7
  295.4 9.8 %shard_map.252 = bf16[8,256,1536]{2,1,0:T(8,128)(2,1)S(1)} custom-call(s32[16]{0:T(128)S(1)} %reshape.824.seq_ref, s32[8]{0:T(128)S(1)} %compare_select_fusion.11.rel_ref, bf16[8,272,1536]{2,1,0:T(8,128)(2,1)S(1)} %constant_dynamic-update-slice_fusion.src_ref), custom_call_target="tpu_custom_call" | custom-call | tf_op jit(solution)/shard_map/pallas_call | solution.py:227
  305.3 4.5 fusion.7
  316.0 3.7 constant_dynamic-update-slice_fusion.5
  319.8 4.8 convolution_bitcast_fusion.1
  324.6 4.1 fusion.44
  330.5 4.8 fusion.10
  335.3 7.8 %fusion.14 = f32[2,8,72,768]{3,2,1,0:T(8,128)} fusion(bf16[2,768,1536]{2,1,0:T(8,128)(2,1)S(1)} %bitcast.519, f32[8,1536,2,72]{1,3,0,2:T(8,128)} %fusion.7, f32[2,8,72]{2,1,0:T(8,128)S(1)} %copy.295), kind=kOutput, calls=%fused_computation.40 | convolution fusion | flops 2721447936 | bytes 15340032 | tf_op jit(solution)/shard_map/lbrd,lfd->lbrf/dot_general | solution.py:562
  343.1 8.6 %fusion.42 = (bf16[2,8,72,768]{3,2,1,0:T(8,128)(2,1)S(1)}, bf16[2,8,72,768]{3,2,1,0:T(8,128)(2,1)}, bf16[2,8,72,768]{3,2,1,0:T(8,128)(2,1)S(1)}) fusion(f32[2,8,72,768]{3,2,1,0:T(8,128)} %fusion.14, f32[2,8,72,768]{3,2,1,0:T(8,128)} %fusion.10, bf16[2,1536,768]{2,1,0:T(8,128)(2,1)S(1)} %bitcast.521, bf16[2,8,72,1536]{3,2,0,1:T(8,128)(2,1)S(1)} %fusion.44), kind=kOutput, calls=%fused_computation.66 | convolution fusion | flops 2740912128 | bytes 20643840 | tf_op jit(solution)/shard_map/lbrd,ldf->lbrf/dot_general | solution.py:524
  351.8 6.6 fusion.1
  358.9 6.6 fusion.18
  365.6 5.5 bitcast_convert_fusion.4
  371.1 6.2 add_convert_fusion
  385.6 9.2 %bitcast_convert_fusion.3 = bf16[2,1536,768]{2,1,0:T(8,128)(2,1)} fusion(bf16[2,8,72,1536]{3,2,0,1:T(8,128)(2,1)} %copy-done.29, bf16[2,8,72,768]{3,2,1,0:T(8,128)(2,1)} %get-tuple-element.115), kind=kOutput, calls=%fused_computation.9 | convolution fusion | flops 2720268288 | bytes 10027008 | tf_op jit(solution)/shard_map/lbrd,lbrf->ldf/dot_general | solution.py:581
  399.4 7.6 bitcast_convert_fusion.2
  408.1 3.4 constant_dynamic-slice_fusion.8
  426.0 24.6 %collective-permute-done.41 = bf16[128,1536]{1,0:T(8,128)(2,1)S(1)} collective-permute-done((bf16[128,1536]{1,0:T(8,128)(2,1)S(1)}, bf16[128,1536]{1,0:T(8,128)(2,1)S(1)}, u32[]{:S(2)}, u32[]{:S(2)}) %collective-permute-start.41) | collective-permute-done | bytes 393248 | tf_op jit(solution)/shard_map/ppermute | solution.py:112
  451.7 16.4 %collective-permute-done.45 = bf16[144,1536]{1,0:T(8,128)(2,1)S(1)} collective-permute-done((bf16[144,1536]{1,0:T(8,128)(2,1)S(1)}, bf16[144,1536]{1,0:T(8,128)(2,1)S(1)}, u32[]{:S(2)}, u32[]{:S(2)}) %collective-permute-start.45) | collective-permute-done | bytes 442400 | tf_op jit(solution)/shard_map/ppermute | solution.py:116
  470.6 3.8 collective-permute-start.46
  474.6 13.6 %collective-permute-done.44 = bf16[128,1536]{1,0:T(8,128)(2,1)S(1)} collective-permute-done((bf16[128,1536]{1,0:T(8,128)(2,1)S(1)}, bf16[128,1536]{1,0:T(8,128)(2,1)S(1)}, u32[]{:S(2)}, u32[]{:S(2)}) %collective-permute-start.44) | collective-permute-done | bytes 393248 | tf_op jit(solution)/shard_map/ppermute | solution.py:116
  492.9 5.1 collective-permute-done.46
  499.7 14.8 %collective-permute-done.51 = bf16[128,1536]{1,0:T(8,128)(2,1)S(1)} collective-permute-done((bf16[128,1536]{1,0:T(8,128)(2,1)S(1)}, bf16[128,1536]{1,0:T(8,128)(2,1)S(1)}, u32[]{:S(2)}, u32[]{:S(2)}) %collective-permute-start.51) | collective-permute-done | bytes 393248 | tf_op jit(solution)/shard_map/ppermute | solution.py:116
  516.7 14.0 %collective-permute-done.53 = bf16[128,1536]{1,0:T(8,128)(2,1)S(1)} collective-permute-done((bf16[128,1536]{1,0:T(8,128)(2,1)S(1)}, bf16[128,1536]{1,0:T(8,128)(2,1)S(1)}, u32[]{:S(2)}, u32[]{:S(2)}) %collective-permute-start.53) | collective-permute-done | bytes 393248 | tf_op jit(solution)/shard_map/ppermute | solution.py:116
  550.9 4.4 all-to-all-start.1
  557.0 3.8 fusion.26
  562.5 3.2 fusion.83
  568.7 3.6 convolution_convert_fusion.1
  577.5 7.8 %shard_map.254 = bf16[32,48,1664]{2,1,0:T(8,128)(2,1)S(1)} custom-call(s32[32]{0:T(128)S(1)} %copy-done.11, bf16[32,48,1664]{2,1,0:T(8,128)(2,1)S(1)} %pad_maximum_fusion.3.src_ref), custom_call_target="tpu_custom_call" | custom-call | tf_op jit(solution)/shard_map/pallas_call | solution.py:227
  588.2 9.9 %shard_map.253 = bf16[32,48,2176]{2,1,0:T(8,128)(2,1)S(1)} custom-call(s32[32]{0:T(128)S(1)} %copy-done.11, bf16[32,48,2176]{2,1,0:T(8,128)(2,1)S(1)} %pad_maximum_fusion.1.src_ref), custom_call_target="tpu_custom_call" | custom-call | tf_op jit(solution)/shard_map/pallas_call | solution.py:227
  598.2 3.2 fusion.169
  608.9 8.7 %collective-permute-done.86 = bf16[1,384,768]{2,1,0:T(8,128)(2,1)S(1)} collective-permute-done((bf16[1,384,768]{2,1,0:T(8,128)(2,1)S(1)}, bf16[1,384,768]{2,1,0:T(8,128)(2,1)S(1)}, u32[]{:S(2)}, u32[]{:S(2)}) %collective-permute-start.86) | collective-permute-done | bytes 589856 | tf_op jit(solution)/shard_map/ppermute | solution.py:100
  622.2 8.1 %collective-permute-done.95 = bf16[1,768,384]{2,1,0:T(8,128)(2,1)S(1)} collective-permute-done((bf16[1,768,384]{2,1,0:T(8,128)(2,1)S(1)}, bf16[1,768,384]{2,1,0:T(8,128)(2,1)S(1)}, u32[]{:S(2)}, u32[]{:S(2)}) %collective-permute-start.95) | collective-permute-done | bytes 589856 | tf_op jit(solution)/shard_map/ppermute | solution.py:100
  637.8 5.4 all-to-all-start.2
  652.1 3.6 collective-permute-done.82
  668.0 3.8 convert_add_fusion.4
  680.6 7.1 collective-permute-done.94
  696.3 3.4 convert_add_fusion.2
  707.9 3.8 fusion.4
  717.9 6.1 collective-permute-done.58
  733.0 3.5 collective-permute-start.77
  737.9 3.1 collective-permute-start.79
  745.7 3.6 collective-permute-start.65
  753.3 3.3 collective-permute-start.66
  (637 shorter events, 309.3 us)
Async XLA Ops:
  2.5 27.7 %collective-permute-start.1 = (bf16[48,2176]{1,0:T(8,128)(2,1)S(1)}, bf16[48,2176]{1,0:T(8,128)(2,1)S(1)}, u32[]{:S(2)}, u32[]{:S(2)}) collective-permute-start(bf16[48,2176]{1,0:T(8,128)(2,1)S(1)} %fusion.147), channel_id=1, source_target_pairs={{0,6},{1,7},{2,0},{3,1},{4,2},{5,3},{6,4},{7,5},{8,14},{9,15},{10,... | collective-permute-start | bytes 626696 | tf_op jit(solution)/shard_map/ppermute | solution.py:116
  7.6 26.5 %collective-permute-start = (bf16[48,2176]{1,0:T(8,128)(2,1)S(1)}, bf16[48,2176]{1,0:T(8,128)(2,1)S(1)}, u32[]{:S(2)}, u32[]{:S(2)}) collective-permute-start(bf16[48,2176]{1,0:T(8,128)(2,1)S(1)} %fusion.147), channel_id=1, source_target_pairs={{0,2},{1,3},{2,4},{3,5},{4,6},{5,7},{6,0},{7,1},{8,10},{9,11},{10,... | collective-permute-start | bytes 626696 | tf_op jit(solution)/shard_map/ppermute | solution.py:112
  16.1 140.9 %all-to-all-start = ((bf16[8,2,16,1536]{3,2,1,0:T(8,128)(2,1)}), bf16[8,2,16,1536]{3,2,1,0:T(8,128)(2,1)}, u32[]{:S(2)}, u32[]{:S(2)}) async-start(bf16[8,2,16,1536]{3,2,1,0:T(8,128)(2,1)} %bitcast.2), calls=%async_computation | async-start | bytes 1572864 | tf_op jit(solution)/shard_map/all_to_all | solution.py:399
  21.2 114.8 %collective-permute-start.32 = (bf16[2,384,768]{2,1,0:T(8,128)(2,1)}, bf16[2,384,768]{2,1,0:T(8,128)(2,1)S(1)}, u32[]{:S(2)}, u32[]{:S(2)}) collective-permute-start(bf16[2,384,768]{2,1,0:T(8,128)(2,1)} %refs_1_.4), channel_id=1, source_target_pairs={{0,8},{8,0},{16,24},{24,16},{1,9},{9,1},{17,25},{25,17},{2,10},{10... | collective-permute-start | bytes 3538952 | tf_op jit(solution)/shard_map/ppermute | solution.py:100
  44.0 19.8 %collective-permute-start.13 = (bf16[4,48,1664]{2,1,0:T(8,128)(2,1)}, bf16[4,48,1664]{2,1,0:T(8,128)(2,1)S(1)}, u32[]{:S(2)}, u32[]{:S(2)}) collective-permute-start(bf16[4,48,1664]{2,1,0:T(8,128)(2,1)} %get-tuple-element.184), channel_id=1, source_target_pairs={{0,8},{8,0},{16,24},{24,16},{1,9},{9,1},{17,25},{25,17},{2,10},{10... | collective-permute-start | bytes 1916936 | tf_op jit(solution)/shard_map/ppermute | solution.py:100
  45.5 20.0 %collective-permute-start.14 = (bf16[4,48,1664]{2,1,0:T(8,128)(2,1)}, bf16[4,48,1664]{2,1,0:T(8,128)(2,1)}, u32[]{:S(2)}, u32[]{:S(2)}) collective-permute-start(bf16[4,48,1664]{2,1,0:T(8,128)(2,1)} %get-tuple-element.184), channel_id=1, source_target_pairs={{0,16},{8,24},{16,0},{24,8},{1,17},{9,25},{17,1},{25,9},{2,18},{10... | collective-permute-start | bytes 1916936 | tf_op jit(solution)/shard_map/ppermute | solution.py:104
  49.3 32.5 %collective-permute-start.4 = (bf16[4,48,2176]{2,1,0:T(8,128)(2,1)}, bf16[4,48,2176]{2,1,0:T(8,128)(2,1)S(1)}, u32[]{:S(2)}, u32[]{:S(2)}) collective-permute-start(bf16[4,48,2176]{2,1,0:T(8,128)(2,1)} %get-tuple-element.177), channel_id=1, source_target_pairs={{0,8},{8,0},{16,24},{24,16},{1,9},{9,1},{17,25},{25,17},{2,10},{10... | collective-permute-start | bytes 2506760 | tf_op jit(solution)/shard_map/ppermute | solution.py:100
  50.7 32.7 %collective-permute-start.5 = (bf16[4,48,2176]{2,1,0:T(8,128)(2,1)}, bf16[4,48,2176]{2,1,0:T(8,128)(2,1)}, u32[]{:S(2)}, u32[]{:S(2)}) collective-permute-start(bf16[4,48,2176]{2,1,0:T(8,128)(2,1)} %get-tuple-element.177), channel_id=1, source_target_pairs={{0,16},{8,24},{16,0},{24,8},{1,17},{9,25},{17,1},{25,9},{2,18},{10... | collective-permute-start | bytes 2506760 | tf_op jit(solution)/shard_map/ppermute | solution.py:104
  63.9 23.5 %collective-permute-start.16 = (bf16[2,48,1664]{2,1,0:T(8,128)(2,1)S(1)}, bf16[2,48,1664]{2,1,0:T(8,128)(2,1)S(1)}, u32[]{:S(2)}, u32[]{:S(2)}) collective-permute-start(bf16[2,48,1664]{2,1,0:T(8,128)(2,1)S(1)} %slice.629), channel_id=1, source_target_pairs={{0,16},{8,24},{16,0},{24,8},{1,17},{9,25},{17,1},{25,9},{2,18},{10... | collective-permute-start | bytes 958472 | tf_op jit(solution)/shard_map/ppermute | solution.py:104
  66.5 22.4 %collective-permute-start.15 = (bf16[2,48,1664]{2,1,0:T(8,128)(2,1)S(1)}, bf16[2,48,1664]{2,1,0:T(8,128)(2,1)S(1)}, u32[]{:S(2)}, u32[]{:S(2)}) collective-permute-start(bf16[2,48,1664]{2,1,0:T(8,128)(2,1)S(1)} %slice.628), channel_id=1, source_target_pairs={{0,8},{8,0},{16,24},{24,16},{1,9},{9,1},{17,25},{25,17},{2,10},{10... | collective-permute-start | bytes 958472 | tf_op jit(solution)/shard_map/ppermute | solution.py:100
  87.4 46.1 %collective-permute-start.33 = (bf16[2,384,768]{2,1,0:T(8,128)(2,1)}, bf16[2,384,768]{2,1,0:T(8,128)(2,1)S(1)}, u32[]{:S(2)}, u32[]{:S(2)}) collective-permute-start(bf16[2,384,768]{2,1,0:T(8,128)(2,1)} %refs_1_.4), channel_id=1, source_target_pairs={{0,16},{8,24},{16,0},{24,8},{1,17},{9,25},{17,1},{25,9},{2,18},{10... | collective-permute-start | bytes 3538952 | tf_op jit(solution)/shard_map/ppermute | solution.py:104
  88.9 41.0 %collective-permute-start.18 = (bf16[272,1536]{1,0:T(8,128)(2,1)S(1)}, bf16[272,1536]{1,0:T(8,128)(2,1)S(1)}, u32[]{:S(2)}, u32[]{:S(2)}) collective-permute-start(bf16[272,1536]{1,0:T(8,128)(2,1)S(1)} %get-tuple-element.179), channel_id=1, source_target_pairs={{0,2},{1,3},{2,4},{3,5},{4,6},{5,7},{6,0},{7,1},{8,10},{9,11},{10,... | collective-permute-start | bytes 2506760 | tf_op jit(solution)/shard_map/ppermute | solution.py:112
  96.3 31.9 %collective-permute-start.19 = (bf16[272,1536]{1,0:T(8,128)(2,1)S(1)}, bf16[272,1536]{1,0:T(8,128)(2,1)S(1)}, u32[]{:S(2)}, u32[]{:S(2)}) collective-permute-start(bf16[272,1536]{1,0:T(8,128)(2,1)S(1)} %get-tuple-element.179), channel_id=1, source_target_pairs={{0,6},{1,7},{2,0},{3,1},{4,2},{5,3},{6,4},{7,5},{8,14},{9,15},{10,... | collective-permute-start | bytes 2506760 | tf_op jit(solution)/shard_map/ppermute | solution.py:116
  102.7 72.3 %collective-permute-start.8 = (bf16[4,4,48,2176]{3,2,1,0:T(8,128)(2,1)}, bf16[4,4,48,2176]{3,2,1,0:T(8,128)(2,1)}, u32[]{:S(2)}, u32[]{:S(2)}) collective-permute-start(bf16[4,4,48,2176]{3,2,1,0:T(8,128)(2,1)} %get-tuple-element.152), channel_id=1, source_target_pairs={{0,1},{1,0},{2,3},{3,2},{4,5},{5,4},{6,7},{7,6},{8,9},{9,8},{10,11... | collective-permute-start | bytes 10027016 | tf_op jit(solution)/shard_map/ppermute | solution.py:108
  128.2 32.8 %collective-permute-start.17 = (bf16[4,4,48,1664]{3,2,1,0:T(8,128)(2,1)}, bf16[4,4,48,1664]{3,2,1,0:T(8,128)(2,1)}, u32[]{:S(2)}, u32[]{:S(2)}) collective-permute-start(bf16[4,4,48,1664]{3,2,1,0:T(8,128)(2,1)} %get-tuple-element.166), channel_id=1, source_target_pairs={{0,1},{1,0},{2,3},{3,2},{4,5},{5,4},{6,7},{7,6},{8,9},{9,8},{10,11... | collective-permute-start | bytes 7667720 | tf_op jit(solution)/shard_map/ppermute | solution.py:108
  129.9 22.6 %collective-permute-start.21 = (bf16[144,1536]{1,0:T(8,128)(2,1)}, bf16[144,1536]{1,0:T(8,128)(2,1)S(1)}, u32[]{:S(2)}, u32[]{:S(2)}) collective-permute-start(bf16[144,1536]{1,0:T(8,128)(2,1)} %slice.632), channel_id=1, source_target_pairs={{0,6},{1,7},{2,0},{3,1},{4,2},{5,3},{6,4},{7,5},{8,14},{9,15},{10,... | collective-permute-start | bytes 1327112 | tf_op jit(solution)/shard_map/ppermute | solution.py:116
  133.5 18.5 %collective-permute-start.20 = (bf16[128,1536]{1,0:T(8,128)(2,1)}, bf16[128,1536]{1,0:T(8,128)(2,1)S(1)}, u32[]{:S(2)}, u32[]{:S(2)}) collective-permute-start(bf16[128,1536]{1,0:T(8,128)(2,1)} %slice.631), channel_id=1, source_target_pairs={{0,2},{1,3},{2,4},{3,5},{4,6},{5,7},{6,0},{7,1},{8,10},{9,11},{10,... | collective-permute-start | bytes 1179656 | tf_op jit(solution)/shard_map/ppermute | solution.py:112
  136.0 89.6 %collective-permute-start.36 = (bf16[2,768,384]{2,1,0:T(8,128)(2,1)}, bf16[2,768,384]{2,1,0:T(8,128)(2,1)}, u32[]{:S(2)}, u32[]{:S(2)}) collective-permute-start(bf16[2,768,384]{2,1,0:T(8,128)(2,1)} %refs_1_.5), channel_id=1, source_target_pairs={{0,8},{8,0},{16,24},{24,16},{1,9},{9,1},{17,25},{25,17},{2,10},{10... | collective-permute-start | bytes 3538952 | tf_op jit(solution)/shard_map/ppermute | solution.py:100
  152.0 75.0 %collective-permute-start.37 = (bf16[2,768,384]{2,1,0:T(8,128)(2,1)}, bf16[2,768,384]{2,1,0:T(8,128)(2,1)}, u32[]{:S(2)}, u32[]{:S(2)}) collective-permute-start(bf16[2,768,384]{2,1,0:T(8,128)(2,1)} %refs_1_.5), channel_id=1, source_target_pairs={{0,16},{8,24},{16,0},{24,8},{1,17},{9,25},{17,1},{25,9},{2,18},{10... | collective-permute-start | bytes 3538952 | tf_op jit(solution)/shard_map/ppermute | solution.py:104
  152.5 76.5 %collective-permute-start.28 = (bf16[2,384,768]{2,1,0:T(8,128)(2,1)}, bf16[2,384,768]{2,1,0:T(8,128)(2,1)}, u32[]{:S(2)}, u32[]{:S(2)}) collective-permute-start(bf16[2,384,768]{2,1,0:T(8,128)(2,1)} %refs_1_.3), channel_id=1, source_target_pairs={{0,8},{8,0},{16,24},{24,16},{1,9},{9,1},{17,25},{25,17},{2,10},{10... | collective-permute-start | bytes 3538952 | tf_op jit(solution)/shard_map/ppermute | solution.py:100
  161.0 69.8 %collective-permute-start.29 = (bf16[2,384,768]{2,1,0:T(8,128)(2,1)}, bf16[2,384,768]{2,1,0:T(8,128)(2,1)}, u32[]{:S(2)}, u32[]{:S(2)}) collective-permute-start(bf16[2,384,768]{2,1,0:T(8,128)(2,1)} %refs_1_.3), channel_id=1, source_target_pairs={{0,16},{8,24},{16,0},{24,8},{1,17},{9,25},{17,1},{25,9},{2,18},{10... | collective-permute-start | bytes 3538952 | tf_op jit(solution)/shard_map/ppermute | solution.py:104
  175.0 118.3 %collective-permute-start.22 = (bf16[4,272,1536]{2,1,0:T(8,128)(2,1)}, bf16[4,272,1536]{2,1,0:T(8,128)(2,1)}, u32[]{:S(2)}, u32[]{:S(2)}) collective-permute-start(bf16[4,272,1536]{2,1,0:T(8,128)(2,1)} %pad_maximum_fusion.6), channel_id=1, source_target_pairs={{0,1},{1,0},{2,3},{3,2},{4,5},{5,4},{6,7},{7,6},{8,9},{9,8},{10,11... | collective-permute-start | bytes 10027016 | tf_op jit(solution)/shard_map/ppermute | solution.py:108
  229.0 22.6 %collective-permute-start.23 = (bf16[256,1536]{1,0:T(8,128)(2,1)}, bf16[256,1536]{1,0:T(8,128)(2,1)}, u32[]{:S(2)}, u32[]{:S(2)}) collective-permute-start(bf16[256,1536]{1,0:T(8,128)(2,1)} %get-tuple-element.113), channel_id=1, source_target_pairs={{0,2},{1,3},{2,4},{3,5},{4,6},{5,7},{6,0},{7,1},{8,10},{9,11},{10,... | collective-permute-start | bytes 2359304 | tf_op jit(solution)/shard_map/ppermute | solution.py:112
  230.8 36.4 %collective-permute-start.24 = (bf16[256,1536]{1,0:T(8,128)(2,1)}, bf16[256,1536]{1,0:T(8,128)(2,1)}, u32[]{:S(2)}, u32[]{:S(2)}) collective-permute-start(bf16[256,1536]{1,0:T(8,128)(2,1)} %get-tuple-element.113), channel_id=1, source_target_pairs={{0,6},{1,7},{2,0},{3,1},{4,2},{5,3},{6,4},{7,5},{8,14},{9,15},{10,... | collective-permute-start | bytes 2359304 | tf_op jit(solution)/shard_map/ppermute | solution.py:116
  241.5 29.4 %collective-permute-start.38 = (bf16[1,768,384]{2,1,0:T(8,128)(2,1)S(1)}, bf16[1,768,384]{2,1,0:T(8,128)(2,1)S(1)}, u32[]{:S(2)}, u32[]{:S(2)}) collective-permute-start(bf16[1,768,384]{2,1,0:T(8,128)(2,1)S(1)} %slice.642), channel_id=1, source_target_pairs={{0,8},{8,0},{16,24},{24,16},{1,9},{9,1},{17,25},{25,17},{2,10},{10... | collective-permute-start | bytes 1769480 | tf_op jit(solution)/shard_map/ppermute | solution.py:100
  243.0 29.8 %collective-permute-start.39 = (bf16[1,768,384]{2,1,0:T(8,128)(2,1)S(1)}, bf16[1,768,384]{2,1,0:T(8,128)(2,1)S(1)}, u32[]{:S(2)}, u32[]{:S(2)}) collective-permute-start(bf16[1,768,384]{2,1,0:T(8,128)(2,1)S(1)} %slice.643), channel_id=1, source_target_pairs={{0,16},{8,24},{16,0},{24,8},{1,17},{9,25},{17,1},{25,9},{2,18},{10... | collective-permute-start | bytes 1769480 | tf_op jit(solution)/shard_map/ppermute | solution.py:104
  251.6 30.5 %collective-permute-start.30 = (bf16[1,384,768]{2,1,0:T(8,128)(2,1)}, bf16[1,384,768]{2,1,0:T(8,128)(2,1)S(1)}, u32[]{:S(2)}, u32[]{:S(2)}) collective-permute-start(bf16[1,384,768]{2,1,0:T(8,128)(2,1)} %slice.638), channel_id=1, source_target_pairs={{0,8},{8,0},{16,24},{24,16},{1,9},{9,1},{17,25},{25,17},{2,10},{10... | collective-permute-start | bytes 1769480 | tf_op jit(solution)/shard_map/ppermute | solution.py:100
  270.9 19.0 %collective-permute-start.26 = (bf16[128,1536]{1,0:T(8,128)(2,1)S(1)}, bf16[128,1536]{1,0:T(8,128)(2,1)S(1)}, u32[]{:S(2)}, u32[]{:S(2)}) collective-permute-start(bf16[128,1536]{1,0:T(8,128)(2,1)S(1)} %slice.637), channel_id=1, source_target_pairs={{0,6},{1,7},{2,0},{3,1},{4,2},{5,3},{6,4},{7,5},{8,14},{9,15},{10,... | collective-permute-start | bytes 1179656 | tf_op jit(solution)/shard_map/ppermute | solution.py:116
  293.2 22.9 %collective-permute-start.27 = (bf16[4,256,1536]{2,1,0:T(8,128)(2,1)}, bf16[4,256,1536]{2,1,0:T(8,128)(2,1)}, u32[]{:S(2)}, u32[]{:S(2)}) collective-permute-start(bf16[4,256,1536]{2,1,0:T(8,128)(2,1)} %pad_maximum_fusion.7), channel_id=1, source_target_pairs={{0,1},{1,0},{2,3},{3,2},{4,5},{5,4},{6,7},{7,6},{8,9},{9,8},{10,11... | collective-permute-start | bytes 9437192 | tf_op jit(solution)/shard_map/ppermute | solution.py:108
  381.1 36.1 %collective-permute-start.47 = (bf16[4,256,1536]{2,1,0:T(8,128)(2,1)}, bf16[4,256,1536]{2,1,0:T(8,128)(2,1)}, u32[]{:S(2)}, u32[]{:S(2)}) collective-permute-start(bf16[4,256,1536]{2,1,0:T(8,128)(2,1)} %slice.657), channel_id=1, source_target_pairs={{0,1},{1,0},{2,3},{3,2},{4,5},{5,4},{6,7},{7,6},{8,9},{9,8},{10,11... | collective-permute-start | bytes 9437192 | tf_op jit(solution)/shard_map/ppermute | solution.py:108
  385.6 36.7 %collective-permute-start.40 = (bf16[4,272,1536]{2,1,0:T(8,128)(2,1)}, bf16[4,272,1536]{2,1,0:T(8,128)(2,1)S(1)}, u32[]{:S(2)}, u32[]{:S(2)}) collective-permute-start(bf16[4,272,1536]{2,1,0:T(8,128)(2,1)} %pad_maximum_fusion.4), channel_id=1, source_target_pairs={{0,1},{1,0},{2,3},{3,2},{4,5},{5,4},{6,7},{7,6},{8,9},{9,8},{10,11... | collective-permute-start | bytes 10027016 | tf_op jit(solution)/shard_map/ppermute | solution.py:108
  407.0 194.4 %collective-permute-start.80 = (bf16[1,384,768]{2,1,0:T(8,128)(2,1)}, bf16[1,384,768]{2,1,0:T(8,128)(2,1)}, u32[]{:S(2)}, u32[]{:S(2)}) collective-permute-start(bf16[1,384,768]{2,1,0:T(8,128)(2,1)} %get-tuple-element.137), channel_id=1, source_target_pairs={{0,8},{8,0},{16,24},{24,16},{1,9},{9,1},{17,25},{25,17},{2,10},{10... | collective-permute-start | bytes 1769480 | tf_op jit(solution)/shard_map/ppermute | solution.py:100
  420.2 50.3 %collective-permute-start.52 = (bf16[128,1536]{1,0:T(8,128)(2,1)S(1)}, bf16[128,1536]{1,0:T(8,128)(2,1)S(1)}, u32[]{:S(2)}, u32[]{:S(2)}) collective-permute-start(bf16[128,1536]{1,0:T(8,128)(2,1)S(1)} %get-tuple-element.154), channel_id=1, source_target_pairs={{0,6},{1,7},{2,0},{3,1},{4,2},{5,3},{6,4},{7,5},{8,14},{9,15},{10,... | collective-permute-start | bytes 1179656 | tf_op jit(solution)/shard_map/ppermute | solution.py:116
  422.0 48.5 %collective-permute-start.48 = (bf16[128,1536]{1,0:T(8,128)(2,1)S(1)}, bf16[128,1536]{1,0:T(8,128)(2,1)S(1)}, u32[]{:S(2)}, u32[]{:S(2)}) collective-permute-start(bf16[128,1536]{1,0:T(8,128)(2,1)S(1)} %get-tuple-element.156), channel_id=1, source_target_pairs={{0,2},{1,3},{2,4},{3,5},{4,6},{5,7},{6,0},{7,1},{8,10},{9,11},{10,... | collective-permute-start | bytes 1179656 | tf_op jit(solution)/shard_map/ppermute | solution.py:112
  423.3 27.4 %collective-permute-start.41 = (bf16[128,1536]{1,0:T(8,128)(2,1)S(1)}, bf16[128,1536]{1,0:T(8,128)(2,1)S(1)}, u32[]{:S(2)}, u32[]{:S(2)}) collective-permute-start(bf16[128,1536]{1,0:T(8,128)(2,1)S(1)} %get-tuple-element.148), channel_id=1, source_target_pairs={{0,2},{1,3},{2,4},{3,5},{4,6},{5,7},{6,0},{7,1},{8,10},{9,11},{10,... | collective-permute-start | bytes 1179656 | tf_op jit(solution)/shard_map/ppermute | solution.py:112
  424.6 63.6 %collective-permute-start.43 = (bf16[144,1536]{1,0:T(8,128)(2,1)S(1)}, bf16[144,1536]{1,0:T(8,128)(2,1)S(1)}, u32[]{:S(2)}, u32[]{:S(2)}) collective-permute-start(bf16[144,1536]{1,0:T(8,128)(2,1)S(1)} %get-tuple-element.150), channel_id=1, source_target_pairs={{0,2},{1,3},{2,4},{3,5},{4,6},{5,7},{6,0},{7,1},{8,10},{9,11},{10,... | collective-permute-start | bytes 1327112 | tf_op jit(solution)/shard_map/ppermute | solution.py:112
  468.1 20.1 %collective-permute-start.44 = (bf16[128,1536]{1,0:T(8,128)(2,1)S(1)}, bf16[128,1536]{1,0:T(8,128)(2,1)S(1)}, u32[]{:S(2)}, u32[]{:S(2)}) collective-permute-start(bf16[128,1536]{1,0:T(8,128)(2,1)S(1)} %get-tuple-element.147), channel_id=1, source_target_pairs={{0,6},{1,7},{2,0},{3,1},{4,2},{5,3},{6,4},{7,5},{8,14},{9,15},{10,... | collective-permute-start | bytes 1179656 | tf_op jit(solution)/shard_map/ppermute | solution.py:116
  470.5 19.7 %collective-permute-start.42 = (bf16[128,1536]{1,0:T(8,128)(2,1)S(1)}, bf16[128,1536]{1,0:T(8,128)(2,1)S(1)}, u32[]{:S(2)}, u32[]{:S(2)}) collective-permute-start(bf16[128,1536]{1,0:T(8,128)(2,1)S(1)} %fusion.119), channel_id=1, source_target_pairs={{0,2},{1,3},{2,4},{3,5},{4,6},{5,7},{6,0},{7,1},{8,10},{9,11},{10,... | collective-permute-start | bytes 1179656 | tf_op jit(solution)/shard_map/ppermute | solution.py:112
  470.6 27.4 %collective-permute-start.46 = (bf16[144,1536]{1,0:T(8,128)(2,1)S(1)}, bf16[144,1536]{1,0:T(8,128)(2,1)S(1)}, u32[]{:S(2)}, u32[]{:S(2)}) collective-permute-start(bf16[144,1536]{1,0:T(8,128)(2,1)S(1)} %fusion.113), channel_id=1, source_target_pairs={{0,6},{1,7},{2,0},{3,1},{4,2},{5,3},{6,4},{7,5},{8,14},{9,15},{10,... | collective-permute-start | bytes 1327112 | tf_op jit(solution)/shard_map/ppermute | solution.py:116
  488.2 26.3 %collective-permute-start.51 = (bf16[128,1536]{1,0:T(8,128)(2,1)S(1)}, bf16[128,1536]{1,0:T(8,128)(2,1)S(1)}, u32[]{:S(2)}, u32[]{:S(2)}) collective-permute-start(bf16[128,1536]{1,0:T(8,128)(2,1)S(1)} %get-tuple-element.153), channel_id=1, source_target_pairs={{0,6},{1,7},{2,0},{3,1},{4,2},{5,3},{6,4},{7,5},{8,14},{9,15},{10,... | collective-permute-start | bytes 1179656 | tf_op jit(solution)/shard_map/ppermute | solution.py:116
  488.2 27.0 %collective-permute-start.50 = (bf16[128,1536]{1,0:T(8,128)(2,1)S(1)}, bf16[128,1536]{1,0:T(8,128)(2,1)S(1)}, u32[]{:S(2)}, u32[]{:S(2)}) collective-permute-start(bf16[128,1536]{1,0:T(8,128)(2,1)S(1)} %get-tuple-element.155), channel_id=1, source_target_pairs={{0,2},{1,3},{2,4},{3,5},{4,6},{5,7},{6,0},{7,1},{8,10},{9,11},{10,... | collective-permute-start | bytes 1179656 | tf_op jit(solution)/shard_map/ppermute | solution.py:112
  490.2 40.5 %collective-permute-start.53 = (bf16[128,1536]{1,0:T(8,128)(2,1)S(1)}, bf16[128,1536]{1,0:T(8,128)(2,1)S(1)}, u32[]{:S(2)}, u32[]{:S(2)}) collective-permute-start(bf16[128,1536]{1,0:T(8,128)(2,1)S(1)} %get-tuple-element.157), channel_id=1, source_target_pairs={{0,6},{1,7},{2,0},{3,1},{4,2},{5,3},{6,4},{7,5},{8,14},{9,15},{10,... | collective-permute-start | bytes 1179656 | tf_op jit(solution)/shard_map/ppermute | solution.py:116
  498.0 32.7 %collective-permute-start.49 = (bf16[128,1536]{1,0:T(8,128)(2,1)S(1)}, bf16[128,1536]{1,0:T(8,128)(2,1)S(1)}, u32[]{:S(2)}, u32[]{:S(2)}) collective-permute-start(bf16[128,1536]{1,0:T(8,128)(2,1)S(1)} %get-tuple-element.158), channel_id=1, source_target_pairs={{0,2},{1,3},{2,4},{3,5},{4,6},{5,7},{6,0},{7,1},{8,10},{9,11},{10,... | collective-permute-start | bytes 1179656 | tf_op jit(solution)/shard_map/ppermute | solution.py:112
  514.5 88.9 %collective-permute-start.85 = (bf16[1,384,768]{2,1,0:T(8,128)(2,1)}, bf16[1,384,768]{2,1,0:T(8,128)(2,1)}, u32[]{:S(2)}, u32[]{:S(2)}) collective-permute-start(bf16[1,384,768]{2,1,0:T(8,128)(2,1)} %get-tuple-element.138), channel_id=1, source_target_pairs={{0,16},{8,24},{16,0},{24,8},{1,17},{9,25},{17,1},{25,9},{2,18},{10... | collective-permute-start | bytes 1769480 | tf_op jit(solution)/shard_map/ppermute | solution.py:104
  515.2 89.8 %collective-permute-start.89 = (bf16[1,384,768]{2,1,0:T(8,128)(2,1)}, bf16[1,384,768]{2,1,0:T(8,128)(2,1)}, u32[]{:S(2)}, u32[]{:S(2)}) collective-permute-start(bf16[1,384,768]{2,1,0:T(8,128)(2,1)} %get-tuple-element.129), channel_id=1, source_target_pairs={{0,8},{8,0},{16,24},{24,16},{1,9},{9,1},{17,25},{25,17},{2,10},{10... | collective-permute-start | bytes 1769480 | tf_op jit(solution)/shard_map/ppermute | solution.py:100
  530.7 77.7 %collective-permute-start.87 = (bf16[1,384,768]{2,1,0:T(8,128)(2,1)}, bf16[1,384,768]{2,1,0:T(8,128)(2,1)}, u32[]{:S(2)}, u32[]{:S(2)}) collective-permute-start(bf16[1,384,768]{2,1,0:T(8,128)(2,1)} %get-tuple-element.130), channel_id=1, source_target_pairs={{0,16},{8,24},{16,0},{24,8},{1,17},{9,25},{17,1},{25,9},{2,18},{10... | collective-permute-start | bytes 1769480 | tf_op jit(solution)/shard_map/ppermute | solution.py:104
  550.9 86.9 %all-to-all-start.1 = ((bf16[1,2,128,1536]{3,1,0,2:T(2,128)(2,1)}), bf16[1,2,128,1536]{3,1,0,2:T(2,128)(2,1)}, u32[]{:S(2)}, u32[]{:S(2)}) async-start(bf16[1,2,128,1536]{3,1,0,2:T(2,128)(2,1)} %copy.300), calls=%async_computation.1 | async-start | bytes 1572864 | tf_op jit(solution)/shard_map/all_to_all | solution.py:654
  585.7 35.5 %collective-permute-start.67 = (bf16[4,4,48,1664]{3,2,1,0:T(8,128)(2,1)S(1)}, bf16[4,4,48,1664]{3,2,1,0:T(8,128)(2,1)S(1)}, u32[]{:S(2)}, u32[]{:S(2)}) collective-permute-start(bf16[4,4,48,1664]{3,2,1,0:T(8,128)(2,1)S(1)} %bitcast.551), channel_id=1, source_target_pairs={{0,1},{1,0},{2,3},{3,2},{4,5},{5,4},{6,7},{7,6},{8,9},{9,8},{10,11... | collective-permute-start | bytes 7667720 | tf_op jit(solution)/shard_map/ppermute | solution.py:108
  605.0 102.9 %collective-permute-start.54 = (bf16[4,4,48,2176]{3,2,1,0:T(8,128)(2,1)}, bf16[4,4,48,2176]{3,2,1,0:T(8,128)(2,1)}, u32[]{:S(2)}, u32[]{:S(2)}) collective-permute-start(bf16[4,4,48,2176]{3,2,1,0:T(8,128)(2,1)} %bitcast.175), channel_id=1, source_target_pairs={{0,1},{1,0},{2,3},{3,2},{4,5},{5,4},{6,7},{7,6},{8,9},{9,8},{10,11... | collective-permute-start | bytes 10027016 | tf_op jit(solution)/shard_map/ppermute | solution.py:108
  608.4 21.8 %collective-permute-start.95 = (bf16[1,768,384]{2,1,0:T(8,128)(2,1)S(1)}, bf16[1,768,384]{2,1,0:T(8,128)(2,1)S(1)}, u32[]{:S(2)}, u32[]{:S(2)}) collective-permute-start(bf16[1,768,384]{2,1,0:T(8,128)(2,1)S(1)} %copy-done.64), channel_id=1, source_target_pairs={{0,8},{8,0},{16,24},{24,16},{1,9},{9,1},{17,25},{25,17},{2,10},{10... | collective-permute-start | bytes 1769480 | tf_op jit(solution)/shard_map/ppermute | solution.py:100
  619.6 23.6 %collective-permute-start.92 = (bf16[1,768,384]{2,1,0:T(8,128)(2,1)}, bf16[1,768,384]{2,1,0:T(8,128)(2,1)}, u32[]{:S(2)}, u32[]{:S(2)}) collective-permute-start(bf16[1,768,384]{2,1,0:T(8,128)(2,1)} %get-tuple-element.125), channel_id=1, source_target_pairs={{0,8},{8,0},{16,24},{24,16},{1,9},{9,1},{17,25},{25,17},{2,10},{10... | collective-permute-start | bytes 1769480 | tf_op jit(solution)/shard_map/ppermute | solution.py:100
  621.2 25.5 %collective-permute-start.97 = (bf16[1,768,384]{2,1,0:T(8,128)(2,1)}, bf16[1,768,384]{2,1,0:T(8,128)(2,1)}, u32[]{:S(2)}, u32[]{:S(2)}) collective-permute-start(bf16[1,768,384]{2,1,0:T(8,128)(2,1)} %get-tuple-element.126), channel_id=1, source_target_pairs={{0,16},{8,24},{16,0},{24,8},{1,17},{9,25},{17,1},{25,9},{2,18},{10... | collective-permute-start | bytes 1769480 | tf_op jit(solution)/shard_map/ppermute | solution.py:104
  630.3 25.4 %collective-permute-start.82 = (bf16[1,384,768]{2,1,0:T(8,128)(2,1)}, bf16[1,384,768]{2,1,0:T(8,128)(2,1)}, u32[]{:S(2)}, u32[]{:S(2)}) collective-permute-start(bf16[1,384,768]{2,1,0:T(8,128)(2,1)} %get-tuple-element.134), channel_id=1, source_target_pairs={{0,8},{8,0},{16,24},{24,16},{1,9},{9,1},{17,25},{25,17},{2,10},{10... | collective-permute-start | bytes 1769480 | tf_op jit(solution)/shard_map/ppermute | solution.py:100
  634.7 24.6 %collective-permute-start.84 = (bf16[1,384,768]{2,1,0:T(8,128)(2,1)}, bf16[1,384,768]{2,1,0:T(8,128)(2,1)}, u32[]{:S(2)}, u32[]{:S(2)}) collective-permute-start(bf16[1,384,768]{2,1,0:T(8,128)(2,1)} %get-tuple-element.133), channel_id=1, source_target_pairs={{0,16},{8,24},{16,0},{24,8},{1,17},{9,25},{17,1},{25,9},{2,18},{10... | collective-permute-start | bytes 1769480 | tf_op jit(solution)/shard_map/ppermute | solution.py:104
  637.8 64.1 %all-to-all-start.2 = ((bf16[1,2,128,1536]{3,1,0,2:T(2,128)(2,1)}), bf16[1,2,128,1536]{3,1,0,2:T(2,128)(2,1)S(1)}, u32[]{:S(2)}, u32[]{:S(2)}) async-start(bf16[1,2,128,1536]{3,1,0,2:T(2,128)(2,1)} %copy.312), calls=%async_computation.2 | async-start | bytes 1572864 | tf_op jit(solution)/shard_map/all_to_all | solution.py:661
  643.2 19.2 %collective-permute-start.71 = (bf16[2,48,1664]{2,1,0:T(8,128)(2,1)}, bf16[2,48,1664]{2,1,0:T(8,128)(2,1)S(1)}, u32[]{:S(2)}, u32[]{:S(2)}) collective-permute-start(bf16[2,48,1664]{2,1,0:T(8,128)(2,1)} %get-tuple-element.161), channel_id=1, source_target_pairs={{0,8},{8,0},{16,24},{24,16},{1,9},{9,1},{17,25},{25,17},{2,10},{10... | collective-permute-start | bytes 958472 | tf_op jit(solution)/shard_map/ppermute | solution.py:100
  646.6 19.4 %collective-permute-start.69 = (bf16[2,48,1664]{2,1,0:T(8,128)(2,1)}, bf16[2,48,1664]{2,1,0:T(8,128)(2,1)S(1)}, u32[]{:S(2)}, u32[]{:S(2)}) collective-permute-start(bf16[2,48,1664]{2,1,0:T(8,128)(2,1)} %get-tuple-element.163), channel_id=1, source_target_pairs={{0,16},{8,24},{16,0},{24,8},{1,17},{9,25},{17,1},{25,9},{2,18},{10... | collective-permute-start | bytes 958472 | tf_op jit(solution)/shard_map/ppermute | solution.py:104
  655.7 19.4 %collective-permute-start.88 = (bf16[1,384,768]{2,1,0:T(8,128)(2,1)S(1)}, bf16[1,384,768]{2,1,0:T(8,128)(2,1)S(1)}, u32[]{:S(2)}, u32[]{:S(2)}) collective-permute-start(bf16[1,384,768]{2,1,0:T(8,128)(2,1)S(1)} %get-tuple-element.128), channel_id=1, source_target_pairs={{0,8},{8,0},{16,24},{24,16},{1,9},{9,1},{17,25},{25,17},{2,10},{10... | collective-permute-start | bytes 1769480 | tf_op jit(solution)/shard_map/ppermute | solution.py:100
  659.3 19.4 %collective-permute-start.90 = (bf16[1,384,768]{2,1,0:T(8,128)(2,1)S(1)}, bf16[1,384,768]{2,1,0:T(8,128)(2,1)S(1)}, u32[]{:S(2)}, u32[]{:S(2)}) collective-permute-start(bf16[1,384,768]{2,1,0:T(8,128)(2,1)S(1)} %get-tuple-element.127), channel_id=1, source_target_pairs={{0,16},{8,24},{16,0},{24,8},{1,17},{9,25},{17,1},{25,9},{2,18},{10... | collective-permute-start | bytes 1769480 | tf_op jit(solution)/shard_map/ppermute | solution.py:104
  662.4 25.3 %collective-permute-start.94 = (bf16[1,768,384]{2,1,0:T(8,128)(2,1)S(1)}, bf16[1,768,384]{2,1,0:T(8,128)(2,1)S(1)}, u32[]{:S(2)}, u32[]{:S(2)}) collective-permute-start(bf16[1,768,384]{2,1,0:T(8,128)(2,1)S(1)} %get-tuple-element.122), channel_id=1, source_target_pairs={{0,8},{8,0},{16,24},{24,16},{1,9},{9,1},{17,25},{25,17},{2,10},{10... | collective-permute-start | bytes 1769480 | tf_op jit(solution)/shard_map/ppermute | solution.py:100
  666.0 25.3 %collective-permute-start.96 = (bf16[1,768,384]{2,1,0:T(8,128)(2,1)S(1)}, bf16[1,768,384]{2,1,0:T(8,128)(2,1)S(1)}, u32[]{:S(2)}, u32[]{:S(2)}) collective-permute-start(bf16[1,768,384]{2,1,0:T(8,128)(2,1)S(1)} %get-tuple-element.121), channel_id=1, source_target_pairs={{0,16},{8,24},{16,0},{24,8},{1,17},{9,25},{17,1},{25,9},{2,18},{10... | collective-permute-start | bytes 1769480 | tf_op jit(solution)/shard_map/ppermute | solution.py:104
  675.0 31.3 %collective-permute-start.68 = (bf16[2,48,1664]{2,1,0:T(8,128)(2,1)}, bf16[2,48,1664]{2,1,0:T(8,128)(2,1)}, u32[]{:S(2)}, u32[]{:S(2)}) collective-permute-start(bf16[2,48,1664]{2,1,0:T(8,128)(2,1)} %get-tuple-element.164), channel_id=1, source_target_pairs={{0,8},{8,0},{16,24},{24,16},{1,9},{9,1},{17,25},{25,17},{2,10},{10... | collective-permute-start | bytes 958472 | tf_op jit(solution)/shard_map/ppermute | solution.py:100
  678.7 27.7 %collective-permute-start.73 = (bf16[2,48,1664]{2,1,0:T(8,128)(2,1)}, bf16[2,48,1664]{2,1,0:T(8,128)(2,1)}, u32[]{:S(2)}, u32[]{:S(2)}) collective-permute-start(bf16[2,48,1664]{2,1,0:T(8,128)(2,1)} %get-tuple-element.162), channel_id=1, source_target_pairs={{0,16},{8,24},{16,0},{24,8},{1,17},{9,25},{17,1},{25,9},{2,18},{10... | collective-permute-start | bytes 958472 | tf_op jit(solution)/shard_map/ppermute | solution.py:104
  687.7 18.7 %collective-permute-start.70 = (bf16[2,48,1664]{2,1,0:T(8,128)(2,1)}, bf16[2,48,1664]{2,1,0:T(8,128)(2,1)}, u32[]{:S(2)}, u32[]{:S(2)}) collective-permute-start(bf16[2,48,1664]{2,1,0:T(8,128)(2,1)} %get-tuple-element.160), channel_id=1, source_target_pairs={{0,8},{8,0},{16,24},{24,16},{1,9},{9,1},{17,25},{25,17},{2,10},{10... | collective-permute-start | bytes 958472 | tf_op jit(solution)/shard_map/ppermute | solution.py:100
  (158 other events, 2438.2 us)

commit v2 on v1

v2 whole, which is shorter than its diff:
```python
import math

import jax
import jax.numpy as jnp
from jax import lax
from jax.experimental import pallas as pl
from jax.experimental.pallas import tpu as pltpu
from jax.sharding import PartitionSpec as P

QUERY_HEADS = 12
KEY_VALUE_HEADS = 2
HEAD_SIZE = 128
TOPK = 4
SEQ_DEV = 2


EPSILON = 1e-06
ROPE_BASE = 1000000.0
NEG_FILL = -1e30


def sequence_layout(doc_lens, seq_len):
    token_steps = jnp.arange(seq_len, dtype=jnp.int32)
    doc_ends = jnp.cumsum(doc_lens)
    doc_index = jnp.sum((token_steps[:, None] >= doc_ends[None, :-1]).astype(jnp.int32), axis=1)
    doc_starts = doc_ends - doc_lens
    doc_slots = jnp.arange(doc_lens.shape[0], dtype=jnp.int32)
    start_of = jnp.sum(
        jnp.where(doc_slots[None, :] == doc_index[:, None], doc_starts[None, :], 0), axis=1
    )
    return ((token_steps - start_of).astype(jnp.float32), doc_index)


def device_layout(dev_lens, seq_len):
    positions, doc_index = jax.vmap(lambda single: sequence_layout(single, seq_len))(dev_lens)
    doc_count = dev_lens.shape[1]
    labels = doc_index + doc_count * jnp.arange(dev_lens.shape[0], dtype=jnp.int32)[:, None]
    return (positions.reshape(-1), labels.reshape(-1))


def rope_tables(positions, head_dim):
    freq_index = jnp.arange(head_dim // 2, dtype=jnp.float32)
    frequency = jnp.exp(freq_index * (-2.0 / head_dim) * math.log(ROPE_BASE))
    angle_table = positions[:, None] * frequency[None, :]
    return (jnp.cos(angle_table), jnp.sin(angle_table))


def slot_ranks(route_flat, prio_flat):
    same = route_flat[:, None] == route_flat[None, :]
    ahead = prio_flat[None, :] < prio_flat[:, None]
    return jnp.sum(jnp.logical_and(same, ahead).astype(jnp.int32), axis=1)


def swap_x(value):
    return lax.ppermute(value, "dp", [(i, i ^ 1) for i in range(4)])


def swap_y(value):
    return lax.ppermute(value, "dp", [(i, i ^ 2) for i in range(4)])


def swap_core(value):
    return lax.ppermute(value, "expert", [(i, i ^ 1) for i in range(8)])


def shift_up(value):
    return lax.ppermute(value, "expert", [(i, (i + 2) % 8) for i in range(8)])


def shift_down(value):
    return lax.ppermute(value, "expert", [(i, (i + 6) % 8) for i in range(8)])


def add_low(left, right):
    return (left.astype(jnp.float32) + right.astype(jnp.float32)).astype(jnp.bfloat16)


def any_spec():
    return pl.BlockSpec(memory_space=pl.ANY)


def smem_spec():
    return pl.BlockSpec(memory_space=pltpu.SMEM)


def staged(out_ref, hold, sems):
    pltpu.make_async_copy(hold, hold, sems.at[0]).wait()
    copy = pltpu.make_async_copy(hold, out_ref, sems.at[1])
    copy.start()
    copy.wait()


def deal_kernel(seq_ref, rel_ref, src_ref, out_ref, hold, sems):
    devices = out_ref.shape[0]
    piece = out_ref.shape[1] // SEQ_DEV // devices
    for b in range(devices):
        for k in range(SEQ_DEV):
            row = pl.multiple_of(seq_ref[b * SEQ_DEV + k] * piece, piece)
            for j in range(devices):
                pltpu.make_async_copy(
                    src_ref.at[rel_ref[j], pl.ds(row, piece), :],
                    hold.at[b, pl.ds((k * devices + j) * piece, piece), :],
                    sems.at[0],
                ).start()
    staged(out_ref, hold, sems)


def move_blocks(kernel, shape, scalars, arrays):
    dtype = arrays[0].dtype
    return pl.pallas_call(
        kernel,
        out_shape=jax.ShapeDtypeStruct(shape, dtype),
        in_specs=[smem_spec()] * len(scalars) + [any_spec()] * len(arrays),
        out_specs=any_spec(),
        scratch_shapes=[pltpu.VMEM(shape, dtype), pltpu.SemaphoreType.DMA((2,))],
        compiler_params=pltpu.CompilerParams(vmem_limit_bytes=40 * 1024 * 1024),
    )(*scalars, *arrays)


def expert_order(tuned, count):
    if not tuned:
        return jnp.arange(count, dtype=jnp.int32)
    me = lax.axis_index("expert")
    level, core = me // 2, me % 2
    order = [
        ((level + off) % 4) * 2 + (core + flip) % 2 for flip in range(2) for off in (0, 3, 1, 2)
    ]
    return jnp.stack(order).astype(jnp.int32)


def all_order():
    me = lax.axis_index("expert")
    plane = lax.axis_index("dp")
    level, core = me // 2, me % 2
    order = [
        ((plane ^ k) * 4 + (level + off) % 4) * 2 + (core + flip) % 2
        for flip in range(2)
        for k in range(4)
        for off in (0, 3, 1, 2)
    ]
    return jnp.stack(order).astype(jnp.int32)


def dot_nn(left, right):
    return lax.dot_general(
        left, right, (((1,), (0,)), ((), ())), preferred_element_type=jnp.float32
    )


def dot_nt(left, right):
    return lax.dot_general(
        left, right, (((1,), (1,)), ((), ())), preferred_element_type=jnp.float32
    )


def dot_tn(left, right):
    return lax.dot_general(
        left, right, (((0,), (0,)), ((), ())), preferred_element_type=jnp.float32
    )


GELU_SCALE = math.sqrt(2.0 / math.pi)
GELU_CUBE = 0.044715
MIB = 1024 * 1024


def expert_kernel(plan, capacity, *refs):
    count = plan["inputs"]
    my_ref, codes_ref, router_ref, grads_ref = refs[:4]
    inputs = refs[4 : 4 + count]
    (
        back_keep,
        back_send,
        out_keep,
        out_send,
        x_out,
        dy_out,
        hid_out,
        dga_out,
        dua_out,
    ) = refs[4 + count : 13 + count]
    (
        gate_w,
        up_w,
        down_w,
        h_buf,
        d_buf,
        hot,
        x_s,
        dy_s,
        y_s,
        dx_s,
        hid_s,
        dga_s,
        dua_s,
        act_s,
        slope_s,
        code_s,
        gates_s,
        sgate_s,
        dg_s,
        stage_b,
        stage_o,
        sem_w,
        sem_h,
        sem_d,
        sem_s,
        sem_b,
        sem_o,
    ) = refs[13 + count :]
    blocks = plan["blocks"]
    pairs = blocks // 2
    per_device, width, ff = gate_w.shape
    tokens = h_buf.shape[1] // 2
    slots = 2 * capacity
    experts = codes_ref.shape[1]
    my_first = my_ref[0] * per_device
    dtype = jnp.bfloat16

    def window(hold, axis, e, owner, step):
        start = (owner or 0) * step
        if axis == 1:
            return hold.at[e, pl.ds(start, step), :]
        return hold.at[e, :, pl.ds(start, step)]

    weight_copies = []
    for t, (hold, axis) in enumerate(((gate_w, 1), (up_w, 1), (down_w, 2))):
        for e in range(per_device):
            copies = []
            for ref_index, lead, owner in plan["weights"][t][e]:
                src = inputs[ref_index].at[lead]
                step = src.shape[axis - 1]
                sem = sem_w.at[t * per_device + e, len(copies)]
                copy = pltpu.make_async_copy(src, window(hold, axis, e, owner, step), sem)
                copy.start()
                copies.append(copy)
            weight_copies.append(copies)

    def fetch(p):
        slot = p % 2
        copies = []
        for half in range(2):
            for k, (ref_index, lead, row, rows) in enumerate(plan["tokens"][2 * p + half]):
                src = inputs[ref_index] if lead is None else inputs[ref_index].at[lead]
                dst = h_buf.at[slot, pl.ds(half * tokens + row, rows), :]
                copies.append(pltpu.make_async_copy(src, dst, sem_h.at[slot, half, k]))
            dst = d_buf.at[slot, pl.ds(half * tokens, tokens), :]
            copies.append(pltpu.make_async_copy(grads_ref.at[2 * p + half], dst, sem_d.at[slot, half]))
        for copy in copies:
            copy.start()
        return copies

    row = lax.broadcasted_iota(jnp.int32, (slots, 2 * tokens), 0)
    col = lax.broadcasted_iota(jnp.int32, (slots, 2 * tokens), 1)
    second = row >= capacity
    same = jnp.logical_xor(second, col < tokens)
    target = (row - jnp.where(second, capacity, 0) + 1).astype(jnp.float32)
    flying = fetch(0)
    for p in range(pairs):
        slot = p % 2
        later = fetch(p + 1) if p + 1 < pairs else []
        for copy in flying:
            copy.wait()
        flying = later
        codes = jnp.concatenate([codes_ref[2 * p], codes_ref[2 * p + 1]], axis=1)
        logits = dot_nt(router_ref[...], h_buf[slot])
        chosen = codes > 0.0
        top = jnp.max(jnp.where(chosen, logits, NEG_FILL), axis=0, keepdims=True)
        raised = jnp.where(chosen, jnp.exp(logits - top), 0.0)
        code_s[...] = codes
        gates_s[...] = raised / jnp.sum(raised, axis=0, keepdims=True)
        for e in range(per_device):
            code_row = code_s[pl.ds(my_first + e, 1), :]
            gate_row = gates_s[pl.ds(my_first + e, 1), :]
            hit = jnp.logical_and(same, code_row == target)
            one = jnp.where(hit, 1.0, 0.0).astype(dtype)
            hot[e, p] = one
            gate_slot = jnp.sum(jnp.where(hit, gate_row, 0.0), axis=1, keepdims=True)
            rows = pl.ds(p * slots, slots)
            sgate_s[e, rows, :] = jnp.broadcast_to(gate_slot, (slots, 128))
            x_s[e, rows, :] = dot_nn(one, h_buf[slot]).astype(dtype)
            dy_s[e, rows, :] = dot_nn(one, d_buf[slot]).astype(dtype)

    saves = []
    for e in range(per_device):
        for copy in weight_copies[e] + weight_copies[per_device + e]:
            copy.wait()
        save = pltpu.make_async_copy(x_s.at[e], x_out.at[e], sem_s.at[0, e])
        save.start()
        saves.append(save)
        gate_slot = sgate_s[e][:, :1]

        @pl.loop(0, ff // 256)
        def _(j):
            cols = pl.ds(pl.multiple_of(j * 256, 256), 256)
            ga = dot_nn(x_s[e], gate_w[e, :, cols])
            ua = dot_nn(x_s[e], up_w[e, :, cols])
            square = ga * ga
            tan = jnp.tanh(GELU_SCALE * (ga + GELU_CUBE * square * ga))
            act = 0.5 * ga * (1.0 + tan)
            slope = 0.5 * (1.0 + tan) + 0.5 * ga * (1.0 - tan * tan) * GELU_SCALE * (
                1.0 + 3.0 * GELU_CUBE * square
            )
            act_s[:, cols] = act
            slope_s[:, cols] = ua * slope
            hid_s[e, :, cols] = (act * ua).astype(dtype)

        save = pltpu.make_async_copy(hid_s.at[e], hid_out.at[e], sem_s.at[1, e])
        save.start()
        saves.append(save)
        for copy in weight_copies[2 * per_device + e]:
            copy.wait()
        dg_s[e] = jnp.zeros(dg_s.shape[1:], jnp.float32)

        @pl.loop(0, width // 256)
        def _(j):
            cols = pl.ds(pl.multiple_of(j * 256, 256), 256)
            y = dot_nn(hid_s[e], down_w[e, :, cols]).astype(dtype).astype(jnp.float32)
            dy = dy_s[e, :, cols].astype(jnp.float32)
            dg_s[e] += jnp.broadcast_to(
                jnp.sum(dy * y, axis=1, keepdims=True), dg_s.shape[1:]
            )
            y_s[e, :, cols] = (gate_slot * y).astype(dtype)
            dy_s[e, :, cols] = (gate_slot * dy).astype(dtype)

        save = pltpu.make_async_copy(dy_s.at[e], dy_out.at[e], sem_s.at[2, e])
        save.start()
        saves.append(save)

        @pl.loop(0, ff // 256)
        def _(j):
            cols = pl.ds(pl.multiple_of(j * 256, 256), 256)
            dhid = dot_nt(dy_s[e], down_w[e, cols, :])
            dga_s[e, :, cols] = (dhid * slope_s[:, cols]).astype(dtype)
            dua_s[e, :, cols] = (dhid * act_s[:, cols]).astype(dtype)

        for k, (hold, out) in enumerate(((dga_s, dga_out), (dua_s, dua_out))):
            save = pltpu.make_async_copy(hold.at[e], out.at[e], sem_s.at[3 + k, e])
            save.start()
            saves.append(save)

        @pl.loop(0, width // 256)
        def _(j):
            cols = pl.ds(pl.multiple_of(j * 256, 256), 256)
            dx = dot_nt(dga_s[e], gate_w[e, cols, :]) + dot_nt(dua_s[e], up_w[e, cols, :])
            dx_s[e, :, cols] = dx.astype(dtype)

    table_rows = stage_b.shape[2] - tokens
    table_row = lax.broadcasted_iota(jnp.int32, (table_rows, 2 * tokens), 0)
    sends = {}
    for p in range(pairs):
        slot = p % 2
        for copy in sends.pop(p - 2, []):
            copy.wait()
        rows = pl.ds(p * slots, slots)

        @pl.loop(0, width // 512)
        def _(j):
            cols = pl.ds(pl.multiple_of(j * 512, 512), 512)
            back = jnp.zeros((2 * tokens, 512), jnp.float32)
            outs = jnp.zeros((2 * tokens, 512), jnp.float32)
            for e in range(per_device):
                back += dot_tn(hot[e, p], dx_s[e, rows, cols])
                outs += dot_tn(hot[e, p], y_s[e, rows, cols])
            for half in range(2):
                part = slice(half * tokens, (half + 1) * tokens)
                stage_b[slot, half, :tokens, cols] = back[part].astype(dtype)
                stage_o[slot, half, :, cols] = outs[part].astype(dtype)

        tables = [jnp.zeros((table_rows, 2 * tokens), jnp.float32) for _ in range(2)]
        for e in range(per_device):
            dg = dg_s[e, rows, :][:, :1]
            line = jnp.sum(hot[e, p].astype(jnp.float32) * dg, axis=0, keepdims=True)
            mine = table_row == my_first + e
            for half in range(2):
                part = line[:, half * tokens : (half + 1) * tokens]
                high = part.astype(dtype).astype(jnp.float32)
                both = jnp.concatenate([high, part - high], axis=1)
                tables[half] = jnp.where(mine, both, tables[half])
        for half in range(2):
            stage_b[slot, half, tokens:, : 2 * tokens] = tables[half].astype(dtype)
            stage_b[slot, half, tokens:, 2 * tokens :] = jnp.zeros(
                (table_rows, width - 2 * tokens), dtype
            )
        first = 2 * p
        keep = first < blocks // 2
        at = pl.ds(first if keep else first - blocks // 2, 2)
        copies = [
            pltpu.make_async_copy(
                stage_b.at[slot], (back_keep if keep else back_send).at[at], sem_b.at[slot]
            ),
            pltpu.make_async_copy(
                stage_o.at[slot], (out_keep if keep else out_send).at[at], sem_o.at[slot]
            ),
        ]
        for copy in copies:
            copy.start()
        sends[p] = copies
    for copies in sends.values():
        for copy in copies:
            copy.wait()
    for save in saves:
        save.wait()


def run_experts(plan, capacity, table_rows, scalars, codes, router_t, grads_all, inputs):
    blocks, tokens, width = grads_all.shape
    experts = codes.shape[1]
    per_device, ff = plan["per_device"], plan["ff"]
    rows = blocks * capacity
    bf, f32 = jnp.bfloat16, jnp.float32
    half = blocks // 2
    back = jax.ShapeDtypeStruct((half, tokens + table_rows, width), bf)
    outs = jax.ShapeDtypeStruct((half, tokens, width), bf)
    wide = jax.ShapeDtypeStruct((per_device, rows, width), bf)
    thin = jax.ShapeDtypeStruct((per_device, rows, ff), bf)
    vmem = pl.BlockSpec(memory_space=pltpu.VMEM)
    sem = pltpu.SemaphoreType.DMA
    return pl.pallas_call(
        lambda *refs: expert_kernel(plan, capacity, *refs),
        out_shape=(back, back, outs, outs, wide, wide, thin, thin, thin),
        in_specs=[smem_spec(), vmem, vmem, any_spec()] + [any_spec()] * len(inputs),
        out_specs=tuple([any_spec()] * 9),
        scratch_shapes=[
            pltpu.VMEM((per_device, width, ff), bf),
            pltpu.VMEM((per_device, width, ff), bf),
            pltpu.VMEM((per_device, ff, width), bf),
            pltpu.VMEM((2, 2 * tokens, width), bf),
            pltpu.VMEM((2, 2 * tokens, width), bf),
            pltpu.VMEM((per_device, blocks // 2, 2 * capacity, 2 * tokens), bf),
            pltpu.VMEM((per_device, rows, width), bf),
            pltpu.VMEM((per_device, rows, width), bf),
            pltpu.VMEM((per_device, rows, width), bf),
            pltpu.VMEM((per_device, rows, width), bf),
            pltpu.VMEM((per_device, rows, ff), bf),
            pltpu.VMEM((per_device, rows, ff), bf),
            pltpu.VMEM((per_device, rows, ff), bf),
            pltpu.VMEM((rows, ff), f32),
            pltpu.VMEM((rows, ff), f32),
            pltpu.VMEM((experts, 2 * tokens), f32),
            pltpu.VMEM((experts, 2 * tokens), f32),
            pltpu.VMEM((per_device, rows, 128), f32),
            pltpu.VMEM((per_device, rows, 128), f32),
            pltpu.VMEM((2, 2, tokens + table_rows, width), bf),
            pltpu.VMEM((2, 2, tokens, width), bf),
            sem((3 * per_device, 4)),
            sem((2, 2, 2)),
            sem((2, 2)),
            sem((5, per_device)),
            sem((2,)),
            sem((2,)),
        ],
        cost_estimate=pl.CostEstimate(flops=55000000000, transcendentals=0, bytes_accessed=50000000),
        compiler_params=pltpu.CompilerParams(vmem_limit_bytes=61 * MIB),
    )(scalars, codes, router_t, grads_all, *inputs)


def down_kernel(hid_ref, dy_ref, out_ref):
    out_ref[0, 0] = dot_tn(hid_ref[0], dy_ref[0]).astype(jnp.bfloat16)


def grad_down_blocks(hid, dy, parts):
    per_device, rows, ff = hid.shape
    step = dy.shape[2] // parts
    return pl.pallas_call(
        down_kernel,
        grid=(per_device, parts),
        out_shape=jax.ShapeDtypeStruct((parts, per_device, ff, step), jnp.bfloat16),
        in_specs=[
            pl.BlockSpec((1, rows, ff), lambda e, d: (e, 0, 0)),
            pl.BlockSpec((1, rows, step), lambda e, d: (e, 0, d)),
        ],
        out_specs=pl.BlockSpec((1, 1, ff, step), lambda e, d: (d, e, 0, 0)),
        cost_estimate=pl.CostEstimate(flops=7700000000, transcendentals=0, bytes_accessed=7000000),
        compiler_params=pltpu.CompilerParams(vmem_limit_bytes=40 * MIB),
    )(hid, dy)


def gate_up_kernel(x_ref, dga_ref, dua_ref, out_ref):
    out_ref[0, 0, 0] = dot_tn(x_ref[0], dga_ref[0]).astype(jnp.bfloat16)
    out_ref[0, 1, 0] = dot_tn(x_ref[0], dua_ref[0]).astype(jnp.bfloat16)


def grad_gate_up_blocks(x, dga, dua, parts):
    per_device, rows, ff = dga.shape
    step = x.shape[2] // parts
    return pl.pallas_call(
        gate_up_kernel,
        grid=(per_device, parts),
        out_shape=jax.ShapeDtypeStruct((parts, 2, per_device, step, ff), jnp.bfloat16),
        in_specs=[
            pl.BlockSpec((1, rows, step), lambda e, d: (e, 0, d)),
            pl.BlockSpec((1, rows, ff), lambda e, d: (e, 0, 0)),
            pl.BlockSpec((1, rows, ff), lambda e, d: (e, 0, 0)),
        ],
        out_specs=pl.BlockSpec((1, 2, 1, step, ff), lambda e, d: (d, 0, e, 0, 0)),
        cost_estimate=pl.CostEstimate(flops=11000000000, transcendentals=0, bytes_accessed=10000000),
        compiler_params=pltpu.CompilerParams(vmem_limit_bytes=40 * MIB),
    )(x, dga, dua)


def gather_weight_pieces(w_gate, w_up, w_down, tuned):
    if not tuned:
        parts = [
            lax.all_gather(w_gate, "dp", axis=1, tiled=True),
            lax.all_gather(w_up, "dp", axis=1, tiled=True),
            lax.all_gather(w_down, "dp", axis=2, tiled=True),
        ]
        count = w_gate.shape[0]
        return parts, [[[(t, (e,), None)] for e in range(count)] for t in range(3)]
    both = jnp.stack([w_gate, w_up])
    flat = lax.all_gather(both.reshape(-1, both.shape[-1]), "dp", axis=0, tiled=True)
    down = lax.all_gather(w_down.reshape(-1, w_down.shape[-1]), "dp", axis=0, tiled=True)
    parts = [flat.reshape((4,) + both.shape), down.reshape((4,) + w_down.shape)]
    places = [
        [[(0, (d, t, e), d) for d in range(4)] for e in range(w_gate.shape[0])] for t in range(2)
    ]
    places.append([[(1, (d, e), d) for d in range(4)] for e in range(w_gate.shape[0])])
    return parts, places


def gather_token_pieces(value, tuned, wait_for):
    rows = value.shape[0]
    if not tuned:
        full = lax.all_gather(value, "expert", axis=0, tiled=False)
        return [full], [[(0, b, 0, rows)] for b in range(full.shape[0])]
    below = shift_up(value)
    above = shift_down(value)
    far_a = shift_up(after(below[: rows // 2], wait_for))
    far_b = shift_down(after(above[rows // 2 :], wait_for))
    arrays = [value, below, above, far_a, far_b]
    arrays = arrays + [swap_core(v) for v in arrays]
    places = []
    for base in (0, 5):
        places += [[(base + k, None, 0, rows)] for k in range(3)]
        places += [[(base + 3, None, 0, rows // 2), (base + 4, None, rows // 2, rows // 2)]]
    return arrays, places


def rotate(values, cos_wide, sin_wide):
    return values * cos_wide + pltpu.roll(values, HEAD_SIZE // 2, 1) * sin_wide


def tile_cols(j, size):
    return pl.ds(pl.multiple_of(j * size, size), size)


def forward_kernel(plan, *refs):
    order_ref, x_ref, cos_ref, sin_ref, lab_col_ref, lab_row_ref = refs[:6]
    count = plan["inputs"]
    inputs = refs[6 : 6 + count]
    (
        h2_ref,
        res_ref,
        h1_ref,
        q_ref,
        k_ref,
        v_ref,
        p_ref,
        o_ref,
        aux_ref,
        w_full_out,
        w_full,
        sem_in,
        sem_save,
    ) = refs[6 + count :]
    width = x_ref.shape[1]
    tokens = x_ref.shape[0]
    bf = jnp.bfloat16
    heads = QUERY_HEADS // KEY_VALUE_HEADS
    kv_width = KEY_VALUE_HEADS * HEAD_SIZE
    main = width + 2 * kv_width
    base = main + 128
    for ref_index, lead, order_index in plan["places"]:
        src = inputs[ref_index]
        for at in lead:
            src = src.at[at]
        rows = src.shape[0]
        if order_index is None:
            dst = w_full
        else:
            start = pl.multiple_of(order_ref[order_index] * rows, rows)
            dst = w_full.at[pl.ds(start, rows), :]
        pltpu.make_async_copy(src, dst, sem_in).start()
    x = x_ref[...].astype(jnp.float32)
    inverse = lax.rsqrt(jnp.mean(x * x, axis=1, keepdims=True) + EPSILON)
    pltpu.make_async_copy(w_full, w_full, sem_in).wait()
    save = pltpu.make_async_copy(w_full, w_full_out, sem_save)
    save.start()
    side = w_full[:, main : main + 128].astype(jnp.float32).T
    gain = side[:1]
    h1_ref[...] = (x * inverse * gain).astype(bf)
    cos_wide, sin_wide = cos_ref[...], sin_ref[...]

    @pl.loop(0, width // 256)
    def _(j):
        raw = dot_nn(h1_ref[...], w_full[:, tile_cols(j, 256)])
        both = [
            rotate(raw[:, half * HEAD_SIZE : (half + 1) * HEAD_SIZE], cos_wide, sin_wide)
            for half in range(2)
        ]
        q_ref[:, tile_cols(j, 256)] = jnp.concatenate(both, axis=1).astype(bf)

    raw = dot_nn(h1_ref[...], w_full[:, width : width + kv_width])
    both = [
        rotate(raw[:, half * HEAD_SIZE : (half + 1) * HEAD_SIZE], cos_wide, sin_wide)
        for half in range(KEY_VALUE_HEADS)
    ]
    k_ref[...] = jnp.concatenate(both, axis=1).astype(bf)
    v_ref[...] = dot_nn(h1_ref[...], w_full[:, width + kv_width : main]).astype(bf)
    seq_len = tokens // SEQ_DEV
    query_step = lax.broadcasted_iota(jnp.int32, (seq_len, seq_len), 0)
    key_step = lax.broadcasted_iota(jnp.int32, (seq_len, seq_len), 1)
    for s in range(SEQ_DEV):
        rows = slice(s * seq_len, (s + 1) * seq_len)
        same = lab_col_ref[rows, :] == lab_row_ref[:, rows]
        allowed = jnp.logical_and(same, query_step >= key_step)[None]
        for h in range(KEY_VALUE_HEADS):
            cols = slice(h * HEAD_SIZE, (h + 1) * HEAD_SIZE)
            stack = jnp.concatenate(
                [
                    q_ref[rows, (h * heads + g) * HEAD_SIZE : (h * heads + g + 1) * HEAD_SIZE]
                    for g in range(heads)
                ],
                axis=0,
            )
            scores = dot_nt(stack, k_ref[rows, cols]) * HEAD_SIZE ** (-0.5)
            scores = scores.reshape(heads, seq_len, seq_len)
            scores = jnp.where(allowed, scores, NEG_FILL)
            top = jnp.max(scores, axis=2, keepdims=True)
            raised = jnp.exp(scores - top)
            probs = raised / jnp.sum(raised, axis=2, keepdims=True)
            probs = probs.reshape(heads * seq_len, seq_len)
            p_ref[s, h] = probs
            mixed = dot_nn(probs.astype(bf), v_ref[rows, cols]).astype(bf)
            for g in range(heads):
                o_ref[rows, (h * heads + g) * HEAD_SIZE : (h * heads + g + 1) * HEAD_SIZE] = mixed[
                    g * seq_len : (g + 1) * seq_len
                ]
    side_out = w_full[:, base + width : base + width + 128].astype(jnp.float32).T
    aux_ref[...] = jnp.concatenate([side_out, side[:8]], axis=0)

    @pl.loop(0, width // 256)
    def _(j):
        cols = tile_cols(j, 256)
        at = pl.ds(pl.multiple_of(base + j * 256, 128), 256)
        res_ref[:, cols] = x_ref[:, cols].astype(jnp.float32) + dot_nn(o_ref[...], w_full[:, at])

    res = res_ref[...]
    inverse = lax.rsqrt(jnp.mean(res * res, axis=1, keepdims=True) + EPSILON)
    moe_row = plan["experts"]
    h2_ref[...] = (res * inverse * side_out[moe_row : moe_row + 1]).astype(bf)
    save.wait()


def run_forward(plan, order, x, cos_wide, sin_wide, lab_col, lab_row, inputs, w_cols):
    tokens, width = x.shape
    bf, f32 = jnp.bfloat16, jnp.float32
    kv_width = KEY_VALUE_HEADS * HEAD_SIZE
    seq_len = tokens // SEQ_DEV
    stack = QUERY_HEADS // KEY_VALUE_HEADS * seq_len
    vmem = pl.BlockSpec(memory_space=pltpu.VMEM)
    shape = jax.ShapeDtypeStruct
    sem = pltpu.SemaphoreType.DMA
    return pl.pallas_call(
        lambda *refs: forward_kernel(plan, *refs),
        out_shape=(
            shape((tokens, width), bf),
            shape((tokens, width), f32),
            shape((tokens, width), bf),
            shape((tokens, width), bf),
            shape((tokens, kv_width), bf),
            shape((tokens, kv_width), bf),
            shape((SEQ_DEV, KEY_VALUE_HEADS, stack, seq_len), f32),
            shape((tokens, width), bf),
            shape((136, width), f32),
            shape((width, w_cols), bf),
        ),
        in_specs=[smem_spec()] + [vmem] * 5 + [any_spec()] * len(inputs),
        out_specs=tuple([vmem] * 9 + [any_spec()]),
        scratch_shapes=[
            pltpu.VMEM((width, w_cols), bf),
            sem,
            sem,
        ],
        cost_estimate=pl.CostEstimate(flops=17600000000, transcendentals=0, bytes_accessed=16000000),
        compiler_params=pltpu.CompilerParams(vmem_limit_bytes=56 * MIB),
    )(order, x, cos_wide, sin_wide, lab_col, lab_row, *inputs)


def send_payload(order_ref, payload, outs, sem):
    if len(outs) == 1:
        copies = [pltpu.make_async_copy(payload, outs[0], sem)]
    else:
        copies = []
        rows = payload.shape[0] // 32
        for j in range(32):
            start = pl.multiple_of(order_ref[j] * rows, rows)
            dst = outs[j // 4].at[j % 4]
            copies.append(pltpu.make_async_copy(payload.at[pl.ds(start, rows), :], dst, sem))
    for copy in copies:
        copy.start()
    pltpu.make_async_copy(payload, payload, sem).wait()


def payload_shapes(tuned, rows, cols):
    if not tuned:
        return (jax.ShapeDtypeStruct((rows, cols), jnp.bfloat16),)
    return (jax.ShapeDtypeStruct((4, rows // 32, cols), jnp.bfloat16),) * 8


def middle_kernel(experts, sums, order_ref, own_ref, dy_all, codes_ref, *refs):
    back_refs = refs[: sums]
    res_ref, h2_ref, o_ref, aux_ref, w_full_ref = refs[sums : sums + 5]
    base = w_full_ref.shape[1] - refs[sums].shape[1] - 128
    rest = refs[sums + 5 :]
    outs = rest[:-8]
    dres_ref, dmix_ref, w_out, dy, payload, dres_low, sem_w, sem_p = rest[-8:]
    tokens, width = res_ref.shape
    bf = jnp.bfloat16
    load = pltpu.make_async_copy(w_full_ref.at[:, pl.ds(base, width)], w_out, sem_w.at[0])
    load.start()
    load_dy = pltpu.make_async_copy(dy_all.at[own_ref[0]], dy, sem_w.at[1])
    load_dy.start()
    back = back_refs[0][...]
    if sums == 5:
        cut = tokens // 2
        up_one, down_one, up_two, down_two = [ref[...].astype(jnp.float32) for ref in back_refs[1:]]
        first = jnp.concatenate([up_two, up_one[cut:]], axis=0)
        second = jnp.concatenate([down_one[:cut], down_two], axis=0)
        back = back + first + second
    grad_pair = (
        back[tokens : tokens + experts, :tokens]
        + back[tokens : tokens + experts, tokens : 2 * tokens]
    )
    back = back[:tokens]
    router_t = aux_ref[:experts, :].astype(bf)
    gain = aux_ref[experts : experts + 1, :]
    logits = dot_nt(router_t, h2_ref[...])
    chosen = codes_ref[...] > 0.0
    top = jnp.max(jnp.where(chosen, logits, NEG_FILL), axis=0, keepdims=True)
    raised = jnp.where(chosen, jnp.exp(logits - top), 0.0)
    gates = raised / jnp.sum(raised, axis=0, keepdims=True)
    inner = jnp.sum(gates * grad_pair, axis=0, keepdims=True)
    dlog = jnp.where(chosen, gates * (grad_pair - inner), 0.0).astype(bf)
    grad_router = dot_nn(dlog, h2_ref[...])
    dh2 = back + dot_tn(dlog, router_t)
    res = res_ref[...]
    inverse = lax.rsqrt(jnp.mean(res * res, axis=1, keepdims=True) + EPSILON)
    scaled = dh2 * gain
    grad_gain = jnp.sum(dh2 * res * inverse, axis=0, keepdims=True)
    load_dy.wait()
    dres = (
        dy[...].astype(jnp.float32)
        + inverse * scaled
        - res * inverse**3 * jnp.mean(scaled * res, axis=1, keepdims=True)
    )
    dres_ref[...] = dres
    dres_low[...] = dres.astype(bf)
    pad = jnp.zeros((128 - experts - 8, width), jnp.float32)
    side = jnp.concatenate(
        [grad_router, jnp.broadcast_to(grad_gain, (8, width)), pad], axis=0
    )
    payload[:, width : width + 128] = side.T.astype(bf)

    @pl.loop(0, width // 256)
    def _(j):
        cols = tile_cols(j, 256)
        payload[:, cols] = dot_tn(o_ref[...], dres_low[:, cols]).astype(bf)

    load.wait()

    @pl.loop(0, width // 256)
    def _(j):
        cols = tile_cols(j, 256)
        dmix_ref[:, cols] = dot_nt(dres_low[...], w_out[cols, :]).astype(bf)

    send_payload(order_ref, payload, outs, sem_p)


def run_middle(tuned, experts, order, own, dy_all, codes, backs, res, h2, o, aux, w_full):
    tokens, width = res.shape
    bf, f32 = jnp.bfloat16, jnp.float32
    vmem = pl.BlockSpec(memory_space=pltpu.VMEM)
    shape = jax.ShapeDtypeStruct
    sem = pltpu.SemaphoreType.DMA
    payload = payload_shapes(tuned, width, width + 128)
    return pl.pallas_call(
        lambda *refs: middle_kernel(experts, len(backs), *refs),
        out_shape=payload + (shape((tokens, width), f32), shape((tokens, width), bf)),
        in_specs=[smem_spec()] * 2 + [any_spec()] + [vmem] * (len(backs) + 5) + [any_spec()],
        out_specs=tuple([any_spec()] * len(payload) + [vmem] * 2),
        scratch_shapes=[
            pltpu.VMEM((width, width), bf),
            pltpu.VMEM((tokens, width), bf),
            pltpu.VMEM((width, width + 128), bf),
            pltpu.VMEM((tokens, width), bf),
            sem((2,)),
            sem,
        ],
        cost_estimate=pl.CostEstimate(flops=17600000000, transcendentals=0, bytes_accessed=16000000),
        compiler_params=pltpu.CompilerParams(vmem_limit_bytes=56 * MIB),
    )(order, own, dy_all, codes, *backs, res, h2, o, aux, w_full)


def backward_kernel(order_ref, x_ref, cos_ref, sin_ref, *refs):
    dres_ref, dmix_ref, h1_ref, q_ref, k_ref, v_ref, p_ref, aux_ref, w_full_ref = refs[:9]
    rest = refs[9:]
    outs = rest[:-7]
    dx_ref, w_in, payload, dqkv, dh1, sem_w, sem_p = rest[-7:]
    tokens, width = x_ref.shape
    bf = jnp.bfloat16
    heads = QUERY_HEADS // KEY_VALUE_HEADS
    kv_width = KEY_VALUE_HEADS * HEAD_SIZE
    main = width + 2 * kv_width
    scale = HEAD_SIZE ** (-0.5)
    load = pltpu.make_async_copy(w_full_ref.at[:, pl.ds(0, main)], w_in, sem_w)
    load.start()
    seq_len = tokens // SEQ_DEV
    for s in range(SEQ_DEV):
        rows = slice(s * seq_len, (s + 1) * seq_len)
        cos_wide, sin_wide = cos_ref[rows, :], -sin_ref[rows, :]
        cos_tall = jnp.concatenate([cos_wide] * heads, axis=0)
        sin_tall = jnp.concatenate([sin_wide] * heads, axis=0)
        for h in range(KEY_VALUE_HEADS):
            cols = slice(h * HEAD_SIZE, (h + 1) * HEAD_SIZE)
            places = [
                slice((h * heads + g) * HEAD_SIZE, (h * heads + g + 1) * HEAD_SIZE)
                for g in range(heads)
            ]
            q_tall = jnp.concatenate([q_ref[rows, place] for place in places], axis=0)
            dmix = jnp.concatenate([dmix_ref[rows, place] for place in places], axis=0)
            probs = p_ref[s, h]
            dprobs = dot_nt(dmix, v_ref[rows, cols])
            dv = dot_tn(probs.astype(bf), dmix)
            inner = jnp.sum(probs * dprobs, axis=1, keepdims=True)
            dscores = (probs * (dprobs - inner)).astype(bf)
            dq = rotate(dot_nn(dscores, k_ref[rows, cols]) * scale, cos_tall, sin_tall)
            dk = rotate(dot_tn(dscores, q_tall) * scale, cos_wide, sin_wide)
            for g, place in enumerate(places):
                dqkv[rows, place] = dq[g * seq_len : (g + 1) * seq_len].astype(bf)
            dqkv[rows, width + h * HEAD_SIZE : width + (h + 1) * HEAD_SIZE] = dk.astype(bf)
            at = width + kv_width + h * HEAD_SIZE
            dqkv[rows, at : at + HEAD_SIZE] = dv.astype(bf)
    load.wait()

    @pl.loop(0, width // 256)
    def _(j):
        cols = tile_cols(j, 256)
        dh1[:, cols] = dot_nt(dqkv[...], w_in[cols, :])

    @pl.loop(0, main // 256)
    def _(j):
        cols = tile_cols(j, 256)
        payload[:, cols] = dot_tn(h1_ref[...], dqkv[:, cols]).astype(bf)

    x = x_ref[...].astype(jnp.float32)
    gain = aux_ref[128:129, :]
    inverse = lax.rsqrt(jnp.mean(x * x, axis=1, keepdims=True) + EPSILON)
    grad = dh1[...]
    scaled = grad * gain
    grad_gain = jnp.sum(grad * x * inverse, axis=0, keepdims=True)
    payload[:, main : main + 128] = jnp.broadcast_to(grad_gain, (128, width)).T.astype(bf)
    dx = (
        dres_ref[...]
        + inverse * scaled
        - x * inverse**3 * jnp.mean(scaled * x, axis=1, keepdims=True)
    )
    dx_ref[...] = dx.astype(bf)
    send_payload(order_ref, payload, outs, sem_p)


def run_backward(tuned, order, x, cos_wide, sin_wide, dres, dmix, h1, q, k, v, p, aux, w_full):
    tokens, width = x.shape
    bf, f32 = jnp.bfloat16, jnp.float32
    vmem = pl.BlockSpec(memory_space=pltpu.VMEM)
    shape = jax.ShapeDtypeStruct
    sem = pltpu.SemaphoreType.DMA
    main = width + 2 * KEY_VALUE_HEADS * HEAD_SIZE
    payload = payload_shapes(tuned, width, main + 128)
    return pl.pallas_call(
        backward_kernel,
        out_shape=payload + (shape((tokens, width), bf),),
        in_specs=[smem_spec()] + [vmem] * 11 + [any_spec()],
        out_specs=tuple([any_spec()] * len(payload) + [vmem]),
        scratch_shapes=[
            pltpu.VMEM((width, main), bf),
            pltpu.VMEM((width, main + 128), bf),
            pltpu.VMEM((tokens, main), bf),
            pltpu.VMEM((tokens, width), f32),
            sem,
            sem,
        ],
        cost_estimate=pl.CostEstimate(flops=18700000000, transcendentals=0, bytes_accessed=17000000),
        compiler_params=pltpu.CompilerParams(vmem_limit_bytes=56 * MIB),
    )(order, x, cos_wide, sin_wide, dres, dmix, h1, q, k, v, p, aux, w_full)


def after(value, *others):
    return lax.optimization_barrier((value,) + others)[0]


def swap_diagonal(value):
    return lax.ppermute(value, "dp", [(i, i ^ 3) for i in range(4)])


def shift_two(value):
    return lax.ppermute(value, "expert", [(i, (i + 4) % 8) for i in range(8)])


def gather_all_pieces(value, tuned):
    if not tuned:
        full = lax.all_gather(value, ("dp", "expert"), axis=0, tiled=True)
        return [full], [(0, (), None)], None
    level = jnp.stack([value, shift_up(value), shift_down(value), shift_two(value)])
    from_x = swap_x(level)
    from_y = swap_y(level)
    far_a = swap_x(from_y[:2])
    far_b = swap_y(from_x[2:])
    arrays = [level, from_x, from_y, far_a, far_b]
    arrays = arrays + [swap_core(v) for v in arrays]
    places = []
    for c in range(2):
        for k in range(4):
            for r in range(4):
                ref, lead = (k, r) if k < 3 else ((3, r) if r < 2 else (4, r - 2))
                places.append((c * 5 + ref, (lead,), (c * 4 + k) * 4 + r))
    return arrays, places, (level, from_x, from_y)


def scatter_payload(outs, tuned):
    if not tuned:
        return lax.psum_scatter(
            outs[0], ("dp", "expert"), scatter_dimension=0, tiled=True
        ).astype(jnp.float32)
    f32, bf = jnp.float32, jnp.bfloat16
    sums = [outs[k].astype(f32) + swap_core(outs[4 + k]).astype(f32) for k in range(4)]
    from_x = swap_x(sums[1].astype(bf))
    from_y = swap_y(sums[2].astype(bf))
    from_far = swap_diagonal(sums[3].astype(bf))
    level = [
        sums[0][r] + from_x[r].astype(f32) + from_y[r].astype(f32) + from_far[r].astype(f32)
        for r in range(4)
    ]
    below, above, far = [v.astype(bf) for v in level[1:]]
    got = [shift_down(below), shift_up(above), shift_two(far)]
    return level[0] + got[0].astype(f32) + got[1].astype(f32) + got[2].astype(f32)


def sum_blocks(keep, send, cut, tuned, got=None, wait_for=()):
    if not tuned:
        blocks = jnp.concatenate([keep, send], axis=0)
        return [
            lax.psum_scatter(blocks, "expert", scatter_dimension=0, tiled=False).astype(jnp.float32)
        ], None
    got = swap_core(send) if got is None else got
    sums = [keep[i].astype(jnp.float32) + got[i].astype(jnp.float32) for i in range(4)]
    own = sums[0]
    to_below, to_above, far = [v.astype(jnp.bfloat16) for v in sums[1:]]
    top = lax.broadcasted_iota(jnp.int32, own.shape, 0) < cut
    messages = (jnp.where(top, far, to_above), jnp.where(top, to_below, far))
    up_one = shift_up(after(messages[0], *wait_for))
    down_one = shift_down(after(messages[1], *wait_for))
    up_two = shift_up(add_low(to_above[:cut], up_one[:cut]))
    down_two = shift_down(add_low(to_below[cut:], down_one[cut:]))
    return [own, up_one, down_one, up_two, down_two], messages


def gather_dealt(value, tuned, level):
    if not tuned:
        return lax.all_gather(value, "expert", axis=0, tiled=False)
    cut = value.shape[0] // 32 * 16
    below = shift_up(value)
    above = shift_down(value)
    far_a = shift_up(after(below[:cut], level[1]))
    far_b = shift_down(after(above[cut:], level[2]))
    parts = jnp.stack([value, below, above, jnp.concatenate([far_a, far_b], axis=0)])
    return jnp.concatenate([parts, swap_core(parts)], axis=0)


def pad_columns(value, width):
    return jnp.pad(value, ((0, 0), (0, width - value.shape[1])))


def body(
    tokens,
    cotangent,
    lengths,
    placement,
    routes,
    priority,
    g_attn,
    w_query,
    key_projection,
    value_projection,
    w_out,
    g_moe,
    w_router,
    w_gate,
    w_up,
    w_down,
):
    row_seqs, piece_len, width = tokens.shape
    expert_devices = lax.axis_size("expert")
    plane_size = lax.axis_size("dp")
    tuned = expert_devices == 8 and plane_size == 4
    my_index = lax.axis_index("expert")
    seq_len = piece_len * expert_devices
    token_count = SEQ_DEV * seq_len
    query_width = w_query.shape[1]
    kv_width = key_projection.shape[1]
    expert_count = w_router.shape[1]
    per_device = expert_count // expert_devices
    capacity = (9 * token_count * TOPK + 64 * expert_count - 1) // (64 * expert_count) * 8
    code_list = jnp.arange(row_seqs, dtype=jnp.int32)
    source = jnp.sum(
        jnp.where(placement[:, None] == code_list[None, :], code_list[:, None], 0), axis=0
    )
    pack = jnp.concatenate(
        [
            w_query,
            key_projection,
            value_projection,
            pad_columns(g_attn[:, None], 128),
            w_out,
            pad_columns(jnp.concatenate([w_router, g_moe[:, None]], axis=1), 128),
        ],
        axis=1,
    )
    pack_parts, pack_places, level = gather_all_pieces(pack, tuned)
    send_tokens = tokens[source].reshape(expert_devices, SEQ_DEV, piece_len, width)
    if tuned:
        send_tokens = after(send_tokens, level[0])
    got_tokens = lax.all_to_all(send_tokens, "expert", split_axis=0, concat_axis=2, tiled=True)
    x_local = got_tokens.reshape(token_count, width)
    ranks = slot_ranks(routes.reshape(-1), priority.reshape(-1)).reshape(token_count, TOPK)
    codes = jnp.minimum(ranks, capacity) + 1
    expert_list = jnp.arange(expert_count, dtype=jnp.int32)
    picks = routes[None, :, :] == expert_list[:, None, None]
    code_table = jnp.sum(jnp.where(picks, codes[None], 0), axis=2)
    table_rows = -(-expert_count // 16) * 16
    table = jnp.zeros((table_rows, width), jnp.bfloat16)
    table = table.at[:expert_count, :token_count].set(code_table.astype(jnp.bfloat16))
    early = jnp.concatenate([cotangent.reshape(token_count, width), table], axis=0)
    if tuned:
        early = after(early, x_local)
    early_all = gather_dealt(early, tuned, level)
    order = expert_order(tuned, expert_devices)
    rel_of = jnp.zeros((expert_devices,), jnp.int32)
    for b in range(expert_devices):
        rel_of = jnp.where(jnp.arange(expert_devices) == order[b], b, rel_of)
    seqs = source.reshape(expert_devices, SEQ_DEV)[order].reshape(-1)
    if piece_len % 16 == 0:
        shape = (expert_devices, token_count, width)
        grads_all = move_blocks(deal_kernel, shape, [seqs, rel_of], [early_all])
    else:
        pieces = early_all[:, :token_count].reshape(expert_devices, row_seqs, piece_len, width)
        pieces = pieces[rel_of][:, seqs].reshape(
            expert_devices, expert_devices, SEQ_DEV, piece_len, width
        )
        grads_all = pieces.transpose(1, 2, 0, 3, 4).reshape(expert_devices, token_count, width)
    codes_all = early_all[:, token_count : token_count + expert_count, :token_count].astype(
        jnp.float32
    )
    own_block = rel_of[my_index].reshape(1)
    weight_parts, weight_places = gather_weight_pieces(w_gate, w_up, w_down, tuned)

    own_seqs = lax.dynamic_slice_in_dim(source, my_index * SEQ_DEV, SEQ_DEV)
    positions, labels = device_layout(lengths[own_seqs], seq_len)
    cosine_table, sine_values = rope_tables(positions, HEAD_SIZE)
    cos_wide = jnp.concatenate([cosine_table, cosine_table], axis=1)
    sin_wide = jnp.concatenate([-sine_values, sine_values], axis=1)
    plan = {
        "inputs": len(pack_parts),
        "experts": expert_count,
        "places": pack_places,
    }
    row_order = all_order()
    normed_moe, residual, h1, q, k, v, probs, mixed, aux, w_full = run_forward(
        plan,
        row_order,
        x_local,
        cos_wide,
        sin_wide,
        labels[:, None],
        labels[None, :],
        pack_parts,
        pack.shape[1],
    )
    token_parts, token_places = gather_token_pieces(normed_moe, tuned, grads_all)
    token_places = [
        [(r + len(weight_parts), lead, row, rows) for r, lead, row, rows in line]
        for line in token_places
    ]
    inputs = weight_parts + token_parts
    plan = {
        "inputs": len(inputs),
        "blocks": expert_devices,
        "per_device": per_device,
        "ff": w_gate.shape[2],
        "weights": weight_places,
        "tokens": token_places,
    }
    scalars = jnp.stack([my_index, lax.axis_index("dp")]).astype(jnp.int32)
    router_t = aux[:expert_count].astype(jnp.bfloat16)
    back_keep, back_send, out_keep, out_send, x_slots, dy_slots, hid, dga, dua = run_experts(
        plan, capacity, table_rows, scalars, codes_all, router_t, grads_all, inputs
    )
    cut = token_count // 2
    back_got, out_got = None, None
    if tuned:
        back_got = swap_core(back_send)
        out_got = swap_core(after(out_send, back_got))
    backs, messages = sum_blocks(back_keep, back_send, cut, tuned, back_got)
    if tuned:
        hid, x_slots = after(hid, *messages), after(x_slots, *messages)
    even = width % (128 * plane_size) == 0
    down_blocks = grad_down_blocks(hid, dy_slots, plane_size if even else 1)
    gate_up_blocks = grad_gate_up_blocks(x_slots, dga, dua, plane_size if even else 1)
    if even:
        flat = down_blocks.reshape(-1, down_blocks.shape[-1])
        owned_down = lax.psum_scatter(flat, "dp", scatter_dimension=0, tiled=True)
        owned_down = owned_down.reshape(down_blocks.shape[1:])
        flat = gate_up_blocks.reshape(-1, gate_up_blocks.shape[-1])
        owned_gate_up = lax.psum_scatter(flat, "dp", scatter_dimension=0, tiled=True)
        owned_gate_up = owned_gate_up.reshape(gate_up_blocks.shape[1:])
    else:
        owned_down = lax.psum_scatter(down_blocks[0], "dp", scatter_dimension=2, tiled=True)
        owned_gate_up = lax.psum_scatter(gate_up_blocks[0], "dp", scatter_dimension=2, tiled=True)
    owned_down = owned_down.astype(jnp.float32)
    owned_gate = owned_gate_up[0].astype(jnp.float32)
    owned_up = owned_gate_up[1].astype(jnp.float32)
    if tuned:
        residual, out_keep = after(residual, out_got), after(out_keep, *backs[1:3])
    sums, messages = sum_blocks(out_keep, out_send, cut, tuned, out_got, backs[3:])
    if tuned:
        backs[0] = after(backs[0], *messages)
    middle = run_middle(
        tuned,
        expert_count,
        row_order,
        own_block,
        grads_all,
        codes_all[0] if tuned else codes_all[own_block[0]],
        backs,
        residual,
        normed_moe,
        mixed,
        aux,
        w_full,
    )
    payload_out, dres, dmix = middle[:-2], middle[-2], middle[-1]
    owned_out = scatter_payload(payload_out, tuned)
    final = run_backward(
        tuned,
        row_order,
        x_local,
        cos_wide,
        sin_wide,
        dres,
        dmix,
        h1,
        q,
        k,
        v,
        probs,
        aux,
        w_full,
    )
    payload_in, grad_x = final[:-1], final[-1]
    if tuned:
        payload_in = [after(v, sums[1], sums[2]) for v in payload_in]
    owned_in = scatter_payload(payload_in, tuned)
    total = residual + sums[0]
    if tuned:
        total = total + jnp.concatenate([sums[3], sums[1][cut:]], axis=0).astype(jnp.float32)
        total = total + jnp.concatenate([sums[2][:cut], sums[4]], axis=0).astype(jnp.float32)
    out_low = total.astype(jnp.bfloat16)
    deal_out, deal_grad = (
        lax.all_to_all(
            out_low.reshape(1, SEQ_DEV, seq_len, width),
            "expert",
            split_axis=2,
            concat_axis=0,
            tiled=True,
        ),
        lax.all_to_all(
            grad_x.reshape(1, SEQ_DEV, seq_len, width),
            "expert",
            split_axis=2,
            concat_axis=0,
            tiled=True,
        ),
    )
    output = deal_out.reshape(row_seqs, piece_len, width)[placement]
    input_grad = deal_grad.reshape(row_seqs, piece_len, width)[placement]
    return (
        output,
        input_grad,
        owned_in[:, query_width + 2 * kv_width],
        owned_in[:, :query_width],
        owned_in[:, query_width : query_width + kv_width],
        owned_in[:, query_width + kv_width : query_width + 2 * kv_width],
        owned_out[:, :width],
        owned_out[:, width + expert_count],
        owned_out[:, width : width + expert_count],
        owned_gate,
        owned_up,
        owned_down,
    )


def solution(mesh):
    return jax.shard_map(
        body,
        mesh=mesh,
        in_specs=(
            P("dp", "expert", None),
            P("dp", "expert", None),
            P("dp", None),
            P("dp"),
            P(("dp", "expert"), None),
            P(("dp", "expert"), None),
            P(("dp", "expert")),
            P(("dp", "expert"), None),
            P(("dp", "expert"), None),
            P(("dp", "expert"), None),
            P(("dp", "expert"), None),
            P(("dp", "expert")),
            P(("dp", "expert"), None),
            P("expert", "dp", None),
            P("expert", "dp", None),
            P("expert", None, "dp"),
        ),
        out_specs=(
            P("dp", "expert", None),
            P("dp", "expert", None),
            P(("dp", "expert")),
            P(("dp", "expert"), None),
            P(("dp", "expert"), None),
            P(("dp", "expert"), None),
            P(("dp", "expert"), None),
            P(("dp", "expert")),
            P(("dp", "expert"), None),
            P("expert", "dp", None),
            P("expert", "dp", None),
            P("expert", None, "dp"),
        ),
        check_vma=False,
    )
```

time: 768 us -> 594 us (0.77)
  matrix products: 124 us -> 0 us
  starting transfers between devices: 156 us -> 63.4 us
  Pallas kernels: 51.4 us -> 127 us
  local copies, waits for them, and re-layouts: 93.9 us -> 50.3 us
  other arithmetic: 87.7 us -> 53.9 us
  waiting for transfers between devices: 243 us -> 275 us
  between operations: 5.35 us -> 15.2 us
    dot_general x35 -> x0, matrix products: 124 us -> none  [the longest x10 24 us: contract(): lax.dot_general(left, right, ((left_dims, right_dims), ((), ())), preferr...]
    pallas_call x0 -> x6, Pallas kernels: none -> 117 us  [the longest x1 50.3 us: run_experts(): pl.pallas_call(lambda *refs: expert_kernel(plan, capacity, *refs), out_sh...]
    ppermute x20 -> x11, waiting for transfers between devices: 110 us -> 45 us  [shift_down(): return lax.ppermute(value, 'expert', [(i, (i + 6) % 8) for i in range(8)])]
    ppermute x20 -> x11, waiting for transfers between devices: 54.8 us -> 113 us  [shift_up(): return lax.ppermute(value, 'expert', [(i, (i + 2) % 8) for i in range(8)])]
    pallas_call x8 -> x1, Pallas kernels: 51.4 us -> 9.76 us  [move_blocks(): pl.pallas_call(kernel, out_shape=jax.ShapeDtypeStruct(shape, dtype), in_s...]
    ppermute x25 -> x4, waiting for transfers between devices: 64.4 us -> 26.9 us  [swap_x(): return lax.ppermute(value, 'dp', [(i, i ^ 1) for i in range(4)])]
    ppermute x20 -> x11, starting transfers between devices: 54.2 us -> 21.8 us  [shift_down(): return lax.ppermute(value, 'expert', [(i, (i + 6) % 8) for i in range(8)])]
    ppermute x25 -> x4, waiting for transfers between devices: 13.6 us -> 45.8 us  [swap_y(): return lax.ppermute(value, 'dp', [(i, i ^ 2) for i in range(4)])]
  transfers between devices with their start and end apart: 101 -> 63, of which waited for: 41 -> 23; matrix products, arithmetic and copies ran while one was open for 29% -> 13% of each run, Pallas kernels for 7% -> 12%
where the time goes in v2:
time: 594 us; the launch traced here: 585 us
  waiting for transfers between devices  275 us (46%)
  Pallas kernels  127 us (21%)
  starting transfers between devices  63.4 us (11%)
  other arithmetic  53.9 us (9%)
  local copies, waits for them, and re-layouts  50.3 us (8%)
  between operations  15.2 us (3%)
    ppermute x11, waiting for transfers between devices, shift_up(): return lax.ppermute(value, 'expert', [(i, (i + 2) % 8) for i in range(8)])  113 us
    pallas_call x1, Pallas kernels, run_experts(): pl.pallas_call(lambda *refs: expert_kernel(plan, capacity, *refs), out_sh...  50.3 us
    ppermute x4, waiting for transfers between devices, swap_y(): return lax.ppermute(value, 'dp', [(i, i ^ 2) for i in range(4)])  45.8 us
    ppermute x11, waiting for transfers between devices, shift_down(): return lax.ppermute(value, 'expert', [(i, (i + 6) % 8) for i in range(8)])  45 us
    ppermute x4, waiting for transfers between devices, swap_x(): return lax.ppermute(value, 'dp', [(i, i ^ 1) for i in range(4)])  26.9 us
    ppermute x3, waiting for transfers between devices, shift_two(): return lax.ppermute(value, 'expert', [(i, (i + 4) % 8) for i in range(8)])  22.5 us
    ppermute x11, starting transfers between devices, shift_down(): return lax.ppermute(value, 'expert', [(i, (i + 6) % 8) for i in range(8)])  21.8 us
    unnamed x129, local copies, waits for them, and re-layouts  19.9 us
  transfers between devices with their start and end apart: 63, of which 23 were waited for; matrix products, arithmetic and copies ran while one was open for 13% of the time, Pallas kernels for 12%

profile of v2, /device:TPU:0, one launch (start us, length us, event | category | flops | bytes accessed | tf_op | source)
XLA Modules:
  0.0 584.8 jit_solution(16209563203132619171)
XLA Ops:
  8.5 2.9 pad_maximum_fusion.1
  12.6 3.1 collective-permute-start
  15.7 2.1 collective-permute-start.1
  21.0 6.2 %collective-permute-done = bf16[48,3840]{1,0:T(8,128)(2,1)S(1)} collective-permute-done((bf16[48,3840]{1,0:T(8,128)(2,1)S(1)}, bf16[48,3840]{1,0:T(8,128)(2,1)S(1)}, u32[]{:S(2)}, u32[]{:S(2)}) %collective-permute-start) | collective-permute-done | bytes 368672 | tf_op jit(solution)/shard_map/ppermute | solution.py:67
  27.1 6.5 %collective-permute-done.1 = bf16[48,3840]{1,0:T(8,128)(2,1)S(1)} collective-permute-done((bf16[48,3840]{1,0:T(8,128)(2,1)S(1)}, bf16[48,3840]{1,0:T(8,128)(2,1)S(1)}, u32[]{:S(2)}, u32[]{:S(2)}) %collective-permute-start.1) | collective-permute-done | bytes 368672 | tf_op jit(solution)/shard_map/ppermute | solution.py:71
  33.6 16.4 %collective-permute-done.2 = bf16[48,3840]{1,0:T(8,128)(2,1)S(1)} collective-permute-done((bf16[48,3840]{1,0:T(8,128)(2,1)S(1)}, bf16[48,3840]{1,0:T(8,128)(2,1)S(1)}, u32[]{:S(2)}, u32[]{:S(2)}) %collective-permute-start.2) | collective-permute-done | bytes 368672 | tf_op jit(solution)/shard_map/ppermute | solution.py:908
  51.3 3.7 all-to-all-start
  56.1 1.6 collective-permute-start.4
  61.9 14.0 %all-to-all-done = bf16[8,2,16,1536]{3,2,1,0:T(8,128)(2,1)S(1)} async-done(((bf16[8,2,16,1536]{3,2,1,0:T(8,128)(2,1)}), bf16[8,2,16,1536]{3,2,1,0:T(8,128)(2,1)S(1)}, u32[]{:S(2)}, u32[]{:S(2)}) %all-to-all-start) | async-done | bytes 786464 | tf_op jit(solution)/shard_map/all_to_all | solution.py:1034
  76.8 3.8 collective-permute-start.13
  80.8 26.8 %collective-permute-done.4.refs_8_ = bf16[4,48,3840]{2,1,0:T(8,128)(2,1)} collective-permute-done((bf16[4,48,3840]{2,1,0:T(8,128)(2,1)}, bf16[4,48,3840]{2,1,0:T(8,128)(2,1)}, u32[]{:S(2)}, u32[]{:S(2)}) %collective-permute-start.4) | collective-permute-done | bytes 1474592 | tf_op jit(solution)/shard_map/ppermute | solution.py:59
  107.6 2.0 slice.341
  111.1 2.0 slice.342
  115.7 2.9 collective-permute-start.15
  121.6 20.5 %collective-permute-done.5.refs_9_ = bf16[2,48,3840]{2,1,0:T(8,128)(2,1)} collective-permute-done((bf16[2,48,3840]{2,1,0:T(8,128)(2,1)}, bf16[2,48,3840]{2,1,0:T(8,128)(2,1)}, u32[]{:S(2)}, u32[]{:S(2)}) %collective-permute-start.5) | collective-permute-done | bytes 737312 | tf_op jit(solution)/shard_map/ppermute | solution.py:55
  145.8 2.5 pad_maximum_fusion
  152.4 16.0 %shard_map.247 = (bf16[256,1536]{1,0:T(8,128)(2,1)}, f32[256,1536]{1,0:T(8,128)}, bf16[256,1536]{1,0:T(8,128)(2,1)}, bf16[256,1536]{1,0:T(8,128)(2,1)}, bf16[256...) custom-call(s32[32]{0:T(128)} %stack.206.refs_0_.order_ref, ...), custom_call_target="tpu_custom_call" | custom-call | flops 17600000000 | bytes 16000000 | tf_op jit(solution)/shard_map/pallas_call | solution.py:665
  168.4 3.4 collective-permute-start.18
  173.1 33.8 %collective-permute-done.17.refs_7_ = bf16[256,1536]{1,0:T(8,128)(2,1)S(1)} collective-permute-done((bf16[256,1536]{1,0:T(8,128)(2,1)}, bf16[256,1536]{1,0:T(8,128)(2,1)S(1)}, u32[]{:S(2)}, u32[]{:S(2)}) %collective-permute-start.17) | collective-permute-done | bytes 786464 | tf_op jit(solution)/shard_map/ppermute | solution.py:67
  207.6 2.2 constant_dynamic-update-slice_fusion.6.src_ref
  209.8 9.8 %shard_map.248.refs_3_.refs_2_ = bf16[8,256,1536]{2,1,0:T(8,128)(2,1)S(1)} custom-call(s32[16]{0:T(128)S(1)} %reshape.624.seq_ref, s32[8]{0:T(128)S(1)} %compare_select_fusion.10.rel_ref, bf16[8,272,1536]{2,1,0:T(8,128)(2,1)S(1)} %constant_dynamic-update-slice_fusion.6.src_ref), custom_call_target="tpu_custom_call" | custom-call | tf_op jit(solution)/shard_map/pallas_call | solution.py:110
  219.6 2.6 copy-done.2
  222.2 1.7 collective-permute-start.20
  224.3 9.6 %collective-permute-done.20.refs_10_ = bf16[128,1536]{1,0:T(8,128)(2,1)} collective-permute-done((bf16[128,1536]{1,0:T(8,128)(2,1)S(1)}, bf16[128,1536]{1,0:T(8,128)(2,1)}, u32[]{:S(2)}, u32[]{:S(2)}) %collective-permute-start.20) | collective-permute-done | bytes 393248 | tf_op jit(solution)/shard_map/ppermute | solution.py:71
  234.0 8.3 %collective-permute-done.19.refs_9_ = bf16[128,1536]{1,0:T(8,128)(2,1)} collective-permute-done((bf16[128,1536]{1,0:T(8,128)(2,1)S(1)}, bf16[128,1536]{1,0:T(8,128)(2,1)}, u32[]{:S(2)}, u32[]{:S(2)}) %collective-permute-start.19) | collective-permute-done | bytes 393248 | tf_op jit(solution)/shard_map/ppermute | solution.py:67
  247.6 50.3 %shard_map.249 = (bf16[4,272,1536]{2,1,0:T(8,128)(2,1)}, bf16[4,272,1536]{2,1,0:T(8,128)(2,1)}, bf16[4,256,1536]{2,1,0:T(8,128)(2,1)}, bf16[4,256,1536]{2,1,0:T(...) custom-call(s32[2]{0:T(128)} %pad_add_fusion.refs_0_, ...), custom_call_target="tpu_custom_call" | custom-call | flops 54999998464 | bytes 50000000 | tf_op jit(solution)/shard_map/pallas_call | solution.py:419
  298.5 5.8 collective-permute-done.26
  304.2 5.0 bitcast_select_fusion
  309.3 6.6 %shard_map.253 = bf16[4,2,768,384]{3,2,1,0:T(8,128)(2,1)S(1)} custom-call(bf16[2,576,768]{2,1,0:T(8,128)(2,1)S(1)} %copy-done.6, bf16[2,576,1536]{2,1,0:T(8,128)(2,1)S(1)} %copy-done.4), custom_call_target="tpu_custom_call" | custom-call | flops 7699999744 | bytes 7000000 | tf_op jit(solution)/shard_map/pallas_call | solution.py:465
  315.9 2.2 copy-done.3
  319.6 2.0 copy-done.5
  323.1 10.4 %shard_map.252 = bf16[4,2,2,384,768]{4,3,2,1,0:T(8,128)(2,1)} custom-call(bf16[2,576,1536]{2,1,0:T(8,128)(2,1)S(1)} %copy-done.5, bf16[2,576,768]{2,1,0:T(8,128)(2,1)S(1)} %copy-done.7, bf16[2,576,768]{2,1,0:T(8,128)(2,1)S(1)} %copy-done.8), custom_call_target="tpu_custom_call" | custom-call | flops 11000000512 | bytes 10000000 | tf_op jit(solution)/shard_map/pallas_call | solution.py:487
  336.3 2.3 collective-permute-start.29
  340.5 3.0 add_bitcast_fusion.refs_4_
  343.5 14.7 %collective-permute-done.28.refs_5_ = bf16[272,1536]{1,0:T(8,128)(2,1)} collective-permute-done((bf16[272,1536]{1,0:T(8,128)(2,1)S(1)}, bf16[272,1536]{1,0:T(8,128)(2,1)}, u32[]{:S(2)}, u32[]{:S(2)}) %collective-permute-start.28) | collective-permute-done | bytes 835616 | tf_op jit(solution)/shard_map/ppermute | solution.py:67
  358.1 16.5 %collective-permute-done.29.refs_6_ = bf16[272,1536]{1,0:T(8,128)(2,1)} collective-permute-done((bf16[272,1536]{1,0:T(8,128)(2,1)S(1)}, bf16[272,1536]{1,0:T(8,128)(2,1)}, u32[]{:S(2)}, u32[]{:S(2)}) %collective-permute-start.29) | collective-permute-done | bytes 835616 | tf_op jit(solution)/shard_map/ppermute | solution.py:71
  375.8 2.1 collective-permute-start.31
  379.5 3.5 bitcast_select_fusion.2
  382.9 13.7 %collective-permute-done.30.refs_7_ = bf16[128,1536]{1,0:T(8,128)(2,1)S(1)} collective-permute-done((bf16[128,1536]{1,0:T(8,128)(2,1)S(1)}, bf16[128,1536]{1,0:T(8,128)(2,1)S(1)}, u32[]{:S(2)}, u32[]{:S(2)}) %collective-permute-start.30) | collective-permute-done | bytes 393248 | tf_op jit(solution)/shard_map/ppermute | solution.py:67
  397.5 16.4 %shard_map.250 = (bf16[4,48,1664]{2,1,0:T(8,128)(2,1)}, bf16[4,48,1664]{2,1,0:T(8,128)(2,1)}, bf16[4,48,1664]{2,1,0:T(8,128)(2,1)}, bf16[4,48,1664]{2,1,0:T(8,12...) custom-call(s32[32]{0:T(128)} %stack.206.refs_0_.order_ref, ...), custom_call_target="tpu_custom_call" | custom-call | flops 17600000000 | bytes 16000000 | tf_op jit(solution)/shard_map/pallas_call | solution.py:788
  415.0 2.9 collective-permute-start.34
  417.9 17.2 %shard_map.251 = (bf16[4,48,2176]{2,1,0:T(8,128)(2,1)}, bf16[4,48,2176]{2,1,0:T(8,128)(2,1)}, bf16[4,48,2176]{2,1,0:T(8,128)(2,1)}, bf16[4,48,2176]{2,1,0:T(8,12...) custom-call(s32[32]{0:T(128)} %stack.206.refs_0_.order_ref, ...), custom_call_target="tpu_custom_call" | custom-call | flops 18699999232 | bytes 17000000 | tf_op jit(solution)/shard_map/pallas_call | solution.py:881
  435.1 2.8 copy.86
  437.9 3.5 all-to-all-start.2
  441.5 2.0 collective-permute-start.32
  449.8 26.3 %collective-permute-done.32 = bf16[256,1536]{1,0:T(8,128)(2,1)S(1)} collective-permute-done((bf16[256,1536]{1,0:T(8,128)(2,1)}, bf16[256,1536]{1,0:T(8,128)(2,1)S(1)}, u32[]{:S(2)}, u32[]{:S(2)}) %collective-permute-start.32) | collective-permute-done | bytes 786464 | tf_op jit(solution)/shard_map/ppermute | solution.py:67
  476.7 1.9 collective-permute-start.33
  480.2 7.6 %collective-permute-done.35 = bf16[128,1536]{1,0:T(8,128)(2,1)S(1)} collective-permute-done((bf16[128,1536]{1,0:T(8,128)(2,1)S(1)}, bf16[128,1536]{1,0:T(8,128)(2,1)S(1)}, u32[]{:S(2)}, u32[]{:S(2)}) %collective-permute-start.35) | collective-permute-done | bytes 393248 | tf_op jit(solution)/shard_map/ppermute | solution.py:71
  489.2 10.0 %collective-permute-done.33 = bf16[128,1536]{1,0:T(8,128)(2,1)S(1)} collective-permute-done((bf16[128,1536]{1,0:T(8,128)(2,1)S(1)}, bf16[128,1536]{1,0:T(8,128)(2,1)S(1)}, u32[]{:S(2)}, u32[]{:S(2)}) %collective-permute-start.33) | collective-permute-done | bytes 393248 | tf_op jit(solution)/shard_map/ppermute | solution.py:67
  499.2 1.9 fusion.3
  501.1 1.7 copy.83
  511.3 3.6 all-to-all-start.1
  517.4 1.9 collective-permute-start.54
  519.3 1.6 convert_add_fusion
  520.9 6.4 %collective-permute-done.38 = bf16[4,48,2176]{2,1,0:T(8,128)(2,1)} collective-permute-done((bf16[4,48,2176]{2,1,0:T(8,128)(2,1)}, bf16[4,48,2176]{2,1,0:T(8,128)(2,1)}, u32[]{:S(2)}, u32[]{:S(2)}) %collective-permute-start.38) | collective-permute-done | bytes 835616 | tf_op jit(solution)/shard_map/ppermute | solution.py:55
  527.3 19.0 %collective-permute-done.40 = bf16[4,48,2176]{2,1,0:T(8,128)(2,1)} collective-permute-done((bf16[4,48,2176]{2,1,0:T(8,128)(2,1)}, bf16[4,48,2176]{2,1,0:T(8,128)(2,1)}, u32[]{:S(2)}, u32[]{:S(2)}) %collective-permute-start.40) | collective-permute-done | bytes 835616 | tf_op jit(solution)/shard_map/ppermute | solution.py:59
  546.3 2.6 fusion.41
  548.9 2.0 collective-permute-start.44
  556.0 4.3 collective-permute-done.43
  560.3 6.2 %collective-permute-done.45 = bf16[48,2176]{1,0:T(8,128)(2,1)} collective-permute-done((bf16[48,2176]{1,0:T(8,128)(2,1)S(1)}, bf16[48,2176]{1,0:T(8,128)(2,1)}, u32[]{:S(2)}, u32[]{:S(2)}) %collective-permute-start.45) | collective-permute-done | bytes 208928 | tf_op jit(solution)/shard_map/ppermute | solution.py:908
  570.0 2.8 convert.41
  572.8 1.8 fusion.54
  574.6 1.6 convert.39
  576.2 1.6 convert.40
  (304 shorter events, 77.9 us)
Async XLA Ops:
  7.2 239.7 %all-gather.5.cloned.1.call-start = ((), (), s32[]{:S(2)}) async-start(), calls=%async_computation.6 | async-start | bytes 5898240 | tf_op jit(solution)/shard_map/all_gather | solution.py:513
  7.9 239.0 %all-gather.3.cloned.1.call-start = ((), (), s32[]{:S(2)}) async-start(), calls=%async_computation.5 | async-start | bytes 11796480 | tf_op jit(solution)/shard_map/all_gather | solution.py:512
  12.6 14.5 %collective-permute-start = (bf16[48,3840]{1,0:T(8,128)(2,1)S(1)}, bf16[48,3840]{1,0:T(8,128)(2,1)S(1)}, u32[]{:S(2)}, u32[]{:S(2)}) collective-permute-start(bf16[48,3840]{1,0:T(8,128)(2,1)S(1)} %constant_dynamic-update-slice_fusion), channel_id=1, source_target_pairs={{0,2},{1,3},{2,4},{3,5},{4,6},{5,7},{6,0},{7,1},{8,10},{9,11},{10,... | collective-permute-start | bytes 1105928 | tf_op jit(solution)/shard_map/ppermute | solution.py:67
  15.7 17.9 %collective-permute-start.1 = (bf16[48,3840]{1,0:T(8,128)(2,1)S(1)}, bf16[48,3840]{1,0:T(8,128)(2,1)S(1)}, u32[]{:S(2)}, u32[]{:S(2)}) collective-permute-start(bf16[48,3840]{1,0:T(8,128)(2,1)S(1)} %constant_dynamic-update-slice_fusion), channel_id=1, source_target_pairs={{0,6},{1,7},{2,0},{3,1},{4,2},{5,3},{6,4},{7,5},{8,14},{9,15},{10,... | collective-permute-start | bytes 1105928 | tf_op jit(solution)/shard_map/ppermute | solution.py:71
  17.7 32.2 %collective-permute-start.2 = (bf16[48,3840]{1,0:T(8,128)(2,1)S(1)}, bf16[48,3840]{1,0:T(8,128)(2,1)S(1)}, u32[]{:S(2)}, u32[]{:S(2)}) collective-permute-start(bf16[48,3840]{1,0:T(8,128)(2,1)S(1)} %constant_dynamic-update-slice_fusion), channel_id=1, source_target_pairs={{0,4},{1,5},{2,6},{3,7},{4,0},{5,1},{6,2},{7,3},{8,12},{9,13},{10,... | collective-permute-start | bytes 1105928 | tf_op jit(solution)/shard_map/ppermute | solution.py:908
  51.3 24.6 %all-to-all-start = ((bf16[8,2,16,1536]{3,2,1,0:T(8,128)(2,1)}), bf16[8,2,16,1536]{3,2,1,0:T(8,128)(2,1)S(1)}, u32[]{:S(2)}, u32[]{:S(2)}) async-start(bf16[8,2,16,1536]{3,2,1,0:T(8,128)(2,1)} %bitcast.34), calls=%async_computation | async-start | bytes 1572864 | tf_op jit(solution)/shard_map/all_to_all | solution.py:1034
  55.0 515.0 %reduce-scatter.5.cloned.1.call-start = ((), (), s32[]{:S(2)}) async-start(), calls=%async_computation.8 | async-start | bytes 5898240 | tf_op jit(solution)/shard_map/reduce_scatter | solution.py:1122
  56.1 51.5 %collective-permute-start.4 = (bf16[4,48,3840]{2,1,0:T(8,128)(2,1)}, bf16[4,48,3840]{2,1,0:T(8,128)(2,1)}, u32[]{:S(2)}, u32[]{:S(2)}) collective-permute-start(bf16[4,48,3840]{2,1,0:T(8,128)(2,1)} %pad_maximum_fusion.2.refs_6_), channel_id=1, source_target_pairs={{0,16},{8,24},{16,0},{24,8},{1,17},{9,25},{17,1},{25,9},{2,18},{10... | collective-permute-start | bytes 4423688 | tf_op jit(solution)/shard_map/ppermute | solution.py:59
  57.6 53.4 %collective-permute-start.3 = (bf16[4,48,3840]{2,1,0:T(8,128)(2,1)}, bf16[4,48,3840]{2,1,0:T(8,128)(2,1)}, u32[]{:S(2)}, u32[]{:S(2)}) collective-permute-start(bf16[4,48,3840]{2,1,0:T(8,128)(2,1)} %pad_maximum_fusion.2.refs_6_), channel_id=1, source_target_pairs={{0,8},{8,0},{16,24},{24,16},{1,9},{9,1},{17,25},{25,17},{2,10},{10... | collective-permute-start | bytes 4423688 | tf_op jit(solution)/shard_map/ppermute | solution.py:55
  76.8 41.8 %collective-permute-start.12 = (bf16[272,1536]{1,0:T(8,128)(2,1)S(1)}, bf16[272,1536]{1,0:T(8,128)(2,1)S(1)}, u32[]{:S(2)}, u32[]{:S(2)}) collective-permute-start(bf16[272,1536]{1,0:T(8,128)(2,1)S(1)} %fusion.5), channel_id=1, source_target_pairs={{0,2},{1,3},{2,4},{3,5},{4,6},{5,7},{6,0},{7,1},{8,10},{9,11},{10,... | collective-permute-start | bytes 2506760 | tf_op jit(solution)/shard_map/ppermute | solution.py:67
  76.8 38.0 %collective-permute-start.13 = (bf16[272,1536]{1,0:T(8,128)(2,1)S(1)}, bf16[272,1536]{1,0:T(8,128)(2,1)S(1)}, u32[]{:S(2)}, u32[]{:S(2)}) collective-permute-start(bf16[272,1536]{1,0:T(8,128)(2,1)S(1)} %fusion.5), channel_id=1, source_target_pairs={{0,6},{1,7},{2,0},{3,1},{4,2},{5,3},{6,4},{7,5},{8,14},{9,15},{10,... | collective-permute-start | bytes 2506760 | tf_op jit(solution)/shard_map/ppermute | solution.py:71
  109.6 32.6 %collective-permute-start.5 = (bf16[2,48,3840]{2,1,0:T(8,128)(2,1)}, bf16[2,48,3840]{2,1,0:T(8,128)(2,1)}, u32[]{:S(2)}, u32[]{:S(2)}) collective-permute-start(bf16[2,48,3840]{2,1,0:T(8,128)(2,1)} %slice.341), channel_id=1, source_target_pairs={{0,8},{8,0},{16,24},{24,16},{1,9},{9,1},{17,25},{25,17},{2,10},{10... | collective-permute-start | bytes 2211848 | tf_op jit(solution)/shard_map/ppermute | solution.py:55
  113.1 29.1 %collective-permute-start.6 = (bf16[2,48,3840]{2,1,0:T(8,128)(2,1)}, bf16[2,48,3840]{2,1,0:T(8,128)(2,1)}, u32[]{:S(2)}, u32[]{:S(2)}) collective-permute-start(bf16[2,48,3840]{2,1,0:T(8,128)(2,1)} %slice.342), channel_id=1, source_target_pairs={{0,16},{8,24},{16,0},{24,8},{1,17},{9,25},{17,1},{25,9},{2,18},{10... | collective-permute-start | bytes 2211848 | tf_op jit(solution)/shard_map/ppermute | solution.py:59
  113.6 34.6 %collective-permute-start.7 = (bf16[4,48,3840]{2,1,0:T(8,128)(2,1)}, bf16[4,48,3840]{2,1,0:T(8,128)(2,1)}, u32[]{:S(2)}, u32[]{:S(2)}) collective-permute-start(bf16[4,48,3840]{2,1,0:T(8,128)(2,1)} %pad_maximum_fusion.2.refs_6_), channel_id=1, source_target_pairs={{0,1},{1,0},{2,3},{3,2},{4,5},{5,4},{6,7},{7,6},{8,9},{9,8},{10,11... | collective-permute-start | bytes 4423688 | tf_op jit(solution)/shard_map/ppermute | solution.py:63
  115.7 28.5 %collective-permute-start.15 = (bf16[144,1536]{1,0:T(8,128)(2,1)}, bf16[144,1536]{1,0:T(8,128)(2,1)S(1)}, u32[]{:S(2)}, u32[]{:S(2)}) collective-permute-start(bf16[144,1536]{1,0:T(8,128)(2,1)} %slice.344), channel_id=1, source_target_pairs={{0,6},{1,7},{2,0},{3,1},{4,2},{5,3},{6,4},{7,5},{8,14},{9,15},{10,... | collective-permute-start | bytes 1327112 | tf_op jit(solution)/shard_map/ppermute | solution.py:71
  119.4 24.8 %collective-permute-start.14 = (bf16[128,1536]{1,0:T(8,128)(2,1)}, bf16[128,1536]{1,0:T(8,128)(2,1)}, u32[]{:S(2)}, u32[]{:S(2)}) collective-permute-start(bf16[128,1536]{1,0:T(8,128)(2,1)} %slice.343), channel_id=1, source_target_pairs={{0,2},{1,3},{2,4},{3,5},{4,6},{5,7},{6,0},{7,1},{8,10},{9,11},{10,... | collective-permute-start | bytes 1179656 | tf_op jit(solution)/shard_map/ppermute | solution.py:67
  142.1 7.7 %collective-permute-start.8 = (bf16[4,48,3840]{2,1,0:T(8,128)(2,1)}, bf16[4,48,3840]{2,1,0:T(8,128)(2,1)S(1)}, u32[]{:S(2)}, u32[]{:S(2)}) collective-permute-start(bf16[4,48,3840]{2,1,0:T(8,128)(2,1)} %collective-permute-done.3.refs_7_), channel_id=1, source_target_pairs={{0,1},{1,0},{2,3},{3,2},{4,5},{5,4},{6,7},{7,6},{8,9},{9,8},{10,11... | collective-permute-start | bytes 4423688 | tf_op jit(solution)/shard_map/ppermute | solution.py:63
  142.1 7.7 %collective-permute-start.9 = (bf16[4,48,3840]{2,1,0:T(8,128)(2,1)}, bf16[4,48,3840]{2,1,0:T(8,128)(2,1)S(1)}, u32[]{:S(2)}, u32[]{:S(2)}) collective-permute-start(bf16[4,48,3840]{2,1,0:T(8,128)(2,1)} %collective-permute-done.4.refs_8_), channel_id=1, source_target_pairs={{0,1},{1,0},{2,3},{3,2},{4,5},{5,4},{6,7},{7,6},{8,9},{9,8},{10,11... | collective-permute-start | bytes 4423688 | tf_op jit(solution)/shard_map/ppermute | solution.py:63
  144.2 4.6 collective-permute-start.10
  144.2 5.6 collective-permute-start.11
  148.2 59.4 %collective-permute-start.16 = (bf16[4,272,1536]{2,1,0:T(8,128)(2,1)}, bf16[4,272,1536]{2,1,0:T(8,128)(2,1)}, u32[]{:S(2)}, u32[]{:S(2)}) collective-permute-start(bf16[4,272,1536]{2,1,0:T(8,128)(2,1)} %pad_maximum_fusion), channel_id=1, source_target_pairs={{0,1},{1,0},{2,3},{3,2},{4,5},{5,4},{6,7},{7,6},{8,9},{9,8},{10,11... | collective-permute-start | bytes 10027016 | tf_op jit(solution)/shard_map/ppermute | solution.py:63
  168.4 38.7 %collective-permute-start.18 = (bf16[256,1536]{1,0:T(8,128)(2,1)}, bf16[256,1536]{1,0:T(8,128)(2,1)S(1)}, u32[]{:S(2)}, u32[]{:S(2)}) collective-permute-start(bf16[256,1536]{1,0:T(8,128)(2,1)} %get-tuple-element.90.refs_6_.refs_10_), channel_id=1, source_target_pairs={{0,6},{1,7},{2,0},{3,1},{4,2},{5,3},{6,4},{7,5},{8,14},{9,15},{10,... | collective-permute-start | bytes 2359304 | tf_op jit(solution)/shard_map/ppermute | solution.py:71
  171.8 35.2 %collective-permute-start.17 = (bf16[256,1536]{1,0:T(8,128)(2,1)}, bf16[256,1536]{1,0:T(8,128)(2,1)S(1)}, u32[]{:S(2)}, u32[]{:S(2)}) collective-permute-start(bf16[256,1536]{1,0:T(8,128)(2,1)} %get-tuple-element.90.refs_6_.refs_10_), channel_id=1, source_target_pairs={{0,2},{1,3},{2,4},{3,5},{4,6},{5,7},{6,0},{7,1},{8,10},{9,11},{10,... | collective-permute-start | bytes 2359304 | tf_op jit(solution)/shard_map/ppermute | solution.py:67
  173.1 71.9 %collective-permute-start.21 = (bf16[256,1536]{1,0:T(8,128)(2,1)S(1)}, bf16[256,1536]{1,0:T(8,128)(2,1)S(1)}, u32[]{:S(2)}, u32[]{:S(2)}) collective-permute-start(bf16[256,1536]{1,0:T(8,128)(2,1)S(1)} %copy-done.49), channel_id=1, source_target_pairs={{0,1},{1,0},{2,3},{3,2},{4,5},{5,4},{6,7},{7,6},{8,9},{9,8},{10,11... | collective-permute-start | bytes 2359304 | tf_op jit(solution)/shard_map/ppermute | solution.py:63
  207.0 38.1 %collective-permute-start.22 = (bf16[256,1536]{1,0:T(8,128)(2,1)S(1)}, bf16[256,1536]{1,0:T(8,128)(2,1)S(1)}, u32[]{:S(2)}, u32[]{:S(2)}) collective-permute-start(bf16[256,1536]{1,0:T(8,128)(2,1)S(1)} %collective-permute-done.17.refs_7_), channel_id=1, source_target_pairs={{0,1},{1,0},{2,3},{3,2},{4,5},{5,4},{6,7},{7,6},{8,9},{9,8},{10,11... | collective-permute-start | bytes 2359304 | tf_op jit(solution)/shard_map/ppermute | solution.py:63
  207.1 39.8 %collective-permute-start.23 = (bf16[256,1536]{1,0:T(8,128)(2,1)S(1)}, bf16[256,1536]{1,0:T(8,128)(2,1)}, u32[]{:S(2)}, u32[]{:S(2)}) collective-permute-start(bf16[256,1536]{1,0:T(8,128)(2,1)S(1)} %collective-permute-done.18.refs_8_), channel_id=1, source_target_pairs={{0,1},{1,0},{2,3},{3,2},{4,5},{5,4},{6,7},{7,6},{8,9},{9,8},{10,11... | collective-permute-start | bytes 2359304 | tf_op jit(solution)/shard_map/ppermute | solution.py:63
  222.2 11.8 %collective-permute-start.20 = (bf16[128,1536]{1,0:T(8,128)(2,1)S(1)}, bf16[128,1536]{1,0:T(8,128)(2,1)}, u32[]{:S(2)}, u32[]{:S(2)}) collective-permute-start(bf16[128,1536]{1,0:T(8,128)(2,1)S(1)} %slice.348), channel_id=1, source_target_pairs={{0,6},{1,7},{2,0},{3,1},{4,2},{5,3},{6,4},{7,5},{8,14},{9,15},{10,... | collective-permute-start | bytes 1179656 | tf_op jit(solution)/shard_map/ppermute | solution.py:71
  223.9 18.4 %collective-permute-start.19 = (bf16[128,1536]{1,0:T(8,128)(2,1)S(1)}, bf16[128,1536]{1,0:T(8,128)(2,1)}, u32[]{:S(2)}, u32[]{:S(2)}) collective-permute-start(bf16[128,1536]{1,0:T(8,128)(2,1)S(1)} %slice.347), channel_id=1, source_target_pairs={{0,2},{1,3},{2,4},{3,5},{4,6},{5,7},{6,0},{7,1},{8,10},{9,11},{10,... | collective-permute-start | bytes 1179656 | tf_op jit(solution)/shard_map/ppermute | solution.py:67
  234.0 12.9 %collective-permute-start.25 = (bf16[128,1536]{1,0:T(8,128)(2,1)}, bf16[128,1536]{1,0:T(8,128)(2,1)}, u32[]{:S(2)}, u32[]{:S(2)}) collective-permute-start(bf16[128,1536]{1,0:T(8,128)(2,1)} %collective-permute-done.20.refs_10_), channel_id=1, source_target_pairs={{0,1},{1,0},{2,3},{3,2},{4,5},{5,4},{6,7},{7,6},{8,9},{9,8},{10,11... | collective-permute-start | bytes 1179656 | tf_op jit(solution)/shard_map/ppermute | solution.py:63
  242.3 4.6 collective-permute-start.24
  297.9 6.3 %collective-permute-start.26 = (bf16[4,272,1536]{2,1,0:T(8,128)(2,1)}, bf16[4,272,1536]{2,1,0:T(8,128)(2,1)S(1)}, u32[]{:S(2)}, u32[]{:S(2)}) collective-permute-start(bf16[4,272,1536]{2,1,0:T(8,128)(2,1)} %get-tuple-element.94), channel_id=1, source_target_pairs={{0,1},{1,0},{2,3},{3,2},{4,5},{5,4},{6,7},{7,6},{8,9},{9,8},{10,11... | collective-permute-start | bytes 10027016 | tf_op jit(solution)/shard_map/ppermute | solution.py:63
  318.1 254.7 %reduce-scatter.3.cloned.1.call-start = ((), (), s32[]{:S(2)}) async-start(), calls=%async_computation.7 | async-start | bytes 11796480 | tf_op jit(solution)/shard_map/reduce_scatter | solution.py:1125
  333.5 45.9 %collective-permute-start.27 = (bf16[4,256,1536]{2,1,0:T(8,128)(2,1)}, bf16[4,256,1536]{2,1,0:T(8,128)(2,1)}, u32[]{:S(2)}, u32[]{:S(2)}) collective-permute-start(bf16[4,256,1536]{2,1,0:T(8,128)(2,1)} %get-tuple-element.95), channel_id=1, source_target_pairs={{0,1},{1,0},{2,3},{3,2},{4,5},{5,4},{6,7},{7,6},{8,9},{9,8},{10,11... | collective-permute-start | bytes 9437192 | tf_op jit(solution)/shard_map/ppermute | solution.py:63
  334.8 23.4 %collective-permute-start.28 = (bf16[272,1536]{1,0:T(8,128)(2,1)S(1)}, bf16[272,1536]{1,0:T(8,128)(2,1)}, u32[]{:S(2)}, u32[]{:S(2)}) collective-permute-start(bf16[272,1536]{1,0:T(8,128)(2,1)S(1)} %copy-done.19), channel_id=1, source_target_pairs={{0,2},{1,3},{2,4},{3,5},{4,6},{5,7},{6,0},{7,1},{8,10},{9,11},{10,... | collective-permute-start | bytes 2506760 | tf_op jit(solution)/shard_map/ppermute | solution.py:67
  336.3 38.4 %collective-permute-start.29 = (bf16[272,1536]{1,0:T(8,128)(2,1)S(1)}, bf16[272,1536]{1,0:T(8,128)(2,1)}, u32[]{:S(2)}, u32[]{:S(2)}) collective-permute-start(bf16[272,1536]{1,0:T(8,128)(2,1)S(1)} %copy-done.18), channel_id=1, source_target_pairs={{0,6},{1,7},{2,0},{3,1},{4,2},{5,3},{6,4},{7,5},{8,14},{9,15},{10,... | collective-permute-start | bytes 2506760 | tf_op jit(solution)/shard_map/ppermute | solution.py:71
  375.8 20.8 %collective-permute-start.31 = (bf16[144,1536]{1,0:T(8,128)(2,1)S(1)}, bf16[144,1536]{1,0:T(8,128)(2,1)S(1)}, u32[]{:S(2)}, u32[]{:S(2)}) collective-permute-start(bf16[144,1536]{1,0:T(8,128)(2,1)S(1)} %fusion.4), channel_id=1, source_target_pairs={{0,6},{1,7},{2,0},{3,1},{4,2},{5,3},{6,4},{7,5},{8,14},{9,15},{10,... | collective-permute-start | bytes 1327112 | tf_op jit(solution)/shard_map/ppermute | solution.py:71
  379.2 17.4 %collective-permute-start.30 = (bf16[128,1536]{1,0:T(8,128)(2,1)S(1)}, bf16[128,1536]{1,0:T(8,128)(2,1)S(1)}, u32[]{:S(2)}, u32[]{:S(2)}) collective-permute-start(bf16[128,1536]{1,0:T(8,128)(2,1)S(1)} %fusion.9), channel_id=1, source_target_pairs={{0,2},{1,3},{2,4},{3,5},{4,6},{5,7},{6,0},{7,1},{8,10},{9,11},{10,... | collective-permute-start | bytes 1179656 | tf_op jit(solution)/shard_map/ppermute | solution.py:67
  413.9 27.6 %collective-permute-start.47 = (bf16[4,48,1664]{2,1,0:T(8,128)(2,1)}, bf16[4,48,1664]{2,1,0:T(8,128)(2,1)}, u32[]{:S(2)}, u32[]{:S(2)}) collective-permute-start(bf16[4,48,1664]{2,1,0:T(8,128)(2,1)} %get-tuple-element.132), channel_id=1, source_target_pairs={{0,1},{1,0},{2,3},{3,2},{4,5},{5,4},{6,7},{7,6},{8,9},{9,8},{10,11... | collective-permute-start | bytes 1916936 | tf_op jit(solution)/shard_map/ppermute | solution.py:63
  414.0 31.0 %collective-permute-start.49 = (bf16[4,48,1664]{2,1,0:T(8,128)(2,1)}, bf16[4,48,1664]{2,1,0:T(8,128)(2,1)}, u32[]{:S(2)}, u32[]{:S(2)}) collective-permute-start(bf16[4,48,1664]{2,1,0:T(8,128)(2,1)} %get-tuple-element.134), channel_id=1, source_target_pairs={{0,1},{1,0},{2,3},{3,2},{4,5},{5,4},{6,7},{7,6},{8,9},{9,8},{10,11... | collective-permute-start | bytes 1916936 | tf_op jit(solution)/shard_map/ppermute | solution.py:63
  414.5 62.3 %collective-permute-start.51 = (bf16[4,48,1664]{2,1,0:T(8,128)(2,1)}, bf16[4,48,1664]{2,1,0:T(8,128)(2,1)}, u32[]{:S(2)}, u32[]{:S(2)}) collective-permute-start(bf16[4,48,1664]{2,1,0:T(8,128)(2,1)} %get-tuple-element.136), channel_id=1, source_target_pairs={{0,1},{1,0},{2,3},{3,2},{4,5},{5,4},{6,7},{7,6},{8,9},{9,8},{10,11... | collective-permute-start | bytes 1916936 | tf_op jit(solution)/shard_map/ppermute | solution.py:63
  414.6 32.7 %collective-permute-start.46 = (bf16[4,48,1664]{2,1,0:T(8,128)(2,1)}, bf16[4,48,1664]{2,1,0:T(8,128)(2,1)}, u32[]{:S(2)}, u32[]{:S(2)}) collective-permute-start(bf16[4,48,1664]{2,1,0:T(8,128)(2,1)} %get-tuple-element.130), channel_id=1, source_target_pairs={{0,1},{1,0},{2,3},{3,2},{4,5},{5,4},{6,7},{7,6},{8,9},{9,8},{10,11... | collective-permute-start | bytes 1916936 | tf_op jit(solution)/shard_map/ppermute | solution.py:63
  415.0 34.8 %collective-permute-start.34 = (bf16[256,1536]{1,0:T(8,128)(2,1)}, bf16[256,1536]{1,0:T(8,128)(2,1)S(1)}, u32[]{:S(2)}, u32[]{:S(2)}) collective-permute-start(bf16[256,1536]{1,0:T(8,128)(2,1)} %get-tuple-element.101), channel_id=1, source_target_pairs={{0,6},{1,7},{2,0},{3,1},{4,2},{5,3},{6,4},{7,5},{8,14},{9,15},{10,... | collective-permute-start | bytes 2359304 | tf_op jit(solution)/shard_map/ppermute | solution.py:71
  437.9 73.3 %all-to-all-start.2 = ((bf16[1,2,128,1536]{3,1,0,2:T(2,128)(2,1)}), bf16[1,2,128,1536]{3,1,0,2:T(2,128)(2,1)S(1)}, u32[]{:S(2)}, u32[]{:S(2)}) async-start(bf16[1,2,128,1536]{3,1,0,2:T(2,128)(2,1)} %copy.86), calls=%async_computation.2 | async-start | bytes 1572864 | tf_op jit(solution)/shard_map/all_to_all | solution.py:1187
  441.5 34.6 %collective-permute-start.32 = (bf16[256,1536]{1,0:T(8,128)(2,1)}, bf16[256,1536]{1,0:T(8,128)(2,1)S(1)}, u32[]{:S(2)}, u32[]{:S(2)}) collective-permute-start(bf16[256,1536]{1,0:T(8,128)(2,1)} %get-tuple-element.100), channel_id=1, source_target_pairs={{0,2},{1,3},{2,4},{3,5},{4,6},{5,7},{6,0},{7,1},{8,10},{9,11},{10,... | collective-permute-start | bytes 2359304 | tf_op jit(solution)/shard_map/ppermute | solution.py:67
  445.0 62.3 %collective-permute-start.48 = (bf16[4,48,1664]{2,1,0:T(8,128)(2,1)S(1)}, bf16[4,48,1664]{2,1,0:T(8,128)(2,1)S(1)}, u32[]{:S(2)}, u32[]{:S(2)}) collective-permute-start(bf16[4,48,1664]{2,1,0:T(8,128)(2,1)S(1)} %add_convert_fusion.11), channel_id=1, source_target_pairs={{0,8},{8,0},{16,24},{24,16},{1,9},{9,1},{17,25},{25,17},{2,10},{10... | collective-permute-start | bytes 1916936 | tf_op jit(solution)/shard_map/ppermute | solution.py:55
  447.3 61.5 %collective-permute-start.50 = (bf16[4,48,1664]{2,1,0:T(8,128)(2,1)S(1)}, bf16[4,48,1664]{2,1,0:T(8,128)(2,1)S(1)}, u32[]{:S(2)}, u32[]{:S(2)}) collective-permute-start(bf16[4,48,1664]{2,1,0:T(8,128)(2,1)S(1)} %add_convert_fusion.10), channel_id=1, source_target_pairs={{0,16},{8,24},{16,0},{24,8},{1,17},{9,25},{17,1},{25,9},{2,18},{10... | collective-permute-start | bytes 1916936 | tf_op jit(solution)/shard_map/ppermute | solution.py:59
  449.8 60.4 %copy-start.11 = (f32[4,48,1664]{2,1,0:T(8,128)}, f32[4,48,1664]{2,1,0:T(8,128)S(1)}, u32[]{:S(2)}) copy-start(f32[4,48,1664]{2,1,0:T(8,128)S(1)} %convert_add_fusion.1) | copy-start | bytes 3833860
  476.1 26.7 %collective-permute-start.37 = (bf16[4,48,2176]{2,1,0:T(8,128)(2,1)S(1)}, bf16[4,48,2176]{2,1,0:T(8,128)(2,1)S(1)}, u32[]{:S(2)}, u32[]{:S(2)}) collective-permute-start(bf16[4,48,2176]{2,1,0:T(8,128)(2,1)S(1)} %copy-done.48), channel_id=1, source_target_pairs={{0,1},{1,0},{2,3},{3,2},{4,5},{5,4},{6,7},{7,6},{8,9},{9,8},{10,11... | collective-permute-start | bytes 2506760 | tf_op jit(solution)/shard_map/ppermute | solution.py:63
  476.2 11.6 %collective-permute-start.35 = (bf16[128,1536]{1,0:T(8,128)(2,1)S(1)}, bf16[128,1536]{1,0:T(8,128)(2,1)S(1)}, u32[]{:S(2)}, u32[]{:S(2)}) collective-permute-start(bf16[128,1536]{1,0:T(8,128)(2,1)S(1)} %fusion.8), channel_id=1, source_target_pairs={{0,6},{1,7},{2,0},{3,1},{4,2},{5,3},{6,4},{7,5},{8,14},{9,15},{10,... | collective-permute-start | bytes 1179656 | tf_op jit(solution)/shard_map/ppermute | solution.py:71
  476.7 22.4 %collective-permute-start.33 = (bf16[128,1536]{1,0:T(8,128)(2,1)S(1)}, bf16[128,1536]{1,0:T(8,128)(2,1)S(1)}, u32[]{:S(2)}, u32[]{:S(2)}) collective-permute-start(bf16[128,1536]{1,0:T(8,128)(2,1)S(1)} %fusion.10), channel_id=1, source_target_pairs={{0,2},{1,3},{2,4},{3,5},{4,6},{5,7},{6,0},{7,1},{8,10},{9,11},{10,... | collective-permute-start | bytes 1179656 | tf_op jit(solution)/shard_map/ppermute | solution.py:67
  487.7 22.4 %collective-permute-start.52 = (bf16[4,48,1664]{2,1,0:T(8,128)(2,1)S(1)}, bf16[4,48,1664]{2,1,0:T(8,128)(2,1)S(1)}, u32[]{:S(2)}, u32[]{:S(2)}) collective-permute-start(bf16[4,48,1664]{2,1,0:T(8,128)(2,1)S(1)} %add_convert_fusion.9), channel_id=1, source_target_pairs={{0,24},{8,16},{16,8},{24,0},{1,25},{9,17},{17,9},{25,1},{2,26},{10... | collective-permute-start | bytes 1916936 | tf_op jit(solution)/shard_map/ppermute | solution.py:904
  499.2 5.3 collective-permute-start.39
  502.8 2.8 collective-permute-start.41
  504.4 12.0 %collective-permute-start.36 = (bf16[4,48,2176]{2,1,0:T(8,128)(2,1)}, bf16[4,48,2176]{2,1,0:T(8,128)(2,1)S(1)}, u32[]{:S(2)}, u32[]{:S(2)}) collective-permute-start(bf16[4,48,2176]{2,1,0:T(8,128)(2,1)} %get-tuple-element.116), channel_id=1, source_target_pairs={{0,1},{1,0},{2,3},{3,2},{4,5},{5,4},{6,7},{7,6},{8,9},{9,8},{10,11... | collective-permute-start | bytes 2506760 | tf_op jit(solution)/shard_map/ppermute | solution.py:63
  505.6 21.7 %collective-permute-start.38 = (bf16[4,48,2176]{2,1,0:T(8,128)(2,1)}, bf16[4,48,2176]{2,1,0:T(8,128)(2,1)}, u32[]{:S(2)}, u32[]{:S(2)}) collective-permute-start(bf16[4,48,2176]{2,1,0:T(8,128)(2,1)} %add_convert_fusion.2), channel_id=1, source_target_pairs={{0,8},{8,0},{16,24},{24,16},{1,9},{9,1},{17,25},{25,17},{2,10},{10... | collective-permute-start | bytes 2506760 | tf_op jit(solution)/shard_map/ppermute | solution.py:55
  507.4 38.9 %collective-permute-start.40 = (bf16[4,48,2176]{2,1,0:T(8,128)(2,1)}, bf16[4,48,2176]{2,1,0:T(8,128)(2,1)}, u32[]{:S(2)}, u32[]{:S(2)}) collective-permute-start(bf16[4,48,2176]{2,1,0:T(8,128)(2,1)} %add_convert_fusion.1), channel_id=1, source_target_pairs={{0,16},{8,24},{16,0},{24,8},{1,17},{9,25},{17,1},{25,9},{2,18},{10... | collective-permute-start | bytes 2506760 | tf_op jit(solution)/shard_map/ppermute | solution.py:59
  508.7 37.6 %collective-permute-start.42 = (bf16[4,48,2176]{2,1,0:T(8,128)(2,1)}, bf16[4,48,2176]{2,1,0:T(8,128)(2,1)}, u32[]{:S(2)}, u32[]{:S(2)}) collective-permute-start(bf16[4,48,2176]{2,1,0:T(8,128)(2,1)} %add_convert_fusion), channel_id=1, source_target_pairs={{0,24},{8,16},{16,8},{24,0},{1,25},{9,17},{17,9},{25,1},{2,26},{10... | collective-permute-start | bytes 2506760 | tf_op jit(solution)/shard_map/ppermute | solution.py:904
  511.2 39.7 %collective-permute-start.53 = (bf16[48,1664]{1,0:T(8,128)(2,1)}, bf16[48,1664]{1,0:T(8,128)(2,1)}, u32[]{:S(2)}, u32[]{:S(2)}) collective-permute-start(bf16[48,1664]{1,0:T(8,128)(2,1)} %get-tuple-element.219), channel_id=1, source_target_pairs={{0,6},{1,7},{2,0},{3,1},{4,2},{5,3},{6,4},{7,5},{8,14},{9,15},{10,... | collective-permute-start | bytes 479240 | tf_op jit(solution)/shard_map/ppermute | solution.py:71
  511.3 43.2 %all-to-all-start.1 = ((bf16[1,2,128,1536]{3,1,0,2:T(2,128)(2,1)}), bf16[1,2,128,1536]{3,1,0,2:T(2,128)(2,1)S(1)}, u32[]{:S(2)}, u32[]{:S(2)}) async-start(bf16[1,2,128,1536]{3,1,0,2:T(2,128)(2,1)} %copy.83), calls=%async_computation.1 | async-start | bytes 1572864 | tf_op jit(solution)/shard_map/all_to_all | solution.py:1180
  517.4 33.6 %collective-permute-start.54 = (bf16[48,1664]{1,0:T(8,128)(2,1)}, bf16[48,1664]{1,0:T(8,128)(2,1)S(1)}, u32[]{:S(2)}, u32[]{:S(2)}) collective-permute-start(bf16[48,1664]{1,0:T(8,128)(2,1)} %get-tuple-element.221), channel_id=1, source_target_pairs={{0,2},{1,3},{2,4},{3,5},{4,6},{5,7},{6,0},{7,1},{8,10},{9,11},{10,... | collective-permute-start | bytes 479240 | tf_op jit(solution)/shard_map/ppermute | solution.py:67
  527.3 23.6 %collective-permute-start.55 = (bf16[48,1664]{1,0:T(8,128)(2,1)}, bf16[48,1664]{1,0:T(8,128)(2,1)S(1)}, u32[]{:S(2)}, u32[]{:S(2)}) collective-permute-start(bf16[48,1664]{1,0:T(8,128)(2,1)} %get-tuple-element.220), channel_id=1, source_target_pairs={{0,4},{1,5},{2,6},{3,7},{4,0},{5,1},{6,2},{7,3},{8,12},{9,13},{10,... | collective-permute-start | bytes 479240 | tf_op jit(solution)/shard_map/ppermute | solution.py:908
  548.9 11.4 %collective-permute-start.43 = (bf16[48,2176]{1,0:T(8,128)(2,1)}, bf16[48,2176]{1,0:T(8,128)(2,1)}, u32[]{:S(2)}, u32[]{:S(2)}) collective-permute-start(bf16[48,2176]{1,0:T(8,128)(2,1)} %get-tuple-element.216), channel_id=1, source_target_pairs={{0,6},{1,7},{2,0},{3,1},{4,2},{5,3},{6,4},{7,5},{8,14},{9,15},{10,... | collective-permute-start | bytes 626696 | tf_op jit(solution)/shard_map/ppermute | solution.py:71
  548.9 11.4 %collective-permute-start.44 = (bf16[48,2176]{1,0:T(8,128)(2,1)}, bf16[48,2176]{1,0:T(8,128)(2,1)}, u32[]{:S(2)}, u32[]{:S(2)}) collective-permute-start(bf16[48,2176]{1,0:T(8,128)(2,1)} %get-tuple-element.218), channel_id=1, source_target_pairs={{0,2},{1,3},{2,4},{3,5},{4,6},{5,7},{6,0},{7,1},{8,10},{9,11},{10,... | collective-permute-start | bytes 626696 | tf_op jit(solution)/shard_map/ppermute | solution.py:67
  550.9 15.6 %collective-permute-start.45 = (bf16[48,2176]{1,0:T(8,128)(2,1)S(1)}, bf16[48,2176]{1,0:T(8,128)(2,1)}, u32[]{:S(2)}, u32[]{:S(2)}) collective-permute-start(bf16[48,2176]{1,0:T(8,128)(2,1)S(1)} %get-tuple-element.217), channel_id=1, source_target_pairs={{0,4},{1,5},{2,6},{3,7},{4,0},{5,1},{6,2},{7,3},{8,12},{9,13},{10,... | collective-permute-start | bytes 626696 | tf_op jit(solution)/shard_map/ppermute | solution.py:908
  (57 other events, 402.0 us)
Sparse Core Ops, SparseCore 0:
  9.9 69.8 all-gather.4
  82.2 117.4 all-gather.2
  318.3 56.0 reduce-scatter.4
  377.3 108.6 reduce-scatter.2

commit v3 on v2

--- a/solution.py
+++ b/solution.py
@@ -81,40 +81,6 @@
 
 def smem_spec():
     return pl.BlockSpec(memory_space=pltpu.SMEM)
-
-
-def staged(out_ref, hold, sems):
-    pltpu.make_async_copy(hold, hold, sems.at[0]).wait()
-    copy = pltpu.make_async_copy(hold, out_ref, sems.at[1])
-    copy.start()
-    copy.wait()
-
-
-def deal_kernel(seq_ref, rel_ref, src_ref, out_ref, hold, sems):
-    devices = out_ref.shape[0]
-    piece = out_ref.shape[1] // SEQ_DEV // devices
-    for b in range(devices):
-        for k in range(SEQ_DEV):
-            row = pl.multiple_of(seq_ref[b * SEQ_DEV + k] * piece, piece)
-            for j in range(devices):
-                pltpu.make_async_copy(
-                    src_ref.at[rel_ref[j], pl.ds(row, piece), :],
-                    hold.at[b, pl.ds((k * devices + j) * piece, piece), :],
-                    sems.at[0],
-                ).start()
-    staged(out_ref, hold, sems)
-
-
-def move_blocks(kernel, shape, scalars, arrays):
-    dtype = arrays[0].dtype
-    return pl.pallas_call(
-        kernel,
-        out_shape=jax.ShapeDtypeStruct(shape, dtype),
-        in_specs=[smem_spec()] * len(scalars) + [any_spec()] * len(arrays),
-        out_specs=any_spec(),
-        scratch_shapes=[pltpu.VMEM(shape, dtype), pltpu.SemaphoreType.DMA((2,))],
-        compiler_params=pltpu.CompilerParams(vmem_limit_bytes=40 * 1024 * 1024),
-    )(*scalars, *arrays)
 
 
 def expert_order(tuned, count):
@@ -164,10 +130,46 @@
 MIB = 1024 * 1024
 
 
+def deal_copies(scalar_ref, early, piece, block, dst, row, sem):
+    devices = len(early)
+    copies = []
+    for k in range(SEQ_DEV):
+        start = pl.multiple_of(scalar_ref[1 + block * SEQ_DEV + k] * piece, piece)
+        for q in range(devices):
+            place = scalar_ref[1 + devices * SEQ_DEV + q] * piece
+            to = pl.multiple_of(row + k * devices * piece + place, piece)
+            copies.append(
+                pltpu.make_async_copy(
+                    early[q].at[pl.ds(start, piece), :], dst.at[pl.ds(to, piece), :], sem
+                )
+            )
+    return copies
+
+
+def give_back(scalar_ref, piece, block, src, keep, send, sem):
+    devices = keep.shape[0] + send.shape[0]
+    half = devices // 2
+    for j in range(devices):
+        to = scalar_ref[1 + devices * SEQ_DEV + devices + j]
+        for k in range(SEQ_DEV):
+            start = pl.multiple_of(scalar_ref[1 + block * SEQ_DEV + k] * piece, piece)
+            part = src.at[pl.ds((k * devices + j) * piece, piece), :]
+
+            @pl.when(to < half)
+            def _(part=part, to=to, start=start):
+                dst = keep.at[to, pl.ds(start, piece), :]
+                pltpu.make_async_copy(part, dst, sem).start()
+
+            @pl.when(to >= half)
+            def _(part=part, to=to, start=start):
+                dst = send.at[to - half, pl.ds(start, piece), :]
+                pltpu.make_async_copy(part, dst, sem).start()
+
+
 def expert_kernel(plan, capacity, *refs):
     count = plan["inputs"]
-    my_ref, codes_ref, router_ref, grads_ref = refs[:4]
-    inputs = refs[4 : 4 + count]
+    my_ref, router_ref, codes_ref, grads_ref, res_ref = refs[:5]
+    inputs = refs[5 : 5 + count]
     (
         back_keep,
         back_send,
@@ -178,7 +180,7 @@
         hid_out,
         dga_out,
         dua_out,
-    ) = refs[4 + count : 13 + count]
+    ) = refs[5 + count : 14 + count]
     (
         gate_w,
         up_w,
@@ -195,6 +197,7 @@
         dua_s,
         act_s,
         slope_s,
+        codes_all,
         code_s,
         gates_s,
         sgate_s,
@@ -204,21 +207,24 @@
         sem_w,
         sem_h,
         sem_d,
+        sem_c,
         sem_s,
         sem_b,
         sem_o,
-    ) = refs[13 + count :]
+    ) = refs[14 + count :]
     blocks = plan["blocks"]
     pairs = blocks // 2
     per_device, width, ff = gate_w.shape
     tokens = h_buf.shape[1] // 2
     slots = 2 * capacity
-    experts = codes_ref.shape[1]
+    experts = router_ref.shape[0]
     my_first = my_ref[0] * per_device
     dtype = jnp.bfloat16
 
-    def window(hold, axis, e, owner, step):
-        start = (owner or 0) * step
+    plane = my_ref[my_ref.shape[0] - 1]
+
+    def window(hold, axis, e, flip, step):
+        start = 0 if flip is None else pl.multiple_of((plane ^ flip) * step, step)
         if axis == 1:
             return hold.at[e, pl.ds(start, step), :]
         return hold.at[e, :, pl.ds(start, step)]
@@ -227,14 +233,22 @@
     for t, (hold, axis) in enumerate(((gate_w, 1), (up_w, 1), (down_w, 2))):
         for e in range(per_device):
             copies = []
-            for ref_index, lead, owner in plan["weights"][t][e]:
+            for ref_index, lead, flip in plan["weights"][t][e]:
                 src = inputs[ref_index].at[lead]
                 step = src.shape[axis - 1]
                 sem = sem_w.at[t * per_device + e, len(copies)]
-                copy = pltpu.make_async_copy(src, window(hold, axis, e, owner, step), sem)
+                copy = pltpu.make_async_copy(src, window(hold, axis, e, flip, step), sem)
                 copy.start()
                 copies.append(copy)
             weight_copies.append(copies)
+
+    early = [inputs[i] for i in plan["early"]]
+    if early:
+        for b, ref in enumerate(early):
+            src = ref.at[pl.ds(tokens, codes_all.shape[1]), pl.ds(0, tokens)]
+            pltpu.make_async_copy(src, codes_all.at[b], sem_c).start()
+    else:
+        pltpu.make_async_copy(codes_ref, codes_all, sem_c).start()
 
     def fetch(p):
         slot = p % 2
@@ -244,11 +258,30 @@
                 src = inputs[ref_index] if lead is None else inputs[ref_index].at[lead]
                 dst = h_buf.at[slot, pl.ds(half * tokens + row, rows), :]
                 copies.append(pltpu.make_async_copy(src, dst, sem_h.at[slot, half, k]))
-            dst = d_buf.at[slot, pl.ds(half * tokens, tokens), :]
-            copies.append(pltpu.make_async_copy(grads_ref.at[2 * p + half], dst, sem_d.at[slot, half]))
-        for copy in copies:
+        if early:
+            deals = []
+            for half in range(2):
+                deals += deal_copies(
+                    my_ref,
+                    early,
+                    plan["piece"],
+                    2 * p + half,
+                    d_buf.at[slot],
+                    half * tokens,
+                    sem_d.at[slot],
+                )
+        else:
+            deals = [
+                pltpu.make_async_copy(
+                    grads_ref.at[2 * p + half],
+                    d_buf.at[slot, pl.ds(half * tokens, tokens), :],
+                    sem_d.at[slot],
+                )
+                for half in range(2)
+            ]
+        for copy in copies + deals:
             copy.start()
-        return copies
+        return copies + [pltpu.make_async_copy(d_buf.at[slot], d_buf.at[slot], sem_d.at[slot])]
 
     row = lax.broadcasted_iota(jnp.int32, (slots, 2 * tokens), 0)
     col = lax.broadcasted_iota(jnp.int32, (slots, 2 * tokens), 1)
@@ -256,13 +289,15 @@
     same = jnp.logical_xor(second, col < tokens)
     target = (row - jnp.where(second, capacity, 0) + 1).astype(jnp.float32)
     flying = fetch(0)
+    pltpu.make_async_copy(codes_all, codes_all, sem_c).wait()
     for p in range(pairs):
         slot = p % 2
         later = fetch(p + 1) if p + 1 < pairs else []
         for copy in flying:
             copy.wait()
         flying = later
-        codes = jnp.concatenate([codes_ref[2 * p], codes_ref[2 * p + 1]], axis=1)
+        codes = jnp.concatenate([codes_all[2 * p], codes_all[2 * p + 1]], axis=1)
+        codes = codes.astype(jnp.float32)[:experts]
         logits = dot_nt(router_ref[...], h_buf[slot])
         chosen = codes > 0.0
         top = jnp.max(jnp.where(chosen, logits, NEG_FILL), axis=0, keepdims=True)
@@ -365,7 +400,10 @@
             for half in range(2):
                 part = slice(half * tokens, (half + 1) * tokens)
                 stage_b[slot, half, :tokens, cols] = back[part].astype(dtype)
-                stage_o[slot, half, :, cols] = outs[part].astype(dtype)
+                mixed = outs[part]
+                if early and p == 0 and half == 0:
+                    mixed = mixed + res_ref[:, cols]
+                stage_o[slot, half, :, cols] = mixed.astype(dtype)
 
         tables = [jnp.zeros((table_rows, 2 * tokens), jnp.float32) for _ in range(2)]
         for e in range(per_device):
@@ -388,13 +426,31 @@
         copies = [
             pltpu.make_async_copy(
                 stage_b.at[slot], (back_keep if keep else back_send).at[at], sem_b.at[slot]
-            ),
-            pltpu.make_async_copy(
-                stage_o.at[slot], (out_keep if keep else out_send).at[at], sem_o.at[slot]
-            ),
+            )
         ]
+        if early:
+            for half in range(2):
+                give_back(
+                    my_ref,
+                    plan["piece"],
+                    first + half,
+                    stage_o.at[slot, half],
+                    out_keep,
+                    out_send,
+                    sem_o.at[slot],
+                )
+        else:
+            copies.append(
+                pltpu.make_async_copy(
+                    stage_o.at[slot], (out_keep if keep else out_send).at[at], sem_o.at[slot]
+                )
+            )
         for copy in copies:
             copy.start()
+        if early:
+            copies.append(
+                pltpu.make_async_copy(stage_o.at[slot], stage_o.at[slot], sem_o.at[slot])
+            )
         sends[p] = copies
     for copies in sends.values():
         for copy in copies:
@@ -403,9 +459,9 @@
         save.wait()
 
 
-def run_experts(plan, capacity, table_rows, scalars, codes, router_t, grads_all, inputs):
-    blocks, tokens, width = grads_all.shape
-    experts = codes.shape[1]
+def run_experts(plan, capacity, table_rows, scalars, router_t, codes, grads_all, res, inputs):
+    experts, width = router_t.shape
+    blocks, tokens = plan["blocks"], plan["token_count"]
     per_device, ff = plan["per_device"], plan["ff"]
     rows = blocks * capacity
     bf, f32 = jnp.bfloat16, jnp.float32
@@ -419,7 +475,7 @@
     return pl.pallas_call(
         lambda *refs: expert_kernel(plan, capacity, *refs),
         out_shape=(back, back, outs, outs, wide, wide, thin, thin, thin),
-        in_specs=[smem_spec(), vmem, vmem, any_spec()] + [any_spec()] * len(inputs),
+        in_specs=[smem_spec(), vmem, any_spec(), any_spec(), vmem] + [any_spec()] * len(inputs),
         out_specs=tuple([any_spec()] * 9),
         scratch_shapes=[
             pltpu.VMEM((per_device, width, ff), bf),
@@ -437,6 +493,7 @@
             pltpu.VMEM((per_device, rows, ff), bf),
             pltpu.VMEM((rows, ff), f32),
             pltpu.VMEM((rows, ff), f32),
+            pltpu.VMEM((blocks, table_rows, tokens), bf),
             pltpu.VMEM((experts, 2 * tokens), f32),
             pltpu.VMEM((experts, 2 * tokens), f32),
             pltpu.VMEM((per_device, rows, 128), f32),
@@ -445,96 +502,104 @@
             pltpu.VMEM((2, 2, tokens, width), bf),
             sem((3 * per_device, 4)),
             sem((2, 2, 2)),
-            sem((2, 2)),
+            sem((2,)),
+            sem,
             sem((5, per_device)),
             sem((2,)),
             sem((2,)),
         ],
         cost_estimate=pl.CostEstimate(flops=55000000000, transcendentals=0, bytes_accessed=50000000),
         compiler_params=pltpu.CompilerParams(vmem_limit_bytes=61 * MIB),
-    )(scalars, codes, router_t, grads_all, *inputs)
+    )(scalars, router_t, codes, grads_all, res, *inputs)
+
+
+def weight_kernel(x_ref, dga_ref, dua_ref, hid_ref, dy_ref, out_ref):
+    dtype = jnp.bfloat16
+    out_ref[0, 0, 0] = dot_tn(x_ref[0], dga_ref[0]).astype(dtype)
+    out_ref[0, 1, 0] = dot_tn(x_ref[0], dua_ref[0]).astype(dtype)
+    ff = hid_ref.shape[2]
+    step = dy_ref.shape[2]
+    for i in range(ff // step):
+        part = dot_tn(hid_ref[0, :, i * step : (i + 1) * step], dy_ref[0])
+        out_ref[0, 2, 0, :, i * step : (i + 1) * step] = part.astype(dtype)
+
+
+def expert_weight_grads(x, dga, dua, hid, dy, parts):
+    per_device, rows, ff = dga.shape
+    step = x.shape[2] // parts
+    whole = pl.BlockSpec((1, rows, ff), lambda e, d: (e, 0, 0))
+    piece = pl.BlockSpec((1, rows, step), lambda e, d: (e, 0, d))
+    return pl.pallas_call(
+        weight_kernel,
+        grid=(per_device, parts),
+        out_shape=jax.ShapeDtypeStruct((parts, 3, per_device, step, ff), jnp.bfloat16),
+        in_specs=[piece, whole, whole, whole, piece],
+        out_specs=pl.BlockSpec((1, 3, 1, step, ff), lambda e, d: (d, 0, e, 0, 0)),
+        cost_estimate=pl.CostEstimate(
+            flops=18700000000, transcendentals=0, bytes_accessed=17000000
+        ),
+        compiler_params=pltpu.CompilerParams(vmem_limit_bytes=56 * MIB),
+    )(x, dga, dua, hid, dy)
 
 
 def down_kernel(hid_ref, dy_ref, out_ref):
-    out_ref[0, 0] = dot_tn(hid_ref[0], dy_ref[0]).astype(jnp.bfloat16)
-
-
-def grad_down_blocks(hid, dy, parts):
-    per_device, rows, ff = hid.shape
-    step = dy.shape[2] // parts
-    return pl.pallas_call(
+    out_ref[0] = dot_tn(hid_ref[0], dy_ref[0]).astype(jnp.bfloat16)
+
+
+def gate_up_kernel(x_ref, dga_ref, dua_ref, out_ref):
+    out_ref[0, 0] = dot_tn(x_ref[0], dga_ref[0]).astype(jnp.bfloat16)
+    out_ref[1, 0] = dot_tn(x_ref[0], dua_ref[0]).astype(jnp.bfloat16)
+
+
+def whole_weight_grads(x, dga, dua, hid, dy):
+    per_device, rows, ff = dga.shape
+    width = x.shape[2]
+    thin = pl.BlockSpec((1, rows, ff), lambda e: (e, 0, 0))
+    wide = pl.BlockSpec((1, rows, width), lambda e: (e, 0, 0))
+    down = pl.pallas_call(
         down_kernel,
-        grid=(per_device, parts),
-        out_shape=jax.ShapeDtypeStruct((parts, per_device, ff, step), jnp.bfloat16),
-        in_specs=[
-            pl.BlockSpec((1, rows, ff), lambda e, d: (e, 0, 0)),
-            pl.BlockSpec((1, rows, step), lambda e, d: (e, 0, d)),
-        ],
-        out_specs=pl.BlockSpec((1, 1, ff, step), lambda e, d: (d, e, 0, 0)),
-        cost_estimate=pl.CostEstimate(flops=7700000000, transcendentals=0, bytes_accessed=7000000),
+        grid=(per_device,),
+        out_shape=jax.ShapeDtypeStruct((per_device, ff, width), jnp.bfloat16),
+        in_specs=[thin, wide],
+        out_specs=pl.BlockSpec((1, ff, width), lambda e: (e, 0, 0)),
         compiler_params=pltpu.CompilerParams(vmem_limit_bytes=40 * MIB),
     )(hid, dy)
-
-
-def gate_up_kernel(x_ref, dga_ref, dua_ref, out_ref):
-    out_ref[0, 0, 0] = dot_tn(x_ref[0], dga_ref[0]).astype(jnp.bfloat16)
-    out_ref[0, 1, 0] = dot_tn(x_ref[0], dua_ref[0]).astype(jnp.bfloat16)
-
-
-def grad_gate_up_blocks(x, dga, dua, parts):
-    per_device, rows, ff = dga.shape
-    step = x.shape[2] // parts
-    return pl.pallas_call(
+    gate_up = pl.pallas_call(
         gate_up_kernel,
-        grid=(per_device, parts),
-        out_shape=jax.ShapeDtypeStruct((parts, 2, per_device, step, ff), jnp.bfloat16),
-        in_specs=[
-            pl.BlockSpec((1, rows, step), lambda e, d: (e, 0, d)),
-            pl.BlockSpec((1, rows, ff), lambda e, d: (e, 0, 0)),
-            pl.BlockSpec((1, rows, ff), lambda e, d: (e, 0, 0)),
-        ],
-        out_specs=pl.BlockSpec((1, 2, 1, step, ff), lambda e, d: (d, 0, e, 0, 0)),
-        cost_estimate=pl.CostEstimate(flops=11000000000, transcendentals=0, bytes_accessed=10000000),
+        grid=(per_device,),
+        out_shape=jax.ShapeDtypeStruct((2, per_device, width, ff), jnp.bfloat16),
+        in_specs=[wide, thin, thin],
+        out_specs=pl.BlockSpec((2, 1, width, ff), lambda e: (0, e, 0, 0)),
         compiler_params=pltpu.CompilerParams(vmem_limit_bytes=40 * MIB),
     )(x, dga, dua)
-
-
-def gather_weight_pieces(w_gate, w_up, w_down, tuned):
-    if not tuned:
-        parts = [
-            lax.all_gather(w_gate, "dp", axis=1, tiled=True),
-            lax.all_gather(w_up, "dp", axis=1, tiled=True),
-            lax.all_gather(w_down, "dp", axis=2, tiled=True),
-        ]
-        count = w_gate.shape[0]
-        return parts, [[[(t, (e,), None)] for e in range(count)] for t in range(3)]
-    both = jnp.stack([w_gate, w_up])
-    flat = lax.all_gather(both.reshape(-1, both.shape[-1]), "dp", axis=0, tiled=True)
-    down = lax.all_gather(w_down.reshape(-1, w_down.shape[-1]), "dp", axis=0, tiled=True)
-    parts = [flat.reshape((4,) + both.shape), down.reshape((4,) + w_down.shape)]
-    places = [
-        [[(0, (d, t, e), d) for d in range(4)] for e in range(w_gate.shape[0])] for t in range(2)
-    ]
-    places.append([[(1, (d, e), d) for d in range(4)] for e in range(w_gate.shape[0])])
-    return parts, places
-
-
-def gather_token_pieces(value, tuned, wait_for):
+    return gate_up, down
+
+
+def gather_inputs(value, weights, count, tuned):
     rows = value.shape[0]
     if not tuned:
         full = lax.all_gather(value, "expert", axis=0, tiled=False)
-        return [full], [[(0, b, 0, rows)] for b in range(full.shape[0])]
+        places = [[[(t, (e,), None)] for e in range(count)] for t in range(3)]
+        return list(weights) + [full], places, [[(3, b, 0, rows)] for b in range(full.shape[0])]
+    both, both_x, both_y, down, down_x, down_y, down_a, down_b = weights
     below = shift_up(value)
     above = shift_down(value)
-    far_a = shift_up(after(below[: rows // 2], wait_for))
-    far_b = shift_down(after(above[rows // 2 :], wait_for))
-    arrays = [value, below, above, far_a, far_b]
-    arrays = arrays + [swap_core(v) for v in arrays]
-    places = []
-    for base in (0, 5):
-        places += [[(base + k, None, 0, rows)] for k in range(3)]
-        places += [[(base + 3, None, 0, rows // 2), (base + 4, None, rows // 2, rows // 2)]]
-    return arrays, places
+    below, above, both_x, both_y = lax.optimization_barrier((below, above, both_x, both_y))
+    tokens = [value, below, above, shift_up(below)]
+    tokens = tokens + [swap_core(v) for v in tokens]
+    arrays = [both, both_x, both_y, swap_x(both_y[0]), swap_y(both_x[1])]
+    arrays = arrays + [down, down_x, down_y, down_a, down_b]
+    places = [
+        [[(k, (t, e), k) for k in range(3)] + [(3 + t, (e,), 3)] for e in range(count)]
+        for t in range(2)
+    ]
+    places.append(
+        [[(5 + k, (e,), k) for k in range(3)] + [(8 + e, (0,), 3)] for e in range(count)]
+    )
+    token_places = []
+    for base in (10, 14):
+        token_places += [[(base + k, None, 0, rows)] for k in range(4)]
+    return arrays + tokens, places, token_places
 
 
 def rotate(values, cos_wide, sin_wide):
@@ -683,52 +748,69 @@
             sem,
             sem,
         ],
-        cost_estimate=pl.CostEstimate(flops=17600000000, transcendentals=0, bytes_accessed=16000000),
+        cost_estimate=pl.CostEstimate(flops=110000000000, transcendentals=0, bytes_accessed=16000000),
         compiler_params=pltpu.CompilerParams(vmem_limit_bytes=56 * MIB),
     )(order, x, cos_wide, sin_wide, lab_col, lab_row, *inputs)
 
 
-def send_payload(order_ref, payload, outs, sem):
+def send_payload(order_ref, payload, start_col, outs, sem):
+    cols = pl.ds(start_col, outs[0].shape[-1])
     if len(outs) == 1:
-        copies = [pltpu.make_async_copy(payload, outs[0], sem)]
-    else:
-        copies = []
-        rows = payload.shape[0] // 32
-        for j in range(32):
-            start = pl.multiple_of(order_ref[j] * rows, rows)
-            dst = outs[j // 4].at[j % 4]
-            copies.append(pltpu.make_async_copy(payload.at[pl.ds(start, rows), :], dst, sem))
-    for copy in copies:
-        copy.start()
-    pltpu.make_async_copy(payload, payload, sem).wait()
+        pltpu.make_async_copy(payload.at[:, cols], outs[0], sem).start()
+        return
+    rows = payload.shape[0] // 32
+    for c in range(2):
+        x_one, y_one, x_two, y_two, own = outs[c * 5 : c * 5 + 5]
+        places = [own.at[r] for r in range(4)]
+        places += [x_one.at[1, 0], x_one.at[1, 1], x_two.at[0], x_two.at[1]]
+        places += [y_two.at[0], y_two.at[1], y_one.at[1, 0], y_one.at[1, 1]]
+        places += [x_one.at[0, 0], x_one.at[0, 1], y_one.at[0, 0], y_one.at[0, 1]]
+        for j, dst in enumerate(places):
+            start = pl.multiple_of(order_ref[c * 16 + j] * rows, rows)
+            pltpu.make_async_copy(payload.at[pl.ds(start, rows), cols], dst, sem).start()
 
 
 def payload_shapes(tuned, rows, cols):
     if not tuned:
         return (jax.ShapeDtypeStruct((rows, cols), jnp.bfloat16),)
-    return (jax.ShapeDtypeStruct((4, rows // 32, cols), jnp.bfloat16),) * 8
-
-
-def middle_kernel(experts, sums, order_ref, own_ref, dy_all, codes_ref, *refs):
-    back_refs = refs[: sums]
-    res_ref, h2_ref, o_ref, aux_ref, w_full_ref = refs[sums : sums + 5]
-    base = w_full_ref.shape[1] - refs[sums].shape[1] - 128
-    rest = refs[sums + 5 :]
-    outs = rest[:-8]
-    dres_ref, dmix_ref, w_out, dy, payload, dres_low, sem_w, sem_p = rest[-8:]
+    piece = rows // 32
+    shapes = [(2, 2), (2, 2), (2,), (2,), (4,)]
+    one = tuple(jax.ShapeDtypeStruct(v + (piece, cols), jnp.bfloat16) for v in shapes)
+    return one + one
+
+
+def backward_kernel(experts, sums, piece, order_ref, own_ref, *refs):
+    given = 8 if piece else 2
+    early, refs = refs[:given], refs[given:]
+    back_refs = refs[:sums]
+    res_ref, h2_ref, o_ref, aux_ref, x_ref, cos_ref, sin_ref = refs[sums : sums + 7]
+    h1_ref, q_ref, k_ref, v_ref, p_ref, w_full_ref = refs[sums + 7 : sums + 13]
+    rest = refs[sums + 13 :]
+    outs = rest[:-13]
+    dx_ref, w_full, dy, codes, payload, dres_ref, dres_low, dmix_ref, dqkv, dh1 = rest[-13:-3]
+    sem_w, sem_d, sem_p = rest[-3:]
     tokens, width = res_ref.shape
     bf = jnp.bfloat16
-    load = pltpu.make_async_copy(w_full_ref.at[:, pl.ds(base, width)], w_out, sem_w.at[0])
+    heads = QUERY_HEADS // KEY_VALUE_HEADS
+    kv_width = KEY_VALUE_HEADS * HEAD_SIZE
+    main = width + 2 * kv_width
+    base = main + 128
+    scale = HEAD_SIZE ** (-0.5)
+    load = pltpu.make_async_copy(w_full_ref, w_full, sem_w.at[0])
     load.start()
-    load_dy = pltpu.make_async_copy(dy_all.at[own_ref[0]], dy, sem_w.at[1])
-    load_dy.start()
+    if piece:
+        src = early[0].at[pl.ds(tokens, codes.shape[0]), pl.ds(0, tokens)]
+        loads = deal_copies(own_ref, early, piece, 0, dy, 0, sem_d)
+    else:
+        src = early[1].at[own_ref[0]]
+        loads = [pltpu.make_async_copy(early[0].at[own_ref[0]], dy, sem_d)]
+    load_codes = pltpu.make_async_copy(src, codes, sem_w.at[1])
+    load_codes.start()
+    for copy in loads:
+        copy.start()
     back = back_refs[0][...]
-    if sums == 5:
-        cut = tokens // 2
-        up_one, down_one, up_two, down_two = [ref[...].astype(jnp.float32) for ref in back_refs[1:]]
-        first = jnp.concatenate([up_two, up_one[cut:]], axis=0)
-        second = jnp.concatenate([down_one[:cut], down_two], axis=0)
-        back = back + first + second
+    for ref in back_refs[1:]:
+        back = back + ref[...].astype(jnp.float32)
     grad_pair = (
         back[tokens : tokens + experts, :tokens]
         + back[tokens : tokens + experts, tokens : 2 * tokens]
@@ -737,7 +819,8 @@
     router_t = aux_ref[:experts, :].astype(bf)
     gain = aux_ref[experts : experts + 1, :]
     logits = dot_nt(router_t, h2_ref[...])
-    chosen = codes_ref[...] > 0.0
+    load_codes.wait()
+    chosen = codes[...].astype(jnp.float32)[:experts] > 0.0
     top = jnp.max(jnp.where(chosen, logits, NEG_FILL), axis=0, keepdims=True)
     raised = jnp.where(chosen, jnp.exp(logits - top), 0.0)
     gates = raised / jnp.sum(raised, axis=0, keepdims=True)
@@ -749,7 +832,7 @@
     inverse = lax.rsqrt(jnp.mean(res * res, axis=1, keepdims=True) + EPSILON)
     scaled = dh2 * gain
     grad_gain = jnp.sum(dh2 * res * inverse, axis=0, keepdims=True)
-    load_dy.wait()
+    pltpu.make_async_copy(dy, dy, sem_d).wait()
     dres = (
         dy[...].astype(jnp.float32)
         + inverse * scaled
@@ -761,61 +844,22 @@
     side = jnp.concatenate(
         [grad_router, jnp.broadcast_to(grad_gain, (8, width)), pad], axis=0
     )
-    payload[:, width : width + 128] = side.T.astype(bf)
+    payload[:, base + width : base + width + 128] = side.T.astype(bf)
 
     @pl.loop(0, width // 256)
     def _(j):
         cols = tile_cols(j, 256)
-        payload[:, cols] = dot_tn(o_ref[...], dres_low[:, cols]).astype(bf)
-
+        at = pl.ds(pl.multiple_of(base + j * 256, 128), 256)
+        payload[:, at] = dot_tn(o_ref[...], dres_low[:, cols]).astype(bf)
+
+    send_payload(order_ref, payload, base, outs[len(outs) // 2 :], sem_p)
     load.wait()
 
     @pl.loop(0, width // 256)
     def _(j):
         cols = tile_cols(j, 256)
-        dmix_ref[:, cols] = dot_nt(dres_low[...], w_out[cols, :]).astype(bf)
-
-    send_payload(order_ref, payload, outs, sem_p)
-
-
-def run_middle(tuned, experts, order, own, dy_all, codes, backs, res, h2, o, aux, w_full):
-    tokens, width = res.shape
-    bf, f32 = jnp.bfloat16, jnp.float32
-    vmem = pl.BlockSpec(memory_space=pltpu.VMEM)
-    shape = jax.ShapeDtypeStruct
-    sem = pltpu.SemaphoreType.DMA
-    payload = payload_shapes(tuned, width, width + 128)
-    return pl.pallas_call(
-        lambda *refs: middle_kernel(experts, len(backs), *refs),
-        out_shape=payload + (shape((tokens, width), f32), shape((tokens, width), bf)),
-        in_specs=[smem_spec()] * 2 + [any_spec()] + [vmem] * (len(backs) + 5) + [any_spec()],
-        out_specs=tuple([any_spec()] * len(payload) + [vmem] * 2),
-        scratch_shapes=[
-            pltpu.VMEM((width, width), bf),
-            pltpu.VMEM((tokens, width), bf),
-            pltpu.VMEM((width, width + 128), bf),
-            pltpu.VMEM((tokens, width), bf),
-            sem((2,)),
-            sem,
-        ],
-        cost_estimate=pl.CostEstimate(flops=17600000000, transcendentals=0, bytes_accessed=16000000),
-        compiler_params=pltpu.CompilerParams(vmem_limit_bytes=56 * MIB),
-    )(order, own, dy_all, codes, *backs, res, h2, o, aux, w_full)
-
-
-def backward_kernel(order_ref, x_ref, cos_ref, sin_ref, *refs):
-    dres_ref, dmix_ref, h1_ref, q_ref, k_ref, v_ref, p_ref, aux_ref, w_full_ref = refs[:9]
-    rest = refs[9:]
-    outs = rest[:-7]
-    dx_ref, w_in, payload, dqkv, dh1, sem_w, sem_p = rest[-7:]
-    tokens, width = x_ref.shape
-    bf = jnp.bfloat16
-    heads = QUERY_HEADS // KEY_VALUE_HEADS
-    kv_width = KEY_VALUE_HEADS * HEAD_SIZE
-    main = width + 2 * kv_width
-    scale = HEAD_SIZE ** (-0.5)
-    load = pltpu.make_async_copy(w_full_ref.at[:, pl.ds(0, main)], w_in, sem_w)
-    load.start()
+        dmix_ref[:, cols] = dot_nt(dres_low[...], w_full[cols, base : base + width]).astype(bf)
+
     seq_len = tokens // SEQ_DEV
     for s in range(SEQ_DEV):
         rows = slice(s * seq_len, (s + 1) * seq_len)
@@ -842,12 +886,10 @@
             dqkv[rows, width + h * HEAD_SIZE : width + (h + 1) * HEAD_SIZE] = dk.astype(bf)
             at = width + kv_width + h * HEAD_SIZE
             dqkv[rows, at : at + HEAD_SIZE] = dv.astype(bf)
-    load.wait()
-
     @pl.loop(0, width // 256)
     def _(j):
         cols = tile_cols(j, 256)
-        dh1[:, cols] = dot_nt(dqkv[...], w_in[cols, :])
+        dh1[:, cols] = dot_nt(dqkv[...], w_full[cols, :main])
 
     @pl.loop(0, main // 256)
     def _(j):
@@ -866,34 +908,47 @@
         + inverse * scaled
         - x * inverse**3 * jnp.mean(scaled * x, axis=1, keepdims=True)
     )
+    send_payload(order_ref, payload, 0, outs[: len(outs) // 2], sem_p)
     dx_ref[...] = dx.astype(bf)
-    send_payload(order_ref, payload, outs, sem_p)
-
-
-def run_backward(tuned, order, x, cos_wide, sin_wide, dres, dmix, h1, q, k, v, p, aux, w_full):
-    tokens, width = x.shape
+    pltpu.make_async_copy(payload, payload, sem_p).wait()
+
+
+def run_backward(tuned, experts, piece, order, own, early, rows, backs, saved, w_full):
+    tokens, width = saved[0].shape
     bf, f32 = jnp.bfloat16, jnp.float32
     vmem = pl.BlockSpec(memory_space=pltpu.VMEM)
     shape = jax.ShapeDtypeStruct
     sem = pltpu.SemaphoreType.DMA
     main = width + 2 * KEY_VALUE_HEADS * HEAD_SIZE
     payload = payload_shapes(tuned, width, main + 128)
+    payload = payload + payload_shapes(tuned, width, width + 128)
     return pl.pallas_call(
-        backward_kernel,
+        lambda *refs: backward_kernel(experts, len(backs), piece, *refs),
         out_shape=payload + (shape((tokens, width), bf),),
-        in_specs=[smem_spec()] + [vmem] * 11 + [any_spec()],
+        in_specs=[smem_spec()] * 2
+        + [any_spec()] * len(early)
+        + [vmem] * (len(backs) + len(saved))
+        + [any_spec()],
         out_specs=tuple([any_spec()] * len(payload) + [vmem]),
         scratch_shapes=[
-            pltpu.VMEM((width, main), bf),
-            pltpu.VMEM((width, main + 128), bf),
+            pltpu.VMEM(w_full.shape, bf),
+            pltpu.VMEM((tokens, width), bf),
+            pltpu.VMEM((rows, tokens), bf),
+            pltpu.VMEM(w_full.shape, bf),
+            pltpu.VMEM((tokens, width), f32),
+            pltpu.VMEM((tokens, width), bf),
+            pltpu.VMEM((tokens, width), bf),
             pltpu.VMEM((tokens, main), bf),
             pltpu.VMEM((tokens, width), f32),
+            sem((2,)),
             sem,
             sem,
         ],
-        cost_estimate=pl.CostEstimate(flops=18700000000, transcendentals=0, bytes_accessed=17000000),
-        compiler_params=pltpu.CompilerParams(vmem_limit_bytes=56 * MIB),
-    )(order, x, cos_wide, sin_wide, dres, dmix, h1, q, k, v, p, aux, w_full)
+        cost_estimate=pl.CostEstimate(
+            flops=181000000000, transcendentals=0, bytes_accessed=32000000
+        ),
+        compiler_params=pltpu.CompilerParams(vmem_limit_bytes=60 * MIB),
+    )(order, own, *early, *backs, *saved, w_full)
 
 
 def after(value, *others):
@@ -908,74 +963,127 @@
     return lax.ppermute(value, "expert", [(i, (i + 4) % 8) for i in range(8)])
 
 
-def gather_all_pieces(value, tuned):
+def gather_front(pack, early, sent, w_gate, w_up, w_down, tuned):
     if not tuned:
-        full = lax.all_gather(value, ("dp", "expert"), axis=0, tiled=True)
-        return [full], [(0, (), None)], None
-    level = jnp.stack([value, shift_up(value), shift_down(value), shift_two(value)])
+        got = lax.all_to_all(sent, "expert", split_axis=0, concat_axis=2, tiled=True)
+        full = lax.all_gather(pack, ("dp", "expert"), axis=0, tiled=True)
+        dealt = [lax.all_gather(early, "expert", axis=0, tiled=False)]
+        weights = [
+            lax.all_gather(w_gate, "dp", axis=1, tiled=True),
+            lax.all_gather(w_up, "dp", axis=1, tiled=True),
+            lax.all_gather(w_down, "dp", axis=2, tiled=True),
+        ]
+        return got, [full], [(0, (), None)], dealt, weights
+    both = jnp.stack([w_gate, w_up])
+    ring = (pack, shift_up(pack), shift_down(pack), shift_two(pack))
+    down_x = swap_x(w_down)
+    down_y = swap_y(w_down)
+    down = [w_down, down_x, down_y, swap_x(down_y[:1]), swap_y(down_x[1:])]
+    *ring, _, _, both = lax.optimization_barrier(ring + tuple(down[1:3]) + (both,))
+    level = after(jnp.stack(ring), *down)
     from_x = swap_x(level)
     from_y = swap_y(level)
+    sent = after(sent, level)
+    got = lax.all_to_all(sent, "expert", split_axis=0, concat_axis=2, tiled=True)
+    early = after(early, level)
+    below = shift_up(early)
+    above = shift_down(early)
     far_a = swap_x(from_y[:2])
     far_b = swap_y(from_x[2:])
+    both = after(both, far_a, far_b)
+    both_x = swap_x(both)
+    both_y = swap_y(both)
+    dealt = [early, below, above, shift_up(below)]
+    dealt = dealt + [swap_core(v) for v in dealt]
     arrays = [level, from_x, from_y, far_a, far_b]
-    arrays = arrays + [swap_core(v) for v in arrays]
+    late = lax.optimization_barrier((far_a, far_b, below, above))[:2]
+    arrays = arrays + [swap_core(v) for v in arrays[:3]] + [swap_core(v) for v in late]
     places = []
     for c in range(2):
         for k in range(4):
             for r in range(4):
                 ref, lead = (k, r) if k < 3 else ((3, r) if r < 2 else (4, r - 2))
                 places.append((c * 5 + ref, (lead,), (c * 4 + k) * 4 + r))
-    return arrays, places, (level, from_x, from_y)
-
-
-def scatter_payload(outs, tuned):
+    return got, arrays, places, dealt, (both, both_x, both_y) + tuple(down)
+
+
+def scatter_core(outs):
+    got = [swap_core(v) for v in outs[5:]]
+    return [add_low(outs[k], got[k]) for k in range(4)] + [outs[4], got[4]]
+
+
+def scatter_planes(sums, first):
+    x_one, y_one, x_two, y_two, own, got_own = sums
+    x_two = swap_x(add_low(x_two, first[1][0]))
+    y_two = swap_y(add_low(y_two, first[0][0]))
+    level = []
+    for r in range(4):
+        near = (first[0][1, r], y_two[r]) if r < 2 else (x_two[r - 2], first[1][1, r - 2])
+        total = own[r].astype(jnp.float32) + got_own[r].astype(jnp.float32)
+        total = total + near[0].astype(jnp.float32) + near[1].astype(jnp.float32)
+        level.append(total if r == 0 else total.astype(jnp.bfloat16))
+    return level
+
+
+def scatter_ring(level, others, short):
+    below, above, far = level[1:]
+    if short:
+        got = [shift_down(below), shift_up(add_low(above, shift_up(far)))]
+    else:
+        got = [shift_down(below), shift_up(above), shift_two(far)]
+    last, *others = lax.optimization_barrier((level[0],) + tuple(others))
+    for v in got:
+        last = last + v.astype(jnp.float32)
+    return last, others
+
+
+def scatter_payload(outs, tuned, others, more, grad_x):
+    half = len(outs) // 2
     if not tuned:
-        return lax.psum_scatter(
-            outs[0], ("dp", "expert"), scatter_dimension=0, tiled=True
-        ).astype(jnp.float32)
-    f32, bf = jnp.float32, jnp.bfloat16
-    sums = [outs[k].astype(f32) + swap_core(outs[4 + k]).astype(f32) for k in range(4)]
-    from_x = swap_x(sums[1].astype(bf))
-    from_y = swap_y(sums[2].astype(bf))
-    from_far = swap_diagonal(sums[3].astype(bf))
-    level = [
-        sums[0][r] + from_x[r].astype(f32) + from_y[r].astype(f32) + from_far[r].astype(f32)
-        for r in range(4)
-    ]
-    below, above, far = [v.astype(bf) for v in level[1:]]
-    got = [shift_down(below), shift_up(above), shift_two(far)]
-    return level[0] + got[0].astype(f32) + got[1].astype(f32) + got[2].astype(f32)
-
-
-def sum_blocks(keep, send, cut, tuned, got=None, wait_for=()):
-    if not tuned:
-        blocks = jnp.concatenate([keep, send], axis=0)
-        return [
-            lax.psum_scatter(blocks, "expert", scatter_dimension=0, tiled=False).astype(jnp.float32)
-        ], None
-    got = swap_core(send) if got is None else got
+        owned = [
+            lax.psum_scatter(v, ("dp", "expert"), scatter_dimension=0, tiled=True) for v in outs
+        ]
+        return [v.astype(jnp.float32) for v in owned], others, more, grad_x
+    first = scatter_core(outs[:half])
+    second = scatter_core(outs[half:])
+    first_got = [swap_x(first[0]), swap_y(first[1])]
+    first_level = scatter_planes(first, first_got)
+    *sent, grad_x = lax.optimization_barrier((second[0], second[1], grad_x))
+    sent = lax.optimization_barrier(tuple(sent) + tuple(first_got))
+    second_got = [swap_x(sent[0]), swap_y(sent[1])]
+    second_level = scatter_planes(second, second_got)
+    more = lax.optimization_barrier(tuple(more) + (first_level[1],))[:-1]
+    owned_in, _ = scatter_ring(first_level, second_level[1:2], True)
+    owned_out, others = scatter_ring(second_level, others, False)
+    return [owned_in, owned_out], others, more, grad_x
+
+
+def sum_whole(keep, send):
+    blocks = jnp.concatenate([keep, send], axis=0)
+    sums = lax.psum_scatter(blocks, "expert", scatter_dimension=0, tiled=False)
+    return [sums.astype(jnp.float32)]
+
+
+def sum_messages(keep, got):
     sums = [keep[i].astype(jnp.float32) + got[i].astype(jnp.float32) for i in range(4)]
-    own = sums[0]
-    to_below, to_above, far = [v.astype(jnp.bfloat16) for v in sums[1:]]
-    top = lax.broadcasted_iota(jnp.int32, own.shape, 0) < cut
-    messages = (jnp.where(top, far, to_above), jnp.where(top, to_below, far))
-    up_one = shift_up(after(messages[0], *wait_for))
-    down_one = shift_down(after(messages[1], *wait_for))
-    up_two = shift_up(add_low(to_above[:cut], up_one[:cut]))
-    down_two = shift_down(add_low(to_below[cut:], down_one[cut:]))
-    return [own, up_one, down_one, up_two, down_two], messages
-
-
-def gather_dealt(value, tuned, level):
-    if not tuned:
-        return lax.all_gather(value, "expert", axis=0, tiled=False)
-    cut = value.shape[0] // 32 * 16
-    below = shift_up(value)
-    above = shift_down(value)
-    far_a = shift_up(after(below[:cut], level[1]))
-    far_b = shift_down(after(above[cut:], level[2]))
-    parts = jnp.stack([value, below, above, jnp.concatenate([far_a, far_b], axis=0)])
-    return jnp.concatenate([parts, swap_core(parts)], axis=0)
+    return [sums[0]] + [v.astype(jnp.bfloat16) for v in sums[1:]]
+
+
+def sum_ring(messages, between):
+    own, to_below, to_above, far = messages
+    got_far = shift_up(far)
+    from_above = shift_down(to_below)
+    if between is not None:
+        to_above = after(to_above, between)
+    onward = add_low(to_above, got_far)
+    return [own, from_above, shift_up(onward)], onward
+
+
+def deal_back(value, placement):
+    tokens, width = value.shape
+    value = value.reshape(1, SEQ_DEV, tokens // SEQ_DEV, width)
+    value = lax.all_to_all(value, "expert", split_axis=2, concat_axis=0, tiled=True)
+    return value.reshape(placement.shape[0], -1, width)[placement]
 
 
 def pad_columns(value, width):
@@ -1027,12 +1135,7 @@
         ],
         axis=1,
     )
-    pack_parts, pack_places, level = gather_all_pieces(pack, tuned)
-    send_tokens = tokens[source].reshape(expert_devices, SEQ_DEV, piece_len, width)
-    if tuned:
-        send_tokens = after(send_tokens, level[0])
-    got_tokens = lax.all_to_all(send_tokens, "expert", split_axis=0, concat_axis=2, tiled=True)
-    x_local = got_tokens.reshape(token_count, width)
+    sent = tokens[source].reshape(expert_devices, SEQ_DEV, piece_len, width)
     ranks = slot_ranks(routes.reshape(-1), priority.reshape(-1)).reshape(token_count, TOPK)
     codes = jnp.minimum(ranks, capacity) + 1
     expert_list = jnp.arange(expert_count, dtype=jnp.int32)
@@ -1042,29 +1145,34 @@
     table = jnp.zeros((table_rows, width), jnp.bfloat16)
     table = table.at[:expert_count, :token_count].set(code_table.astype(jnp.bfloat16))
     early = jnp.concatenate([cotangent.reshape(token_count, width), table], axis=0)
-    if tuned:
-        early = after(early, x_local)
-    early_all = gather_dealt(early, tuned, level)
+    got_tokens, pack_parts, pack_places, early_parts, weights = gather_front(
+        pack, early, sent, w_gate, w_up, w_down, tuned
+    )
+    x_local = got_tokens.reshape(token_count, width)
     order = expert_order(tuned, expert_devices)
-    rel_of = jnp.zeros((expert_devices,), jnp.int32)
-    for b in range(expert_devices):
-        rel_of = jnp.where(jnp.arange(expert_devices) == order[b], b, rel_of)
     seqs = source.reshape(expert_devices, SEQ_DEV)[order].reshape(-1)
-    if piece_len % 16 == 0:
-        shape = (expert_devices, token_count, width)
-        grads_all = move_blocks(deal_kernel, shape, [seqs, rel_of], [early_all])
-    else:
+    rel_of = jnp.sum(
+        jnp.where(
+            order[None, :] == jnp.arange(expert_devices)[:, None],
+            jnp.arange(expert_devices)[None, :],
+            0,
+        ),
+        axis=1,
+    )
+    plane = lax.axis_index("dp").reshape(1)
+    scalars = jnp.concatenate([my_index.reshape(1), seqs, order, rel_of, plane])
+    scalars = scalars.astype(jnp.int32)
+    grads_all = jnp.zeros((16, 128), jnp.bfloat16)
+    codes_all = grads_all
+    if not tuned:
+        early_all = early_parts[0]
         pieces = early_all[:, :token_count].reshape(expert_devices, row_seqs, piece_len, width)
-        pieces = pieces[rel_of][:, seqs].reshape(
+        pieces = pieces[:, seqs].reshape(
             expert_devices, expert_devices, SEQ_DEV, piece_len, width
         )
         grads_all = pieces.transpose(1, 2, 0, 3, 4).reshape(expert_devices, token_count, width)
-    codes_all = early_all[:, token_count : token_count + expert_count, :token_count].astype(
-        jnp.float32
-    )
-    own_block = rel_of[my_index].reshape(1)
-    weight_parts, weight_places = gather_weight_pieces(w_gate, w_up, w_down, tuned)
-
+        codes_all = early_all[:, token_count:, :token_count]
+        early_parts = []
     own_seqs = lax.dynamic_slice_in_dim(source, my_index * SEQ_DEV, SEQ_DEV)
     positions, labels = device_layout(lengths[own_seqs], seq_len)
     cosine_table, sine_values = rope_tables(positions, HEAD_SIZE)
@@ -1087,12 +1195,8 @@
         pack_parts,
         pack.shape[1],
     )
-    token_parts, token_places = gather_token_pieces(normed_moe, tuned, grads_all)
-    token_places = [
-        [(r + len(weight_parts), lead, row, rows) for r, lead, row, rows in line]
-        for line in token_places
-    ]
-    inputs = weight_parts + token_parts
+    inputs, weight_places, token_places = gather_inputs(normed_moe, weights, per_device, tuned)
+    inputs = inputs + early_parts
     plan = {
         "inputs": len(inputs),
         "blocks": expert_devices,
@@ -1100,100 +1204,83 @@
         "ff": w_gate.shape[2],
         "weights": weight_places,
         "tokens": token_places,
+        "token_count": token_count,
+        "piece": piece_len,
+        "early": list(range(len(inputs) - len(early_parts), len(inputs))),
     }
-    scalars = jnp.stack([my_index, lax.axis_index("dp")]).astype(jnp.int32)
     router_t = aux[:expert_count].astype(jnp.bfloat16)
     back_keep, back_send, out_keep, out_send, x_slots, dy_slots, hid, dga, dua = run_experts(
-        plan, capacity, table_rows, scalars, codes_all, router_t, grads_all, inputs
-    )
-    cut = token_count // 2
-    back_got, out_got = None, None
+        plan, capacity, table_rows, scalars, router_t, codes_all, grads_all, residual, inputs
+    )
     if tuned:
         back_got = swap_core(back_send)
         out_got = swap_core(after(out_send, back_got))
-    backs, messages = sum_blocks(back_keep, back_send, cut, tuned, back_got)
+        messages = sum_messages(back_keep, back_got)
+        x_slots = after(x_slots, *messages)
+    if width // plane_size * 2 == w_gate.shape[2] and width % (128 * plane_size) == 0:
+        weight_grads = expert_weight_grads(x_slots, dga, dua, hid, dy_slots, plane_size)
+        flat = weight_grads.reshape(-1, weight_grads.shape[-1])
+        owned = lax.psum_scatter(flat, "dp", scatter_dimension=0, tiled=True)
+        owned = owned.reshape(weight_grads.shape[1:])
+        half = owned.shape[-1] // 2
+        owned_gate, owned_up = owned[0].astype(jnp.float32), owned[1].astype(jnp.float32)
+        owned_down = jnp.concatenate([owned[2, :, :, :half], owned[2, :, :, half:]], axis=1)
+    else:
+        gate_up, down = whole_weight_grads(x_slots, dga, dua, hid, dy_slots)
+        owned = lax.psum_scatter(gate_up, "dp", scatter_dimension=2, tiled=True)
+        owned_gate, owned_up = owned[0].astype(jnp.float32), owned[1].astype(jnp.float32)
+        owned_down = lax.psum_scatter(down, "dp", scatter_dimension=2, tiled=True)
+    owned_down = owned_down.astype(jnp.float32)
     if tuned:
-        hid, x_slots = after(hid, *messages), after(x_slots, *messages)
-    even = width % (128 * plane_size) == 0
-    down_blocks = grad_down_blocks(hid, dy_slots, plane_size if even else 1)
-    gate_up_blocks = grad_gate_up_blocks(x_slots, dga, dua, plane_size if even else 1)
-    if even:
-        flat = down_blocks.reshape(-1, down_blocks.shape[-1])
-        owned_down = lax.psum_scatter(flat, "dp", scatter_dimension=0, tiled=True)
-        owned_down = owned_down.reshape(down_blocks.shape[1:])
-        flat = gate_up_blocks.reshape(-1, gate_up_blocks.shape[-1])
-        owned_gate_up = lax.psum_scatter(flat, "dp", scatter_dimension=0, tiled=True)
-        owned_gate_up = owned_gate_up.reshape(gate_up_blocks.shape[1:])
+        backs, _ = sum_ring(messages, weight_grads)
+        messages = sum_messages(after(out_keep, backs[1]), out_got)
+        backs[0] = after(backs[0], *messages)
+        messages[1:] = lax.optimization_barrier(tuple(messages[1:]) + tuple(backs[1:]))[:3]
     else:
-        owned_down = lax.psum_scatter(down_blocks[0], "dp", scatter_dimension=2, tiled=True)
-        owned_gate_up = lax.psum_scatter(gate_up_blocks[0], "dp", scatter_dimension=2, tiled=True)
-    owned_down = owned_down.astype(jnp.float32)
-    owned_gate = owned_gate_up[0].astype(jnp.float32)
-    owned_up = owned_gate_up[1].astype(jnp.float32)
-    if tuned:
-        residual, out_keep = after(residual, out_got), after(out_keep, *backs[1:3])
-    sums, messages = sum_blocks(out_keep, out_send, cut, tuned, out_got, backs[3:])
-    if tuned:
-        backs[0] = after(backs[0], *messages)
-    middle = run_middle(
+        backs = sum_whole(back_keep, back_send)
+        sums = sum_whole(out_keep, out_send)
+    final = run_backward(
         tuned,
         expert_count,
+        piece_len if tuned else 0,
         row_order,
-        own_block,
-        grads_all,
-        codes_all[0] if tuned else codes_all[own_block[0]],
+        scalars,
+        early_parts if tuned else [grads_all, codes_all],
+        table_rows,
         backs,
-        residual,
-        normed_moe,
-        mixed,
-        aux,
+        [
+            residual,
+            normed_moe,
+            mixed,
+            aux,
+            x_local,
+            cos_wide,
+            sin_wide,
+            h1,
+            q,
+            k,
+            v,
+            probs,
+        ],
         w_full,
     )
-    payload_out, dres, dmix = middle[:-2], middle[-2], middle[-1]
-    owned_out = scatter_payload(payload_out, tuned)
-    final = run_backward(
-        tuned,
-        row_order,
-        x_local,
-        cos_wide,
-        sin_wide,
-        dres,
-        dmix,
-        h1,
-        q,
-        k,
-        v,
-        probs,
-        aux,
-        w_full,
-    )
-    payload_in, grad_x = final[:-1], final[-1]
+    payload, grad_x = final[:-1], final[-1]
     if tuned:
-        payload_in = [after(v, sums[1], sums[2]) for v in payload_in]
-    owned_in = scatter_payload(payload_in, tuned)
-    total = residual + sums[0]
+        sums, onward = sum_ring(messages, grad_x)
+        *payload, _ = lax.optimization_barrier(tuple(payload) + (onward,))
+    others = (owned_gate, owned_up, owned_down)
+    (owned_in, owned_out), others, more, grad_x = scatter_payload(
+        payload, tuned, others, sums, grad_x
+    )
+    owned_gate, owned_up, owned_down = others
     if tuned:
-        total = total + jnp.concatenate([sums[3], sums[1][cut:]], axis=0).astype(jnp.float32)
-        total = total + jnp.concatenate([sums[2][:cut], sums[4]], axis=0).astype(jnp.float32)
-    out_low = total.astype(jnp.bfloat16)
-    deal_out, deal_grad = (
-        lax.all_to_all(
-            out_low.reshape(1, SEQ_DEV, seq_len, width),
-            "expert",
-            split_axis=2,
-            concat_axis=0,
-            tiled=True,
-        ),
-        lax.all_to_all(
-            grad_x.reshape(1, SEQ_DEV, seq_len, width),
-            "expert",
-            split_axis=2,
-            concat_axis=0,
-            tiled=True,
-        ),
-    )
-    output = deal_out.reshape(row_seqs, piece_len, width)[placement]
-    input_grad = deal_grad.reshape(row_seqs, piece_len, width)[placement]
+        sums = list(more)
+    if tuned:
+        total = sums[0] + sums[1].astype(jnp.float32) + sums[2].astype(jnp.float32)
+        output = total.astype(jnp.bfloat16).reshape(row_seqs, piece_len, width)
+    else:
+        output = deal_back((residual + sums[0]).astype(jnp.bfloat16), placement)
+    input_grad = deal_back(grad_x, placement)
     return (
         output,
         input_grad,

time: 594 us -> 507 us (0.85)
  waiting for transfers between devices: 275 us -> 225 us
  other arithmetic: 53.9 us -> 40.8 us
  Pallas kernels: 127 us -> 114 us
  local copies, waits for them, and re-layouts: 50.3 us -> 40.3 us
    ppermute x11 -> x7, waiting for transfers between devices: 45 us -> 15.5 us  [shift_down(): return lax.ppermute(value, 'expert', [(i, (i + 6) % 8) for i in range(8)])]
    ppermute x4 -> x10, waiting for transfers between devices: 26.9 us -> 48.1 us  [swap_x(): return lax.ppermute(value, 'dp', [(i, i ^ 1) for i in range(4)])]
    ppermute x11 -> x12, waiting for transfers between devices: 113 us -> 91.7 us  [shift_up(): return lax.ppermute(value, 'expert', [(i, (i + 2) % 8) for i in range(8)])]
    pallas_call x5 -> x2, Pallas kernels: 60.4 us -> 46.9 us  [the longest x1 29 us: run_backward(): pl.pallas_call(lambda *refs: backward_kernel(experts, len(backs), piece,...]
    ppermute x3 -> x2, waiting for transfers between devices: 22.5 us -> 10 us  [shift_two(): return lax.ppermute(value, 'expert', [(i, (i + 4) % 8) for i in range(8)])]
    convert_element_type x4 -> x11, other arithmetic: 2.51 us -> 12.4 us  [add_low(): (left.astype(jnp.float32) + right.astype(jnp.float32)).astype(jnp.bfloat16)]
    unnamed x129 -> x92, local copies, waits for them, and re-layouts: 19.9 us -> 10.7 us
    select_n x5 -> x2, other arithmetic: 8.51 us -> 0.01 us  [the longest x1 0.01 us: body(): sent = tokens[source].reshape(expert_devices, SEQ_DEV, piece_len, width)]
  transfers between devices with their start and end apart: 63 -> 69, of which waited for: 23 -> 27; matrix products, arithmetic and copies ran while one was open for 13% -> 15% of each run, Pallas kernels for 12% -> 13%
where the time goes in v3:
time: 507 us; the launch traced here: 500 us
  waiting for transfers between devices  225 us (44%)
  Pallas kernels  114 us (22%)
  starting transfers between devices  64.1 us (13%)
  other arithmetic  40.8 us (8%)
  local copies, waits for them, and re-layouts  40.3 us (8%)
  between operations  15.1 us (3%)
    ppermute x12, waiting for transfers between devices, shift_up(): return lax.ppermute(value, 'expert', [(i, (i + 2) % 8) for i in range(8)])  91.7 us
    pallas_call x1, Pallas kernels, run_experts(): pl.pallas_call(lambda *refs: expert_kernel(plan, capacity, *refs), out_sh...  51.5 us
    ppermute x10, waiting for transfers between devices, swap_x(): return lax.ppermute(value, 'dp', [(i, i ^ 1) for i in range(4)])  48.1 us
    ppermute x10, waiting for transfers between devices, swap_y(): return lax.ppermute(value, 'dp', [(i, i ^ 2) for i in range(4)])  43.1 us
    pallas_call x1, Pallas kernels, run_backward(): pl.pallas_call(lambda *refs: backward_kernel(experts, len(backs), piece,...  29 us
    ppermute x7, starting transfers between devices, shift_down(): return lax.ppermute(value, 'expert', [(i, (i + 6) % 8) for i in range(8)])  19.2 us
    pallas_call x1, Pallas kernels, expert_weight_grads(): pl.pallas_call(weight_kernel, grid=(per_device, parts), out_shape=jax.Sha...  17.8 us
    pallas_call x1, Pallas kernels, run_forward(): pl.pallas_call(lambda *refs: forward_kernel(plan, *refs), out_shape=(shap...  16.1 us
  transfers between devices with their start and end apart: 69, of which 27 were waited for; matrix products, arithmetic and copies ran while one was open for 15% of the time, Pallas kernels for 13%

profile of v3, /device:TPU:0, one launch (start us, length us, event | category | flops | bytes accessed | tf_op | source)
XLA Modules:
  0.0 499.6 jit_solution(2802582973700214563)
XLA Ops:
  7.2 3.0 collective-permute-start.4
  10.2 1.5 collective-permute-start.3
  17.6 1.6 collective-permute-start
  19.2 2.2 collective-permute-start.1
  28.3 8.2 %collective-permute-done.4.refs_12_ = bf16[2,768,384]{2,1,0:T(8,128)(2,1)} collective-permute-done((bf16[2,768,384]{2,1,0:T(8,128)(2,1)}, bf16[2,768,384]{2,1,0:T(8,128)(2,1)}, u32[]{:S(2)}, u32[]{:S(2)}) %collective-permute-start.4) | collective-permute-done | bytes 1179680 | tf_op jit(solution)/shard_map/ppermute | solution.py:59
  37.6 1.8 collective-permute-start.5
  40.5 1.6 collective-permute-start.6
  42.1 1.6 pad_maximum_fusion.refs_5_
  43.8 9.3 %collective-permute-done.2 = bf16[48,3840]{1,0:T(8,128)(2,1)} collective-permute-done((bf16[48,3840]{1,0:T(8,128)(2,1)S(1)}, bf16[48,3840]{1,0:T(8,128)(2,1)}, u32[]{:S(2)}, u32[]{:S(2)}) %collective-permute-start.2) | collective-permute-done | bytes 368672 | tf_op jit(solution)/shard_map/ppermute | solution.py:963
  53.1 2.5 pad_maximum_fusion.1.refs_6_
  58.3 1.5 collective-permute-start.14
  59.9 2.4 collective-permute-start.15
  62.3 27.9 %collective-permute-done.7.refs_7_ = bf16[4,48,3840]{2,1,0:T(8,128)(2,1)} collective-permute-done((bf16[4,48,3840]{2,1,0:T(8,128)(2,1)}, bf16[4,48,3840]{2,1,0:T(8,128)(2,1)}, u32[]{:S(2)}, u32[]{:S(2)}) %collective-permute-start.7) | collective-permute-done | bytes 1474592 | tf_op jit(solution)/shard_map/ppermute | solution.py:55
  90.2 2.0 slice.314
  92.7 2.0 slice.313
  98.4 3.7 all-to-all-start
  103.3 6.8 %collective-permute-done.10.refs_10_ = bf16[2,48,3840]{2,1,0:T(8,128)(2,1)} collective-permute-done((bf16[2,48,3840]{2,1,0:T(8,128)(2,1)}, bf16[2,48,3840]{2,1,0:T(8,128)(2,1)}, u32[]{:S(2)}, u32[]{:S(2)}) %collective-permute-start.10) | collective-permute-done | bytes 737312 | tf_op jit(solution)/shard_map/ppermute | solution.py:59
  110.1 2.3 collective-permute-done.9.refs_9_
  116.5 6.6 %all-to-all-done = bf16[8,2,16,1536]{3,2,1,0:T(8,128)(2,1)S(1)} async-done(((bf16[8,2,16,1536]{3,2,1,0:T(8,128)(2,1)}), bf16[8,2,16,1536]{3,2,1,0:T(8,128)(2,1)S(1)}, u32[]{:S(2)}, u32[]{:S(2)}) %all-to-all-start) | async-done | bytes 786464 | tf_op jit(solution)/shard_map/all_to_all | solution.py:987
  125.1 1.5 collective-permute-start.21
  126.7 16.1 %shard_map.247 = (bf16[256,1536]{1,0:T(8,128)(2,1)}, f32[256,1536]{1,0:T(8,128)}, bf16[256,1536]{1,0:T(8,128)(2,1)}, bf16[256,1536]{1,0:T(8,128)(2,1)}, bf16[256...) custom-call(s32[32]{0:T(128)} %stack.218.refs_0_, ...), custom_call_target="tpu_custom_call" | custom-call | flops 109999996928 | bytes 16000000 | tf_op jit(solution)/shard_map/pallas_call | solution.py:730
  143.0 3.7 collective-permute-start.19
  146.7 18.8 %collective-permute-done.18.refs_16_ = bf16[256,1536]{1,0:T(8,128)(2,1)} collective-permute-done((bf16[256,1536]{1,0:T(8,128)(2,1)}, bf16[256,1536]{1,0:T(8,128)(2,1)}, u32[]{:S(2)}, u32[]{:S(2)}) %collective-permute-start.18) | collective-permute-done | bytes 786464 | tf_op jit(solution)/shard_map/ppermute | solution.py:67
  165.4 14.5 %collective-permute-done.19.refs_17_ = bf16[256,1536]{1,0:T(8,128)(2,1)} collective-permute-done((bf16[256,1536]{1,0:T(8,128)(2,1)}, bf16[256,1536]{1,0:T(8,128)(2,1)}, u32[]{:S(2)}, u32[]{:S(2)}) %collective-permute-start.19) | collective-permute-done | bytes 786464 | tf_op jit(solution)/shard_map/ppermute | solution.py:71
  185.0 1.5 collective-permute-start.23
  187.4 16.5 %collective-permute-done.24.refs_18_ = bf16[256,1536]{1,0:T(8,128)(2,1)} collective-permute-done((bf16[256,1536]{1,0:T(8,128)(2,1)}, bf16[256,1536]{1,0:T(8,128)(2,1)}, u32[]{:S(2)}, u32[]{:S(2)}) %collective-permute-start.24) | collective-permute-done | bytes 786464 | tf_op jit(solution)/shard_map/ppermute | solution.py:67
  205.6 1.5 slice.454.refs_1_
  207.1 5.3 %collective-permute-done.22.refs_8_ = bf16[2,384,768]{2,1,0:T(8,128)(2,1)} collective-permute-done((bf16[2,384,768]{2,1,0:T(8,128)(2,1)S(1)}, bf16[2,384,768]{2,1,0:T(8,128)(2,1)}, u32[]{:S(2)}, u32[]{:S(2)}) %collective-permute-start.22) | collective-permute-done | bytes 1179680 | tf_op jit(solution)/shard_map/ppermute | solution.py:55
  213.5 51.5 %shard_map.248 = (bf16[4,272,1536]{2,1,0:T(8,128)(2,1)}, bf16[4,272,1536]{2,1,0:T(8,128)(2,1)}, bf16[4,256,1536]{2,1,0:T(8,128)(2,1)}, bf16[4,256,1536]{2,1,0:T(...) custom-call(s32[34]{0:T(128)} %concatenate.43.refs_0_.refs_1_, ...), custom_call_target="tpu_custom_call" | custom-call | flops 54999998464 | bytes 50000000 | tf_op jit(solution)/shard_map/pallas_call | solution.py:475
  265.1 6.1 %collective-permute-done.34 = bf16[4,272,1536]{2,1,0:T(8,128)(2,1)S(1)} collective-permute-done((bf16[4,272,1536]{2,1,0:T(8,128)(2,1)}, bf16[4,272,1536]{2,1,0:T(8,128)(2,1)S(1)}, u32[]{:S(2)}, u32[]{:S(2)}) %collective-permute-start.34) | collective-permute-done | bytes 3342368 | tf_op jit(solution)/shard_map/ppermute | solution.py:63
  271.3 4.3 add_bitcast_fusion
  275.6 3.3 collective-permute-start.35
  278.9 17.8 %shard_map.249 = bf16[4,3,2,384,768]{4,3,2,1,0:T(8,128)(2,1)} custom-call(bf16[2,576,1536]{2,1,0:T(8,128)(2,1)} %get-tuple-element.146.x_ref, bf16[2,576,768]{2,1,0:T(8,128)(2,1)} %get-tuple-element.147.dga_ref, bf16[2,576,768]{2,1,0:T(8,128)(2,1)} %get-tuple-element.148.dua_ref, bf16[2,576,768]{2,1,0:T(8,128)(2,1)} %get-tuple-element.149.hid_ref, ...), custom_call_target="tpu_custom_call" | custom-call | flops 18699999232 | bytes 17000000 | tf_op jit(solution)/shard_map/pallas_call | solution.py:532
  296.8 19.2 %collective-permute-done.37 = bf16[272,1536]{1,0:T(8,128)(2,1)S(1)} collective-permute-done((bf16[272,1536]{1,0:T(8,128)(2,1)}, bf16[272,1536]{1,0:T(8,128)(2,1)S(1)}, u32[]{:S(2)}, u32[]{:S(2)}) %collective-permute-start.37) | collective-permute-done | bytes 835616 | tf_op jit(solution)/shard_map/ppermute | solution.py:67
  316.1 1.8 collective-permute-start.38
  318.0 5.3 %fusion.9 = (bf16[256,1536]{1,0:T(8,128)(2,1)}, bf16[256,1536]{1,0:T(8,128)(2,1)}, bf16[256,1536]{1,0:T(8,128)(2,1)}, f32[256,1536]{1,0:T(8,128)}) fusion(bf16[4,256,1536]{2,1,0:T(8,128)(2,1)} %collective-permute-done.36, bf16[4,256,1536]{2,1,0:T(8,128)(2,1)} %get-tuple-element.142), kind=kLoop, calls=%fused_computation.39 | loop fusion | flops 5898240 | bytes 10223616 | tf_op jit(solution)/shard_map/convert_element_type | solution.py:1069
  323.2 15.0 %collective-permute-done.38.refs_12_ = bf16[272,1536]{1,0:T(8,128)(2,1)S(1)} collective-permute-done((bf16[272,1536]{1,0:T(8,128)(2,1)S(1)}, bf16[272,1536]{1,0:T(8,128)(2,1)S(1)}, u32[]{:S(2)}, u32[]{:S(2)}) %collective-permute-start.38) | collective-permute-done | bytes 835616 | tf_op jit(solution)/shard_map/ppermute | solution.py:67
  339.2 29.0 %shard_map.250 = (bf16[2,2,48,2176]{3,2,1,0:T(8,128)(2,1)}, bf16[2,2,48,2176]{3,2,1,0:T(8,128)(2,1)}, bf16[2,48,2176]{2,1,0:T(8,128)(2,1)}, bf16[2,48,2176]{2,1,...) custom-call(s32[32]{0:T(128)} %stack.218.refs_0_, ...), custom_call_target="tpu_custom_call" | custom-call | flops 180999995392 | bytes 32000000 | tf_op jit(solution)/shard_map/pallas_call | solution.py:925
  368.3 2.4 add_convert_fusion.7
  371.7 2.1 collective-permute-done.48
  377.8 1.5 collective-permute-start.51
  382.0 1.7 copy.79
  383.6 4.5 all-to-all-start.1
  388.1 16.7 %collective-permute-done.51 = bf16[2,2,48,2176]{3,2,1,0:T(8,128)(2,1)S(1)} collective-permute-done((bf16[2,2,48,2176]{3,2,1,0:T(8,128)(2,1)}, bf16[2,2,48,2176]{3,2,1,0:T(8,128)(2,1)S(1)}, u32[]{:S(2)}, u32[]{:S(2)}) %collective-permute-start.51) | collective-permute-done | bytes 835616 | tf_op jit(solution)/shard_map/ppermute | solution.py:59
  404.8 2.0 fusion.5
  406.8 1.5 collective-permute-start.57
  408.4 2.2 fusion.6
  411.2 3.3 collective-permute-start.39
  416.3 11.8 %collective-permute-done.57 = bf16[2,48,2176]{2,1,0:T(8,128)(2,1)} collective-permute-done((bf16[2,48,2176]{2,1,0:T(8,128)(2,1)}, bf16[2,48,2176]{2,1,0:T(8,128)(2,1)}, u32[]{:S(2)}, u32[]{:S(2)}) %collective-permute-start.57) | collective-permute-done | bytes 417824 | tf_op jit(solution)/shard_map/ppermute | solution.py:55
  428.1 3.7 collective-permute-done.46
  432.3 1.6 convert_add_fusion.6
  434.0 14.4 %collective-permute-done.41 = bf16[256,1536]{1,0:T(8,128)(2,1)} collective-permute-done((bf16[256,1536]{1,0:T(8,128)(2,1)}, bf16[256,1536]{1,0:T(8,128)(2,1)}, u32[]{:S(2)}, u32[]{:S(2)}) %collective-permute-start.41) | collective-permute-done | bytes 786464 | tf_op jit(solution)/shard_map/ppermute | solution.py:67
  449.0 2.6 add_convert_fusion.6
  451.6 1.7 collective-permute-start.55
  453.4 6.9 %collective-permute-done.62 = bf16[2,2,48,1664]{3,2,1,0:T(8,128)(2,1)S(1)} collective-permute-done((bf16[2,2,48,1664]{3,2,1,0:T(8,128)(2,1)}, bf16[2,2,48,1664]{3,2,1,0:T(8,128)(2,1)S(1)}, u32[]{:S(2)}, u32[]{:S(2)}) %collective-permute-start.62) | collective-permute-done | bytes 639008 | tf_op jit(solution)/shard_map/ppermute | solution.py:59
  461.9 1.5 collective-permute-start.63
  464.2 4.0 collective-permute-done.58
  471.1 2.5 collective-permute-start.60
  473.6 2.0 collective-permute-start.65
  475.6 3.8 collective-permute-done.59
  482.9 1.8 fusion.26
  484.6 1.6 convert.35
  486.2 1.6 convert.36
  487.8 1.6 maximum_convert_fusion
  (259 shorter events, 62.1 us)
Async XLA Ops:
  7.2 29.3 %collective-permute-start.4 = (bf16[2,768,384]{2,1,0:T(8,128)(2,1)}, bf16[2,768,384]{2,1,0:T(8,128)(2,1)}, u32[]{:S(2)}, u32[]{:S(2)}) collective-permute-start(bf16[2,768,384]{2,1,0:T(8,128)(2,1)} %refs_10_.1), channel_id=1, source_target_pairs={{0,16},{8,24},{16,0},{24,8},{1,17},{9,25},{17,1},{25,9},{2,18},{10... | collective-permute-start | bytes 3538952 | tf_op jit(solution)/shard_map/ppermute | solution.py:59
  10.2 29.2 %collective-permute-start.3 = (bf16[2,768,384]{2,1,0:T(8,128)(2,1)}, bf16[2,768,384]{2,1,0:T(8,128)(2,1)}, u32[]{:S(2)}, u32[]{:S(2)}) collective-permute-start(bf16[2,768,384]{2,1,0:T(8,128)(2,1)} %refs_10_.1), channel_id=1, source_target_pairs={{0,8},{8,0},{16,24},{24,16},{1,9},{9,1},{17,25},{25,17},{2,10},{10... | collective-permute-start | bytes 3538952 | tf_op jit(solution)/shard_map/ppermute | solution.py:55
  17.6 26.2 %collective-permute-start = (bf16[48,3840]{1,0:T(8,128)(2,1)S(1)}, bf16[48,3840]{1,0:T(8,128)(2,1)}, u32[]{:S(2)}, u32[]{:S(2)}) collective-permute-start(bf16[48,3840]{1,0:T(8,128)(2,1)S(1)} %fusion.22), channel_id=1, source_target_pairs={{0,2},{1,3},{2,4},{3,5},{4,6},{5,7},{6,0},{7,1},{8,10},{9,11},{10,... | collective-permute-start | bytes 1105928 | tf_op jit(solution)/shard_map/ppermute | solution.py:67
  19.2 24.6 %collective-permute-start.1 = (bf16[48,3840]{1,0:T(8,128)(2,1)S(1)}, bf16[48,3840]{1,0:T(8,128)(2,1)}, u32[]{:S(2)}, u32[]{:S(2)}) collective-permute-start(bf16[48,3840]{1,0:T(8,128)(2,1)S(1)} %fusion.22), channel_id=1, source_target_pairs={{0,6},{1,7},{2,0},{3,1},{4,2},{5,3},{6,4},{7,5},{8,14},{9,15},{10,... | collective-permute-start | bytes 1105928 | tf_op jit(solution)/shard_map/ppermute | solution.py:71
  21.4 31.6 %collective-permute-start.2 = (bf16[48,3840]{1,0:T(8,128)(2,1)S(1)}, bf16[48,3840]{1,0:T(8,128)(2,1)}, u32[]{:S(2)}, u32[]{:S(2)}) collective-permute-start(bf16[48,3840]{1,0:T(8,128)(2,1)S(1)} %fusion.22), channel_id=1, source_target_pairs={{0,4},{1,5},{2,6},{3,7},{4,0},{5,1},{6,2},{7,3},{8,12},{9,13},{10,... | collective-permute-start | bytes 1105928 | tf_op jit(solution)/shard_map/ppermute | solution.py:963
  37.6 17.9 %collective-permute-start.5 = (bf16[1,768,384]{2,1,0:T(8,128)(2,1)S(1)}, bf16[1,768,384]{2,1,0:T(8,128)(2,1)S(1)}, u32[]{:S(2)}, u32[]{:S(2)}) collective-permute-start(bf16[1,768,384]{2,1,0:T(8,128)(2,1)S(1)} %slice.311), channel_id=1, source_target_pairs={{0,8},{8,0},{16,24},{24,16},{1,9},{9,1},{17,25},{25,17},{2,10},{10... | collective-permute-start | bytes 1769480 | tf_op jit(solution)/shard_map/ppermute | solution.py:55
  40.5 15.0 %collective-permute-start.6 = (bf16[1,768,384]{2,1,0:T(8,128)(2,1)S(1)}, bf16[1,768,384]{2,1,0:T(8,128)(2,1)S(1)}, u32[]{:S(2)}, u32[]{:S(2)}) collective-permute-start(bf16[1,768,384]{2,1,0:T(8,128)(2,1)S(1)} %slice.312), channel_id=1, source_target_pairs={{0,16},{8,24},{16,0},{24,8},{1,17},{9,25},{17,1},{25,9},{2,18},{10... | collective-permute-start | bytes 1769480 | tf_op jit(solution)/shard_map/ppermute | solution.py:59
  55.6 34.6 %collective-permute-start.7 = (bf16[4,48,3840]{2,1,0:T(8,128)(2,1)}, bf16[4,48,3840]{2,1,0:T(8,128)(2,1)}, u32[]{:S(2)}, u32[]{:S(2)}) collective-permute-start(bf16[4,48,3840]{2,1,0:T(8,128)(2,1)} %pad_maximum_fusion.1.refs_6_), channel_id=1, source_target_pairs={{0,8},{8,0},{16,24},{24,16},{1,9},{9,1},{17,25},{25,17},{2,10},{10... | collective-permute-start | bytes 4423688 | tf_op jit(solution)/shard_map/ppermute | solution.py:55
  56.2 36.5 %collective-permute-start.8 = (bf16[4,48,3840]{2,1,0:T(8,128)(2,1)}, bf16[4,48,3840]{2,1,0:T(8,128)(2,1)}, u32[]{:S(2)}, u32[]{:S(2)}) collective-permute-start(bf16[4,48,3840]{2,1,0:T(8,128)(2,1)} %pad_maximum_fusion.1.refs_6_), channel_id=1, source_target_pairs={{0,16},{8,24},{16,0},{24,8},{1,17},{9,25},{17,1},{25,9},{2,18},{10... | collective-permute-start | bytes 4423688 | tf_op jit(solution)/shard_map/ppermute | solution.py:59
  58.3 37.0 %collective-permute-start.14 = (bf16[272,1536]{1,0:T(8,128)(2,1)S(1)}, bf16[272,1536]{1,0:T(8,128)(2,1)S(1)}, u32[]{:S(2)}, u32[]{:S(2)}) collective-permute-start(bf16[272,1536]{1,0:T(8,128)(2,1)S(1)} %fusion.1.refs_23_.refs_2_), channel_id=1, source_target_pairs={{0,2},{1,3},{2,4},{3,5},{4,6},{5,7},{6,0},{7,1},{8,10},{9,11},{10,... | collective-permute-start | bytes 2506760 | tf_op jit(solution)/shard_map/ppermute | solution.py:67
  59.9 37.0 %collective-permute-start.15 = (bf16[272,1536]{1,0:T(8,128)(2,1)S(1)}, bf16[272,1536]{1,0:T(8,128)(2,1)}, u32[]{:S(2)}, u32[]{:S(2)}) collective-permute-start(bf16[272,1536]{1,0:T(8,128)(2,1)S(1)} %fusion.1.refs_23_.refs_2_), channel_id=1, source_target_pairs={{0,6},{1,7},{2,0},{3,1},{4,2},{5,3},{6,4},{7,5},{8,14},{9,15},{10,... | collective-permute-start | bytes 2506760 | tf_op jit(solution)/shard_map/ppermute | solution.py:71
  92.2 17.9 %collective-permute-start.10 = (bf16[2,48,3840]{2,1,0:T(8,128)(2,1)}, bf16[2,48,3840]{2,1,0:T(8,128)(2,1)}, u32[]{:S(2)}, u32[]{:S(2)}) collective-permute-start(bf16[2,48,3840]{2,1,0:T(8,128)(2,1)} %slice.314), channel_id=1, source_target_pairs={{0,16},{8,24},{16,0},{24,8},{1,17},{9,25},{17,1},{25,9},{2,18},{10... | collective-permute-start | bytes 2211848 | tf_op jit(solution)/shard_map/ppermute | solution.py:59
  94.7 17.6 %collective-permute-start.9 = (bf16[2,48,3840]{2,1,0:T(8,128)(2,1)}, bf16[2,48,3840]{2,1,0:T(8,128)(2,1)}, u32[]{:S(2)}, u32[]{:S(2)}) collective-permute-start(bf16[2,48,3840]{2,1,0:T(8,128)(2,1)} %slice.313), channel_id=1, source_target_pairs={{0,8},{8,0},{16,24},{24,16},{1,9},{9,1},{17,25},{25,17},{2,10},{10... | collective-permute-start | bytes 2211848 | tf_op jit(solution)/shard_map/ppermute | solution.py:55
  95.4 28.7 %collective-permute-start.11 = (bf16[4,48,3840]{2,1,0:T(8,128)(2,1)}, bf16[4,48,3840]{2,1,0:T(8,128)(2,1)}, u32[]{:S(2)}, u32[]{:S(2)}) collective-permute-start(bf16[4,48,3840]{2,1,0:T(8,128)(2,1)} %pad_maximum_fusion.1.refs_6_), channel_id=1, source_target_pairs={{0,1},{1,0},{2,3},{3,2},{4,5},{5,4},{6,7},{7,6},{8,9},{9,8},{10,11... | collective-permute-start | bytes 4423688 | tf_op jit(solution)/shard_map/ppermute | solution.py:63
  95.4 31.3 %collective-permute-start.12 = (bf16[4,48,3840]{2,1,0:T(8,128)(2,1)}, bf16[4,48,3840]{2,1,0:T(8,128)(2,1)}, u32[]{:S(2)}, u32[]{:S(2)}) collective-permute-start(bf16[4,48,3840]{2,1,0:T(8,128)(2,1)} %collective-permute-done.7.refs_7_), channel_id=1, source_target_pairs={{0,1},{1,0},{2,3},{3,2},{4,5},{5,4},{6,7},{7,6},{8,9},{9,8},{10,11... | collective-permute-start | bytes 4423688 | tf_op jit(solution)/shard_map/ppermute | solution.py:63
  96.9 29.8 %collective-permute-start.13 = (bf16[4,48,3840]{2,1,0:T(8,128)(2,1)}, bf16[4,48,3840]{2,1,0:T(8,128)(2,1)}, u32[]{:S(2)}, u32[]{:S(2)}) collective-permute-start(bf16[4,48,3840]{2,1,0:T(8,128)(2,1)} %collective-permute-done.8.refs_8_), channel_id=1, source_target_pairs={{0,1},{1,0},{2,3},{3,2},{4,5},{5,4},{6,7},{7,6},{8,9},{9,8},{10,11... | collective-permute-start | bytes 4423688 | tf_op jit(solution)/shard_map/ppermute | solution.py:63
  98.4 24.7 %all-to-all-start = ((bf16[8,2,16,1536]{3,2,1,0:T(8,128)(2,1)}), bf16[8,2,16,1536]{3,2,1,0:T(8,128)(2,1)S(1)}, u32[]{:S(2)}, u32[]{:S(2)}) async-start(bf16[8,2,16,1536]{3,2,1,0:T(8,128)(2,1)} %bitcast.53), calls=%async_computation | async-start | bytes 1572864 | tf_op jit(solution)/shard_map/all_to_all | solution.py:987
  102.1 379.4 %reduce-scatter.2.cloned.1.call-start = ((), (), s32[]{:S(2)}) async-start(), calls=%async_computation.3 | async-start | bytes 17694720 | tf_op jit(solution)/shard_map/reduce_scatter | solution.py:1223
  112.4 11.7 %collective-permute-start.16 = (bf16[2,48,3840]{2,1,0:T(8,128)(2,1)}, bf16[2,48,3840]{2,1,0:T(8,128)(2,1)}, u32[]{:S(2)}, u32[]{:S(2)}) collective-permute-start(bf16[2,48,3840]{2,1,0:T(8,128)(2,1)} %collective-permute-done.9.refs_9_), channel_id=1, source_target_pairs={{0,1},{1,0},{2,3},{3,2},{4,5},{5,4},{6,7},{7,6},{8,9},{9,8},{10,11... | collective-permute-start | bytes 2211848 | tf_op jit(solution)/shard_map/ppermute | solution.py:63
  112.4 12.8 %collective-permute-start.17 = (bf16[2,48,3840]{2,1,0:T(8,128)(2,1)}, bf16[2,48,3840]{2,1,0:T(8,128)(2,1)}, u32[]{:S(2)}, u32[]{:S(2)}) collective-permute-start(bf16[2,48,3840]{2,1,0:T(8,128)(2,1)} %collective-permute-done.10.refs_10_), channel_id=1, source_target_pairs={{0,1},{1,0},{2,3},{3,2},{4,5},{5,4},{6,7},{7,6},{8,9},{9,8},{10,11... | collective-permute-start | bytes 2211848 | tf_op jit(solution)/shard_map/ppermute | solution.py:63
  124.0 22.6 %collective-permute-start.29 = (bf16[272,1536]{1,0:T(8,128)(2,1)}, bf16[272,1536]{1,0:T(8,128)(2,1)}, u32[]{:S(2)}, u32[]{:S(2)}) collective-permute-start(bf16[272,1536]{1,0:T(8,128)(2,1)} %copy-done.26), channel_id=1, source_target_pairs={{0,2},{1,3},{2,4},{3,5},{4,6},{5,7},{6,0},{7,1},{8,10},{9,11},{10,... | collective-permute-start | bytes 2506760 | tf_op jit(solution)/shard_map/ppermute | solution.py:67
  124.0 55.9 %collective-permute-start.20 = (bf16[2,2,384,768]{3,2,1,0:T(8,128)(2,1)S(1)}, bf16[2,2,384,768]{3,2,1,0:T(8,128)(2,1)S(1)}, u32[]{:S(2)}, u32[]{:S(2)}) collective-permute-start(bf16[2,2,384,768]{3,2,1,0:T(8,128)(2,1)S(1)} %copy-done.4), channel_id=1, source_target_pairs={{0,8},{8,0},{16,24},{24,16},{1,9},{9,1},{17,25},{25,17},{2,10},{10... | collective-permute-start | bytes 7077896 | tf_op jit(solution)/shard_map/ppermute | solution.py:55
  125.1 55.3 %collective-permute-start.21 = (bf16[2,2,384,768]{3,2,1,0:T(8,128)(2,1)S(1)}, bf16[2,2,384,768]{3,2,1,0:T(8,128)(2,1)}, u32[]{:S(2)}, u32[]{:S(2)}) collective-permute-start(bf16[2,2,384,768]{3,2,1,0:T(8,128)(2,1)S(1)} %copy-done.4), channel_id=1, source_target_pairs={{0,16},{8,24},{16,0},{24,8},{1,17},{9,25},{17,1},{25,9},{2,18},{10... | collective-permute-start | bytes 7077896 | tf_op jit(solution)/shard_map/ppermute | solution.py:59
  142.8 22.7 %collective-permute-start.18 = (bf16[256,1536]{1,0:T(8,128)(2,1)}, bf16[256,1536]{1,0:T(8,128)(2,1)}, u32[]{:S(2)}, u32[]{:S(2)}) collective-permute-start(bf16[256,1536]{1,0:T(8,128)(2,1)} %get-tuple-element.134.refs_15_.refs_14_), channel_id=1, source_target_pairs={{0,2},{1,3},{2,4},{3,5},{4,6},{5,7},{6,0},{7,1},{8,10},{9,11},{10,... | collective-permute-start | bytes 2359304 | tf_op jit(solution)/shard_map/ppermute | solution.py:67
  143.0 37.0 %collective-permute-start.19 = (bf16[256,1536]{1,0:T(8,128)(2,1)}, bf16[256,1536]{1,0:T(8,128)(2,1)}, u32[]{:S(2)}, u32[]{:S(2)}) collective-permute-start(bf16[256,1536]{1,0:T(8,128)(2,1)} %get-tuple-element.134.refs_15_.refs_14_), channel_id=1, source_target_pairs={{0,6},{1,7},{2,0},{3,1},{4,2},{5,3},{6,4},{7,5},{8,14},{9,15},{10,... | collective-permute-start | bytes 2359304 | tf_op jit(solution)/shard_map/ppermute | solution.py:71
  146.6 33.9 %collective-permute-start.30 = (bf16[272,1536]{1,0:T(8,128)(2,1)S(1)}, bf16[272,1536]{1,0:T(8,128)(2,1)S(1)}, u32[]{:S(2)}, u32[]{:S(2)}) collective-permute-start(bf16[272,1536]{1,0:T(8,128)(2,1)S(1)} %copy-done.12), channel_id=1, source_target_pairs={{0,1},{1,0},{2,3},{3,2},{4,5},{5,4},{6,7},{7,6},{8,9},{9,8},{10,11... | collective-permute-start | bytes 2506760 | tf_op jit(solution)/shard_map/ppermute | solution.py:63
  165.4 18.7 %collective-permute-start.31 = (bf16[272,1536]{1,0:T(8,128)(2,1)S(1)}, bf16[272,1536]{1,0:T(8,128)(2,1)S(1)}, u32[]{:S(2)}, u32[]{:S(2)}) collective-permute-start(bf16[272,1536]{1,0:T(8,128)(2,1)S(1)} %copy-done.27), channel_id=1, source_target_pairs={{0,1},{1,0},{2,3},{3,2},{4,5},{5,4},{6,7},{7,6},{8,9},{9,8},{10,11... | collective-permute-start | bytes 2506760 | tf_op jit(solution)/shard_map/ppermute | solution.py:63
  180.5 6.9 %collective-permute-start.25 = (bf16[256,1536]{1,0:T(8,128)(2,1)}, bf16[256,1536]{1,0:T(8,128)(2,1)S(1)}, u32[]{:S(2)}, u32[]{:S(2)}) collective-permute-start(bf16[256,1536]{1,0:T(8,128)(2,1)} %get-tuple-element.134.refs_15_.refs_14_), channel_id=1, source_target_pairs={{0,1},{1,0},{2,3},{3,2},{4,5},{5,4},{6,7},{7,6},{8,9},{9,8},{10,11... | collective-permute-start | bytes 2359304 | tf_op jit(solution)/shard_map/ppermute | solution.py:63
  181.7 22.2 %collective-permute-start.24 = (bf16[256,1536]{1,0:T(8,128)(2,1)}, bf16[256,1536]{1,0:T(8,128)(2,1)}, u32[]{:S(2)}, u32[]{:S(2)}) collective-permute-start(bf16[256,1536]{1,0:T(8,128)(2,1)} %collective-permute-done.18.refs_16_), channel_id=1, source_target_pairs={{0,2},{1,3},{2,4},{3,5},{4,6},{5,7},{6,0},{7,1},{8,10},{9,11},{10,... | collective-permute-start | bytes 2359304 | tf_op jit(solution)/shard_map/ppermute | solution.py:67
  184.2 28.3 %collective-permute-start.22 = (bf16[2,384,768]{2,1,0:T(8,128)(2,1)S(1)}, bf16[2,384,768]{2,1,0:T(8,128)(2,1)}, u32[]{:S(2)}, u32[]{:S(2)}) collective-permute-start(bf16[2,384,768]{2,1,0:T(8,128)(2,1)S(1)} %slice_bitcast_fusion.1), channel_id=1, source_target_pairs={{0,8},{8,0},{16,24},{24,16},{1,9},{9,1},{17,25},{25,17},{2,10},{10... | collective-permute-start | bytes 3538952 | tf_op jit(solution)/shard_map/ppermute | solution.py:55
  185.0 27.9 %collective-permute-start.23 = (bf16[2,384,768]{2,1,0:T(8,128)(2,1)S(1)}, bf16[2,384,768]{2,1,0:T(8,128)(2,1)}, u32[]{:S(2)}, u32[]{:S(2)}) collective-permute-start(bf16[2,384,768]{2,1,0:T(8,128)(2,1)S(1)} %slice_bitcast_fusion), channel_id=1, source_target_pairs={{0,16},{8,24},{16,0},{24,8},{1,17},{9,25},{17,1},{25,9},{2,18},{10... | collective-permute-start | bytes 3538952 | tf_op jit(solution)/shard_map/ppermute | solution.py:59
  186.5 20.6 %collective-permute-start.26 = (bf16[256,1536]{1,0:T(8,128)(2,1)}, bf16[256,1536]{1,0:T(8,128)(2,1)}, u32[]{:S(2)}, u32[]{:S(2)}) collective-permute-start(bf16[256,1536]{1,0:T(8,128)(2,1)} %collective-permute-done.18.refs_16_), channel_id=1, source_target_pairs={{0,1},{1,0},{2,3},{3,2},{4,5},{5,4},{6,7},{7,6},{8,9},{9,8},{10,11... | collective-permute-start | bytes 2359304 | tf_op jit(solution)/shard_map/ppermute | solution.py:63
  187.4 19.7 %collective-permute-start.27 = (bf16[256,1536]{1,0:T(8,128)(2,1)}, bf16[256,1536]{1,0:T(8,128)(2,1)}, u32[]{:S(2)}, u32[]{:S(2)}) collective-permute-start(bf16[256,1536]{1,0:T(8,128)(2,1)} %collective-permute-done.19.refs_17_), channel_id=1, source_target_pairs={{0,1},{1,0},{2,3},{3,2},{4,5},{5,4},{6,7},{7,6},{8,9},{9,8},{10,11... | collective-permute-start | bytes 2359304 | tf_op jit(solution)/shard_map/ppermute | solution.py:63
  203.9 9.0 %collective-permute-start.28 = (bf16[256,1536]{1,0:T(8,128)(2,1)}, bf16[256,1536]{1,0:T(8,128)(2,1)}, u32[]{:S(2)}, u32[]{:S(2)}) collective-permute-start(bf16[256,1536]{1,0:T(8,128)(2,1)} %collective-permute-done.24.refs_18_), channel_id=1, source_target_pairs={{0,1},{1,0},{2,3},{3,2},{4,5},{5,4},{6,7},{7,6},{8,9},{9,8},{10,11... | collective-permute-start | bytes 2359304 | tf_op jit(solution)/shard_map/ppermute | solution.py:63
  271.2 46.8 %collective-permute-start.36 = (bf16[4,256,1536]{2,1,0:T(8,128)(2,1)}, bf16[4,256,1536]{2,1,0:T(8,128)(2,1)}, u32[]{:S(2)}, u32[]{:S(2)}) collective-permute-start(bf16[4,256,1536]{2,1,0:T(8,128)(2,1)} %get-tuple-element.144), channel_id=1, source_target_pairs={{0,1},{1,0},{2,3},{3,2},{4,5},{5,4},{6,7},{7,6},{8,9},{9,8},{10,11... | collective-permute-start | bytes 9437192 | tf_op jit(solution)/shard_map/ppermute | solution.py:63
  275.6 42.4 %collective-permute-start.35 = (bf16[272,1536]{1,0:T(8,128)(2,1)S(1)}, bf16[272,1536]{1,0:T(8,128)(2,1)}, u32[]{:S(2)}, u32[]{:S(2)}) collective-permute-start(bf16[272,1536]{1,0:T(8,128)(2,1)S(1)} %get-tuple-element.281), channel_id=1, source_target_pairs={{0,6},{1,7},{2,0},{3,1},{4,2},{5,3},{6,4},{7,5},{8,14},{9,15},{10,... | collective-permute-start | bytes 2506760 | tf_op jit(solution)/shard_map/ppermute | solution.py:71
  278.9 37.0 %collective-permute-start.37 = (bf16[272,1536]{1,0:T(8,128)(2,1)}, bf16[272,1536]{1,0:T(8,128)(2,1)S(1)}, u32[]{:S(2)}, u32[]{:S(2)}) collective-permute-start(bf16[272,1536]{1,0:T(8,128)(2,1)} %get-tuple-element.279), channel_id=1, source_target_pairs={{0,2},{1,3},{2,4},{3,5},{4,6},{5,7},{6,0},{7,1},{8,10},{9,11},{10,... | collective-permute-start | bytes 2506760 | tf_op jit(solution)/shard_map/ppermute | solution.py:67
  316.1 22.1 %collective-permute-start.38 = (bf16[272,1536]{1,0:T(8,128)(2,1)S(1)}, bf16[272,1536]{1,0:T(8,128)(2,1)S(1)}, u32[]{:S(2)}, u32[]{:S(2)}) collective-permute-start(bf16[272,1536]{1,0:T(8,128)(2,1)S(1)} %add_convert_fusion.2), channel_id=1, source_target_pairs={{0,2},{1,3},{2,4},{3,5},{4,6},{5,7},{6,0},{7,1},{8,10},{9,11},{10,... | collective-permute-start | bytes 2506760 | tf_op jit(solution)/shard_map/ppermute | solution.py:67
  338.3 30.0 %collective-permute-start.40 = (bf16[256,1536]{1,0:T(8,128)(2,1)}, bf16[256,1536]{1,0:T(8,128)(2,1)}, u32[]{:S(2)}, u32[]{:S(2)}) collective-permute-start(bf16[256,1536]{1,0:T(8,128)(2,1)} %get-tuple-element.164), channel_id=1, source_target_pairs={{0,2},{1,3},{2,4},{3,5},{4,6},{5,7},{6,0},{7,1},{8,10},{9,11},{10,... | collective-permute-start | bytes 2359304 | tf_op jit(solution)/shard_map/ppermute | solution.py:67
  371.1 9.3 %collective-permute-start.47 = (bf16[2,2,48,1664]{3,2,1,0:T(8,128)(2,1)}, bf16[2,2,48,1664]{3,2,1,0:T(8,128)(2,1)S(1)}, u32[]{:S(2)}, u32[]{:S(2)}) collective-permute-start(bf16[2,2,48,1664]{3,2,1,0:T(8,128)(2,1)} %get-tuple-element.195), channel_id=1, source_target_pairs={{0,1},{1,0},{2,3},{3,2},{4,5},{5,4},{6,7},{7,6},{8,9},{9,8},{10,11... | collective-permute-start | bytes 1916936 | tf_op jit(solution)/shard_map/ppermute | solution.py:63
  371.2 6.7 %collective-permute-start.43 = (bf16[2,2,48,2176]{3,2,1,0:T(8,128)(2,1)S(1)}, bf16[2,2,48,2176]{3,2,1,0:T(8,128)(2,1)S(1)}, u32[]{:S(2)}, u32[]{:S(2)}) collective-permute-start(bf16[2,2,48,2176]{3,2,1,0:T(8,128)(2,1)S(1)} %copy-done.32), channel_id=1, source_target_pairs={{0,1},{1,0},{2,3},{3,2},{4,5},{5,4},{6,7},{7,6},{8,9},{9,8},{10,11... | collective-permute-start | bytes 2506760 | tf_op jit(solution)/shard_map/ppermute | solution.py:63
  371.7 16.5 %collective-permute-start.56 = (bf16[2,48,2176]{2,1,0:T(8,128)(2,1)}, bf16[2,48,2176]{2,1,0:T(8,128)(2,1)}, u32[]{:S(2)}, u32[]{:S(2)}) collective-permute-start(bf16[2,48,2176]{2,1,0:T(8,128)(2,1)} %get-tuple-element.210), channel_id=1, source_target_pairs={{0,1},{1,0},{2,3},{3,2},{4,5},{5,4},{6,7},{7,6},{8,9},{9,8},{10,11... | collective-permute-start | bytes 1253384 | tf_op jit(solution)/shard_map/ppermute | solution.py:63
  373.8 34.6 %collective-permute-start.45 = (bf16[2,48,2176]{2,1,0:T(8,128)(2,1)}, bf16[2,48,2176]{2,1,0:T(8,128)(2,1)}, u32[]{:S(2)}, u32[]{:S(2)}) collective-permute-start(bf16[2,48,2176]{2,1,0:T(8,128)(2,1)} %get-tuple-element.190), channel_id=1, source_target_pairs={{0,1},{1,0},{2,3},{3,2},{4,5},{5,4},{6,7},{7,6},{8,9},{9,8},{10,11... | collective-permute-start | bytes 1253384 | tf_op jit(solution)/shard_map/ppermute | solution.py:63
  374.9 41.2 %collective-permute-start.42 = (bf16[4,48,2176]{2,1,0:T(8,128)(2,1)}, bf16[4,48,2176]{2,1,0:T(8,128)(2,1)S(1)}, u32[]{:S(2)}, u32[]{:S(2)}) collective-permute-start(bf16[4,48,2176]{2,1,0:T(8,128)(2,1)} %get-tuple-element.186), channel_id=1, source_target_pairs={{0,1},{1,0},{2,3},{3,2},{4,5},{5,4},{6,7},{7,6},{8,9},{9,8},{10,11... | collective-permute-start | bytes 2506760 | tf_op jit(solution)/shard_map/ppermute | solution.py:63
  377.8 27.0 %collective-permute-start.51 = (bf16[2,2,48,2176]{3,2,1,0:T(8,128)(2,1)}, bf16[2,2,48,2176]{3,2,1,0:T(8,128)(2,1)S(1)}, u32[]{:S(2)}, u32[]{:S(2)}) collective-permute-start(bf16[2,2,48,2176]{3,2,1,0:T(8,128)(2,1)} %add_convert_fusion), channel_id=1, source_target_pairs={{0,16},{8,24},{16,0},{24,8},{1,17},{9,25},{17,1},{25,9},{2,18},{10... | collective-permute-start | bytes 2506760 | tf_op jit(solution)/shard_map/ppermute | solution.py:59
  380.4 28.0 %collective-permute-start.44 = (bf16[2,2,48,2176]{3,2,1,0:T(8,128)(2,1)}, bf16[2,2,48,2176]{3,2,1,0:T(8,128)(2,1)S(1)}, u32[]{:S(2)}, u32[]{:S(2)}) collective-permute-start(bf16[2,2,48,2176]{3,2,1,0:T(8,128)(2,1)} %add_convert_fusion.1), channel_id=1, source_target_pairs={{0,8},{8,0},{16,24},{24,16},{1,9},{9,1},{17,25},{25,17},{2,10},{10... | collective-permute-start | bytes 2506760 | tf_op jit(solution)/shard_map/ppermute | solution.py:55
  383.6 30.9 %all-to-all-start.1 = ((bf16[1,2,128,1536]{3,1,0,2:T(2,128)(2,1)}), bf16[1,2,128,1536]{3,1,0,2:T(2,128)(2,1)S(1)}, u32[]{:S(2)}, u32[]{:S(2)}) async-start(bf16[1,2,128,1536]{3,1,0,2:T(2,128)(2,1)} %copy.79), calls=%async_computation.1 | async-start | bytes 1572864 | tf_op jit(solution)/shard_map/all_to_all | solution.py:1085
  406.8 21.2 %collective-permute-start.57 = (bf16[2,48,2176]{2,1,0:T(8,128)(2,1)}, bf16[2,48,2176]{2,1,0:T(8,128)(2,1)}, u32[]{:S(2)}, u32[]{:S(2)}) collective-permute-start(bf16[2,48,2176]{2,1,0:T(8,128)(2,1)} %fusion.5), channel_id=1, source_target_pairs={{0,8},{8,0},{16,24},{24,16},{1,9},{9,1},{17,25},{25,17},{2,10},{10... | collective-permute-start | bytes 1253384 | tf_op jit(solution)/shard_map/ppermute | solution.py:55
  410.6 21.1 %collective-permute-start.46 = (bf16[2,48,2176]{2,1,0:T(8,128)(2,1)}, bf16[2,48,2176]{2,1,0:T(8,128)(2,1)}, u32[]{:S(2)}, u32[]{:S(2)}) collective-permute-start(bf16[2,48,2176]{2,1,0:T(8,128)(2,1)} %fusion.6), channel_id=1, source_target_pairs={{0,16},{8,24},{16,0},{24,8},{1,17},{9,25},{17,1},{25,9},{2,18},{10... | collective-permute-start | bytes 1253384 | tf_op jit(solution)/shard_map/ppermute | solution.py:59
  411.2 22.7 %collective-permute-start.39 = (bf16[256,1536]{1,0:T(8,128)(2,1)}, bf16[256,1536]{1,0:T(8,128)(2,1)}, u32[]{:S(2)}, u32[]{:S(2)}) collective-permute-start(bf16[256,1536]{1,0:T(8,128)(2,1)} %get-tuple-element.152), channel_id=1, source_target_pairs={{0,6},{1,7},{2,0},{3,1},{4,2},{5,3},{6,4},{7,5},{8,14},{9,15},{10,... | collective-permute-start | bytes 2359304 | tf_op jit(solution)/shard_map/ppermute | solution.py:71
  414.5 33.9 %collective-permute-start.41 = (bf16[256,1536]{1,0:T(8,128)(2,1)}, bf16[256,1536]{1,0:T(8,128)(2,1)}, u32[]{:S(2)}, u32[]{:S(2)}) collective-permute-start(bf16[256,1536]{1,0:T(8,128)(2,1)} %add_convert_fusion.7), channel_id=1, source_target_pairs={{0,2},{1,3},{2,4},{3,5},{4,6},{5,7},{6,0},{7,1},{8,10},{9,11},{10,... | collective-permute-start | bytes 2359304 | tf_op jit(solution)/shard_map/ppermute | solution.py:67
  416.2 35.4 %collective-permute-start.61 = (bf16[2,48,1664]{2,1,0:T(8,128)(2,1)}, bf16[2,48,1664]{2,1,0:T(8,128)(2,1)S(1)}, u32[]{:S(2)}, u32[]{:S(2)}) collective-permute-start(bf16[2,48,1664]{2,1,0:T(8,128)(2,1)} %get-tuple-element.213), channel_id=1, source_target_pairs={{0,1},{1,0},{2,3},{3,2},{4,5},{5,4},{6,7},{7,6},{8,9},{9,8},{10,11... | collective-permute-start | bytes 958472 | tf_op jit(solution)/shard_map/ppermute | solution.py:63
  428.1 33.8 %collective-permute-start.53 = (bf16[2,48,1664]{2,1,0:T(8,128)(2,1)}, bf16[2,48,1664]{2,1,0:T(8,128)(2,1)S(1)}, u32[]{:S(2)}, u32[]{:S(2)}) collective-permute-start(bf16[2,48,1664]{2,1,0:T(8,128)(2,1)} %get-tuple-element.207), channel_id=1, source_target_pairs={{0,1},{1,0},{2,3},{3,2},{4,5},{5,4},{6,7},{7,6},{8,9},{9,8},{10,11... | collective-permute-start | bytes 958472 | tf_op jit(solution)/shard_map/ppermute | solution.py:63
  431.7 28.5 %collective-permute-start.62 = (bf16[2,2,48,1664]{3,2,1,0:T(8,128)(2,1)}, bf16[2,2,48,1664]{3,2,1,0:T(8,128)(2,1)S(1)}, u32[]{:S(2)}, u32[]{:S(2)}) collective-permute-start(bf16[2,2,48,1664]{3,2,1,0:T(8,128)(2,1)} %add_convert_fusion.11), channel_id=1, source_target_pairs={{0,16},{8,24},{16,0},{24,8},{1,17},{9,25},{17,1},{25,9},{2,18},{10... | collective-permute-start | bytes 1916936 | tf_op jit(solution)/shard_map/ppermute | solution.py:59
  433.9 35.5 %collective-permute-start.49 = (bf16[4,48,1664]{2,1,0:T(8,128)(2,1)S(1)}, bf16[4,48,1664]{2,1,0:T(8,128)(2,1)S(1)}, u32[]{:S(2)}, u32[]{:S(2)}) collective-permute-start(bf16[4,48,1664]{2,1,0:T(8,128)(2,1)S(1)} %copy-done.36), channel_id=1, source_target_pairs={{0,1},{1,0},{2,3},{3,2},{4,5},{5,4},{6,7},{7,6},{8,9},{9,8},{10,11... | collective-permute-start | bytes 1916936 | tf_op jit(solution)/shard_map/ppermute | solution.py:63
  448.4 15.0 %collective-permute-start.52 = (bf16[2,2,48,1664]{3,2,1,0:T(8,128)(2,1)S(1)}, bf16[2,2,48,1664]{3,2,1,0:T(8,128)(2,1)S(1)}, u32[]{:S(2)}, u32[]{:S(2)}) collective-permute-start(bf16[2,2,48,1664]{3,2,1,0:T(8,128)(2,1)S(1)} %copy-done.16), channel_id=1, source_target_pairs={{0,8},{8,0},{16,24},{24,16},{1,9},{9,1},{17,25},{25,17},{2,10},{10... | collective-permute-start | bytes 1916936 | tf_op jit(solution)/shard_map/ppermute | solution.py:55
  451.6 23.9 %collective-permute-start.55 = (bf16[48,2176]{1,0:T(8,128)(2,1)S(1)}, bf16[48,2176]{1,0:T(8,128)(2,1)S(1)}, u32[]{:S(2)}, u32[]{:S(2)}) collective-permute-start(bf16[48,2176]{1,0:T(8,128)(2,1)S(1)} %get-tuple-element.291), channel_id=1, source_target_pairs={{0,6},{1,7},{2,0},{3,1},{4,2},{5,3},{6,4},{7,5},{8,14},{9,15},{10,... | collective-permute-start | bytes 626696 | tf_op jit(solution)/shard_map/ppermute | solution.py:71
  460.3 8.0 %collective-permute-start.58 = (bf16[48,2176]{1,0:T(8,128)(2,1)S(1)}, bf16[48,2176]{1,0:T(8,128)(2,1)S(1)}, u32[]{:S(2)}, u32[]{:S(2)}) collective-permute-start(bf16[48,2176]{1,0:T(8,128)(2,1)S(1)} %get-tuple-element.296), channel_id=1, source_target_pairs={{0,2},{1,3},{2,4},{3,5},{4,6},{5,7},{6,0},{7,1},{8,10},{9,11},{10,... | collective-permute-start | bytes 626696 | tf_op jit(solution)/shard_map/ppermute | solution.py:67
  461.9 8.4 %collective-permute-start.63 = (bf16[2,48,1664]{2,1,0:T(8,128)(2,1)S(1)}, bf16[2,48,1664]{2,1,0:T(8,128)(2,1)S(1)}, u32[]{:S(2)}, u32[]{:S(2)}) collective-permute-start(bf16[2,48,1664]{2,1,0:T(8,128)(2,1)S(1)} %fusion.10), channel_id=1, source_target_pairs={{0,8},{8,0},{16,24},{24,16},{1,9},{9,1},{17,25},{25,17},{2,10},{10... | collective-permute-start | bytes 958472 | tf_op jit(solution)/shard_map/ppermute | solution.py:55
  463.6 7.2 %collective-permute-start.54 = (bf16[2,48,1664]{2,1,0:T(8,128)(2,1)S(1)}, bf16[2,48,1664]{2,1,0:T(8,128)(2,1)S(1)}, u32[]{:S(2)}, u32[]{:S(2)}) collective-permute-start(bf16[2,48,1664]{2,1,0:T(8,128)(2,1)S(1)} %fusion.11), channel_id=1, source_target_pairs={{0,16},{8,24},{16,0},{24,8},{1,17},{9,25},{17,1},{25,9},{2,18},{10... | collective-permute-start | bytes 958472 | tf_op jit(solution)/shard_map/ppermute | solution.py:59
  469.3 10.1 %collective-permute-start.59 = (bf16[48,2176]{1,0:T(8,128)(2,1)S(1)}, bf16[48,2176]{1,0:T(8,128)(2,1)S(1)}, u32[]{:S(2)}, u32[]{:S(2)}) collective-permute-start(bf16[48,2176]{1,0:T(8,128)(2,1)S(1)} %add_convert_fusion.17), channel_id=1, source_target_pairs={{0,2},{1,3},{2,4},{3,5},{4,6},{5,7},{6,0},{7,1},{8,10},{9,11},{10,... | collective-permute-start | bytes 626696 | tf_op jit(solution)/shard_map/ppermute | solution.py:67
  471.1 18.3 %collective-permute-start.60 = (bf16[48,1664]{1,0:T(8,128)(2,1)S(1)}, bf16[48,1664]{1,0:T(8,128)(2,1)S(1)}, u32[]{:S(2)}, u32[]{:S(2)}) collective-permute-start(bf16[48,1664]{1,0:T(8,128)(2,1)S(1)} %get-tuple-element.293), channel_id=1, source_target_pairs={{0,6},{1,7},{2,0},{3,1},{4,2},{5,3},{6,4},{7,5},{8,14},{9,15},{10,... | collective-permute-start | bytes 479240 | tf_op jit(solution)/shard_map/ppermute | solution.py:71
  473.6 15.8 %collective-permute-start.64 = (bf16[48,1664]{1,0:T(8,128)(2,1)S(1)}, bf16[48,1664]{1,0:T(8,128)(2,1)S(1)}, u32[]{:S(2)}, u32[]{:S(2)}) collective-permute-start(bf16[48,1664]{1,0:T(8,128)(2,1)S(1)} %get-tuple-element.298), channel_id=1, source_target_pairs={{0,2},{1,3},{2,4},{3,5},{4,6},{5,7},{6,0},{7,1},{8,10},{9,11},{10,... | collective-permute-start | bytes 479240 | tf_op jit(solution)/shard_map/ppermute | solution.py:67
  473.6 16.5 %collective-permute-start.65 = (bf16[48,1664]{1,0:T(8,128)(2,1)S(1)}, bf16[48,1664]{1,0:T(8,128)(2,1)S(1)}, u32[]{:S(2)}, u32[]{:S(2)}) collective-permute-start(bf16[48,1664]{1,0:T(8,128)(2,1)S(1)} %get-tuple-element.297), channel_id=1, source_target_pairs={{0,4},{1,5},{2,6},{3,7},{4,0},{5,1},{6,2},{7,3},{8,12},{9,13},{10,... | collective-permute-start | bytes 479240 | tf_op jit(solution)/shard_map/ppermute | solution.py:963
  (46 other events, 640.7 us)
Sparse Core Ops, SparseCore 0:
  296.9 164.3 reduce-scatter.1

commit v4 on v3

--- a/solution.py
+++ b/solution.py
@@ -198,6 +198,7 @@
         act_s,
         slope_s,
         codes_all,
+        code_lines,
         code_s,
         gates_s,
         sgate_s,
@@ -218,6 +219,7 @@
     tokens = h_buf.shape[1] // 2
     slots = 2 * capacity
     experts = router_ref.shape[0]
+    rows_all = x_s.shape[1]
     my_first = my_ref[0] * per_device
     dtype = jnp.bfloat16
 
@@ -283,11 +285,14 @@
             copy.start()
         return copies + [pltpu.make_async_copy(d_buf.at[slot], d_buf.at[slot], sem_d.at[slot])]
 
-    row = lax.broadcasted_iota(jnp.int32, (slots, 2 * tokens), 0)
-    col = lax.broadcasted_iota(jnp.int32, (slots, 2 * tokens), 1)
-    second = row >= capacity
-    same = jnp.logical_xor(second, col < tokens)
-    target = (row - jnp.where(second, capacity, 0) + 1).astype(jnp.float32)
+    def hits(codes_of, shape, slot_axis):
+        slot = lax.broadcasted_iota(jnp.int32, shape, slot_axis)
+        token = lax.broadcasted_iota(jnp.int32, shape, 1 - slot_axis)
+        second = slot >= capacity
+        same = jnp.logical_xor(second, token < tokens)
+        rank = slot - jnp.where(second, capacity, 0)
+        return jnp.logical_and(same, codes_of == (rank + 1).astype(jnp.float32))
+
     flying = fetch(0)
     pltpu.make_async_copy(codes_all, codes_all, sem_c).wait()
     for p in range(pairs):
@@ -304,17 +309,27 @@
         raised = jnp.where(chosen, jnp.exp(logits - top), 0.0)
         code_s[...] = codes
         gates_s[...] = raised / jnp.sum(raised, axis=0, keepdims=True)
+        flipped = codes.T
+        lane = lax.broadcasted_iota(jnp.int32, flipped.shape, 1)
+        picks, ones = [], []
         for e in range(per_device):
             code_row = code_s[pl.ds(my_first + e, 1), :]
             gate_row = gates_s[pl.ds(my_first + e, 1), :]
-            hit = jnp.logical_and(same, code_row == target)
-            one = jnp.where(hit, 1.0, 0.0).astype(dtype)
-            hot[e, p] = one
+            hit = hits(code_row, (slots, 2 * tokens), 0)
+            code_lines[e, p] = code_row
+            picks.append(jnp.where(hit, 1.0, 0.0).astype(dtype))
             gate_slot = jnp.sum(jnp.where(hit, gate_row, 0.0), axis=1, keepdims=True)
-            rows = pl.ds(p * slots, slots)
-            sgate_s[e, rows, :] = jnp.broadcast_to(gate_slot, (slots, 128))
-            x_s[e, rows, :] = dot_nn(one, h_buf[slot]).astype(dtype)
-            dy_s[e, rows, :] = dot_nn(one, d_buf[slot]).astype(dtype)
+            sgate_s[e, pl.ds(p * slots, slots), :] = jnp.broadcast_to(gate_slot, (slots, 128))
+            code_col = jnp.sum(
+                jnp.where(lane == my_first + e, flipped, 0.0), axis=1, keepdims=True
+            )
+            ones.append(jnp.where(hits(code_col, (2 * tokens, slots), 1), 1.0, 0.0).astype(dtype))
+        pick = jnp.concatenate(picks, axis=0)
+        hot[p] = jnp.concatenate(ones, axis=1)
+        for hold, buf in ((x_s, h_buf), (dy_s, d_buf)):
+            taken = dot_nn(pick, buf[slot]).astype(dtype)
+            for e in range(per_device):
+                hold[e, pl.ds(p * slots, slots), :] = taken[e * slots : (e + 1) * slots]
 
     saves = []
     for e in range(per_device):
@@ -325,20 +340,23 @@
         saves.append(save)
         gate_slot = sgate_s[e][:, :1]
 
-        @pl.loop(0, ff // 256)
+        act_s[...] = dot_nn(x_s[e], gate_w[e])
+        slope_s[...] = dot_nn(x_s[e], up_w[e])
+
+        @pl.loop(0, rows_all // slots)
         def _(j):
-            cols = pl.ds(pl.multiple_of(j * 256, 256), 256)
-            ga = dot_nn(x_s[e], gate_w[e, :, cols])
-            ua = dot_nn(x_s[e], up_w[e, :, cols])
+            rows = pl.ds(pl.multiple_of(j * slots, slots), slots)
+            ga = act_s[rows, :]
+            ua = slope_s[rows, :]
             square = ga * ga
             tan = jnp.tanh(GELU_SCALE * (ga + GELU_CUBE * square * ga))
             act = 0.5 * ga * (1.0 + tan)
             slope = 0.5 * (1.0 + tan) + 0.5 * ga * (1.0 - tan * tan) * GELU_SCALE * (
                 1.0 + 3.0 * GELU_CUBE * square
             )
-            act_s[:, cols] = act
-            slope_s[:, cols] = ua * slope
-            hid_s[e, :, cols] = (act * ua).astype(dtype)
+            act_s[rows, :] = act
+            slope_s[rows, :] = ua * slope
+            hid_s[e, rows, :] = (act * ua).astype(dtype)
 
         save = pltpu.make_async_copy(hid_s.at[e], hid_out.at[e], sem_s.at[1, e])
         save.start()
@@ -347,9 +365,9 @@
             copy.wait()
         dg_s[e] = jnp.zeros(dg_s.shape[1:], jnp.float32)
 
-        @pl.loop(0, width // 256)
+        @pl.loop(0, width // 768)
         def _(j):
-            cols = pl.ds(pl.multiple_of(j * 256, 256), 256)
+            cols = pl.ds(pl.multiple_of(j * 768, 768), 768)
             y = dot_nn(hid_s[e], down_w[e, :, cols]).astype(dtype).astype(jnp.float32)
             dy = dy_s[e, :, cols].astype(jnp.float32)
             dg_s[e] += jnp.broadcast_to(
@@ -362,21 +380,18 @@
         save.start()
         saves.append(save)
 
-        @pl.loop(0, ff // 256)
-        def _(j):
-            cols = pl.ds(pl.multiple_of(j * 256, 256), 256)
-            dhid = dot_nt(dy_s[e], down_w[e, cols, :])
-            dga_s[e, :, cols] = (dhid * slope_s[:, cols]).astype(dtype)
-            dua_s[e, :, cols] = (dhid * act_s[:, cols]).astype(dtype)
+        dhid = dot_nt(dy_s[e], down_w[e])
+        dga_s[e] = (dhid * slope_s[...]).astype(dtype)
+        dua_s[e] = (dhid * act_s[...]).astype(dtype)
 
         for k, (hold, out) in enumerate(((dga_s, dga_out), (dua_s, dua_out))):
             save = pltpu.make_async_copy(hold.at[e], out.at[e], sem_s.at[3 + k, e])
             save.start()
             saves.append(save)
 
-        @pl.loop(0, width // 256)
+        @pl.loop(0, width // 768)
         def _(j):
-            cols = pl.ds(pl.multiple_of(j * 256, 256), 256)
+            cols = pl.ds(pl.multiple_of(j * 768, 768), 768)
             dx = dot_nt(dga_s[e], gate_w[e, cols, :]) + dot_nt(dua_s[e], up_w[e, cols, :])
             dx_s[e, :, cols] = dx.astype(dtype)
 
@@ -389,14 +404,16 @@
             copy.wait()
         rows = pl.ds(p * slots, slots)
 
-        @pl.loop(0, width // 512)
+        @pl.loop(0, width // 768)
         def _(j):
-            cols = pl.ds(pl.multiple_of(j * 512, 512), 512)
-            back = jnp.zeros((2 * tokens, 512), jnp.float32)
-            outs = jnp.zeros((2 * tokens, 512), jnp.float32)
-            for e in range(per_device):
-                back += dot_tn(hot[e, p], dx_s[e, rows, cols])
-                outs += dot_tn(hot[e, p], y_s[e, rows, cols])
+            cols = pl.ds(pl.multiple_of(j * 768, 768), 768)
+            back, outs = [
+                dot_nn(
+                    hot[p],
+                    jnp.concatenate([hold[e, rows, cols] for e in range(per_device)], axis=0),
+                )
+                for hold in (dx_s, y_s)
+            ]
             for half in range(2):
                 part = slice(half * tokens, (half + 1) * tokens)
                 stage_b[slot, half, :tokens, cols] = back[part].astype(dtype)
@@ -408,7 +425,10 @@
         tables = [jnp.zeros((table_rows, 2 * tokens), jnp.float32) for _ in range(2)]
         for e in range(per_device):
             dg = dg_s[e, rows, :][:, :1]
-            line = jnp.sum(hot[e, p].astype(jnp.float32) * dg, axis=0, keepdims=True)
+            code_row = code_lines[e, p]
+            line = jnp.sum(
+                jnp.where(hits(code_row, (slots, 2 * tokens), 0), dg, 0.0), axis=0, keepdims=True
+            )
             mine = table_row == my_first + e
             for half in range(2):
                 part = line[:, half * tokens : (half + 1) * tokens]
@@ -483,7 +503,7 @@
             pltpu.VMEM((per_device, ff, width), bf),
             pltpu.VMEM((2, 2 * tokens, width), bf),
             pltpu.VMEM((2, 2 * tokens, width), bf),
-            pltpu.VMEM((per_device, blocks // 2, 2 * capacity, 2 * tokens), bf),
+            pltpu.VMEM((blocks // 2, 2 * tokens, per_device * 2 * capacity), bf),
             pltpu.VMEM((per_device, rows, width), bf),
             pltpu.VMEM((per_device, rows, width), bf),
             pltpu.VMEM((per_device, rows, width), bf),
@@ -494,6 +514,7 @@
             pltpu.VMEM((rows, ff), f32),
             pltpu.VMEM((rows, ff), f32),
             pltpu.VMEM((blocks, table_rows, tokens), bf),
+            pltpu.VMEM((per_device, blocks // 2, 1, 2 * tokens), f32),
             pltpu.VMEM((experts, 2 * tokens), f32),
             pltpu.VMEM((experts, 2 * tokens), f32),
             pltpu.VMEM((per_device, rows, 128), f32),
@@ -657,22 +678,22 @@
     h1_ref[...] = (x * inverse * gain).astype(bf)
     cos_wide, sin_wide = cos_ref[...], sin_ref[...]
 
-    @pl.loop(0, width // 256)
+    @pl.loop(0, width // 768)
     def _(j):
-        raw = dot_nn(h1_ref[...], w_full[:, tile_cols(j, 256)])
+        raw = dot_nn(h1_ref[...], w_full[:, tile_cols(j, 768)])
         both = [
             rotate(raw[:, half * HEAD_SIZE : (half + 1) * HEAD_SIZE], cos_wide, sin_wide)
-            for half in range(2)
+            for half in range(768 // HEAD_SIZE)
         ]
-        q_ref[:, tile_cols(j, 256)] = jnp.concatenate(both, axis=1).astype(bf)
-
-    raw = dot_nn(h1_ref[...], w_full[:, width : width + kv_width])
+        q_ref[:, tile_cols(j, 768)] = jnp.concatenate(both, axis=1).astype(bf)
+
+    raw = dot_nn(h1_ref[...], w_full[:, width:main])
     both = [
         rotate(raw[:, half * HEAD_SIZE : (half + 1) * HEAD_SIZE], cos_wide, sin_wide)
         for half in range(KEY_VALUE_HEADS)
     ]
     k_ref[...] = jnp.concatenate(both, axis=1).astype(bf)
-    v_ref[...] = dot_nn(h1_ref[...], w_full[:, width + kv_width : main]).astype(bf)
+    v_ref[...] = raw[:, kv_width:].astype(bf)
     seq_len = tokens // SEQ_DEV
     query_step = lax.broadcasted_iota(jnp.int32, (seq_len, seq_len), 0)
     key_step = lax.broadcasted_iota(jnp.int32, (seq_len, seq_len), 1)
@@ -705,10 +726,10 @@
     side_out = w_full[:, base + width : base + width + 128].astype(jnp.float32).T
     aux_ref[...] = jnp.concatenate([side_out, side[:8]], axis=0)
 
-    @pl.loop(0, width // 256)
+    @pl.loop(0, width // 768)
     def _(j):
-        cols = tile_cols(j, 256)
-        at = pl.ds(pl.multiple_of(base + j * 256, 128), 256)
+        cols = tile_cols(j, 768)
+        at = pl.ds(pl.multiple_of(base + j * 768, 128), 768)
         res_ref[:, cols] = x_ref[:, cols].astype(jnp.float32) + dot_nn(o_ref[...], w_full[:, at])
 
     res = res_ref[...]
@@ -846,18 +867,18 @@
     )
     payload[:, base + width : base + width + 128] = side.T.astype(bf)
 
-    @pl.loop(0, width // 256)
+    @pl.loop(0, width // 768)
     def _(j):
-        cols = tile_cols(j, 256)
-        at = pl.ds(pl.multiple_of(base + j * 256, 128), 256)
+        cols = tile_cols(j, 768)
+        at = pl.ds(pl.multiple_of(base + j * 768, 128), 768)
         payload[:, at] = dot_tn(o_ref[...], dres_low[:, cols]).astype(bf)
 
     send_payload(order_ref, payload, base, outs[len(outs) // 2 :], sem_p)
     load.wait()
 
-    @pl.loop(0, width // 256)
+    @pl.loop(0, width // 768)
     def _(j):
-        cols = tile_cols(j, 256)
+        cols = tile_cols(j, 768)
         dmix_ref[:, cols] = dot_nt(dres_low[...], w_full[cols, base : base + width]).astype(bf)
 
     seq_len = tokens // SEQ_DEV
@@ -886,14 +907,14 @@
             dqkv[rows, width + h * HEAD_SIZE : width + (h + 1) * HEAD_SIZE] = dk.astype(bf)
             at = width + kv_width + h * HEAD_SIZE
             dqkv[rows, at : at + HEAD_SIZE] = dv.astype(bf)
-    @pl.loop(0, width // 256)
+    @pl.loop(0, width // 768)
     def _(j):
-        cols = tile_cols(j, 256)
+        cols = tile_cols(j, 768)
         dh1[:, cols] = dot_nt(dqkv[...], w_full[cols, :main])
 
-    @pl.loop(0, main // 256)
+    @pl.loop(0, main // 1024)
     def _(j):
-        cols = tile_cols(j, 256)
+        cols = tile_cols(j, 1024)
         payload[:, cols] = dot_tn(h1_ref[...], dqkv[:, cols]).astype(bf)
 
     x = x_ref[...].astype(jnp.float32)
@@ -945,7 +966,7 @@
             sem,
         ],
         cost_estimate=pl.CostEstimate(
-            flops=181000000000, transcendentals=0, bytes_accessed=32000000
+            flops=165000000000, transcendentals=0, bytes_accessed=32000000
         ),
         compiler_params=pltpu.CompilerParams(vmem_limit_bytes=60 * MIB),
     )(order, own, *early, *backs, *saved, w_full)
@@ -1047,9 +1068,10 @@
     first = scatter_core(outs[:half])
     second = scatter_core(outs[half:])
     first_got = [swap_x(first[0]), swap_y(first[1])]
+    tied = lax.optimization_barrier(tuple(first_got) + (first[2], first[3], grad_x) + tuple(more[1:]))
+    first_got, first[2:4], grad_x, more[1:] = list(tied[:2]), tied[2:4], tied[4], tied[5:]
     first_level = scatter_planes(first, first_got)
-    *sent, grad_x = lax.optimization_barrier((second[0], second[1], grad_x))
-    sent = lax.optimization_barrier(tuple(sent) + tuple(first_got))
+    sent = lax.optimization_barrier((second[0], second[1]) + tuple(first_got))
     second_got = [swap_x(sent[0]), swap_y(sent[1])]
     second_level = scatter_planes(second, second_got)
     more = lax.optimization_barrier(tuple(more) + (first_level[1],))[:-1]

time: 507 us -> 497 us (0.980)
  Pallas kernels: 114 us -> 105 us
    ppermute x7, waiting for transfers between devices: 15.5 us -> 45.3 us  [shift_down(): return lax.ppermute(value, 'expert', [(i, (i + 6) % 8) for i in range(8)])]
    ppermute x12, waiting for transfers between devices: 91.7 us -> 69.9 us  [shift_up(): return lax.ppermute(value, 'expert', [(i, (i + 2) % 8) for i in range(8)])]
    convert_element_type x11 -> x13, other arithmetic: 12.4 us -> 9.5 us  [add_low(): (left.astype(jnp.float32) + right.astype(jnp.float32)).astype(jnp.bfloat16)]
    unnamed x92 -> x104, local copies, waits for them, and re-layouts: 10.7 us -> 11.2 us
  transfers between devices with their start and end apart: 69 -> 69, of which waited for: 27 -> 27; matrix products, arithmetic and copies ran while one was open for 15% -> 15% of each run, Pallas kernels for 13% -> 12%
where the time goes in v4:
time: 497 us; the launch traced here: 489 us
  waiting for transfers between devices  229 us (46%)
  Pallas kernels  105 us (21%)
  starting transfers between devices  63 us (13%)
  local copies, waits for them, and re-layouts  40.8 us (8%)
  other arithmetic  36.9 us (7%)
  between operations  15 us (3%)
    ppermute x12, waiting for transfers between devices, shift_up(): return lax.ppermute(value, 'expert', [(i, (i + 2) % 8) for i in range(8)])  69.9 us
    ppermute x10, waiting for transfers between devices, swap_x(): return lax.ppermute(value, 'dp', [(i, i ^ 1) for i in range(4)])  48.4 us
    pallas_call x1, Pallas kernels, run_experts(): pl.pallas_call(lambda *refs: expert_kernel(plan, capacity, *refs), out_sh...  47.1 us
    ppermute x7, waiting for transfers between devices, shift_down(): return lax.ppermute(value, 'expert', [(i, (i + 6) % 8) for i in range(8)])  45.3 us
    ppermute x10, waiting for transfers between devices, swap_y(): return lax.ppermute(value, 'dp', [(i, i ^ 2) for i in range(4)])  40.8 us
    pallas_call x1, Pallas kernels, run_backward(): pl.pallas_call(lambda *refs: backward_kernel(experts, len(backs), piece,...  25.2 us
    ppermute x7, starting transfers between devices, shift_down(): return lax.ppermute(value, 'expert', [(i, (i + 6) % 8) for i in range(8)])  19 us
    pallas_call x1, Pallas kernels, expert_weight_grads(): pl.pallas_call(weight_kernel, grid=(per_device, parts), out_shape=jax.Sha...  17.8 us
  transfers between devices with their start and end apart: 69, of which 27 were waited for; matrix products, arithmetic and copies ran while one was open for 15% of the time, Pallas kernels for 12%

profile of v4, /device:TPU:0, one launch (start us, length us, event | category | flops | bytes accessed | tf_op | source)
XLA Modules:
  0.0 489.2 jit_solution(4802244653646072850)
XLA Ops:
  7.2 3.0 collective-permute-start.4
  10.2 1.5 collective-permute-start.3
  17.6 1.6 collective-permute-start
  19.2 2.2 collective-permute-start.1
  22.2 1.5 copy.75
  24.7 1.5 copy.76
  28.3 8.2 %collective-permute-done.4.refs_12_ = bf16[2,768,384]{2,1,0:T(8,128)(2,1)} collective-permute-done((bf16[2,768,384]{2,1,0:T(8,128)(2,1)}, bf16[2,768,384]{2,1,0:T(8,128)(2,1)}, u32[]{:S(2)}, u32[]{:S(2)}) %collective-permute-start.4) | collective-permute-done | bytes 1179680 | tf_op jit(solution)/shard_map/ppermute | solution.py:59
  37.6 1.8 collective-permute-start.5
  40.5 1.6 collective-permute-start.6
  42.1 1.6 pad_maximum_fusion.refs_5_
  43.8 9.3 %collective-permute-done.2 = bf16[48,3840]{1,0:T(8,128)(2,1)} collective-permute-done((bf16[48,3840]{1,0:T(8,128)(2,1)S(1)}, bf16[48,3840]{1,0:T(8,128)(2,1)}, u32[]{:S(2)}, u32[]{:S(2)}) %collective-permute-start.2) | collective-permute-done | bytes 368672 | tf_op jit(solution)/shard_map/ppermute | solution.py:984
  53.1 2.5 pad_maximum_fusion.1.refs_6_
  58.3 1.5 collective-permute-start.14
  59.9 2.4 collective-permute-start.15
  62.3 27.9 %collective-permute-done.7.refs_7_ = bf16[4,48,3840]{2,1,0:T(8,128)(2,1)} collective-permute-done((bf16[4,48,3840]{2,1,0:T(8,128)(2,1)}, bf16[4,48,3840]{2,1,0:T(8,128)(2,1)}, u32[]{:S(2)}, u32[]{:S(2)}) %collective-permute-start.7) | collective-permute-done | bytes 1474592 | tf_op jit(solution)/shard_map/ppermute | solution.py:55
  90.2 2.0 slice.314
  92.7 2.0 slice.313
  96.9 1.5 gather_fusion.1
  98.4 3.7 all-to-all-start
  103.3 6.7 %collective-permute-done.10.refs_10_ = bf16[2,48,3840]{2,1,0:T(8,128)(2,1)} collective-permute-done((bf16[2,48,3840]{2,1,0:T(8,128)(2,1)}, bf16[2,48,3840]{2,1,0:T(8,128)(2,1)}, u32[]{:S(2)}, u32[]{:S(2)}) %collective-permute-start.10) | collective-permute-done | bytes 737312 | tf_op jit(solution)/shard_map/ppermute | solution.py:59
  110.1 2.3 collective-permute-done.9.refs_9_
  116.4 6.7 %all-to-all-done = bf16[8,2,16,1536]{3,2,1,0:T(8,128)(2,1)S(1)} async-done(((bf16[8,2,16,1536]{3,2,1,0:T(8,128)(2,1)}), bf16[8,2,16,1536]{3,2,1,0:T(8,128)(2,1)S(1)}, u32[]{:S(2)}, u32[]{:S(2)}) %all-to-all-start) | async-done | bytes 786464 | tf_op jit(solution)/shard_map/all_to_all | solution.py:1008
  125.1 1.5 collective-permute-start.21
  126.7 14.6 %shard_map.247 = (bf16[256,1536]{1,0:T(8,128)(2,1)}, f32[256,1536]{1,0:T(8,128)}, bf16[256,1536]{1,0:T(8,128)(2,1)}, bf16[256,1536]{1,0:T(8,128)(2,1)}, bf16[256...) custom-call(s32[32]{0:T(128)} %stack.218.refs_0_, ...), custom_call_target="tpu_custom_call" | custom-call | flops 109999996928 | bytes 16000000 | tf_op jit(solution)/shard_map/pallas_call | solution.py:751
  141.4 3.7 collective-permute-start.19
  145.1 2.4 collective-permute-done.29.refs_26_.refs_5_
  147.6 16.7 %collective-permute-done.18.refs_16_ = bf16[256,1536]{1,0:T(8,128)(2,1)} collective-permute-done((bf16[256,1536]{1,0:T(8,128)(2,1)}, bf16[256,1536]{1,0:T(8,128)(2,1)}, u32[]{:S(2)}, u32[]{:S(2)}) %collective-permute-start.18) | collective-permute-done | bytes 786464 | tf_op jit(solution)/shard_map/ppermute | solution.py:67
  164.3 15.7 %collective-permute-done.19.refs_17_ = bf16[256,1536]{1,0:T(8,128)(2,1)} collective-permute-done((bf16[256,1536]{1,0:T(8,128)(2,1)}, bf16[256,1536]{1,0:T(8,128)(2,1)}, u32[]{:S(2)}, u32[]{:S(2)}) %collective-permute-start.19) | collective-permute-done | bytes 786464 | tf_op jit(solution)/shard_map/ppermute | solution.py:71
  185.0 1.5 collective-permute-start.23
  187.4 16.5 %collective-permute-done.24.refs_18_ = bf16[256,1536]{1,0:T(8,128)(2,1)} collective-permute-done((bf16[256,1536]{1,0:T(8,128)(2,1)}, bf16[256,1536]{1,0:T(8,128)(2,1)}, u32[]{:S(2)}, u32[]{:S(2)}) %collective-permute-start.24) | collective-permute-done | bytes 786464 | tf_op jit(solution)/shard_map/ppermute | solution.py:67
  205.7 1.5 slice.436.refs_1_
  207.2 5.0 %collective-permute-done.22.refs_8_ = bf16[2,384,768]{2,1,0:T(8,128)(2,1)} collective-permute-done((bf16[2,384,768]{2,1,0:T(8,128)(2,1)S(1)}, bf16[2,384,768]{2,1,0:T(8,128)(2,1)}, u32[]{:S(2)}, u32[]{:S(2)}) %collective-permute-start.22) | collective-permute-done | bytes 1179680 | tf_op jit(solution)/shard_map/ppermute | solution.py:55
  213.5 47.1 %shard_map.248 = (bf16[4,272,1536]{2,1,0:T(8,128)(2,1)}, bf16[4,272,1536]{2,1,0:T(8,128)(2,1)}, bf16[4,256,1536]{2,1,0:T(8,128)(2,1)}, bf16[4,256,1536]{2,1,0:T(...) custom-call(s32[34]{0:T(128)} %concatenate.43.refs_0_.refs_1_, ...), custom_call_target="tpu_custom_call" | custom-call | flops 54999998464 | bytes 50000000 | tf_op jit(solution)/shard_map/pallas_call | solution.py:495
  260.7 6.1 %collective-permute-done.34 = bf16[4,272,1536]{2,1,0:T(8,128)(2,1)S(1)} collective-permute-done((bf16[4,272,1536]{2,1,0:T(8,128)(2,1)}, bf16[4,272,1536]{2,1,0:T(8,128)(2,1)S(1)}, u32[]{:S(2)}, u32[]{:S(2)}) %collective-permute-start.34) | collective-permute-done | bytes 3342368 | tf_op jit(solution)/shard_map/ppermute | solution.py:63
  266.9 4.2 fusion.3
  271.9 17.8 %shard_map.249 = bf16[4,3,2,384,768]{4,3,2,1,0:T(8,128)(2,1)} custom-call(bf16[2,576,1536]{2,1,0:T(8,128)(2,1)} %get-tuple-element.151.x_ref, bf16[2,576,768]{2,1,0:T(8,128)(2,1)} %get-tuple-element.152.dga_ref, bf16[2,576,768]{2,1,0:T(8,128)(2,1)} %get-tuple-element.153.dua_ref, bf16[2,576,768]{2,1,0:T(8,128)(2,1)} %get-tuple-element.154.hid_ref, ...), custom_call_target="tpu_custom_call" | custom-call | flops 18699999232 | bytes 17000000 | tf_op jit(solution)/shard_map/pallas_call | solution.py:553
  289.7 3.2 collective-permute-start.35
  294.4 17.5 %collective-permute-done.35.refs_11_ = bf16[272,1536]{1,0:T(8,128)(2,1)S(1)} collective-permute-done((bf16[272,1536]{1,0:T(8,128)(2,1)S(1)}, bf16[272,1536]{1,0:T(8,128)(2,1)S(1)}, u32[]{:S(2)}, u32[]{:S(2)}) %collective-permute-start.35) | collective-permute-done | bytes 835616 | tf_op jit(solution)/shard_map/ppermute | solution.py:71
  312.9 5.7 %fusion.9 = (bf16[256,1536]{1,0:T(8,128)(2,1)}, bf16[256,1536]{1,0:T(8,128)(2,1)}, bf16[256,1536]{1,0:T(8,128)(2,1)}, f32[256,1536]{1,0:T(8,128)}) fusion(bf16[4,256,1536]{2,1,0:T(8,128)(2,1)} %collective-permute-done.36, bf16[4,256,1536]{2,1,0:T(8,128)(2,1)} %get-tuple-element.146), kind=kLoop, calls=%fused_computation.39 | loop fusion | flops 5898240 | bytes 10223616 | tf_op jit(solution)/shard_map/convert_element_type | solution.py:1091
  318.6 12.2 %collective-permute-done.38.refs_12_ = bf16[272,1536]{1,0:T(8,128)(2,1)S(1)} collective-permute-done((bf16[272,1536]{1,0:T(8,128)(2,1)S(1)}, bf16[272,1536]{1,0:T(8,128)(2,1)S(1)}, u32[]{:S(2)}, u32[]{:S(2)}) %collective-permute-start.38) | collective-permute-done | bytes 835616 | tf_op jit(solution)/shard_map/ppermute | solution.py:67
  331.8 25.2 %shard_map.250 = (bf16[2,2,48,2176]{3,2,1,0:T(8,128)(2,1)}, bf16[2,2,48,2176]{3,2,1,0:T(8,128)(2,1)}, bf16[2,48,2176]{2,1,0:T(8,128)(2,1)}, bf16[2,48,2176]{2,1,...) custom-call(s32[32]{0:T(128)} %stack.218.refs_0_, ...), custom_call_target="tpu_custom_call" | custom-call | flops 165000003584 | bytes 32000000 | tf_op jit(solution)/shard_map/pallas_call | solution.py:946
  357.1 1.5 add_convert_fusion.7
  359.2 3.1 collective-permute-start.46
  363.3 2.2 collective-permute-done.40
  365.6 1.5 collective-permute-start.43
  369.1 11.1 %collective-permute-done.46 = bf16[256,1536]{1,0:T(8,128)(2,1)S(1)} collective-permute-done((bf16[256,1536]{1,0:T(8,128)(2,1)S(1)}, bf16[256,1536]{1,0:T(8,128)(2,1)S(1)}, u32[]{:S(2)}, u32[]{:S(2)}) %collective-permute-start.46) | collective-permute-done | bytes 786464 | tf_op jit(solution)/shard_map/ppermute | solution.py:71
  380.2 17.0 %collective-permute-done.47 = bf16[256,1536]{1,0:T(8,128)(2,1)S(1)} collective-permute-done((bf16[256,1536]{1,0:T(8,128)(2,1)S(1)}, bf16[256,1536]{1,0:T(8,128)(2,1)S(1)}, u32[]{:S(2)}, u32[]{:S(2)}) %collective-permute-start.47) | collective-permute-done | bytes 786464 | tf_op jit(solution)/shard_map/ppermute | solution.py:67
  402.7 1.7 copy.79
  404.4 3.5 all-to-all-start.1
  408.5 11.7 %collective-permute-done.57 = bf16[2,48,2176]{2,1,0:T(8,128)(2,1)} collective-permute-done((bf16[2,48,2176]{2,1,0:T(8,128)(2,1)}, bf16[2,48,2176]{2,1,0:T(8,128)(2,1)}, u32[]{:S(2)}, u32[]{:S(2)}) %collective-permute-start.57) | collective-permute-done | bytes 417824 | tf_op jit(solution)/shard_map/ppermute | solution.py:55
  420.2 1.6 collective-permute-start.62
  423.0 1.6 convert_add_fusion.6
  425.9 1.9 collective-permute-start.56
  427.8 23.0 %collective-permute-done.62 = bf16[2,2,48,1664]{3,2,1,0:T(8,128)(2,1)S(1)} collective-permute-done((bf16[2,2,48,1664]{3,2,1,0:T(8,128)(2,1)}, bf16[2,2,48,1664]{3,2,1,0:T(8,128)(2,1)S(1)}, u32[]{:S(2)}, u32[]{:S(2)}) %collective-permute-start.62) | collective-permute-done | bytes 639008 | tf_op jit(solution)/shard_map/ppermute | solution.py:59
  456.6 1.7 collective-permute-done.58
  459.5 1.5 collective-permute-done.63
  461.0 1.9 collective-permute-done.55
  463.2 2.6 collective-permute-start.60
  466.4 2.0 collective-permute-done.59
  470.6 1.5 gather_fusion.3
  473.5 1.8 fusion.26
  475.2 1.6 convert.35
  476.8 1.6 convert.36
  478.4 1.6 maximum_convert_fusion
  (273 shorter events, 63.8 us)
Async XLA Ops:
  7.2 29.3 %collective-permute-start.4 = (bf16[2,768,384]{2,1,0:T(8,128)(2,1)}, bf16[2,768,384]{2,1,0:T(8,128)(2,1)}, u32[]{:S(2)}, u32[]{:S(2)}) collective-permute-start(bf16[2,768,384]{2,1,0:T(8,128)(2,1)} %refs_10_.1), channel_id=1, source_target_pairs={{0,16},{8,24},{16,0},{24,8},{1,17},{9,25},{17,1},{25,9},{2,18},{10... | collective-permute-start | bytes 3538952 | tf_op jit(solution)/shard_map/ppermute | solution.py:59
  10.2 29.2 %collective-permute-start.3 = (bf16[2,768,384]{2,1,0:T(8,128)(2,1)}, bf16[2,768,384]{2,1,0:T(8,128)(2,1)}, u32[]{:S(2)}, u32[]{:S(2)}) collective-permute-start(bf16[2,768,384]{2,1,0:T(8,128)(2,1)} %refs_10_.1), channel_id=1, source_target_pairs={{0,8},{8,0},{16,24},{24,16},{1,9},{9,1},{17,25},{25,17},{2,10},{10... | collective-permute-start | bytes 3538952 | tf_op jit(solution)/shard_map/ppermute | solution.py:55
  17.6 26.2 %collective-permute-start = (bf16[48,3840]{1,0:T(8,128)(2,1)S(1)}, bf16[48,3840]{1,0:T(8,128)(2,1)}, u32[]{:S(2)}, u32[]{:S(2)}) collective-permute-start(bf16[48,3840]{1,0:T(8,128)(2,1)S(1)} %fusion.22), channel_id=1, source_target_pairs={{0,2},{1,3},{2,4},{3,5},{4,6},{5,7},{6,0},{7,1},{8,10},{9,11},{10,... | collective-permute-start | bytes 1105928 | tf_op jit(solution)/shard_map/ppermute | solution.py:67
  19.2 24.6 %collective-permute-start.1 = (bf16[48,3840]{1,0:T(8,128)(2,1)S(1)}, bf16[48,3840]{1,0:T(8,128)(2,1)}, u32[]{:S(2)}, u32[]{:S(2)}) collective-permute-start(bf16[48,3840]{1,0:T(8,128)(2,1)S(1)} %fusion.22), channel_id=1, source_target_pairs={{0,6},{1,7},{2,0},{3,1},{4,2},{5,3},{6,4},{7,5},{8,14},{9,15},{10,... | collective-permute-start | bytes 1105928 | tf_op jit(solution)/shard_map/ppermute | solution.py:71
  21.4 31.6 %collective-permute-start.2 = (bf16[48,3840]{1,0:T(8,128)(2,1)S(1)}, bf16[48,3840]{1,0:T(8,128)(2,1)}, u32[]{:S(2)}, u32[]{:S(2)}) collective-permute-start(bf16[48,3840]{1,0:T(8,128)(2,1)S(1)} %fusion.22), channel_id=1, source_target_pairs={{0,4},{1,5},{2,6},{3,7},{4,0},{5,1},{6,2},{7,3},{8,12},{9,13},{10,... | collective-permute-start | bytes 1105928 | tf_op jit(solution)/shard_map/ppermute | solution.py:984
  37.6 17.9 %collective-permute-start.5 = (bf16[1,768,384]{2,1,0:T(8,128)(2,1)S(1)}, bf16[1,768,384]{2,1,0:T(8,128)(2,1)S(1)}, u32[]{:S(2)}, u32[]{:S(2)}) collective-permute-start(bf16[1,768,384]{2,1,0:T(8,128)(2,1)S(1)} %slice.311), channel_id=1, source_target_pairs={{0,8},{8,0},{16,24},{24,16},{1,9},{9,1},{17,25},{25,17},{2,10},{10... | collective-permute-start | bytes 1769480 | tf_op jit(solution)/shard_map/ppermute | solution.py:55
  40.5 15.0 %collective-permute-start.6 = (bf16[1,768,384]{2,1,0:T(8,128)(2,1)S(1)}, bf16[1,768,384]{2,1,0:T(8,128)(2,1)S(1)}, u32[]{:S(2)}, u32[]{:S(2)}) collective-permute-start(bf16[1,768,384]{2,1,0:T(8,128)(2,1)S(1)} %slice.312), channel_id=1, source_target_pairs={{0,16},{8,24},{16,0},{24,8},{1,17},{9,25},{17,1},{25,9},{2,18},{10... | collective-permute-start | bytes 1769480 | tf_op jit(solution)/shard_map/ppermute | solution.py:59
  55.6 34.6 %collective-permute-start.7 = (bf16[4,48,3840]{2,1,0:T(8,128)(2,1)}, bf16[4,48,3840]{2,1,0:T(8,128)(2,1)}, u32[]{:S(2)}, u32[]{:S(2)}) collective-permute-start(bf16[4,48,3840]{2,1,0:T(8,128)(2,1)} %pad_maximum_fusion.1.refs_6_), channel_id=1, source_target_pairs={{0,8},{8,0},{16,24},{24,16},{1,9},{9,1},{17,25},{25,17},{2,10},{10... | collective-permute-start | bytes 4423688 | tf_op jit(solution)/shard_map/ppermute | solution.py:55
  56.2 36.5 %collective-permute-start.8 = (bf16[4,48,3840]{2,1,0:T(8,128)(2,1)}, bf16[4,48,3840]{2,1,0:T(8,128)(2,1)}, u32[]{:S(2)}, u32[]{:S(2)}) collective-permute-start(bf16[4,48,3840]{2,1,0:T(8,128)(2,1)} %pad_maximum_fusion.1.refs_6_), channel_id=1, source_target_pairs={{0,16},{8,24},{16,0},{24,8},{1,17},{9,25},{17,1},{25,9},{2,18},{10... | collective-permute-start | bytes 4423688 | tf_op jit(solution)/shard_map/ppermute | solution.py:59
  58.3 37.0 %collective-permute-start.14 = (bf16[272,1536]{1,0:T(8,128)(2,1)S(1)}, bf16[272,1536]{1,0:T(8,128)(2,1)S(1)}, u32[]{:S(2)}, u32[]{:S(2)}) collective-permute-start(bf16[272,1536]{1,0:T(8,128)(2,1)S(1)} %fusion.1.refs_23_.refs_2_), channel_id=1, source_target_pairs={{0,2},{1,3},{2,4},{3,5},{4,6},{5,7},{6,0},{7,1},{8,10},{9,11},{10,... | collective-permute-start | bytes 2506760 | tf_op jit(solution)/shard_map/ppermute | solution.py:67
  59.9 37.0 %collective-permute-start.15 = (bf16[272,1536]{1,0:T(8,128)(2,1)S(1)}, bf16[272,1536]{1,0:T(8,128)(2,1)}, u32[]{:S(2)}, u32[]{:S(2)}) collective-permute-start(bf16[272,1536]{1,0:T(8,128)(2,1)S(1)} %fusion.1.refs_23_.refs_2_), channel_id=1, source_target_pairs={{0,6},{1,7},{2,0},{3,1},{4,2},{5,3},{6,4},{7,5},{8,14},{9,15},{10,... | collective-permute-start | bytes 2506760 | tf_op jit(solution)/shard_map/ppermute | solution.py:71
  92.2 17.9 %collective-permute-start.10 = (bf16[2,48,3840]{2,1,0:T(8,128)(2,1)}, bf16[2,48,3840]{2,1,0:T(8,128)(2,1)}, u32[]{:S(2)}, u32[]{:S(2)}) collective-permute-start(bf16[2,48,3840]{2,1,0:T(8,128)(2,1)} %slice.314), channel_id=1, source_target_pairs={{0,16},{8,24},{16,0},{24,8},{1,17},{9,25},{17,1},{25,9},{2,18},{10... | collective-permute-start | bytes 2211848 | tf_op jit(solution)/shard_map/ppermute | solution.py:59
  94.7 17.6 %collective-permute-start.9 = (bf16[2,48,3840]{2,1,0:T(8,128)(2,1)}, bf16[2,48,3840]{2,1,0:T(8,128)(2,1)}, u32[]{:S(2)}, u32[]{:S(2)}) collective-permute-start(bf16[2,48,3840]{2,1,0:T(8,128)(2,1)} %slice.313), channel_id=1, source_target_pairs={{0,8},{8,0},{16,24},{24,16},{1,9},{9,1},{17,25},{25,17},{2,10},{10... | collective-permute-start | bytes 2211848 | tf_op jit(solution)/shard_map/ppermute | solution.py:55
  95.4 28.7 %collective-permute-start.11 = (bf16[4,48,3840]{2,1,0:T(8,128)(2,1)}, bf16[4,48,3840]{2,1,0:T(8,128)(2,1)}, u32[]{:S(2)}, u32[]{:S(2)}) collective-permute-start(bf16[4,48,3840]{2,1,0:T(8,128)(2,1)} %pad_maximum_fusion.1.refs_6_), channel_id=1, source_target_pairs={{0,1},{1,0},{2,3},{3,2},{4,5},{5,4},{6,7},{7,6},{8,9},{9,8},{10,11... | collective-permute-start | bytes 4423688 | tf_op jit(solution)/shard_map/ppermute | solution.py:63
  95.4 31.3 %collective-permute-start.12 = (bf16[4,48,3840]{2,1,0:T(8,128)(2,1)}, bf16[4,48,3840]{2,1,0:T(8,128)(2,1)}, u32[]{:S(2)}, u32[]{:S(2)}) collective-permute-start(bf16[4,48,3840]{2,1,0:T(8,128)(2,1)} %collective-permute-done.7.refs_7_), channel_id=1, source_target_pairs={{0,1},{1,0},{2,3},{3,2},{4,5},{5,4},{6,7},{7,6},{8,9},{9,8},{10,11... | collective-permute-start | bytes 4423688 | tf_op jit(solution)/shard_map/ppermute | solution.py:63
  96.9 29.8 %collective-permute-start.13 = (bf16[4,48,3840]{2,1,0:T(8,128)(2,1)}, bf16[4,48,3840]{2,1,0:T(8,128)(2,1)}, u32[]{:S(2)}, u32[]{:S(2)}) collective-permute-start(bf16[4,48,3840]{2,1,0:T(8,128)(2,1)} %collective-permute-done.8.refs_8_), channel_id=1, source_target_pairs={{0,1},{1,0},{2,3},{3,2},{4,5},{5,4},{6,7},{7,6},{8,9},{9,8},{10,11... | collective-permute-start | bytes 4423688 | tf_op jit(solution)/shard_map/ppermute | solution.py:63
  98.4 24.7 %all-to-all-start = ((bf16[8,2,16,1536]{3,2,1,0:T(8,128)(2,1)}), bf16[8,2,16,1536]{3,2,1,0:T(8,128)(2,1)S(1)}, u32[]{:S(2)}, u32[]{:S(2)}) async-start(bf16[8,2,16,1536]{3,2,1,0:T(8,128)(2,1)} %bitcast.53), calls=%async_computation | async-start | bytes 1572864 | tf_op jit(solution)/shard_map/all_to_all | solution.py:1008
  102.1 370.0 %reduce-scatter.2.cloned.1.call-start = ((), (), s32[]{:S(2)}) async-start(), calls=%async_computation.3 | async-start | bytes 17694720 | tf_op jit(solution)/shard_map/reduce_scatter | solution.py:1245
  112.4 11.7 %collective-permute-start.16 = (bf16[2,48,3840]{2,1,0:T(8,128)(2,1)}, bf16[2,48,3840]{2,1,0:T(8,128)(2,1)}, u32[]{:S(2)}, u32[]{:S(2)}) collective-permute-start(bf16[2,48,3840]{2,1,0:T(8,128)(2,1)} %collective-permute-done.9.refs_9_), channel_id=1, source_target_pairs={{0,1},{1,0},{2,3},{3,2},{4,5},{5,4},{6,7},{7,6},{8,9},{9,8},{10,11... | collective-permute-start | bytes 2211848 | tf_op jit(solution)/shard_map/ppermute | solution.py:63
  112.4 12.8 %collective-permute-start.17 = (bf16[2,48,3840]{2,1,0:T(8,128)(2,1)}, bf16[2,48,3840]{2,1,0:T(8,128)(2,1)}, u32[]{:S(2)}, u32[]{:S(2)}) collective-permute-start(bf16[2,48,3840]{2,1,0:T(8,128)(2,1)} %collective-permute-done.10.refs_10_), channel_id=1, source_target_pairs={{0,1},{1,0},{2,3},{3,2},{4,5},{5,4},{6,7},{7,6},{8,9},{9,8},{10,11... | collective-permute-start | bytes 2211848 | tf_op jit(solution)/shard_map/ppermute | solution.py:63
  124.0 23.5 %collective-permute-start.29 = (bf16[272,1536]{1,0:T(8,128)(2,1)}, bf16[272,1536]{1,0:T(8,128)(2,1)}, u32[]{:S(2)}, u32[]{:S(2)}) collective-permute-start(bf16[272,1536]{1,0:T(8,128)(2,1)} %copy-done.31), channel_id=1, source_target_pairs={{0,2},{1,3},{2,4},{3,5},{4,6},{5,7},{6,0},{7,1},{8,10},{9,11},{10,... | collective-permute-start | bytes 2506760 | tf_op jit(solution)/shard_map/ppermute | solution.py:67
  124.1 56.0 %collective-permute-start.20 = (bf16[2,2,384,768]{3,2,1,0:T(8,128)(2,1)S(1)}, bf16[2,2,384,768]{3,2,1,0:T(8,128)(2,1)S(1)}, u32[]{:S(2)}, u32[]{:S(2)}) collective-permute-start(bf16[2,2,384,768]{3,2,1,0:T(8,128)(2,1)S(1)} %copy-done.4), channel_id=1, source_target_pairs={{0,8},{8,0},{16,24},{24,16},{1,9},{9,1},{17,25},{25,17},{2,10},{10... | collective-permute-start | bytes 7077896 | tf_op jit(solution)/shard_map/ppermute | solution.py:55
  125.1 55.4 %collective-permute-start.21 = (bf16[2,2,384,768]{3,2,1,0:T(8,128)(2,1)S(1)}, bf16[2,2,384,768]{3,2,1,0:T(8,128)(2,1)}, u32[]{:S(2)}, u32[]{:S(2)}) collective-permute-start(bf16[2,2,384,768]{3,2,1,0:T(8,128)(2,1)S(1)} %copy-done.4), channel_id=1, source_target_pairs={{0,16},{8,24},{16,0},{24,8},{1,17},{9,25},{17,1},{25,9},{2,18},{10... | collective-permute-start | bytes 7077896 | tf_op jit(solution)/shard_map/ppermute | solution.py:59
  141.3 23.1 %collective-permute-start.18 = (bf16[256,1536]{1,0:T(8,128)(2,1)}, bf16[256,1536]{1,0:T(8,128)(2,1)}, u32[]{:S(2)}, u32[]{:S(2)}) collective-permute-start(bf16[256,1536]{1,0:T(8,128)(2,1)} %get-tuple-element.138.refs_15_.refs_14_), channel_id=1, source_target_pairs={{0,2},{1,3},{2,4},{3,5},{4,6},{5,7},{6,0},{7,1},{8,10},{9,11},{10,... | collective-permute-start | bytes 2359304 | tf_op jit(solution)/shard_map/ppermute | solution.py:67
  141.4 38.5 %collective-permute-start.19 = (bf16[256,1536]{1,0:T(8,128)(2,1)}, bf16[256,1536]{1,0:T(8,128)(2,1)}, u32[]{:S(2)}, u32[]{:S(2)}) collective-permute-start(bf16[256,1536]{1,0:T(8,128)(2,1)} %get-tuple-element.138.refs_15_.refs_14_), channel_id=1, source_target_pairs={{0,6},{1,7},{2,0},{3,1},{4,2},{5,3},{6,4},{7,5},{8,14},{9,15},{10,... | collective-permute-start | bytes 2359304 | tf_op jit(solution)/shard_map/ppermute | solution.py:71
  147.6 33.0 %collective-permute-start.30 = (bf16[272,1536]{1,0:T(8,128)(2,1)S(1)}, bf16[272,1536]{1,0:T(8,128)(2,1)S(1)}, u32[]{:S(2)}, u32[]{:S(2)}) collective-permute-start(bf16[272,1536]{1,0:T(8,128)(2,1)S(1)} %copy-done.12), channel_id=1, source_target_pairs={{0,1},{1,0},{2,3},{3,2},{4,5},{5,4},{6,7},{7,6},{8,9},{9,8},{10,11... | collective-permute-start | bytes 2506760 | tf_op jit(solution)/shard_map/ppermute | solution.py:63
  164.3 19.6 %collective-permute-start.31 = (bf16[272,1536]{1,0:T(8,128)(2,1)S(1)}, bf16[272,1536]{1,0:T(8,128)(2,1)S(1)}, u32[]{:S(2)}, u32[]{:S(2)}) collective-permute-start(bf16[272,1536]{1,0:T(8,128)(2,1)S(1)} %copy-done.32), channel_id=1, source_target_pairs={{0,1},{1,0},{2,3},{3,2},{4,5},{5,4},{6,7},{7,6},{8,9},{9,8},{10,11... | collective-permute-start | bytes 2506760 | tf_op jit(solution)/shard_map/ppermute | solution.py:63
  180.0 6.5 %collective-permute-start.33 = (bf16[272,1536]{1,0:T(8,128)(2,1)}, bf16[272,1536]{1,0:T(8,128)(2,1)S(1)}, u32[]{:S(2)}, u32[]{:S(2)}) collective-permute-start(bf16[272,1536]{1,0:T(8,128)(2,1)} %collective-permute-done.29.refs_26_.refs_5_), channel_id=1, source_target_pairs={{0,1},{1,0},{2,3},{3,2},{4,5},{5,4},{6,7},{7,6},{8,9},{9,8},{10,11... | collective-permute-start | bytes 2506760 | tf_op jit(solution)/shard_map/ppermute | solution.py:63
  180.5 6.9 %collective-permute-start.25 = (bf16[256,1536]{1,0:T(8,128)(2,1)}, bf16[256,1536]{1,0:T(8,128)(2,1)S(1)}, u32[]{:S(2)}, u32[]{:S(2)}) collective-permute-start(bf16[256,1536]{1,0:T(8,128)(2,1)} %get-tuple-element.138.refs_15_.refs_14_), channel_id=1, source_target_pairs={{0,1},{1,0},{2,3},{3,2},{4,5},{5,4},{6,7},{7,6},{8,9},{9,8},{10,11... | collective-permute-start | bytes 2359304 | tf_op jit(solution)/shard_map/ppermute | solution.py:63
  181.7 22.2 %collective-permute-start.24 = (bf16[256,1536]{1,0:T(8,128)(2,1)}, bf16[256,1536]{1,0:T(8,128)(2,1)}, u32[]{:S(2)}, u32[]{:S(2)}) collective-permute-start(bf16[256,1536]{1,0:T(8,128)(2,1)} %collective-permute-done.18.refs_16_), channel_id=1, source_target_pairs={{0,2},{1,3},{2,4},{3,5},{4,6},{5,7},{6,0},{7,1},{8,10},{9,11},{10,... | collective-permute-start | bytes 2359304 | tf_op jit(solution)/shard_map/ppermute | solution.py:67
  183.9 28.3 %collective-permute-start.22 = (bf16[2,384,768]{2,1,0:T(8,128)(2,1)S(1)}, bf16[2,384,768]{2,1,0:T(8,128)(2,1)}, u32[]{:S(2)}, u32[]{:S(2)}) collective-permute-start(bf16[2,384,768]{2,1,0:T(8,128)(2,1)S(1)} %slice_bitcast_fusion.1), channel_id=1, source_target_pairs={{0,8},{8,0},{16,24},{24,16},{1,9},{9,1},{17,25},{25,17},{2,10},{10... | collective-permute-start | bytes 3538952 | tf_op jit(solution)/shard_map/ppermute | solution.py:55
  185.0 27.9 %collective-permute-start.23 = (bf16[2,384,768]{2,1,0:T(8,128)(2,1)S(1)}, bf16[2,384,768]{2,1,0:T(8,128)(2,1)}, u32[]{:S(2)}, u32[]{:S(2)}) collective-permute-start(bf16[2,384,768]{2,1,0:T(8,128)(2,1)S(1)} %slice_bitcast_fusion), channel_id=1, source_target_pairs={{0,16},{8,24},{16,0},{24,8},{1,17},{9,25},{17,1},{25,9},{2,18},{10... | collective-permute-start | bytes 3538952 | tf_op jit(solution)/shard_map/ppermute | solution.py:59
  186.5 20.6 %collective-permute-start.26 = (bf16[256,1536]{1,0:T(8,128)(2,1)}, bf16[256,1536]{1,0:T(8,128)(2,1)}, u32[]{:S(2)}, u32[]{:S(2)}) collective-permute-start(bf16[256,1536]{1,0:T(8,128)(2,1)} %collective-permute-done.18.refs_16_), channel_id=1, source_target_pairs={{0,1},{1,0},{2,3},{3,2},{4,5},{5,4},{6,7},{7,6},{8,9},{9,8},{10,11... | collective-permute-start | bytes 2359304 | tf_op jit(solution)/shard_map/ppermute | solution.py:63
  187.4 19.7 %collective-permute-start.27 = (bf16[256,1536]{1,0:T(8,128)(2,1)}, bf16[256,1536]{1,0:T(8,128)(2,1)}, u32[]{:S(2)}, u32[]{:S(2)}) collective-permute-start(bf16[256,1536]{1,0:T(8,128)(2,1)} %collective-permute-done.19.refs_17_), channel_id=1, source_target_pairs={{0,1},{1,0},{2,3},{3,2},{4,5},{5,4},{6,7},{7,6},{8,9},{9,8},{10,11... | collective-permute-start | bytes 2359304 | tf_op jit(solution)/shard_map/ppermute | solution.py:63
  203.9 9.0 %collective-permute-start.28 = (bf16[256,1536]{1,0:T(8,128)(2,1)}, bf16[256,1536]{1,0:T(8,128)(2,1)}, u32[]{:S(2)}, u32[]{:S(2)}) collective-permute-start(bf16[256,1536]{1,0:T(8,128)(2,1)} %collective-permute-done.24.refs_18_), channel_id=1, source_target_pairs={{0,1},{1,0},{2,3},{3,2},{4,5},{5,4},{6,7},{7,6},{8,9},{9,8},{10,11... | collective-permute-start | bytes 2359304 | tf_op jit(solution)/shard_map/ppermute | solution.py:63
  260.6 6.2 %collective-permute-start.34 = (bf16[4,272,1536]{2,1,0:T(8,128)(2,1)}, bf16[4,272,1536]{2,1,0:T(8,128)(2,1)S(1)}, u32[]{:S(2)}, u32[]{:S(2)}) collective-permute-start(bf16[4,272,1536]{2,1,0:T(8,128)(2,1)} %get-tuple-element.145), channel_id=1, source_target_pairs={{0,1},{1,0},{2,3},{3,2},{4,5},{5,4},{6,7},{7,6},{8,9},{9,8},{10,11... | collective-permute-start | bytes 10027016 | tf_op jit(solution)/shard_map/ppermute | solution.py:63
  266.8 46.1 %collective-permute-start.36 = (bf16[4,256,1536]{2,1,0:T(8,128)(2,1)}, bf16[4,256,1536]{2,1,0:T(8,128)(2,1)}, u32[]{:S(2)}, u32[]{:S(2)}) collective-permute-start(bf16[4,256,1536]{2,1,0:T(8,128)(2,1)} %get-tuple-element.148), channel_id=1, source_target_pairs={{0,1},{1,0},{2,3},{3,2},{4,5},{5,4},{6,7},{7,6},{8,9},{9,8},{10,11... | collective-permute-start | bytes 9437192 | tf_op jit(solution)/shard_map/ppermute | solution.py:63
  271.2 23.0 %collective-permute-start.37 = (bf16[272,1536]{1,0:T(8,128)(2,1)}, bf16[272,1536]{1,0:T(8,128)(2,1)S(1)}, u32[]{:S(2)}, u32[]{:S(2)}) collective-permute-start(bf16[272,1536]{1,0:T(8,128)(2,1)} %get-tuple-element.287), channel_id=1, source_target_pairs={{0,2},{1,3},{2,4},{3,5},{4,6},{5,7},{6,0},{7,1},{8,10},{9,11},{10,... | collective-permute-start | bytes 2506760 | tf_op jit(solution)/shard_map/ppermute | solution.py:67
  289.7 22.3 %collective-permute-start.35 = (bf16[272,1536]{1,0:T(8,128)(2,1)S(1)}, bf16[272,1536]{1,0:T(8,128)(2,1)S(1)}, u32[]{:S(2)}, u32[]{:S(2)}) collective-permute-start(bf16[272,1536]{1,0:T(8,128)(2,1)S(1)} %get-tuple-element.289), channel_id=1, source_target_pairs={{0,6},{1,7},{2,0},{3,1},{4,2},{5,3},{6,4},{7,5},{8,14},{9,15},{10,... | collective-permute-start | bytes 2506760 | tf_op jit(solution)/shard_map/ppermute | solution.py:71
  294.4 36.5 %collective-permute-start.38 = (bf16[272,1536]{1,0:T(8,128)(2,1)S(1)}, bf16[272,1536]{1,0:T(8,128)(2,1)S(1)}, u32[]{:S(2)}, u32[]{:S(2)}) collective-permute-start(bf16[272,1536]{1,0:T(8,128)(2,1)S(1)} %add_convert_fusion.2), channel_id=1, source_target_pairs={{0,2},{1,3},{2,4},{3,5},{4,6},{5,7},{6,0},{7,1},{8,10},{9,11},{10,... | collective-permute-start | bytes 2506760 | tf_op jit(solution)/shard_map/ppermute | solution.py:67
  330.8 26.2 %collective-permute-start.39 = (bf16[256,1536]{1,0:T(8,128)(2,1)}, bf16[256,1536]{1,0:T(8,128)(2,1)}, u32[]{:S(2)}, u32[]{:S(2)}) collective-permute-start(bf16[256,1536]{1,0:T(8,128)(2,1)} %get-tuple-element.187), channel_id=1, source_target_pairs={{0,2},{1,3},{2,4},{3,5},{4,6},{5,7},{6,0},{7,1},{8,10},{9,11},{10,... | collective-permute-start | bytes 2359304 | tf_op jit(solution)/shard_map/ppermute | solution.py:67
  359.2 21.0 %collective-permute-start.46 = (bf16[256,1536]{1,0:T(8,128)(2,1)S(1)}, bf16[256,1536]{1,0:T(8,128)(2,1)S(1)}, u32[]{:S(2)}, u32[]{:S(2)}) collective-permute-start(bf16[256,1536]{1,0:T(8,128)(2,1)S(1)} %copy-done.13), channel_id=1, source_target_pairs={{0,6},{1,7},{2,0},{3,1},{4,2},{5,3},{6,4},{7,5},{8,14},{9,15},{10,... | collective-permute-start | bytes 2359304 | tf_op jit(solution)/shard_map/ppermute | solution.py:71
  362.3 35.0 %collective-permute-start.47 = (bf16[256,1536]{1,0:T(8,128)(2,1)S(1)}, bf16[256,1536]{1,0:T(8,128)(2,1)S(1)}, u32[]{:S(2)}, u32[]{:S(2)}) collective-permute-start(bf16[256,1536]{1,0:T(8,128)(2,1)S(1)} %add_convert_fusion.7), channel_id=1, source_target_pairs={{0,2},{1,3},{2,4},{3,5},{4,6},{5,7},{6,0},{7,1},{8,10},{9,11},{10,... | collective-permute-start | bytes 2359304 | tf_op jit(solution)/shard_map/ppermute | solution.py:67
  362.3 5.7 %collective-permute-start.52 = (bf16[2,2,48,1664]{3,2,1,0:T(8,128)(2,1)}, bf16[2,2,48,1664]{3,2,1,0:T(8,128)(2,1)S(1)}, u32[]{:S(2)}, u32[]{:S(2)}) collective-permute-start(bf16[2,2,48,1664]{3,2,1,0:T(8,128)(2,1)} %get-tuple-element.212), channel_id=1, source_target_pairs={{0,1},{1,0},{2,3},{3,2},{4,5},{5,4},{6,7},{7,6},{8,9},{9,8},{10,11... | collective-permute-start | bytes 1916936 | tf_op jit(solution)/shard_map/ppermute | solution.py:63
  365.6 31.7 %collective-permute-start.43 = (bf16[2,2,48,2176]{3,2,1,0:T(8,128)(2,1)S(1)}, bf16[2,2,48,2176]{3,2,1,0:T(8,128)(2,1)S(1)}, u32[]{:S(2)}, u32[]{:S(2)}) collective-permute-start(bf16[2,2,48,2176]{3,2,1,0:T(8,128)(2,1)S(1)} %add_convert_fusion), channel_id=1, source_target_pairs={{0,16},{8,24},{16,0},{24,8},{1,17},{9,25},{17,1},{25,9},{2,18},{10... | collective-permute-start | bytes 2506760 | tf_op jit(solution)/shard_map/ppermute | solution.py:59
  367.2 30.6 %collective-permute-start.41 = (bf16[2,2,48,2176]{3,2,1,0:T(8,128)(2,1)S(1)}, bf16[2,2,48,2176]{3,2,1,0:T(8,128)(2,1)S(1)}, u32[]{:S(2)}, u32[]{:S(2)}) collective-permute-start(bf16[2,2,48,2176]{3,2,1,0:T(8,128)(2,1)S(1)} %add_convert_fusion.1), channel_id=1, source_target_pairs={{0,8},{8,0},{16,24},{24,16},{1,9},{9,1},{17,25},{25,17},{2,10},{10... | collective-permute-start | bytes 2506760 | tf_op jit(solution)/shard_map/ppermute | solution.py:55
  368.0 32.7 %collective-permute-start.51 = (bf16[2,2,48,1664]{3,2,1,0:T(8,128)(2,1)S(1)}, bf16[2,2,48,1664]{3,2,1,0:T(8,128)(2,1)S(1)}, u32[]{:S(2)}, u32[]{:S(2)}) collective-permute-start(bf16[2,2,48,1664]{3,2,1,0:T(8,128)(2,1)S(1)} %copy-done.41), channel_id=1, source_target_pairs={{0,1},{1,0},{2,3},{3,2},{4,5},{5,4},{6,7},{7,6},{8,9},{9,8},{10,11... | collective-permute-start | bytes 1916936 | tf_op jit(solution)/shard_map/ppermute | solution.py:63
  380.2 45.6 %collective-permute-start.61 = (bf16[2,48,1664]{2,1,0:T(8,128)(2,1)}, bf16[2,48,1664]{2,1,0:T(8,128)(2,1)}, u32[]{:S(2)}, u32[]{:S(2)}) collective-permute-start(bf16[2,48,1664]{2,1,0:T(8,128)(2,1)} %get-tuple-element.221), channel_id=1, source_target_pairs={{0,1},{1,0},{2,3},{3,2},{4,5},{5,4},{6,7},{7,6},{8,9},{9,8},{10,11... | collective-permute-start | bytes 958472 | tf_op jit(solution)/shard_map/ppermute | solution.py:63
  397.3 56.0 %collective-permute-start.54 = (bf16[2,48,1664]{2,1,0:T(8,128)(2,1)}, bf16[2,48,1664]{2,1,0:T(8,128)(2,1)}, u32[]{:S(2)}, u32[]{:S(2)}) collective-permute-start(bf16[2,48,1664]{2,1,0:T(8,128)(2,1)} %get-tuple-element.216), channel_id=1, source_target_pairs={{0,1},{1,0},{2,3},{3,2},{4,5},{5,4},{6,7},{7,6},{8,9},{9,8},{10,11... | collective-permute-start | bytes 958472 | tf_op jit(solution)/shard_map/ppermute | solution.py:63
  397.3 10.7 %collective-permute-start.48 = (bf16[4,48,2176]{2,1,0:T(8,128)(2,1)}, bf16[4,48,2176]{2,1,0:T(8,128)(2,1)S(1)}, u32[]{:S(2)}, u32[]{:S(2)}) collective-permute-start(bf16[4,48,2176]{2,1,0:T(8,128)(2,1)} %get-tuple-element.200), channel_id=1, source_target_pairs={{0,1},{1,0},{2,3},{3,2},{4,5},{5,4},{6,7},{7,6},{8,9},{9,8},{10,11... | collective-permute-start | bytes 2506760 | tf_op jit(solution)/shard_map/ppermute | solution.py:63
  398.8 21.4 %collective-permute-start.57 = (bf16[2,48,2176]{2,1,0:T(8,128)(2,1)}, bf16[2,48,2176]{2,1,0:T(8,128)(2,1)}, u32[]{:S(2)}, u32[]{:S(2)}) collective-permute-start(bf16[2,48,2176]{2,1,0:T(8,128)(2,1)} %fusion.5), channel_id=1, source_target_pairs={{0,8},{8,0},{16,24},{24,16},{1,9},{9,1},{17,25},{25,17},{2,10},{10... | collective-permute-start | bytes 1253384 | tf_op jit(solution)/shard_map/ppermute | solution.py:55
  400.7 21.4 %collective-permute-start.49 = (bf16[2,48,2176]{2,1,0:T(8,128)(2,1)}, bf16[2,48,2176]{2,1,0:T(8,128)(2,1)}, u32[]{:S(2)}, u32[]{:S(2)}) collective-permute-start(bf16[2,48,2176]{2,1,0:T(8,128)(2,1)} %fusion.6), channel_id=1, source_target_pairs={{0,16},{8,24},{16,0},{24,8},{1,17},{9,25},{17,1},{25,9},{2,18},{10... | collective-permute-start | bytes 1253384 | tf_op jit(solution)/shard_map/ppermute | solution.py:59
  404.4 66.0 %all-to-all-start.1 = ((bf16[1,2,128,1536]{3,1,0,2:T(2,128)(2,1)}), bf16[1,2,128,1536]{3,1,0,2:T(2,128)(2,1)S(1)}, u32[]{:S(2)}, u32[]{:S(2)}) async-start(bf16[1,2,128,1536]{3,1,0,2:T(2,128)(2,1)} %copy.79), calls=%async_computation.1 | async-start | bytes 1572864 | tf_op jit(solution)/shard_map/all_to_all | solution.py:1107
  408.0 51.5 %collective-permute-start.50 = (bf16[4,48,1664]{2,1,0:T(8,128)(2,1)}, bf16[4,48,1664]{2,1,0:T(8,128)(2,1)S(1)}, u32[]{:S(2)}, u32[]{:S(2)}) collective-permute-start(bf16[4,48,1664]{2,1,0:T(8,128)(2,1)} %get-tuple-element.208), channel_id=1, source_target_pairs={{0,1},{1,0},{2,3},{3,2},{4,5},{5,4},{6,7},{7,6},{8,9},{9,8},{10,11... | collective-permute-start | bytes 1916936 | tf_op jit(solution)/shard_map/ppermute | solution.py:63
  420.2 30.5 %collective-permute-start.62 = (bf16[2,2,48,1664]{3,2,1,0:T(8,128)(2,1)}, bf16[2,2,48,1664]{3,2,1,0:T(8,128)(2,1)S(1)}, u32[]{:S(2)}, u32[]{:S(2)}) collective-permute-start(bf16[2,2,48,1664]{3,2,1,0:T(8,128)(2,1)} %add_convert_fusion.11), channel_id=1, source_target_pairs={{0,16},{8,24},{16,0},{24,8},{1,17},{9,25},{17,1},{25,9},{2,18},{10... | collective-permute-start | bytes 1916936 | tf_op jit(solution)/shard_map/ppermute | solution.py:59
  422.1 32.3 %collective-permute-start.53 = (bf16[2,2,48,1664]{3,2,1,0:T(8,128)(2,1)}, bf16[2,2,48,1664]{3,2,1,0:T(8,128)(2,1)S(1)}, u32[]{:S(2)}, u32[]{:S(2)}) collective-permute-start(bf16[2,2,48,1664]{3,2,1,0:T(8,128)(2,1)} %add_convert_fusion.12), channel_id=1, source_target_pairs={{0,8},{8,0},{16,24},{24,16},{1,9},{9,1},{17,25},{25,17},{2,10},{10... | collective-permute-start | bytes 1916936 | tf_op jit(solution)/shard_map/ppermute | solution.py:55
  425.9 40.5 %collective-permute-start.56 = (bf16[48,2176]{1,0:T(8,128)(2,1)S(1)}, bf16[48,2176]{1,0:T(8,128)(2,1)S(1)}, u32[]{:S(2)}, u32[]{:S(2)}) collective-permute-start(bf16[48,2176]{1,0:T(8,128)(2,1)S(1)} %get-tuple-element.299), channel_id=1, source_target_pairs={{0,6},{1,7},{2,0},{3,1},{4,2},{5,3},{6,4},{7,5},{8,14},{9,15},{10,... | collective-permute-start | bytes 626696 | tf_op jit(solution)/shard_map/ppermute | solution.py:71
  450.8 7.6 %collective-permute-start.58 = (bf16[48,2176]{1,0:T(8,128)(2,1)S(1)}, bf16[48,2176]{1,0:T(8,128)(2,1)S(1)}, u32[]{:S(2)}, u32[]{:S(2)}) collective-permute-start(bf16[48,2176]{1,0:T(8,128)(2,1)S(1)} %get-tuple-element.304), channel_id=1, source_target_pairs={{0,2},{1,3},{2,4},{3,5},{4,6},{5,7},{6,0},{7,1},{8,10},{9,11},{10,... | collective-permute-start | bytes 626696 | tf_op jit(solution)/shard_map/ppermute | solution.py:67
  453.3 7.7 %collective-permute-start.63 = (bf16[2,48,1664]{2,1,0:T(8,128)(2,1)S(1)}, bf16[2,48,1664]{2,1,0:T(8,128)(2,1)S(1)}, u32[]{:S(2)}, u32[]{:S(2)}) collective-permute-start(bf16[2,48,1664]{2,1,0:T(8,128)(2,1)S(1)} %fusion.10), channel_id=1, source_target_pairs={{0,8},{8,0},{16,24},{24,16},{1,9},{9,1},{17,25},{25,17},{2,10},{10... | collective-permute-start | bytes 958472 | tf_op jit(solution)/shard_map/ppermute | solution.py:55
  455.4 7.4 %collective-permute-start.55 = (bf16[2,48,1664]{2,1,0:T(8,128)(2,1)S(1)}, bf16[2,48,1664]{2,1,0:T(8,128)(2,1)S(1)}, u32[]{:S(2)}, u32[]{:S(2)}) collective-permute-start(bf16[2,48,1664]{2,1,0:T(8,128)(2,1)S(1)} %fusion.11), channel_id=1, source_target_pairs={{0,16},{8,24},{16,0},{24,8},{1,17},{9,25},{17,1},{25,9},{2,18},{10... | collective-permute-start | bytes 958472 | tf_op jit(solution)/shard_map/ppermute | solution.py:59
  459.4 9.0 %collective-permute-start.59 = (bf16[48,2176]{1,0:T(8,128)(2,1)S(1)}, bf16[48,2176]{1,0:T(8,128)(2,1)S(1)}, u32[]{:S(2)}, u32[]{:S(2)}) collective-permute-start(bf16[48,2176]{1,0:T(8,128)(2,1)S(1)} %add_convert_fusion.17), channel_id=1, source_target_pairs={{0,2},{1,3},{2,4},{3,5},{4,6},{5,7},{6,0},{7,1},{8,10},{9,11},{10,... | collective-permute-start | bytes 626696 | tf_op jit(solution)/shard_map/ppermute | solution.py:67
  463.2 16.8 %collective-permute-start.60 = (bf16[48,1664]{1,0:T(8,128)(2,1)S(1)}, bf16[48,1664]{1,0:T(8,128)(2,1)S(1)}, u32[]{:S(2)}, u32[]{:S(2)}) collective-permute-start(bf16[48,1664]{1,0:T(8,128)(2,1)S(1)} %get-tuple-element.301), channel_id=1, source_target_pairs={{0,6},{1,7},{2,0},{3,1},{4,2},{5,3},{6,4},{7,5},{8,14},{9,15},{10,... | collective-permute-start | bytes 479240 | tf_op jit(solution)/shard_map/ppermute | solution.py:71
  465.8 14.2 %collective-permute-start.64 = (bf16[48,1664]{1,0:T(8,128)(2,1)S(1)}, bf16[48,1664]{1,0:T(8,128)(2,1)S(1)}, u32[]{:S(2)}, u32[]{:S(2)}) collective-permute-start(bf16[48,1664]{1,0:T(8,128)(2,1)S(1)} %get-tuple-element.306), channel_id=1, source_target_pairs={{0,2},{1,3},{2,4},{3,5},{4,6},{5,7},{6,0},{7,1},{8,10},{9,11},{10,... | collective-permute-start | bytes 479240 | tf_op jit(solution)/shard_map/ppermute | solution.py:67
  465.8 14.2 %collective-permute-start.65 = (bf16[48,1664]{1,0:T(8,128)(2,1)S(1)}, bf16[48,1664]{1,0:T(8,128)(2,1)S(1)}, u32[]{:S(2)}, u32[]{:S(2)}) collective-permute-start(bf16[48,1664]{1,0:T(8,128)(2,1)S(1)} %get-tuple-element.305), channel_id=1, source_target_pairs={{0,4},{1,5},{2,6},{3,7},{4,0},{5,1},{6,2},{7,3},{8,12},{9,13},{10,... | collective-permute-start | bytes 479240 | tf_op jit(solution)/shard_map/ppermute | solution.py:984
  (52 other events, 670.3 us)
Sparse Core Ops, SparseCore 0:
  289.8 164.8 reduce-scatter.1

commit v5 on v4

--- a/solution.py
+++ b/solution.py
@@ -535,27 +535,31 @@
 
 
 def weight_kernel(x_ref, dga_ref, dua_ref, hid_ref, dy_ref, out_ref):
+    group, _, _, step, ff = out_ref.shape
     dtype = jnp.bfloat16
-    out_ref[0, 0, 0] = dot_tn(x_ref[0], dga_ref[0]).astype(dtype)
-    out_ref[0, 1, 0] = dot_tn(x_ref[0], dua_ref[0]).astype(dtype)
-    ff = hid_ref.shape[2]
-    step = dy_ref.shape[2]
-    for i in range(ff // step):
-        part = dot_tn(hid_ref[0, :, i * step : (i + 1) * step], dy_ref[0])
-        out_ref[0, 2, 0, :, i * step : (i + 1) * step] = part.astype(dtype)
+    for i, right in enumerate((dga_ref, dua_ref)):
+        grads = dot_tn(x_ref[0], right[0]).astype(dtype)
+        for d in range(group):
+            out_ref[d, i, 0] = grads[d * step : (d + 1) * step]
+    grads = dot_tn(hid_ref[0], dy_ref[0]).astype(dtype)
+    for d in range(group):
+        for i in range(ff // step):
+            part = slice(i * step, (i + 1) * step)
+            out_ref[d, 2, 0, :, part] = grads[part, d * step : (d + 1) * step]
 
 
 def expert_weight_grads(x, dga, dua, hid, dy, parts):
     per_device, rows, ff = dga.shape
     step = x.shape[2] // parts
+    group = 2
     whole = pl.BlockSpec((1, rows, ff), lambda e, d: (e, 0, 0))
-    piece = pl.BlockSpec((1, rows, step), lambda e, d: (e, 0, d))
+    piece = pl.BlockSpec((1, rows, group * step), lambda e, d: (e, 0, d))
     return pl.pallas_call(
         weight_kernel,
-        grid=(per_device, parts),
+        grid=(per_device, parts // group),
         out_shape=jax.ShapeDtypeStruct((parts, 3, per_device, step, ff), jnp.bfloat16),
         in_specs=[piece, whole, whole, whole, piece],
-        out_specs=pl.BlockSpec((1, 3, 1, step, ff), lambda e, d: (d, 0, e, 0, 0)),
+        out_specs=pl.BlockSpec((group, 3, 1, step, ff), lambda e, d: (d, 0, e, 0, 0)),
         cost_estimate=pl.CostEstimate(
             flops=18700000000, transcendentals=0, bytes_accessed=17000000
         ),

time: 497 us -> 496 us (level)
  no operation moved by 1% of the time
where the time goes in v5:
time: 496 us; the launch traced here: 488 us
  waiting for transfers between devices  230 us (46%)
  Pallas kernels  104 us (21%)
  starting transfers between devices  62.4 us (13%)
  local copies, waits for them, and re-layouts  41.2 us (8%)
  other arithmetic  36.4 us (7%)
  between operations  15 us (3%)
    ppermute x12, waiting for transfers between devices, shift_up(): return lax.ppermute(value, 'expert', [(i, (i + 2) % 8) for i in range(8)])  69.8 us
    ppermute x10, waiting for transfers between devices, swap_x(): return lax.ppermute(value, 'dp', [(i, i ^ 1) for i in range(4)])  48.6 us
    pallas_call x1, Pallas kernels, run_experts(): pl.pallas_call(lambda *refs: expert_kernel(plan, capacity, *refs), out_sh...  47.2 us
    ppermute x7, waiting for transfers between devices, shift_down(): return lax.ppermute(value, 'expert', [(i, (i + 6) % 8) for i in range(8)])  45.5 us
    ppermute x10, waiting for transfers between devices, swap_y(): return lax.ppermute(value, 'dp', [(i, i ^ 2) for i in range(4)])  41.1 us
    pallas_call x1, Pallas kernels, run_backward(): pl.pallas_call(lambda *refs: backward_kernel(experts, len(backs), piece,...  25.4 us
    ppermute x7, starting transfers between devices, shift_down(): return lax.ppermute(value, 'expert', [(i, (i + 6) % 8) for i in range(8)])  18.6 us
    pallas_call x1, Pallas kernels, expert_weight_grads(): pl.pallas_call(weight_kernel, grid=(per_device, parts // group), out_shap...  16.5 us
  transfers between devices with their start and end apart: 69, of which 27 were waited for; matrix products, arithmetic and copies ran while one was open for 15% of the time, Pallas kernels for 12%

profile of v5, /device:TPU:0, one launch (start us, length us, event | category | flops | bytes accessed | tf_op | source)
XLA Modules:
  0.0 488.2 jit_solution(6102018189503815410)
XLA Ops:
  7.2 3.0 collective-permute-start.4
  10.2 1.5 collective-permute-start.3
  17.6 1.6 collective-permute-start
  19.2 2.2 collective-permute-start.1
  22.2 1.5 copy.75
  24.7 1.5 copy.76
  28.3 8.2 %collective-permute-done.4.refs_12_ = bf16[2,768,384]{2,1,0:T(8,128)(2,1)} collective-permute-done((bf16[2,768,384]{2,1,0:T(8,128)(2,1)}, bf16[2,768,384]{2,1,0:T(8,128)(2,1)}, u32[]{:S(2)}, u32[]{:S(2)}) %collective-permute-start.4) | collective-permute-done | bytes 1179680 | tf_op jit(solution)/shard_map/ppermute | solution.py:59
  37.6 1.8 collective-permute-start.5
  40.5 1.6 collective-permute-start.6
  42.1 1.6 pad_maximum_fusion.refs_5_
  43.8 9.3 %collective-permute-done.2 = bf16[48,3840]{1,0:T(8,128)(2,1)} collective-permute-done((bf16[48,3840]{1,0:T(8,128)(2,1)S(1)}, bf16[48,3840]{1,0:T(8,128)(2,1)}, u32[]{:S(2)}, u32[]{:S(2)}) %collective-permute-start.2) | collective-permute-done | bytes 368672 | tf_op jit(solution)/shard_map/ppermute | solution.py:988
  53.1 2.5 pad_maximum_fusion.1.refs_6_
  58.3 1.5 collective-permute-start.14
  59.9 2.4 collective-permute-start.15
  62.3 27.9 %collective-permute-done.7.refs_7_ = bf16[4,48,3840]{2,1,0:T(8,128)(2,1)} collective-permute-done((bf16[4,48,3840]{2,1,0:T(8,128)(2,1)}, bf16[4,48,3840]{2,1,0:T(8,128)(2,1)}, u32[]{:S(2)}, u32[]{:S(2)}) %collective-permute-start.7) | collective-permute-done | bytes 1474592 | tf_op jit(solution)/shard_map/ppermute | solution.py:55
  90.2 2.0 slice.314
  92.7 2.0 slice.313
  96.9 1.5 gather_fusion.1
  98.4 3.7 all-to-all-start
  103.3 6.7 %collective-permute-done.10.refs_10_ = bf16[2,48,3840]{2,1,0:T(8,128)(2,1)} collective-permute-done((bf16[2,48,3840]{2,1,0:T(8,128)(2,1)}, bf16[2,48,3840]{2,1,0:T(8,128)(2,1)}, u32[]{:S(2)}, u32[]{:S(2)}) %collective-permute-start.10) | collective-permute-done | bytes 737312 | tf_op jit(solution)/shard_map/ppermute | solution.py:59
  110.1 2.3 collective-permute-done.9.refs_9_
  116.4 6.7 %all-to-all-done = bf16[8,2,16,1536]{3,2,1,0:T(8,128)(2,1)S(1)} async-done(((bf16[8,2,16,1536]{3,2,1,0:T(8,128)(2,1)}), bf16[8,2,16,1536]{3,2,1,0:T(8,128)(2,1)S(1)}, u32[]{:S(2)}, u32[]{:S(2)}) %all-to-all-start) | async-done | bytes 786464 | tf_op jit(solution)/shard_map/all_to_all | solution.py:1012
  125.1 1.5 collective-permute-start.21
  126.7 14.6 %shard_map.247 = (bf16[256,1536]{1,0:T(8,128)(2,1)}, f32[256,1536]{1,0:T(8,128)}, bf16[256,1536]{1,0:T(8,128)(2,1)}, bf16[256,1536]{1,0:T(8,128)(2,1)}, bf16[256...) custom-call(s32[32]{0:T(128)} %stack.218.refs_0_, ...), custom_call_target="tpu_custom_call" | custom-call | flops 109999996928 | bytes 16000000 | tf_op jit(solution)/shard_map/pallas_call | solution.py:755
  141.4 3.7 collective-permute-start.19
  145.1 2.4 collective-permute-done.29.refs_26_.refs_5_
  147.6 16.7 %collective-permute-done.18.refs_16_ = bf16[256,1536]{1,0:T(8,128)(2,1)} collective-permute-done((bf16[256,1536]{1,0:T(8,128)(2,1)}, bf16[256,1536]{1,0:T(8,128)(2,1)}, u32[]{:S(2)}, u32[]{:S(2)}) %collective-permute-start.18) | collective-permute-done | bytes 786464 | tf_op jit(solution)/shard_map/ppermute | solution.py:67
  164.3 15.7 %collective-permute-done.19.refs_17_ = bf16[256,1536]{1,0:T(8,128)(2,1)} collective-permute-done((bf16[256,1536]{1,0:T(8,128)(2,1)}, bf16[256,1536]{1,0:T(8,128)(2,1)}, u32[]{:S(2)}, u32[]{:S(2)}) %collective-permute-start.19) | collective-permute-done | bytes 786464 | tf_op jit(solution)/shard_map/ppermute | solution.py:71
  185.0 1.5 collective-permute-start.23
  187.5 16.5 %collective-permute-done.24.refs_18_ = bf16[256,1536]{1,0:T(8,128)(2,1)} collective-permute-done((bf16[256,1536]{1,0:T(8,128)(2,1)}, bf16[256,1536]{1,0:T(8,128)(2,1)}, u32[]{:S(2)}, u32[]{:S(2)}) %collective-permute-start.24) | collective-permute-done | bytes 786464 | tf_op jit(solution)/shard_map/ppermute | solution.py:67
  205.7 1.5 slice.436.refs_1_
  207.2 5.0 %collective-permute-done.22.refs_8_ = bf16[2,384,768]{2,1,0:T(8,128)(2,1)} collective-permute-done((bf16[2,384,768]{2,1,0:T(8,128)(2,1)S(1)}, bf16[2,384,768]{2,1,0:T(8,128)(2,1)}, u32[]{:S(2)}, u32[]{:S(2)}) %collective-permute-start.22) | collective-permute-done | bytes 1179680 | tf_op jit(solution)/shard_map/ppermute | solution.py:55
  213.6 47.2 %shard_map.248 = (bf16[4,272,1536]{2,1,0:T(8,128)(2,1)}, bf16[4,272,1536]{2,1,0:T(8,128)(2,1)}, bf16[4,256,1536]{2,1,0:T(8,128)(2,1)}, bf16[4,256,1536]{2,1,0:T(...) custom-call(s32[34]{0:T(128)} %concatenate.43.refs_0_.refs_1_, ...), custom_call_target="tpu_custom_call" | custom-call | flops 54999998464 | bytes 50000000 | tf_op jit(solution)/shard_map/pallas_call | solution.py:495
  260.9 6.1 %collective-permute-done.34 = bf16[4,272,1536]{2,1,0:T(8,128)(2,1)S(1)} collective-permute-done((bf16[4,272,1536]{2,1,0:T(8,128)(2,1)}, bf16[4,272,1536]{2,1,0:T(8,128)(2,1)S(1)}, u32[]{:S(2)}, u32[]{:S(2)}) %collective-permute-start.34) | collective-permute-done | bytes 3342368 | tf_op jit(solution)/shard_map/ppermute | solution.py:63
  267.2 4.2 fusion.3
  272.0 16.5 %shard_map.249 = bf16[4,3,2,384,768]{4,3,2,1,0:T(8,128)(2,1)} custom-call(bf16[2,576,1536]{2,1,0:T(8,128)(2,1)} %get-tuple-element.151.x_ref, bf16[2,576,768]{2,1,0:T(8,128)(2,1)} %get-tuple-element.152.dga_ref, bf16[2,576,768]{2,1,0:T(8,128)(2,1)} %get-tuple-element.153.dua_ref, bf16[2,576,768]{2,1,0:T(8,128)(2,1)} %get-tuple-element.154.hid_ref, ...), custom_call_target="tpu_custom_call" | custom-call | flops 18699999232 | bytes 17000000 | tf_op jit(solution)/shard_map/pallas_call | solution.py:557
  288.6 3.3 collective-permute-start.35
  291.8 2.8 collective-permute-done.37
  294.9 17.7 %collective-permute-done.35.refs_11_ = bf16[272,1536]{1,0:T(8,128)(2,1)S(1)} collective-permute-done((bf16[272,1536]{1,0:T(8,128)(2,1)S(1)}, bf16[272,1536]{1,0:T(8,128)(2,1)S(1)}, u32[]{:S(2)}, u32[]{:S(2)}) %collective-permute-start.35) | collective-permute-done | bytes 835616 | tf_op jit(solution)/shard_map/ppermute | solution.py:71
  313.5 5.3 %fusion.9 = (bf16[256,1536]{1,0:T(8,128)(2,1)}, bf16[256,1536]{1,0:T(8,128)(2,1)}, bf16[256,1536]{1,0:T(8,128)(2,1)}, f32[256,1536]{1,0:T(8,128)}) fusion(bf16[4,256,1536]{2,1,0:T(8,128)(2,1)} %collective-permute-done.36, bf16[4,256,1536]{2,1,0:T(8,128)(2,1)} %get-tuple-element.146), kind=kLoop, calls=%fused_computation.39 | loop fusion | flops 5898240 | bytes 10223616 | tf_op jit(solution)/shard_map/convert_element_type | solution.py:1095
  318.9 11.2 %collective-permute-done.38.refs_12_ = bf16[272,1536]{1,0:T(8,128)(2,1)S(1)} collective-permute-done((bf16[272,1536]{1,0:T(8,128)(2,1)S(1)}, bf16[272,1536]{1,0:T(8,128)(2,1)S(1)}, u32[]{:S(2)}, u32[]{:S(2)}) %collective-permute-start.38) | collective-permute-done | bytes 835616 | tf_op jit(solution)/shard_map/ppermute | solution.py:67
  331.0 25.4 %shard_map.250 = (bf16[2,2,48,2176]{3,2,1,0:T(8,128)(2,1)}, bf16[2,2,48,2176]{3,2,1,0:T(8,128)(2,1)}, bf16[2,48,2176]{2,1,0:T(8,128)(2,1)}, bf16[2,48,2176]{2,1,...) custom-call(s32[32]{0:T(128)} %stack.218.refs_0_, ...), custom_call_target="tpu_custom_call" | custom-call | flops 165000003584 | bytes 32000000 | tf_op jit(solution)/shard_map/pallas_call | solution.py:950
  356.5 1.5 add_convert_fusion.7
  358.6 3.0 collective-permute-start.46
  362.6 2.2 collective-permute-done.40
  364.8 1.4 collective-permute-start.43
  368.5 11.1 %collective-permute-done.46 = bf16[256,1536]{1,0:T(8,128)(2,1)S(1)} collective-permute-done((bf16[256,1536]{1,0:T(8,128)(2,1)S(1)}, bf16[256,1536]{1,0:T(8,128)(2,1)S(1)}, u32[]{:S(2)}, u32[]{:S(2)}) %collective-permute-start.46) | collective-permute-done | bytes 786464 | tf_op jit(solution)/shard_map/ppermute | solution.py:71
  379.5 16.7 %collective-permute-done.47 = bf16[256,1536]{1,0:T(8,128)(2,1)S(1)} collective-permute-done((bf16[256,1536]{1,0:T(8,128)(2,1)S(1)}, bf16[256,1536]{1,0:T(8,128)(2,1)S(1)}, u32[]{:S(2)}, u32[]{:S(2)}) %collective-permute-start.47) | collective-permute-done | bytes 786464 | tf_op jit(solution)/shard_map/ppermute | solution.py:67
  401.8 1.7 copy.79
  403.5 3.5 all-to-all-start.1
  407.5 11.7 %collective-permute-done.57 = bf16[2,48,2176]{2,1,0:T(8,128)(2,1)} collective-permute-done((bf16[2,48,2176]{2,1,0:T(8,128)(2,1)}, bf16[2,48,2176]{2,1,0:T(8,128)(2,1)}, u32[]{:S(2)}, u32[]{:S(2)}) %collective-permute-start.57) | collective-permute-done | bytes 417824 | tf_op jit(solution)/shard_map/ppermute | solution.py:55
  422.0 1.6 convert_add_fusion.6
  424.8 1.8 collective-permute-start.56
  426.7 23.1 %collective-permute-done.62 = bf16[2,2,48,1664]{3,2,1,0:T(8,128)(2,1)S(1)} collective-permute-done((bf16[2,2,48,1664]{3,2,1,0:T(8,128)(2,1)}, bf16[2,2,48,1664]{3,2,1,0:T(8,128)(2,1)S(1)}, u32[]{:S(2)}, u32[]{:S(2)}) %collective-permute-start.62) | collective-permute-done | bytes 639008 | tf_op jit(solution)/shard_map/ppermute | solution.py:59
  449.7 1.7 collective-permute-start.58
  458.5 1.8 collective-permute-done.63
  460.3 1.9 collective-permute-done.55
  462.6 2.2 collective-permute-start.60
  465.4 2.0 collective-permute-done.59
  469.6 1.5 gather_fusion.3
  472.4 1.8 fusion.26
  474.2 1.6 convert.35
  475.8 1.6 convert.36
  477.4 1.6 maximum_convert_fusion
  (273 shorter events, 64.2 us)
Async XLA Ops:
  7.2 29.3 %collective-permute-start.4 = (bf16[2,768,384]{2,1,0:T(8,128)(2,1)}, bf16[2,768,384]{2,1,0:T(8,128)(2,1)}, u32[]{:S(2)}, u32[]{:S(2)}) collective-permute-start(bf16[2,768,384]{2,1,0:T(8,128)(2,1)} %refs_10_.1), channel_id=1, source_target_pairs={{0,16},{8,24},{16,0},{24,8},{1,17},{9,25},{17,1},{25,9},{2,18},{10... | collective-permute-start | bytes 3538952 | tf_op jit(solution)/shard_map/ppermute | solution.py:59
  10.2 29.2 %collective-permute-start.3 = (bf16[2,768,384]{2,1,0:T(8,128)(2,1)}, bf16[2,768,384]{2,1,0:T(8,128)(2,1)}, u32[]{:S(2)}, u32[]{:S(2)}) collective-permute-start(bf16[2,768,384]{2,1,0:T(8,128)(2,1)} %refs_10_.1), channel_id=1, source_target_pairs={{0,8},{8,0},{16,24},{24,16},{1,9},{9,1},{17,25},{25,17},{2,10},{10... | collective-permute-start | bytes 3538952 | tf_op jit(solution)/shard_map/ppermute | solution.py:55
  17.6 26.2 %collective-permute-start = (bf16[48,3840]{1,0:T(8,128)(2,1)S(1)}, bf16[48,3840]{1,0:T(8,128)(2,1)}, u32[]{:S(2)}, u32[]{:S(2)}) collective-permute-start(bf16[48,3840]{1,0:T(8,128)(2,1)S(1)} %fusion.22), channel_id=1, source_target_pairs={{0,2},{1,3},{2,4},{3,5},{4,6},{5,7},{6,0},{7,1},{8,10},{9,11},{10,... | collective-permute-start | bytes 1105928 | tf_op jit(solution)/shard_map/ppermute | solution.py:67
  19.2 24.6 %collective-permute-start.1 = (bf16[48,3840]{1,0:T(8,128)(2,1)S(1)}, bf16[48,3840]{1,0:T(8,128)(2,1)}, u32[]{:S(2)}, u32[]{:S(2)}) collective-permute-start(bf16[48,3840]{1,0:T(8,128)(2,1)S(1)} %fusion.22), channel_id=1, source_target_pairs={{0,6},{1,7},{2,0},{3,1},{4,2},{5,3},{6,4},{7,5},{8,14},{9,15},{10,... | collective-permute-start | bytes 1105928 | tf_op jit(solution)/shard_map/ppermute | solution.py:71
  21.4 31.6 %collective-permute-start.2 = (bf16[48,3840]{1,0:T(8,128)(2,1)S(1)}, bf16[48,3840]{1,0:T(8,128)(2,1)}, u32[]{:S(2)}, u32[]{:S(2)}) collective-permute-start(bf16[48,3840]{1,0:T(8,128)(2,1)S(1)} %fusion.22), channel_id=1, source_target_pairs={{0,4},{1,5},{2,6},{3,7},{4,0},{5,1},{6,2},{7,3},{8,12},{9,13},{10,... | collective-permute-start | bytes 1105928 | tf_op jit(solution)/shard_map/ppermute | solution.py:988
  37.6 17.9 %collective-permute-start.5 = (bf16[1,768,384]{2,1,0:T(8,128)(2,1)S(1)}, bf16[1,768,384]{2,1,0:T(8,128)(2,1)S(1)}, u32[]{:S(2)}, u32[]{:S(2)}) collective-permute-start(bf16[1,768,384]{2,1,0:T(8,128)(2,1)S(1)} %slice.311), channel_id=1, source_target_pairs={{0,8},{8,0},{16,24},{24,16},{1,9},{9,1},{17,25},{25,17},{2,10},{10... | collective-permute-start | bytes 1769480 | tf_op jit(solution)/shard_map/ppermute | solution.py:55
  40.5 15.0 %collective-permute-start.6 = (bf16[1,768,384]{2,1,0:T(8,128)(2,1)S(1)}, bf16[1,768,384]{2,1,0:T(8,128)(2,1)S(1)}, u32[]{:S(2)}, u32[]{:S(2)}) collective-permute-start(bf16[1,768,384]{2,1,0:T(8,128)(2,1)S(1)} %slice.312), channel_id=1, source_target_pairs={{0,16},{8,24},{16,0},{24,8},{1,17},{9,25},{17,1},{25,9},{2,18},{10... | collective-permute-start | bytes 1769480 | tf_op jit(solution)/shard_map/ppermute | solution.py:59
  55.6 34.6 %collective-permute-start.7 = (bf16[4,48,3840]{2,1,0:T(8,128)(2,1)}, bf16[4,48,3840]{2,1,0:T(8,128)(2,1)}, u32[]{:S(2)}, u32[]{:S(2)}) collective-permute-start(bf16[4,48,3840]{2,1,0:T(8,128)(2,1)} %pad_maximum_fusion.1.refs_6_), channel_id=1, source_target_pairs={{0,8},{8,0},{16,24},{24,16},{1,9},{9,1},{17,25},{25,17},{2,10},{10... | collective-permute-start | bytes 4423688 | tf_op jit(solution)/shard_map/ppermute | solution.py:55
  56.2 36.5 %collective-permute-start.8 = (bf16[4,48,3840]{2,1,0:T(8,128)(2,1)}, bf16[4,48,3840]{2,1,0:T(8,128)(2,1)}, u32[]{:S(2)}, u32[]{:S(2)}) collective-permute-start(bf16[4,48,3840]{2,1,0:T(8,128)(2,1)} %pad_maximum_fusion.1.refs_6_), channel_id=1, source_target_pairs={{0,16},{8,24},{16,0},{24,8},{1,17},{9,25},{17,1},{25,9},{2,18},{10... | collective-permute-start | bytes 4423688 | tf_op jit(solution)/shard_map/ppermute | solution.py:59
  58.3 37.0 %collective-permute-start.14 = (bf16[272,1536]{1,0:T(8,128)(2,1)S(1)}, bf16[272,1536]{1,0:T(8,128)(2,1)S(1)}, u32[]{:S(2)}, u32[]{:S(2)}) collective-permute-start(bf16[272,1536]{1,0:T(8,128)(2,1)S(1)} %fusion.1.refs_23_.refs_2_), channel_id=1, source_target_pairs={{0,2},{1,3},{2,4},{3,5},{4,6},{5,7},{6,0},{7,1},{8,10},{9,11},{10,... | collective-permute-start | bytes 2506760 | tf_op jit(solution)/shard_map/ppermute | solution.py:67
  59.9 37.0 %collective-permute-start.15 = (bf16[272,1536]{1,0:T(8,128)(2,1)S(1)}, bf16[272,1536]{1,0:T(8,128)(2,1)}, u32[]{:S(2)}, u32[]{:S(2)}) collective-permute-start(bf16[272,1536]{1,0:T(8,128)(2,1)S(1)} %fusion.1.refs_23_.refs_2_), channel_id=1, source_target_pairs={{0,6},{1,7},{2,0},{3,1},{4,2},{5,3},{6,4},{7,5},{8,14},{9,15},{10,... | collective-permute-start | bytes 2506760 | tf_op jit(solution)/shard_map/ppermute | solution.py:71
  92.2 17.9 %collective-permute-start.10 = (bf16[2,48,3840]{2,1,0:T(8,128)(2,1)}, bf16[2,48,3840]{2,1,0:T(8,128)(2,1)}, u32[]{:S(2)}, u32[]{:S(2)}) collective-permute-start(bf16[2,48,3840]{2,1,0:T(8,128)(2,1)} %slice.314), channel_id=1, source_target_pairs={{0,16},{8,24},{16,0},{24,8},{1,17},{9,25},{17,1},{25,9},{2,18},{10... | collective-permute-start | bytes 2211848 | tf_op jit(solution)/shard_map/ppermute | solution.py:59
  94.7 17.6 %collective-permute-start.9 = (bf16[2,48,3840]{2,1,0:T(8,128)(2,1)}, bf16[2,48,3840]{2,1,0:T(8,128)(2,1)}, u32[]{:S(2)}, u32[]{:S(2)}) collective-permute-start(bf16[2,48,3840]{2,1,0:T(8,128)(2,1)} %slice.313), channel_id=1, source_target_pairs={{0,8},{8,0},{16,24},{24,16},{1,9},{9,1},{17,25},{25,17},{2,10},{10... | collective-permute-start | bytes 2211848 | tf_op jit(solution)/shard_map/ppermute | solution.py:55
  95.4 28.7 %collective-permute-start.11 = (bf16[4,48,3840]{2,1,0:T(8,128)(2,1)}, bf16[4,48,3840]{2,1,0:T(8,128)(2,1)}, u32[]{:S(2)}, u32[]{:S(2)}) collective-permute-start(bf16[4,48,3840]{2,1,0:T(8,128)(2,1)} %pad_maximum_fusion.1.refs_6_), channel_id=1, source_target_pairs={{0,1},{1,0},{2,3},{3,2},{4,5},{5,4},{6,7},{7,6},{8,9},{9,8},{10,11... | collective-permute-start | bytes 4423688 | tf_op jit(solution)/shard_map/ppermute | solution.py:63
  95.4 31.3 %collective-permute-start.12 = (bf16[4,48,3840]{2,1,0:T(8,128)(2,1)}, bf16[4,48,3840]{2,1,0:T(8,128)(2,1)}, u32[]{:S(2)}, u32[]{:S(2)}) collective-permute-start(bf16[4,48,3840]{2,1,0:T(8,128)(2,1)} %collective-permute-done.7.refs_7_), channel_id=1, source_target_pairs={{0,1},{1,0},{2,3},{3,2},{4,5},{5,4},{6,7},{7,6},{8,9},{9,8},{10,11... | collective-permute-start | bytes 4423688 | tf_op jit(solution)/shard_map/ppermute | solution.py:63
  96.9 29.8 %collective-permute-start.13 = (bf16[4,48,3840]{2,1,0:T(8,128)(2,1)}, bf16[4,48,3840]{2,1,0:T(8,128)(2,1)}, u32[]{:S(2)}, u32[]{:S(2)}) collective-permute-start(bf16[4,48,3840]{2,1,0:T(8,128)(2,1)} %collective-permute-done.8.refs_8_), channel_id=1, source_target_pairs={{0,1},{1,0},{2,3},{3,2},{4,5},{5,4},{6,7},{7,6},{8,9},{9,8},{10,11... | collective-permute-start | bytes 4423688 | tf_op jit(solution)/shard_map/ppermute | solution.py:63
  98.4 24.7 %all-to-all-start = ((bf16[8,2,16,1536]{3,2,1,0:T(8,128)(2,1)}), bf16[8,2,16,1536]{3,2,1,0:T(8,128)(2,1)S(1)}, u32[]{:S(2)}, u32[]{:S(2)}) async-start(bf16[8,2,16,1536]{3,2,1,0:T(8,128)(2,1)} %bitcast.53), calls=%async_computation | async-start | bytes 1572864 | tf_op jit(solution)/shard_map/all_to_all | solution.py:1012
  102.1 369.0 %reduce-scatter.2.cloned.1.call-start = ((), (), s32[]{:S(2)}) async-start(), calls=%async_computation.3 | async-start | bytes 17694720 | tf_op jit(solution)/shard_map/reduce_scatter | solution.py:1249
  112.4 11.7 %collective-permute-start.16 = (bf16[2,48,3840]{2,1,0:T(8,128)(2,1)}, bf16[2,48,3840]{2,1,0:T(8,128)(2,1)}, u32[]{:S(2)}, u32[]{:S(2)}) collective-permute-start(bf16[2,48,3840]{2,1,0:T(8,128)(2,1)} %collective-permute-done.9.refs_9_), channel_id=1, source_target_pairs={{0,1},{1,0},{2,3},{3,2},{4,5},{5,4},{6,7},{7,6},{8,9},{9,8},{10,11... | collective-permute-start | bytes 2211848 | tf_op jit(solution)/shard_map/ppermute | solution.py:63
  112.4 12.8 %collective-permute-start.17 = (bf16[2,48,3840]{2,1,0:T(8,128)(2,1)}, bf16[2,48,3840]{2,1,0:T(8,128)(2,1)}, u32[]{:S(2)}, u32[]{:S(2)}) collective-permute-start(bf16[2,48,3840]{2,1,0:T(8,128)(2,1)} %collective-permute-done.10.refs_10_), channel_id=1, source_target_pairs={{0,1},{1,0},{2,3},{3,2},{4,5},{5,4},{6,7},{7,6},{8,9},{9,8},{10,11... | collective-permute-start | bytes 2211848 | tf_op jit(solution)/shard_map/ppermute | solution.py:63
  124.0 23.5 %collective-permute-start.29 = (bf16[272,1536]{1,0:T(8,128)(2,1)}, bf16[272,1536]{1,0:T(8,128)(2,1)}, u32[]{:S(2)}, u32[]{:S(2)}) collective-permute-start(bf16[272,1536]{1,0:T(8,128)(2,1)} %copy-done.31), channel_id=1, source_target_pairs={{0,2},{1,3},{2,4},{3,5},{4,6},{5,7},{6,0},{7,1},{8,10},{9,11},{10,... | collective-permute-start | bytes 2506760 | tf_op jit(solution)/shard_map/ppermute | solution.py:67
  124.1 56.0 %collective-permute-start.20 = (bf16[2,2,384,768]{3,2,1,0:T(8,128)(2,1)S(1)}, bf16[2,2,384,768]{3,2,1,0:T(8,128)(2,1)S(1)}, u32[]{:S(2)}, u32[]{:S(2)}) collective-permute-start(bf16[2,2,384,768]{3,2,1,0:T(8,128)(2,1)S(1)} %copy-done.4), channel_id=1, source_target_pairs={{0,8},{8,0},{16,24},{24,16},{1,9},{9,1},{17,25},{25,17},{2,10},{10... | collective-permute-start | bytes 7077896 | tf_op jit(solution)/shard_map/ppermute | solution.py:55
  125.1 55.4 %collective-permute-start.21 = (bf16[2,2,384,768]{3,2,1,0:T(8,128)(2,1)S(1)}, bf16[2,2,384,768]{3,2,1,0:T(8,128)(2,1)}, u32[]{:S(2)}, u32[]{:S(2)}) collective-permute-start(bf16[2,2,384,768]{3,2,1,0:T(8,128)(2,1)S(1)} %copy-done.4), channel_id=1, source_target_pairs={{0,16},{8,24},{16,0},{24,8},{1,17},{9,25},{17,1},{25,9},{2,18},{10... | collective-permute-start | bytes 7077896 | tf_op jit(solution)/shard_map/ppermute | solution.py:59
  141.3 23.1 %collective-permute-start.18 = (bf16[256,1536]{1,0:T(8,128)(2,1)}, bf16[256,1536]{1,0:T(8,128)(2,1)}, u32[]{:S(2)}, u32[]{:S(2)}) collective-permute-start(bf16[256,1536]{1,0:T(8,128)(2,1)} %get-tuple-element.138.refs_15_.refs_14_), channel_id=1, source_target_pairs={{0,2},{1,3},{2,4},{3,5},{4,6},{5,7},{6,0},{7,1},{8,10},{9,11},{10,... | collective-permute-start | bytes 2359304 | tf_op jit(solution)/shard_map/ppermute | solution.py:67
  141.4 38.5 %collective-permute-start.19 = (bf16[256,1536]{1,0:T(8,128)(2,1)}, bf16[256,1536]{1,0:T(8,128)(2,1)}, u32[]{:S(2)}, u32[]{:S(2)}) collective-permute-start(bf16[256,1536]{1,0:T(8,128)(2,1)} %get-tuple-element.138.refs_15_.refs_14_), channel_id=1, source_target_pairs={{0,6},{1,7},{2,0},{3,1},{4,2},{5,3},{6,4},{7,5},{8,14},{9,15},{10,... | collective-permute-start | bytes 2359304 | tf_op jit(solution)/shard_map/ppermute | solution.py:71
  147.6 33.0 %collective-permute-start.30 = (bf16[272,1536]{1,0:T(8,128)(2,1)S(1)}, bf16[272,1536]{1,0:T(8,128)(2,1)S(1)}, u32[]{:S(2)}, u32[]{:S(2)}) collective-permute-start(bf16[272,1536]{1,0:T(8,128)(2,1)S(1)} %copy-done.12), channel_id=1, source_target_pairs={{0,1},{1,0},{2,3},{3,2},{4,5},{5,4},{6,7},{7,6},{8,9},{9,8},{10,11... | collective-permute-start | bytes 2506760 | tf_op jit(solution)/shard_map/ppermute | solution.py:63
  164.3 19.6 %collective-permute-start.31 = (bf16[272,1536]{1,0:T(8,128)(2,1)S(1)}, bf16[272,1536]{1,0:T(8,128)(2,1)S(1)}, u32[]{:S(2)}, u32[]{:S(2)}) collective-permute-start(bf16[272,1536]{1,0:T(8,128)(2,1)S(1)} %copy-done.32), channel_id=1, source_target_pairs={{0,1},{1,0},{2,3},{3,2},{4,5},{5,4},{6,7},{7,6},{8,9},{9,8},{10,11... | collective-permute-start | bytes 2506760 | tf_op jit(solution)/shard_map/ppermute | solution.py:63
  180.0 6.5 %collective-permute-start.33 = (bf16[272,1536]{1,0:T(8,128)(2,1)}, bf16[272,1536]{1,0:T(8,128)(2,1)S(1)}, u32[]{:S(2)}, u32[]{:S(2)}) collective-permute-start(bf16[272,1536]{1,0:T(8,128)(2,1)} %collective-permute-done.29.refs_26_.refs_5_), channel_id=1, source_target_pairs={{0,1},{1,0},{2,3},{3,2},{4,5},{5,4},{6,7},{7,6},{8,9},{9,8},{10,11... | collective-permute-start | bytes 2506760 | tf_op jit(solution)/shard_map/ppermute | solution.py:63
  180.5 7.0 %collective-permute-start.25 = (bf16[256,1536]{1,0:T(8,128)(2,1)}, bf16[256,1536]{1,0:T(8,128)(2,1)S(1)}, u32[]{:S(2)}, u32[]{:S(2)}) collective-permute-start(bf16[256,1536]{1,0:T(8,128)(2,1)} %get-tuple-element.138.refs_15_.refs_14_), channel_id=1, source_target_pairs={{0,1},{1,0},{2,3},{3,2},{4,5},{5,4},{6,7},{7,6},{8,9},{9,8},{10,11... | collective-permute-start | bytes 2359304 | tf_op jit(solution)/shard_map/ppermute | solution.py:63
  181.7 22.2 %collective-permute-start.24 = (bf16[256,1536]{1,0:T(8,128)(2,1)}, bf16[256,1536]{1,0:T(8,128)(2,1)}, u32[]{:S(2)}, u32[]{:S(2)}) collective-permute-start(bf16[256,1536]{1,0:T(8,128)(2,1)} %collective-permute-done.18.refs_16_), channel_id=1, source_target_pairs={{0,2},{1,3},{2,4},{3,5},{4,6},{5,7},{6,0},{7,1},{8,10},{9,11},{10,... | collective-permute-start | bytes 2359304 | tf_op jit(solution)/shard_map/ppermute | solution.py:67
  183.9 28.3 %collective-permute-start.22 = (bf16[2,384,768]{2,1,0:T(8,128)(2,1)S(1)}, bf16[2,384,768]{2,1,0:T(8,128)(2,1)}, u32[]{:S(2)}, u32[]{:S(2)}) collective-permute-start(bf16[2,384,768]{2,1,0:T(8,128)(2,1)S(1)} %slice_bitcast_fusion.1), channel_id=1, source_target_pairs={{0,8},{8,0},{16,24},{24,16},{1,9},{9,1},{17,25},{25,17},{2,10},{10... | collective-permute-start | bytes 3538952 | tf_op jit(solution)/shard_map/ppermute | solution.py:55
  185.0 27.9 %collective-permute-start.23 = (bf16[2,384,768]{2,1,0:T(8,128)(2,1)S(1)}, bf16[2,384,768]{2,1,0:T(8,128)(2,1)}, u32[]{:S(2)}, u32[]{:S(2)}) collective-permute-start(bf16[2,384,768]{2,1,0:T(8,128)(2,1)S(1)} %slice_bitcast_fusion), channel_id=1, source_target_pairs={{0,16},{8,24},{16,0},{24,8},{1,17},{9,25},{17,1},{25,9},{2,18},{10... | collective-permute-start | bytes 3538952 | tf_op jit(solution)/shard_map/ppermute | solution.py:59
  186.6 20.6 %collective-permute-start.26 = (bf16[256,1536]{1,0:T(8,128)(2,1)}, bf16[256,1536]{1,0:T(8,128)(2,1)}, u32[]{:S(2)}, u32[]{:S(2)}) collective-permute-start(bf16[256,1536]{1,0:T(8,128)(2,1)} %collective-permute-done.18.refs_16_), channel_id=1, source_target_pairs={{0,1},{1,0},{2,3},{3,2},{4,5},{5,4},{6,7},{7,6},{8,9},{9,8},{10,11... | collective-permute-start | bytes 2359304 | tf_op jit(solution)/shard_map/ppermute | solution.py:63
  187.5 19.7 %collective-permute-start.27 = (bf16[256,1536]{1,0:T(8,128)(2,1)}, bf16[256,1536]{1,0:T(8,128)(2,1)}, u32[]{:S(2)}, u32[]{:S(2)}) collective-permute-start(bf16[256,1536]{1,0:T(8,128)(2,1)} %collective-permute-done.19.refs_17_), channel_id=1, source_target_pairs={{0,1},{1,0},{2,3},{3,2},{4,5},{5,4},{6,7},{7,6},{8,9},{9,8},{10,11... | collective-permute-start | bytes 2359304 | tf_op jit(solution)/shard_map/ppermute | solution.py:63
  204.0 9.0 %collective-permute-start.28 = (bf16[256,1536]{1,0:T(8,128)(2,1)}, bf16[256,1536]{1,0:T(8,128)(2,1)}, u32[]{:S(2)}, u32[]{:S(2)}) collective-permute-start(bf16[256,1536]{1,0:T(8,128)(2,1)} %collective-permute-done.24.refs_18_), channel_id=1, source_target_pairs={{0,1},{1,0},{2,3},{3,2},{4,5},{5,4},{6,7},{7,6},{8,9},{9,8},{10,11... | collective-permute-start | bytes 2359304 | tf_op jit(solution)/shard_map/ppermute | solution.py:63
  260.8 6.2 %collective-permute-start.34 = (bf16[4,272,1536]{2,1,0:T(8,128)(2,1)}, bf16[4,272,1536]{2,1,0:T(8,128)(2,1)S(1)}, u32[]{:S(2)}, u32[]{:S(2)}) collective-permute-start(bf16[4,272,1536]{2,1,0:T(8,128)(2,1)} %get-tuple-element.145), channel_id=1, source_target_pairs={{0,1},{1,0},{2,3},{3,2},{4,5},{5,4},{6,7},{7,6},{8,9},{9,8},{10,11... | collective-permute-start | bytes 10027016 | tf_op jit(solution)/shard_map/ppermute | solution.py:63
  267.0 46.5 %collective-permute-start.36 = (bf16[4,256,1536]{2,1,0:T(8,128)(2,1)}, bf16[4,256,1536]{2,1,0:T(8,128)(2,1)}, u32[]{:S(2)}, u32[]{:S(2)}) collective-permute-start(bf16[4,256,1536]{2,1,0:T(8,128)(2,1)} %get-tuple-element.148), channel_id=1, source_target_pairs={{0,1},{1,0},{2,3},{3,2},{4,5},{5,4},{6,7},{7,6},{8,9},{9,8},{10,11... | collective-permute-start | bytes 9437192 | tf_op jit(solution)/shard_map/ppermute | solution.py:63
  271.4 23.2 %collective-permute-start.37 = (bf16[272,1536]{1,0:T(8,128)(2,1)}, bf16[272,1536]{1,0:T(8,128)(2,1)S(1)}, u32[]{:S(2)}, u32[]{:S(2)}) collective-permute-start(bf16[272,1536]{1,0:T(8,128)(2,1)} %get-tuple-element.287), channel_id=1, source_target_pairs={{0,2},{1,3},{2,4},{3,5},{4,6},{5,7},{6,0},{7,1},{8,10},{9,11},{10,... | collective-permute-start | bytes 2506760 | tf_op jit(solution)/shard_map/ppermute | solution.py:67
  288.6 24.1 %collective-permute-start.35 = (bf16[272,1536]{1,0:T(8,128)(2,1)S(1)}, bf16[272,1536]{1,0:T(8,128)(2,1)S(1)}, u32[]{:S(2)}, u32[]{:S(2)}) collective-permute-start(bf16[272,1536]{1,0:T(8,128)(2,1)S(1)} %get-tuple-element.289), channel_id=1, source_target_pairs={{0,6},{1,7},{2,0},{3,1},{4,2},{5,3},{6,4},{7,5},{8,14},{9,15},{10,... | collective-permute-start | bytes 2506760 | tf_op jit(solution)/shard_map/ppermute | solution.py:71
  294.8 35.2 %collective-permute-start.38 = (bf16[272,1536]{1,0:T(8,128)(2,1)S(1)}, bf16[272,1536]{1,0:T(8,128)(2,1)S(1)}, u32[]{:S(2)}, u32[]{:S(2)}) collective-permute-start(bf16[272,1536]{1,0:T(8,128)(2,1)S(1)} %add_convert_fusion.2), channel_id=1, source_target_pairs={{0,2},{1,3},{2,4},{3,5},{4,6},{5,7},{6,0},{7,1},{8,10},{9,11},{10,... | collective-permute-start | bytes 2506760 | tf_op jit(solution)/shard_map/ppermute | solution.py:67
  330.1 26.4 %collective-permute-start.39 = (bf16[256,1536]{1,0:T(8,128)(2,1)}, bf16[256,1536]{1,0:T(8,128)(2,1)}, u32[]{:S(2)}, u32[]{:S(2)}) collective-permute-start(bf16[256,1536]{1,0:T(8,128)(2,1)} %get-tuple-element.187), channel_id=1, source_target_pairs={{0,2},{1,3},{2,4},{3,5},{4,6},{5,7},{6,0},{7,1},{8,10},{9,11},{10,... | collective-permute-start | bytes 2359304 | tf_op jit(solution)/shard_map/ppermute | solution.py:67
  358.6 21.0 %collective-permute-start.46 = (bf16[256,1536]{1,0:T(8,128)(2,1)S(1)}, bf16[256,1536]{1,0:T(8,128)(2,1)S(1)}, u32[]{:S(2)}, u32[]{:S(2)}) collective-permute-start(bf16[256,1536]{1,0:T(8,128)(2,1)S(1)} %copy-done.13), channel_id=1, source_target_pairs={{0,6},{1,7},{2,0},{3,1},{4,2},{5,3},{6,4},{7,5},{8,14},{9,15},{10,... | collective-permute-start | bytes 2359304 | tf_op jit(solution)/shard_map/ppermute | solution.py:71
  361.6 34.7 %collective-permute-start.47 = (bf16[256,1536]{1,0:T(8,128)(2,1)S(1)}, bf16[256,1536]{1,0:T(8,128)(2,1)S(1)}, u32[]{:S(2)}, u32[]{:S(2)}) collective-permute-start(bf16[256,1536]{1,0:T(8,128)(2,1)S(1)} %add_convert_fusion.7), channel_id=1, source_target_pairs={{0,2},{1,3},{2,4},{3,5},{4,6},{5,7},{6,0},{7,1},{8,10},{9,11},{10,... | collective-permute-start | bytes 2359304 | tf_op jit(solution)/shard_map/ppermute | solution.py:67
  361.6 5.8 %collective-permute-start.52 = (bf16[2,2,48,1664]{3,2,1,0:T(8,128)(2,1)}, bf16[2,2,48,1664]{3,2,1,0:T(8,128)(2,1)S(1)}, u32[]{:S(2)}, u32[]{:S(2)}) collective-permute-start(bf16[2,2,48,1664]{3,2,1,0:T(8,128)(2,1)} %get-tuple-element.212), channel_id=1, source_target_pairs={{0,1},{1,0},{2,3},{3,2},{4,5},{5,4},{6,7},{7,6},{8,9},{9,8},{10,11... | collective-permute-start | bytes 1916936 | tf_op jit(solution)/shard_map/ppermute | solution.py:63
  364.8 31.4 %collective-permute-start.43 = (bf16[2,2,48,2176]{3,2,1,0:T(8,128)(2,1)S(1)}, bf16[2,2,48,2176]{3,2,1,0:T(8,128)(2,1)S(1)}, u32[]{:S(2)}, u32[]{:S(2)}) collective-permute-start(bf16[2,2,48,2176]{3,2,1,0:T(8,128)(2,1)S(1)} %add_convert_fusion), channel_id=1, source_target_pairs={{0,16},{8,24},{16,0},{24,8},{1,17},{9,25},{17,1},{25,9},{2,18},{10... | collective-permute-start | bytes 2506760 | tf_op jit(solution)/shard_map/ppermute | solution.py:59
  366.5 30.3 %collective-permute-start.41 = (bf16[2,2,48,2176]{3,2,1,0:T(8,128)(2,1)S(1)}, bf16[2,2,48,2176]{3,2,1,0:T(8,128)(2,1)S(1)}, u32[]{:S(2)}, u32[]{:S(2)}) collective-permute-start(bf16[2,2,48,2176]{3,2,1,0:T(8,128)(2,1)S(1)} %add_convert_fusion.1), channel_id=1, source_target_pairs={{0,8},{8,0},{16,24},{24,16},{1,9},{9,1},{17,25},{25,17},{2,10},{10... | collective-permute-start | bytes 2506760 | tf_op jit(solution)/shard_map/ppermute | solution.py:55
  367.4 32.3 %collective-permute-start.51 = (bf16[2,2,48,1664]{3,2,1,0:T(8,128)(2,1)S(1)}, bf16[2,2,48,1664]{3,2,1,0:T(8,128)(2,1)S(1)}, u32[]{:S(2)}, u32[]{:S(2)}) collective-permute-start(bf16[2,2,48,1664]{3,2,1,0:T(8,128)(2,1)S(1)} %copy-done.41), channel_id=1, source_target_pairs={{0,1},{1,0},{2,3},{3,2},{4,5},{5,4},{6,7},{7,6},{8,9},{9,8},{10,11... | collective-permute-start | bytes 1916936 | tf_op jit(solution)/shard_map/ppermute | solution.py:63
  379.5 45.3 %collective-permute-start.61 = (bf16[2,48,1664]{2,1,0:T(8,128)(2,1)}, bf16[2,48,1664]{2,1,0:T(8,128)(2,1)}, u32[]{:S(2)}, u32[]{:S(2)}) collective-permute-start(bf16[2,48,1664]{2,1,0:T(8,128)(2,1)} %get-tuple-element.221), channel_id=1, source_target_pairs={{0,1},{1,0},{2,3},{3,2},{4,5},{5,4},{6,7},{7,6},{8,9},{9,8},{10,11... | collective-permute-start | bytes 958472 | tf_op jit(solution)/shard_map/ppermute | solution.py:63
  396.3 56.3 %collective-permute-start.54 = (bf16[2,48,1664]{2,1,0:T(8,128)(2,1)}, bf16[2,48,1664]{2,1,0:T(8,128)(2,1)}, u32[]{:S(2)}, u32[]{:S(2)}) collective-permute-start(bf16[2,48,1664]{2,1,0:T(8,128)(2,1)} %get-tuple-element.216), channel_id=1, source_target_pairs={{0,1},{1,0},{2,3},{3,2},{4,5},{5,4},{6,7},{7,6},{8,9},{9,8},{10,11... | collective-permute-start | bytes 958472 | tf_op jit(solution)/shard_map/ppermute | solution.py:63
  396.3 10.8 %collective-permute-start.48 = (bf16[4,48,2176]{2,1,0:T(8,128)(2,1)}, bf16[4,48,2176]{2,1,0:T(8,128)(2,1)S(1)}, u32[]{:S(2)}, u32[]{:S(2)}) collective-permute-start(bf16[4,48,2176]{2,1,0:T(8,128)(2,1)} %get-tuple-element.200), channel_id=1, source_target_pairs={{0,1},{1,0},{2,3},{3,2},{4,5},{5,4},{6,7},{7,6},{8,9},{9,8},{10,11... | collective-permute-start | bytes 2506760 | tf_op jit(solution)/shard_map/ppermute | solution.py:63
  397.8 21.4 %collective-permute-start.57 = (bf16[2,48,2176]{2,1,0:T(8,128)(2,1)}, bf16[2,48,2176]{2,1,0:T(8,128)(2,1)}, u32[]{:S(2)}, u32[]{:S(2)}) collective-permute-start(bf16[2,48,2176]{2,1,0:T(8,128)(2,1)} %fusion.5), channel_id=1, source_target_pairs={{0,8},{8,0},{16,24},{24,16},{1,9},{9,1},{17,25},{25,17},{2,10},{10... | collective-permute-start | bytes 1253384 | tf_op jit(solution)/shard_map/ppermute | solution.py:55
  399.7 21.4 %collective-permute-start.49 = (bf16[2,48,2176]{2,1,0:T(8,128)(2,1)}, bf16[2,48,2176]{2,1,0:T(8,128)(2,1)}, u32[]{:S(2)}, u32[]{:S(2)}) collective-permute-start(bf16[2,48,2176]{2,1,0:T(8,128)(2,1)} %fusion.6), channel_id=1, source_target_pairs={{0,16},{8,24},{16,0},{24,8},{1,17},{9,25},{17,1},{25,9},{2,18},{10... | collective-permute-start | bytes 1253384 | tf_op jit(solution)/shard_map/ppermute | solution.py:59
  403.5 66.0 %all-to-all-start.1 = ((bf16[1,2,128,1536]{3,1,0,2:T(2,128)(2,1)}), bf16[1,2,128,1536]{3,1,0,2:T(2,128)(2,1)S(1)}, u32[]{:S(2)}, u32[]{:S(2)}) async-start(bf16[1,2,128,1536]{3,1,0,2:T(2,128)(2,1)} %copy.79), calls=%async_computation.1 | async-start | bytes 1572864 | tf_op jit(solution)/shard_map/all_to_all | solution.py:1111
  407.1 51.4 %collective-permute-start.50 = (bf16[4,48,1664]{2,1,0:T(8,128)(2,1)}, bf16[4,48,1664]{2,1,0:T(8,128)(2,1)S(1)}, u32[]{:S(2)}, u32[]{:S(2)}) collective-permute-start(bf16[4,48,1664]{2,1,0:T(8,128)(2,1)} %get-tuple-element.208), channel_id=1, source_target_pairs={{0,1},{1,0},{2,3},{3,2},{4,5},{5,4},{6,7},{7,6},{8,9},{9,8},{10,11... | collective-permute-start | bytes 1916936 | tf_op jit(solution)/shard_map/ppermute | solution.py:63
  419.2 30.5 %collective-permute-start.62 = (bf16[2,2,48,1664]{3,2,1,0:T(8,128)(2,1)}, bf16[2,2,48,1664]{3,2,1,0:T(8,128)(2,1)S(1)}, u32[]{:S(2)}, u32[]{:S(2)}) collective-permute-start(bf16[2,2,48,1664]{3,2,1,0:T(8,128)(2,1)} %add_convert_fusion.11), channel_id=1, source_target_pairs={{0,16},{8,24},{16,0},{24,8},{1,17},{9,25},{17,1},{25,9},{2,18},{10... | collective-permute-start | bytes 1916936 | tf_op jit(solution)/shard_map/ppermute | solution.py:59
  421.0 32.6 %collective-permute-start.53 = (bf16[2,2,48,1664]{3,2,1,0:T(8,128)(2,1)}, bf16[2,2,48,1664]{3,2,1,0:T(8,128)(2,1)S(1)}, u32[]{:S(2)}, u32[]{:S(2)}) collective-permute-start(bf16[2,2,48,1664]{3,2,1,0:T(8,128)(2,1)} %add_convert_fusion.12), channel_id=1, source_target_pairs={{0,8},{8,0},{16,24},{24,16},{1,9},{9,1},{17,25},{25,17},{2,10},{10... | collective-permute-start | bytes 1916936 | tf_op jit(solution)/shard_map/ppermute | solution.py:55
  424.8 40.6 %collective-permute-start.56 = (bf16[48,2176]{1,0:T(8,128)(2,1)S(1)}, bf16[48,2176]{1,0:T(8,128)(2,1)S(1)}, u32[]{:S(2)}, u32[]{:S(2)}) collective-permute-start(bf16[48,2176]{1,0:T(8,128)(2,1)S(1)} %get-tuple-element.299), channel_id=1, source_target_pairs={{0,6},{1,7},{2,0},{3,1},{4,2},{5,3},{6,4},{7,5},{8,14},{9,15},{10,... | collective-permute-start | bytes 626696 | tf_op jit(solution)/shard_map/ppermute | solution.py:71
  449.7 7.6 %collective-permute-start.58 = (bf16[48,2176]{1,0:T(8,128)(2,1)S(1)}, bf16[48,2176]{1,0:T(8,128)(2,1)S(1)}, u32[]{:S(2)}, u32[]{:S(2)}) collective-permute-start(bf16[48,2176]{1,0:T(8,128)(2,1)S(1)} %get-tuple-element.304), channel_id=1, source_target_pairs={{0,2},{1,3},{2,4},{3,5},{4,6},{5,7},{6,0},{7,1},{8,10},{9,11},{10,... | collective-permute-start | bytes 626696 | tf_op jit(solution)/shard_map/ppermute | solution.py:67
  452.6 7.7 %collective-permute-start.63 = (bf16[2,48,1664]{2,1,0:T(8,128)(2,1)S(1)}, bf16[2,48,1664]{2,1,0:T(8,128)(2,1)S(1)}, u32[]{:S(2)}, u32[]{:S(2)}) collective-permute-start(bf16[2,48,1664]{2,1,0:T(8,128)(2,1)S(1)} %fusion.10), channel_id=1, source_target_pairs={{0,8},{8,0},{16,24},{24,16},{1,9},{9,1},{17,25},{25,17},{2,10},{10... | collective-permute-start | bytes 958472 | tf_op jit(solution)/shard_map/ppermute | solution.py:55
  454.8 7.4 %collective-permute-start.55 = (bf16[2,48,1664]{2,1,0:T(8,128)(2,1)S(1)}, bf16[2,48,1664]{2,1,0:T(8,128)(2,1)S(1)}, u32[]{:S(2)}, u32[]{:S(2)}) collective-permute-start(bf16[2,48,1664]{2,1,0:T(8,128)(2,1)S(1)} %fusion.11), channel_id=1, source_target_pairs={{0,16},{8,24},{16,0},{24,8},{1,17},{9,25},{17,1},{25,9},{2,18},{10... | collective-permute-start | bytes 958472 | tf_op jit(solution)/shard_map/ppermute | solution.py:59
  458.4 9.0 %collective-permute-start.59 = (bf16[48,2176]{1,0:T(8,128)(2,1)S(1)}, bf16[48,2176]{1,0:T(8,128)(2,1)S(1)}, u32[]{:S(2)}, u32[]{:S(2)}) collective-permute-start(bf16[48,2176]{1,0:T(8,128)(2,1)S(1)} %add_convert_fusion.17), channel_id=1, source_target_pairs={{0,2},{1,3},{2,4},{3,5},{4,6},{5,7},{6,0},{7,1},{8,10},{9,11},{10,... | collective-permute-start | bytes 626696 | tf_op jit(solution)/shard_map/ppermute | solution.py:67
  462.6 16.4 %collective-permute-start.60 = (bf16[48,1664]{1,0:T(8,128)(2,1)S(1)}, bf16[48,1664]{1,0:T(8,128)(2,1)S(1)}, u32[]{:S(2)}, u32[]{:S(2)}) collective-permute-start(bf16[48,1664]{1,0:T(8,128)(2,1)S(1)} %get-tuple-element.301), channel_id=1, source_target_pairs={{0,6},{1,7},{2,0},{3,1},{4,2},{5,3},{6,4},{7,5},{8,14},{9,15},{10,... | collective-permute-start | bytes 479240 | tf_op jit(solution)/shard_map/ppermute | solution.py:71
  464.8 14.2 %collective-permute-start.64 = (bf16[48,1664]{1,0:T(8,128)(2,1)S(1)}, bf16[48,1664]{1,0:T(8,128)(2,1)S(1)}, u32[]{:S(2)}, u32[]{:S(2)}) collective-permute-start(bf16[48,1664]{1,0:T(8,128)(2,1)S(1)} %get-tuple-element.306), channel_id=1, source_target_pairs={{0,2},{1,3},{2,4},{3,5},{4,6},{5,7},{6,0},{7,1},{8,10},{9,11},{10,... | collective-permute-start | bytes 479240 | tf_op jit(solution)/shard_map/ppermute | solution.py:67
  464.8 14.2 %collective-permute-start.65 = (bf16[48,1664]{1,0:T(8,128)(2,1)S(1)}, bf16[48,1664]{1,0:T(8,128)(2,1)S(1)}, u32[]{:S(2)}, u32[]{:S(2)}) collective-permute-start(bf16[48,1664]{1,0:T(8,128)(2,1)S(1)} %get-tuple-element.305), channel_id=1, source_target_pairs={{0,4},{1,5},{2,6},{3,7},{4,0},{5,1},{6,2},{7,3},{8,12},{9,13},{10,... | collective-permute-start | bytes 479240 | tf_op jit(solution)/shard_map/ppermute | solution.py:988
  (52 other events, 670.3 us)
Sparse Core Ops, SparseCore 0:
  288.7 164.7 reduce-scatter.1
